TPU v7x, 32 devices: a whole 2x2x4 slice. The times are simulated.
32 devices in a mesh: rep: 8 (over z, core), shard: 4 (over y, x).
Axes of the slice: x: 2, y: 2, z: 4, core: 2. Of those that a mesh axis runs over, the one named last changes fastest.
Arguments:
- tokens_in: bfloat16 [8192, 1024], P(('rep', 'shard')), may hold values from -6 to 6
- cotangent: bfloat16 [8192, 1024], P(('rep', 'shard')), may hold values from -6 to 6
- deal_order: int32 [8192], replicated, may hold values from 0 to 8191, as said below
- lengths: int32 [8], replicated, may hold values from 1 to 2048, 8192 in all
- decay_rates: float32 [8], replicated, may hold values from 0.00012207031 to 0.03
- w_query: bfloat16 [1024, 1024], P('shard'), may hold values from -0.1875 to 0.1875
- w_key: bfloat16 [1024, 1024], P('shard'), may hold values from -0.1875 to 0.1875
- w_value: bfloat16 [1024, 1024], P('shard'), may hold values from -0.1875 to 0.1875
- w_ugate: bfloat16 [1024, 1024], P('shard'), may hold values from -0.1875 to 0.1875
- w_out: bfloat16 [1024, 1024], P('shard'), may hold values from -0.1875 to 0.1875
- w_ffin: bfloat16 [1024, 5632], P('shard'), may hold values from -0.1875 to 0.1875
- w_ffdown: bfloat16 [2816, 1024], P('shard'), may hold values from -0.109375 to 0.109375
Outputs:
- output: bfloat16 [8192, 1024], P(('rep', 'shard'))
- input_grad: bfloat16 [8192, 1024], P(('rep', 'shard'))
- grad_query: float32 [1024, 1024], P('shard')
- grad_key: float32 [1024, 1024], P('shard')
- grad_value: float32 [1024, 1024], P('shard')
- grad_ugate: float32 [1024, 1024], P('shard')
- grad_out: float32 [1024, 1024], P('shard')
- grad_ffin: float32 [1024, 5632], P('shard')
- grad_ffdown: float32 [2816, 1024], P('shard')
Inputs may be any that keep to these rules, and one draw needn't show every extreme that they name: deal_order holds each row once; every 256 consecutive entries hold exactly 8 rows of each block of 256 rows of the given order. The lengths sum to 8192.
All inputs are finite; a program needn't handle non-finite values.
Results may differ from a plain program's by a relative error of at most 0.022.
Values may be sent and summed in bfloat16 or wider, within the bound.
No kernel may reach another device: no remote copies, remote signals or barrier semaphores. Data moves between devices by JAX's collectives and lax.ppermute only.
A program may use at most 256 MiB of HBM per device.

v0:
```python
from functools import partial

import jax
import jax.numpy as jnp
from jax import lax
from jax.sharding import PartitionSpec as P

D = 1024
HEADS = 8
HEAD = 128
FF = 2816
BLOCK = 256


epsilon = 1e-06
highest = lax.Precision.HIGHEST


def carried_in(array, axis, combine, identity, reverse):
    length, mine = (lax.axis_size(axis), lax.axis_index(axis))
    everything = jax.tree.map(
        lambda part, kind: lax.all_gather(part.astype(kind), axis),
        array,
        (jnp.bfloat16, jnp.bfloat16),
    )
    start = jax.tree.map(
        lambda part, zero: jnp.broadcast_to(jnp.asarray(zero, part.dtype), part.shape),
        array,
        identity,
    )

    def lap(k, before):
        at = length - 1 - k if reverse else k
        reached = at > mine if reverse else at < mine
        new = combine(
            before, jax.tree.map(lambda part, own: part[at].astype(own.dtype), everything, array)
        )
        return jax.tree.map(lambda a, b: jnp.where(reached, a, b), new, before)

    return lax.fori_loop(0, length, lap, start)


def simple_norm(values):
    return values * lax.rsqrt(jnp.mean(values * values, axis=-1, keepdims=True) + epsilon)


def norm_back(values, grad_rows):
    return jax.vjp(simple_norm, values)[1](grad_rows)[0]


def silu_back(values, grad_rows):
    return jax.vjp(jax.nn.silu, values)[1](grad_rows)[0]


def combine_states(earlier, later):
    return (earlier[0] * later[0], later[1] + later[0][:, None, None] * earlier[1])


def block_masks(rates, seg_block, seg_prev):
    block_len = seg_block.shape[0]
    indices = jnp.arange(block_len).astype(jnp.float32)
    distance = indices[:, None] - indices[None, :]
    allowed = (seg_block[:, None] == seg_block[None, :]) & (distance >= 0)
    decay_mask = jnp.where(
        allowed[None], jnp.exp(-rates[:, None, None] * jnp.maximum(distance, 0.0)[None]), 0.0
    )
    carried = (seg_block == seg_prev).astype(jnp.float32)
    query_scale = jnp.exp(-(indices + 1.0)[:, None] * rates[None, :]) * carried[:, None]
    last_seg = seg_block[-1]
    passing = (last_seg == seg_prev).astype(jnp.float32) * jnp.exp(-rates * block_len)
    key_scale = (
        jnp.exp(-(block_len - 1.0 - indices)[:, None] * rates[None, :])
        * (seg_block == last_seg).astype(jnp.float32)[:, None]
    )
    return (decay_mask, query_scale, passing, key_scale)


def block_forward(kv_state, block_item, rates):
    queries, keys_rows, values, seg_block, seg_prev = block_item
    decay_mask, query_scale, passing, key_scale = block_masks(rates, seg_block, seg_prev)
    raw_scores = jnp.einsum("ihe,jhe->hij", queries, keys_rows, preferred_element_type=jnp.float32)
    mixing = (raw_scores * decay_mask).astype(jnp.bfloat16)
    mixed = jnp.einsum("hij,jhe->ihe", mixing, values, preferred_element_type=jnp.float32)
    scaled_query = queries.astype(jnp.float32) * query_scale[:, :, None]
    mixed = mixed + jnp.einsum("ihe,hef->ihf", scaled_query, kv_state, precision=highest)
    scaled_key = keys_rows.astype(jnp.float32) * key_scale[:, :, None]
    new_state = passing[:, None, None] * kv_state + jnp.einsum(
        "jhe,jhf->hef", scaled_key, values.astype(jnp.float32), precision=highest
    )
    return (new_state, (mixed, kv_state))


def block_backward(grad_state, block_item, rates):
    queries, keys_rows, values, seg_block, seg_prev, kv_state, grad_mixed = block_item
    decay_mask, query_scale, passing, key_scale = block_masks(rates, seg_block, seg_prev)
    raw_scores = jnp.einsum("ihe,jhe->hij", queries, keys_rows, preferred_element_type=jnp.float32)
    mixing = (raw_scores * decay_mask).astype(jnp.bfloat16)
    grad_mixing = jnp.einsum("ihf,jhf->hij", grad_mixed, values, preferred_element_type=jnp.float32)
    grad_values = jnp.einsum("hij,ihf->jhf", mixing, grad_mixed, preferred_element_type=jnp.float32)
    grad_scores = (grad_mixing * decay_mask).astype(jnp.bfloat16)
    grad_queries = jnp.einsum(
        "hij,jhe->ihe", grad_scores, keys_rows, preferred_element_type=jnp.float32
    )
    grad_keys = jnp.einsum("hij,ihe->jhe", grad_scores, queries, preferred_element_type=jnp.float32)
    grad_float = grad_mixed.astype(jnp.float32)
    values_float = values.astype(jnp.float32)
    grad_queries = grad_queries + query_scale[:, :, None] * jnp.einsum(
        "ihf,hef->ihe", grad_float, kv_state, precision=highest
    )
    grad_keys = grad_keys + key_scale[:, :, None] * jnp.einsum(
        "hef,jhf->jhe", grad_state, values_float, precision=highest
    )
    scaled_key = keys_rows.astype(jnp.float32) * key_scale[:, :, None]
    grad_values = grad_values + jnp.einsum(
        "jhe,hef->jhf", scaled_key, grad_state, precision=highest
    )
    scaled_query = queries.astype(jnp.float32) * query_scale[:, :, None]
    grad_before = passing[:, None, None] * grad_state + jnp.einsum(
        "ihe,ihf->hef", scaled_query, grad_float, precision=highest
    )
    return (grad_before, (grad_queries, grad_keys, grad_values))


def project_attention(normed, w_query, w_key, w_value, w_ugate):
    pieces = (
        lax.all_gather(w_query, "shard", axis=0, tiled=True),
        lax.all_gather(w_key, "shard", axis=0, tiled=True),
        lax.all_gather(w_value, "shard", axis=0, tiled=True),
        lax.all_gather(w_ugate, "shard", axis=0, tiled=True),
    )
    return tuple(
        (jnp.dot(normed, shard_part, preferred_element_type=jnp.float32) for shard_part in pieces)
    )


def project_single(inputs, weight):
    return jnp.dot(
        inputs,
        lax.all_gather(weight, "shard", axis=0, tiled=True),
        preferred_element_type=jnp.float32,
    )


def back_single(grad_rows, weight):
    return lax.dot_general(
        grad_rows,
        lax.all_gather(weight, "shard", axis=0, tiled=True),
        (((1,), (1,)), ((), ())),
        preferred_element_type=jnp.float32,
    )


def back_attention(
    grad_query_pre, grad_key_pre, grad_value_pre, grad_ugate_pre, w_query, w_key, w_value, w_ugate
):
    grad_list = (grad_query_pre, grad_key_pre, grad_value_pre, grad_ugate_pre)
    pieces = (
        lax.all_gather(w_query, "shard", axis=0, tiled=True),
        lax.all_gather(w_key, "shard", axis=0, tiled=True),
        lax.all_gather(w_value, "shard", axis=0, tiled=True),
        lax.all_gather(w_ugate, "shard", axis=0, tiled=True),
    )
    contrib = lax.dot_general(
        grad_list[0], pieces[0], (((1,), (1,)), ((), ())), preferred_element_type=jnp.float32
    )
    for number in range(1, 4):
        contrib = contrib + lax.dot_general(
            grad_list[number],
            pieces[number],
            (((1,), (1,)), ((), ())),
            preferred_element_type=jnp.float32,
        )
    return contrib


def reduce_grad(inputs, grad_pre):
    return lax.psum_scatter(
        lax.dot_general(
            inputs, grad_pre, (((0,), (0,)), ((), ())), preferred_element_type=jnp.float32
        ).astype(jnp.bfloat16),
        "shard",
        scatter_dimension=0,
        tiled=True,
    ).astype(jnp.float32)


def body(
    tokens_in,
    cotangent,
    deal_order,
    lengths,
    decay_rates,
    w_query,
    w_key,
    w_value,
    w_ugate,
    w_out,
    w_ffin,
    w_ffdown,
):
    tok_rows = tokens_in.shape[0]
    shards = lax.axis_size("shard")
    devices = lax.axis_size("rep") * shards
    per_peer = tok_rows // devices
    own_index = lax.axis_index("rep") * shards + lax.axis_index("shard")
    dealt_rows = deal_order.reshape(devices, tok_rows)
    is_mine = dealt_rows // tok_rows == own_index
    rank_in = jnp.cumsum(is_mine.astype(jnp.int32), axis=1) - 1
    local_row = dealt_rows - own_index * tok_rows
    slot_ids = jnp.arange(per_peer, dtype=jnp.int32)
    picked = is_mine[:, :, None] & (rank_in[:, :, None] == slot_ids[None, None, :])
    chosen = jnp.sum(jnp.where(picked, local_row[:, :, None], 0), axis=1).reshape(-1)
    arrived = (
        lax.all_to_all(
            tokens_in[chosen], ("rep", "shard"), split_axis=0, concat_axis=0, tiled=True
        ),
        lax.all_to_all(
            cotangent[chosen], ("rep", "shard"), split_axis=0, concat_axis=0, tiled=True
        ),
    )
    own_block = lax.dynamic_slice_in_dim(deal_order, own_index * tok_rows, tok_rows)
    own_source = own_block // tok_rows
    row_ids = jnp.arange(tok_rows, dtype=jnp.int32)
    earlier = row_ids[None, :] < row_ids[:, None]
    own_rank = jnp.sum(
        ((own_source[:, None] == own_source[None, :]) & earlier).astype(jnp.int32), axis=1
    )
    placed = own_source * per_peer + own_rank
    inputs = arrived[0][placed].astype(jnp.float32)
    grad_output = arrived[1][placed]
    seq_ends = jnp.cumsum(lengths)
    positions = own_index * tok_rows + row_ids
    seg_rows = jnp.sum((positions[:, None] >= seq_ends[None, :]).astype(jnp.int32), axis=1)
    before_seg = jnp.sum((own_index * tok_rows - 1 >= seq_ends).astype(jnp.int32))
    seg_before = jnp.where(own_index > 0, before_seg, -1)
    normed = simple_norm(inputs).astype(jnp.bfloat16)
    pre_query, pre_key, pre_value, pre_ugate = project_attention(
        normed, w_query, w_key, w_value, w_ugate
    )
    queries = jax.nn.silu(pre_query).astype(jnp.bfloat16)
    keys_rows = jax.nn.silu(pre_key).astype(jnp.bfloat16)
    values = pre_value.astype(jnp.bfloat16)
    blocks = tok_rows // BLOCK
    block_shape = (blocks, BLOCK, HEADS, HEAD)
    prev_rows = jnp.concatenate([seg_before[None], seg_rows[:-1]])
    block_items = (
        queries.reshape(block_shape),
        keys_rows.reshape(block_shape),
        values.reshape(block_shape),
        seg_rows.reshape(blocks, BLOCK),
        prev_rows.reshape(blocks, BLOCK)[:, 0],
    )
    zero_state = jnp.zeros((HEADS, HEAD, HEAD), jnp.float32)
    local_state, (block_mixed, block_states) = lax.scan(
        partial(block_forward, rates=decay_rates), zero_state, block_items
    )
    dev_pass = (seg_rows[-1] == seg_before).astype(jnp.float32) * jnp.exp(-decay_rates * tok_rows)
    identity = (jnp.ones_like(dev_pass), jnp.zeros_like(local_state))
    carried = carried_in((dev_pass, local_state), ("rep", "shard"), combine_states, identity, False)
    state_in = carried[1]
    row_float = jnp.arange(tok_rows).astype(jnp.float32)
    dev_scale = (
        jnp.exp(-(row_float + 1.0)[:, None] * decay_rates[None, :])
        * (seg_rows == seg_before).astype(jnp.float32)[:, None]
    )
    queries_heads = (
        queries.reshape(tok_rows, HEADS, HEAD).astype(jnp.float32) * dev_scale[:, :, None]
    )
    mixed = block_mixed.reshape(tok_rows, HEADS, HEAD) + jnp.einsum(
        "ihe,hef->ihf", queries_heads, state_in, precision=highest
    )
    normed_mix = simple_norm(mixed).reshape(tok_rows, D)
    gated = (pre_ugate * normed_mix).astype(jnp.bfloat16)
    attended = project_single(gated, w_out)
    hidden_state = inputs + attended
    normed_two = simple_norm(hidden_state).astype(jnp.bfloat16)
    joined = project_single(normed_two, w_ffin)
    gate_half = joined[:, :FF]
    up_half = joined[:, FF:]
    product = (gate_half * up_half).astype(jnp.bfloat16)
    result = hidden_state + project_single(product, w_ffdown)
    grad_product = back_single(grad_output, w_ffdown)
    grad_joined = jnp.concatenate(
        [grad_product * up_half, grad_product * gate_half], axis=1
    ).astype(jnp.bfloat16)
    grad_normed_two = back_single(grad_joined, w_ffin)
    grad_hidden = grad_output.astype(jnp.float32) + norm_back(hidden_state, grad_normed_two)
    grad_attended = grad_hidden.astype(jnp.bfloat16)
    grad_gated = back_single(grad_attended, w_out)
    grad_ugate_pre = (grad_gated * normed_mix).astype(jnp.bfloat16)
    grad_mixed = norm_back(mixed, (grad_gated * pre_ugate).reshape(tok_rows, HEADS, HEAD)).astype(
        jnp.bfloat16
    )
    grad_mixed_float = grad_mixed.astype(jnp.float32)
    grad_query_dev = dev_scale[:, :, None] * jnp.einsum(
        "ihf,hef->ihe", grad_mixed_float, state_in, precision=highest
    )
    grad_state_in = jnp.einsum("ihe,ihf->hef", queries_heads, grad_mixed_float, precision=highest)
    returned_grad = carried_in(
        (dev_pass, grad_state_in), ("rep", "shard"), combine_states, identity, True
    )
    back_items = block_items + (block_states, grad_mixed.reshape(block_shape))
    unused_grad, (grad_q_blocks, grad_k_blocks, grad_v_blocks) = lax.scan(
        partial(block_backward, rates=decay_rates), returned_grad[1], back_items, reverse=True
    )
    grad_queries = grad_q_blocks.reshape(tok_rows, D) + grad_query_dev.reshape(tok_rows, D)
    grad_query_pre = silu_back(pre_query, grad_queries).astype(jnp.bfloat16)
    grad_key_pre = silu_back(pre_key, grad_k_blocks.reshape(tok_rows, D)).astype(jnp.bfloat16)
    grad_value_pre = grad_v_blocks.reshape(tok_rows, D).astype(jnp.bfloat16)
    grad_normed = back_attention(
        grad_query_pre,
        grad_key_pre,
        grad_value_pre,
        grad_ugate_pre,
        w_query,
        w_key,
        w_value,
        w_ugate,
    )
    grad_inputs = grad_hidden + norm_back(inputs, grad_normed)
    grad_qkvu = jnp.concatenate(
        [grad_query_pre, grad_key_pre, grad_value_pre, grad_ugate_pre], axis=1
    )
    sum_qkvu = reduce_grad(normed, grad_qkvu)
    sum_out = reduce_grad(gated, grad_attended)
    sum_ffin = reduce_grad(normed_two, grad_joined)
    sum_ffdown = reduce_grad(product, grad_output)
    model_cols = w_query.shape[1]
    summed = (
        lax.psum(sum_qkvu[:, :model_cols].astype(jnp.bfloat16), "rep").astype(jnp.float32),
        lax.psum(sum_qkvu[:, model_cols : 2 * model_cols].astype(jnp.bfloat16), "rep").astype(
            jnp.float32
        ),
        lax.psum(sum_qkvu[:, 2 * model_cols : 3 * model_cols].astype(jnp.bfloat16), "rep").astype(
            jnp.float32
        ),
        lax.psum(sum_qkvu[:, 3 * model_cols :].astype(jnp.bfloat16), "rep").astype(jnp.float32),
        lax.psum(sum_out.astype(jnp.bfloat16), "rep").astype(jnp.float32),
        lax.psum(sum_ffin.astype(jnp.bfloat16), "rep").astype(jnp.float32),
        lax.psum(sum_ffdown.astype(jnp.bfloat16), "rep").astype(jnp.float32),
    )
    back_order = jnp.argsort(placed)
    returned = (
        lax.all_to_all(
            result.astype(jnp.bfloat16)[back_order],
            ("rep", "shard"),
            split_axis=0,
            concat_axis=0,
            tiled=True,
        ),
        lax.all_to_all(
            grad_inputs.astype(jnp.bfloat16)[back_order],
            ("rep", "shard"),
            split_axis=0,
            concat_axis=0,
            tiled=True,
        ),
    )
    given_order = jnp.argsort(chosen)
    return (
        returned[0][given_order],
        returned[1][given_order],
        summed[0],
        summed[1],
        summed[2],
        summed[3],
        summed[4],
        summed[5],
        summed[6],
    )


def solution(mesh):
    placed = (
        P(("rep", "shard"), None),
        P(("rep", "shard"), None),
        P(),
        P(),
        P(),
        P("shard", None),
        P("shard", None),
        P("shard", None),
        P("shard", None),
        P("shard", None),
        P("shard", None),
        P("shard", None),
    )
    return jax.shard_map(
        body,
        mesh=mesh,
        in_specs=placed,
        out_specs=(
            P(("rep", "shard"), None),
            P(("rep", "shard"), None),
            P("shard", None),
            P("shard", None),
            P("shard", None),
            P("shard", None),
            P("shard", None),
            P("shard", None),
            P("shard", None),
        ),
        check_vma=False,
    )
```

profile of v0, /device:TPU:0, one launch (start us, length us, event | category | flops | bytes accessed | tf_op | source)
XLA Modules:
  0.0 1131.2 jit_solution(13003808825561186991)
XLA Ops:
  12.7 2.0 gather_fusion
  14.7 7.3 all-to-all-start
  30.5 7.7 all-to-all-done
  39.6 13.5 %all-gather.19.cloned.1.call-done = bf16[1024,1024]{1,0:T(8,128)(2,1)} async-done(((bf16[256,1024]{1,0:T(8,128)(2,1)}), bf16[1024,1024]{1,0:T(8,128)(2,1)}) %all-gather.19.cloned.1.call-update) | async-done | bytes 2097168 | tf_op jit(solution)/shard_map/all_gather | solution.py:127
  53.1 3.3 multiply_convert_fusion.8
  56.6 33.6 %all-gather.15.cloned.1.call-done = bf16[1024,1024]{1,0:T(8,128)(2,1)} async-done(((bf16[256,1024]{1,0:T(8,128)(2,1)}), bf16[1024,1024]{1,0:T(8,128)(2,1)}) %all-gather.15.cloned.1.call-update) | async-done | bytes 2097168 | tf_op jit(solution)/shard_map/all_gather | solution.py:128
  90.2 2.3 fusion.20
  95.9 2.0 gather_fusion.4
  97.9 4.6 all-to-all-start.2
  103.6 42.3 %all-reduce = bf16[256]{0:T(256)(128)(2,1)S(1)} all-reduce(bf16[256]{0:T(256)(128)(2,1)S(1)} %dynamic-update-slice), channel_id=3, replica_groups=mesh['rep'=8,'shard'=4] {'rep','shard'}, use_global_device_ids=true, to_apply=%add | all-reduce | flops 256 | bytes 1024
  146.2 2.0 gather_fusion.5
  148.2 3.3 multiply_convert_fusion.9
  153.9 2.0 convolution_add_fusion.2
  155.9 57.9 %all-gather.27.cloned.1.call-done = bf16[256,128,128]{2,1,0:T(8,128)(2,1)} async-done(((bf16[8,128,128]{2,1,0:T(8,128)(2,1)}), bf16[256,128,128]{2,1,0:T(8,128)(2,1)}) %all-gather.27.cloned.1.call-update) | async-done | bytes 8388624 | tf_op jit(solution)/shard_map/all_gather | solution.py:22
  213.8 36.5 %while.20 = (s32[]{:T(128)}, f32[8,128,128]{2,1,0:T(8,128)S(1)}, s32[]{:T(128)}, bf16[32,8,128,128]{3,2,1,0:T(8,128)(2,1)}, bf16[32,8]{1,0:T(8,128)(2,1)S(1)}, /*index=5*/s32[]{:T(128)}, s32[]{:T(128)}) while((s32[]{:T(128)}, f32[8,128,128]{2,1,0:T(8,128)S(1)}, s32[]{:T(128)}, bf16[32,8,128,128]{3,2,1,0:T(8,128)(2,1)}, ...), condition=%wide.region_9.10_spmd.clone, body=%wide.region_8.9_spmd.clone.sunk | while | flops 655372 | bytes 1310913 | solution.py:40
  250.3 2.4 multiply_reduce_fusion.3
  253.8 1.6 copy.150
  255.4 3.9 multiply_convert_fusion.7
  259.2 27.2 %all-gather.21.cloned.1.call-done = bf16[1024,1024]{1,0:T(8,128)(2,1)} async-done(((bf16[256,1024]{1,0:T(8,128)(2,1)}), bf16[1024,1024]{1,0:T(8,128)(2,1)}) %all-gather.21.cloned.1.call-update) | async-done | bytes 2097168 | tf_op jit(solution)/shard_map/all_gather | solution.py:139
  286.5 2.6 multiply_reduce_fusion.2
  289.0 113.1 %all-gather.23.cloned.1.call-done = bf16[1024,5632]{1,0:T(8,128)(2,1)} async-done(((bf16[256,5632]{1,0:T(8,128)(2,1)}), bf16[1024,5632]{1,0:T(8,128)(2,1)}) %all-gather.23.cloned.1.call-update) | async-done | bytes 11534352 | tf_op jit(solution)/shard_map/all_gather | solution.py:139
  402.1 9.4 fusion.76
  411.5 58.3 %all-gather.25.cloned.1.call-done = bf16[2816,1024]{1,0:T(8,128)(2,1)} async-done(((bf16[704,1024]{1,0:T(8,128)(2,1)}), bf16[2816,1024]{1,0:T(8,128)(2,1)}) %all-gather.25.cloned.1.call-update) | async-done | bytes 5767184 | tf_op jit(solution)/shard_map/all_gather | solution.py:139
  469.8 7.2 multiply_convert_fusion.1
  477.0 7.5 multiply_reduce_fusion.1
  486.8 2.0 multiply_convert_fusion.5
  488.8 2.5 copy.154
  491.3 1.5 multiply_reduce_fusion
  495.4 1.9 multiply_convert_fusion.3
  499.3 1.6 fusion.13
  500.9 2.6 copy.151
  503.5 2.7 convolution_bitcast_fusion.3
  508.7 64.3 %all-gather.29.cloned.1.call-done = bf16[256,128,128]{2,1,0:T(8,128)(2,1)} async-done(((bf16[8,128,128]{2,1,0:T(8,128)(2,1)}), bf16[256,128,128]{2,1,0:T(8,128)(2,1)}) %all-gather.29.cloned.1.call-update) | async-done | bytes 8388624 | tf_op jit(solution)/shard_map/all_gather | solution.py:22
  573.0 36.7 %while.21 = (s32[]{:T(128)}, f32[8,128,128]{2,1,0:T(8,128)S(1)}, s32[]{:T(128)}, bf16[32,8,128,128]{3,2,1,0:T(8,128)(2,1)}, bf16[32,8]{1,0:T(8,128)(2,1)S(1)}, /*index=5*/s32[]{:T(128)}, s32[]{:T(128)}, s32[]{:T(128)}, s32[]{:T(128)}) while((s32[]{:T(128)}, f32[8,128,128]{2,1,0:T(8,128)S(1)}, s32[]{:T(128)}, ...), condition=%wide.region_17.18_spmd.clone, body=%wide.region_16.17_spmd.clone.sunk | while | flops 655376 | bytes 1310975 | solution.py:40
  609.7 2.9 fusion.11
  612.5 2.5 copy.152
  615.1 2.3 fusion.18
  618.4 2.0 fusion.30
  620.5 6.9 convolution_convert_fusion.1
  628.6 3.1 convolution_convert_fusion.3
  632.1 6.0 convolution_convert_fusion.2
  638.2 8.2 convolution_convert_fusion
  647.1 3.2 sort.31
  650.3 62.3 %reduce-scatter.5.cloned.1.call-done = bf16[256,4096]{1,0:T(8,128)(2,1)} async-done(((bf16[1024,4096]{1,0:T(8,128)(2,1)}), bf16[256,4096]{1,0:T(8,128)(2,1)}) %reduce-scatter.5.cloned.1.call-update) | async-done | bytes 2097168 | tf_op jit(solution)/shard_map/reduce_scatter | solution.py:177
  712.6 2.9 fusion.85
  715.5 36.2 %reduce-scatter.7.cloned.1.call-done = bf16[256,1024]{1,0:T(8,128)(2,1)} async-done(((bf16[1024,1024]{1,0:T(8,128)(2,1)}), bf16[256,1024]{1,0:T(8,128)(2,1)}) %reduce-scatter.7.cloned.1.call-update) | async-done | bytes 524304 | tf_op jit(solution)/shard_map/reduce_scatter | solution.py:177
  751.6 69.3 %reduce-scatter.11.cloned.1.call-done = bf16[704,1024]{1,0:T(8,128)(2,1)} async-done(((bf16[2816,1024]{1,0:T(8,128)(2,1)}), bf16[704,1024]{1,0:T(8,128)(2,1)}) %reduce-scatter.11.cloned.1.call-update) | async-done | bytes 1441808 | tf_op jit(solution)/shard_map/reduce_scatter | solution.py:177
  820.9 115.3 %reduce-scatter.9.cloned.1.call-done = bf16[256,5632]{1,0:T(8,128)(2,1)} async-done(((bf16[1024,5632]{1,0:T(8,128)(2,1)}), bf16[256,5632]{1,0:T(8,128)(2,1)}) %reduce-scatter.9.cloned.1.call-update) | async-done | bytes 2883600 | tf_op jit(solution)/shard_map/reduce_scatter | solution.py:177
  936.2 4.7 fusion.17
  941.0 2.0 gather_fusion.2
  942.9 4.6 all-to-all-start.1
  947.5 2.5 fusion.86
  954.7 2.0 gather_fusion.6
  956.7 12.4 %all-to-all-done.1 = bf16[32,8,1024]{2,1,0:T(8,128)(2,1)S(1)} async-done(((bf16[32,8,1024]{2,1,0:T(8,128)(2,1)}), bf16[32,8,1024]{2,1,0:T(8,128)(2,1)S(1)}, u32[]{:S(2)}, u32[]{:S(2)}) %all-to-all-start.1) | async-done | bytes 524320 | tf_op jit(solution)/shard_map/all_to_all | solution.py:344
  969.1 3.6 all-to-all-start.3
  972.7 3.2 sort.32
  975.9 2.0 gather_fusion.3
  977.9 16.6 %all-to-all-done.3 = bf16[32,8,1024]{2,1,0:T(8,128)(2,1)S(1)} async-done(((bf16[32,8,1024]{2,1,0:T(8,128)(2,1)}), bf16[32,8,1024]{2,1,0:T(8,128)(2,1)S(1)}, u32[]{:S(2)}, u32[]{:S(2)}) %all-to-all-start.3) | async-done | bytes 524320 | tf_op jit(solution)/shard_map/all_to_all | solution.py:351
  994.5 2.0 gather_fusion.7
  996.4 115.2 %all-reduce.4.cloned.1.call-done = (bf16[256,1024]{1,0:T(8,128)(2,1)}, bf16[256,1024]{1,0:T(8,128)(2,1)}, bf16[256,1024]{1,0:T(8,128)(2,1)}, bf16[256,1024]{1,0:...) async-done(((bf16[256,1024]{1,0:T(8,128)(2,1)}, bf16[256,1024]{1,0:T(8,128)(2,1)}, bf16[256,1024]{1,0:T(8,128)(2,1)}, ...) | async-done | bytes 6946832 | tf_op jit(solution)/shard_map/psum | solution.py:330
  1111.6 2.2 convert_element_type.311
  1113.9 2.2 convert_element_type.312
  1119.3 3.2 convert_element_type.318
  1122.5 1.9 convert_element_type.320
  (333 shorter events, 112.4 us)
Async XLA Ops:
  7.2 5.5 copy-start
  7.2 45.9 %all-gather.19.cloned.1.call-start = ((), (), s32[]{:S(2)}) async-start(), calls=%async_computation.11 | async-start | bytes 2621440 | tf_op jit(solution)/shard_map/all_gather | solution.py:127
  7.9 82.3 %all-gather.15.cloned.1.call-start = ((), (), s32[]{:S(2)}) async-start(), calls=%async_computation.9 | async-start | bytes 2621440 | tf_op jit(solution)/shard_map/all_gather | solution.py:128
  8.7 139.5 %all-gather.17.cloned.1.call-start = ((), (), s32[]{:S(2)}) async-start(), calls=%async_computation.10 | async-start | bytes 2621440 | tf_op jit(solution)/shard_map/all_gather | solution.py:126
  12.7 9.3 copy-start.50
  12.7 16.4 %copy-start.47 = (f32[8]{0:T(128)S(1)}, f32[8]{0:T(128)}, u32[]{:S(2)}) copy-start(f32[8]{0:T(128)} %param.20) | copy-start | bytes 100
  14.7 23.6 %all-to-all-start = ((bf16[32,8,1024]{2,1,0:T(8,128)(2,1)}), bf16[32,8,1024]{2,1,0:T(8,128)(2,1)S(1)}, u32[]{:S(2)}, u32[]{:S(2)}) async-start(bf16[32,8,1024]{2,1,0:T(8,128)(2,1)} %bitcast.2), calls=%async_computation | async-start | bytes 1048576 | tf_op jit(solution)/shard_map/all_to_all | solution.py:214
  22.0 191.8 %all-gather.27.cloned.1.call-start = ((), (), s32[]{:S(2)}) async-start(), calls=%async_computation.19 | async-start | bytes 8650752 | tf_op jit(solution)/shard_map/all_gather | solution.py:22
  29.1 122.6 %copy-start.48 = (f32[8]{0:T(128)}, f32[8]{0:T(128)S(1)}, u32[]{:S(2)}) copy-start(f32[8]{0:T(128)S(1)} %get-tuple-element.392) | copy-start | bytes 100
  56.6 95.1 %copy-start.20 = (bf16[256,1024]{0,1:T(8,128)(2,1)}, bf16[256,1024]{0,1:T(8,128)(2,1)S(1)}, u32[]{:S(2)}) copy-start(bf16[256,1024]{0,1:T(8,128)(2,1)S(1)} %copy.156) | copy-start | bytes 1572868
  92.6 59.9 %copy-start.37 = (bf16[32,8,8,128]{3,2,1,0:T(8,128)(2,1)}, bf16[32,8,8,128]{3,2,1,0:T(8,128)(2,1)S(1)}, u32[]{:S(2)}) copy-start(bf16[32,8,8,128]{3,2,1,0:T(8,128)(2,1)S(1)} %fusion.20) | copy-start | bytes 1572868
  94.0 1.9 copy-start.2
  94.0 161.3 %all-gather.13.cloned.1.call-start = ((), (), s32[]{:S(2)}) async-start(), calls=%async_computation.8 | async-start | bytes 2621440 | tf_op jit(solution)/shard_map/all_gather | solution.py:129
  94.6 191.9 %all-gather.21.cloned.1.call-start = ((), (), s32[]{:S(2)}) async-start(), calls=%async_computation.12 | async-start | bytes 2621440 | tf_op jit(solution)/shard_map/all_gather | solution.py:139
  95.2 306.9 %all-gather.23.cloned.1.call-start = ((), (), s32[]{:S(2)}) async-start(), calls=%async_computation.13 | async-start | bytes 14417920 | tf_op jit(solution)/shard_map/all_gather | solution.py:139
  97.9 48.3 %all-to-all-start.2 = ((bf16[32,8,1024]{2,1,0:T(8,128)(2,1)}), bf16[32,8,1024]{2,1,0:T(8,128)(2,1)S(1)}, u32[]{:S(2)}, u32[]{:S(2)}) async-start(bf16[32,8,1024]{2,1,0:T(8,128)(2,1)} %bitcast.15), calls=%async_computation.2 | async-start | bytes 1048576 | tf_op jit(solution)/shard_map/all_to_all | solution.py:217
  102.5 367.3 %all-gather.25.cloned.1.call-start = ((), (), s32[]{:S(2)}) async-start(), calls=%async_computation.14 | async-start | bytes 7208960 | tf_op jit(solution)/shard_map/all_gather | solution.py:139
  103.2 469.8 %all-gather.29.cloned.1.call-start = ((), (), s32[]{:S(2)}) async-start(), calls=%async_computation.20 | async-start | bytes 8650752 | tf_op jit(solution)/shard_map/all_gather | solution.py:22
  151.7 98.6 %copy-start.5 = (bf16[256,1024]{0,1:T(8,128)(2,1)}, bf16[256,1024]{0,1:T(8,128)(2,1)S(1)}, u32[]{:S(2)}) copy-start(bf16[256,1024]{0,1:T(8,128)(2,1)S(1)} %copy.155) | copy-start | bytes 1572868
  255.3 3.9 copy-start.12
  477.0 7.5 copy-start.18
  477.0 7.5 copy-start.19
  477.0 7.5 copy-start.16
  477.0 7.8 copy-start.29
  484.5 1.2 copy-start.13
  484.5 2.3 copy-start.14
  484.9 3.9 copy-start.3
  491.3 1.5 copy-start.11
  491.3 2.5 copy-start.6
  492.9 2.5 copy-start.49
  495.3 2.0 copy-start.21
  495.3 217.3 %reduce-scatter.5.cloned.1.call-start = ((), (), s32[]{:S(2)}) async-start(), calls=%async_computation.15 | async-start | bytes 10485760 | tf_op jit(solution)/shard_map/reduce_scatter | solution.py:177
  497.3 2.0 copy-start.27
  497.3 1.4 copy-start.9
  499.3 4.2 copy-start.7
  500.9 5.3 copy-start.10
  503.5 2.7 copy-start.26
  503.5 4.0 copy-start.28
  503.5 4.0 copy-start.41
  573.0 36.7 %copy-start.38 = (bf16[32,8,8,128]{3,2,1,0:T(8,128)(2,1)S(1)}, bf16[32,8,8,128]{3,2,1,0:T(8,128)(2,1)}, u32[]{:S(2)}) copy-start(bf16[32,8,8,128]{3,2,1,0:T(8,128)(2,1)} %copy-done.37) | copy-start | bytes 1572868
  609.7 5.4 copy-start.22
  617.4 10.0 copy-start.23
  617.4 3.1 copy-start.31
  618.4 2.1 copy-start.45
  620.5 6.9 copy-start.33
  627.4 4.6 copy-start.17
  627.5 124.2 %reduce-scatter.7.cloned.1.call-start = ((), (), s32[]{:S(2)}) async-start(), calls=%async_computation.16 | async-start | bytes 2621440 | tf_op jit(solution)/shard_map/reduce_scatter | solution.py:177
  631.8 189.1 %reduce-scatter.11.cloned.1.call-start = ((), (), s32[]{:S(2)}) async-start(), calls=%async_computation.18 | async-start | bytes 7208960 | tf_op jit(solution)/shard_map/reduce_scatter | solution.py:177
  638.1 298.0 %reduce-scatter.9.cloned.1.call-start = ((), (), s32[]{:S(2)}) async-start(), calls=%async_computation.17 | async-start | bytes 14417920 | tf_op jit(solution)/shard_map/reduce_scatter | solution.py:177
  646.5 465.2 %all-reduce.4.cloned.1.call-start = ((), (), s32[]{:S(2)}) async-start(), calls=%async_computation.21 | async-start | bytes 13893632 | tf_op jit(solution)/shard_map/psum | solution.py:330
  940.9 6.5 copy-start.32
  942.9 26.1 %all-to-all-start.1 = ((bf16[32,8,1024]{2,1,0:T(8,128)(2,1)}), bf16[32,8,1024]{2,1,0:T(8,128)(2,1)S(1)}, u32[]{:S(2)}, u32[]{:S(2)}) async-start(bf16[32,8,1024]{2,1,0:T(8,128)(2,1)} %bitcast.150), calls=%async_computation.1 | async-start | bytes 1048576 | tf_op jit(solution)/shard_map/all_to_all | solution.py:344
  947.5 2.5 copy-start.34
  947.5 2.5 copy-start.35
  950.0 1.8 copy-start.36
  951.9 1.6 copy-start.15
  951.9 1.7 copy-start.39
  969.1 25.4 %all-to-all-start.3 = ((bf16[32,8,1024]{2,1,0:T(8,128)(2,1)}), bf16[32,8,1024]{2,1,0:T(8,128)(2,1)S(1)}, u32[]{:S(2)}, u32[]{:S(2)}) async-start(bf16[32,8,1024]{2,1,0:T(8,128)(2,1)} %bitcast.27), calls=%async_computation.3 | async-start | bytes 1048576 | tf_op jit(solution)/shard_map/all_to_all | solution.py:351
  1111.6 4.4 copy-start.44
  1111.6 5.5 copy-start.43
  1113.9 4.4 copy-start.42
  1116.0 3.3 copy-start.30
  1119.3 3.2 copy-start.40
  1122.5 2.0 copy-start.1
  (5 other events, 4.7 us)
Sparse Core Ops, SparseCore 0:
  9.9 43.1 all-gather.18
  54.9 35.2 all-gather.14
  92.0 40.6 all-gather.16
  136.1 77.6 all-gather.26
  215.5 33.9 all-gather.12
  251.1 35.2 all-gather.20
  288.3 113.7 all-gather.22
  404.0 65.7 all-gather.24
  495.4 77.5 all-gather.28
  627.6 84.9 reduce-scatter.4
  716.4 35.1 reduce-scatter.6
  755.1 65.8 reduce-scatter.10
  824.0 112.1 reduce-scatter.8
  939.5 172.0 all-reduce.3
where the time goes:
time: 1140 us; the launch traced here: 1130 us
  waiting for transfers between devices  807 us (71%)
  other arithmetic  104 us (9%)
  matrix products  97.4 us (9%)
  blocking collectives  42.3 us (4%)
  local copies, waits for them, and re-layouts  39.5 us (3%)
  starting transfers between devices  20.8 us (2%)
  between operations  17.5 us (2%)
    reduce_scatter x4, waiting for transfers between devices, reduce_grad(): lax.psum_scatter(lax.dot_general(inputs, grad_pre, (((0,), (0,)), ((), ()...  283 us
    all_gather x3, waiting for transfers between devices, project_single(): lax.all_gather(weight, 'shard', axis=0, tiled=True)  199 us
    all_gather x2, waiting for transfers between devices, carried_in(): lax.all_gather(part.astype(kind), axis)  122 us
    psum x1, waiting for transfers between devices, body(): lax.psum(sum_qkvu[:, :model_cols].astype(jnp.bfloat16), 'rep')  115 us
    select_n x64, other arithmetic, lap(): return jax.tree.map(lambda a, b: jnp.where(reached, a, b), new, before)  70.2 us
    unnamed x1, blocking collectives  42.3 us
    all_gather x1, waiting for transfers between devices, project_attention(): lax.all_gather(w_value, 'shard', axis=0, tiled=True)  33.6 us
    dot_general x4, matrix products, reduce_grad(): lax.dot_general(inputs, grad_pre, (((0,), (0,)), ((), ())), preferred_ele...  24.3 us
  transfers between devices with their start and end apart: 18, of which 15 were waited for; matrix products, arithmetic and copies ran while one was open for 13% of the time, Pallas kernels for 0%

commit v1 on v0

v1 whole, which is shorter than its diff:
```python
import jax
import jax.numpy as jnp
from jax import lax
from jax.sharding import Mesh, PartitionSpec as P

HEAD = 128
BLOCK = 256
TEAM = 4
EPS = 1e-06
BF = jnp.bfloat16
F32 = jnp.float32
ALL = ("zh", "zl", "core", "shard")


def send(value, axis, mask):
    size = lax.axis_size(axis)
    return lax.ppermute(value, axis, [(i, i ^ mask) for i in range(size)])


def dot(a, b, dims=((1,), (0,))):
    return lax.dot_general(a, b, (dims, ((), ())), preferred_element_type=F32)


def norm_scale(values):
    return lax.rsqrt(jnp.mean(values * values, axis=-1, keepdims=True) + EPS)


def norm_back(values, grad):
    scale = norm_scale(values)
    return scale * grad - values * (scale**3) * jnp.mean(values * grad, axis=-1, keepdims=True)


def in_order(pieces, index):
    pieces = list(pieces)
    bit = 1
    while bit < len(pieces):
        flip = (index & bit) != 0
        pieces = [jnp.where(flip, pieces[j ^ bit], pieces[j]) for j in range(len(pieces))]
        bit *= 2
    return pieces


def gather_shard(part):
    size = lax.axis_size("shard")
    if size != 4:
        every = lax.all_gather(part, "shard", axis=0)
        return [every[j] for j in range(size)]
    half = part.shape[0] // 2
    by_x, by_y = send(part, "shard", 1), send(part, "shard", 2)
    far = jnp.concatenate([send(by_x[:half], "shard", 2), send(by_y[half:], "shard", 1)], 0)
    return in_order([part, by_x, by_y, far], lax.axis_index("shard"))


def scatter_shard(parts):
    size = lax.axis_size("shard")
    if size != 4:
        return lax.psum_scatter(jnp.stack(parts), "shard", scatter_dimension=0, tiled=False)
    rel = in_order(parts, lax.axis_index("shard"))
    total = rel[0].astype(F32)
    for j in (1, 2, 3):
        total = total + send(rel[j].astype(BF), "shard", j).astype(F32)
    return total


def sum_zh(part):
    size = lax.axis_size("zh")
    part = part.astype(BF)
    if size != 2:
        return lax.psum(part.astype(F32), "zh").astype(BF)
    return (part.astype(F32) + send(part, "zh", 1).astype(F32)).astype(BF)


def team_gather(own):
    pair = send(own, "zl", 1)
    return [own, send(own, "core", 1), pair, send(pair, "core", 1)]


def team_reduce(parts):
    low = [p.astype(BF) for p in parts]
    here = parts[0] + send(low[1], "core", 1).astype(F32)
    there = parts[2] + send(low[3], "core", 1).astype(F32)
    return here + send(there.astype(BF), "zl", 1).astype(F32)


def place_mix(state, weights):
    groups = lax.axis_size("zh") * lax.axis_size("shard")
    mine = lax.axis_index("zh") * lax.axis_size("shard") + lax.axis_index("shard")
    low = state.astype(BF)
    if groups != 8:
        every = lax.all_gather(low, ("zh", "shard"), axis=0).astype(F32)
        return jnp.sum(every * weights[:, :, None, None], axis=0)
    total = jnp.zeros_like(state)
    for j in range(1, groups):
        got = lax.ppermute(low, ("zh", "shard"), [(i, i ^ j) for i in range(groups)])
        factor = lax.dynamic_index_in_dim(weights, mine ^ j, 0, keepdims=False)
        total = total + factor[:, None, None] * got.astype(F32)
    return total


def after(value, *others):
    return lax.optimization_barrier((value, *others))[0]


def body(tokens_in, cotangent, deal_order, lengths, decay_rates, w_query, w_key, w_value, w_ugate, w_out, w_ffin, w_ffdown):
    rows, width = tokens_in.shape
    n_zh, n_shard = lax.axis_size("zh"), lax.axis_size("shard")
    groups = n_zh * n_shard
    devices = groups * TEAM
    zh, zl, core, shard = (lax.axis_index(a) for a in ALL)
    me = zl * 2 + core
    group = zh * n_shard + shard
    device = (zh * TEAM + me) * n_shard + shard
    heads = width // HEAD // TEAM
    cols = heads * HEAD
    depth = w_query.shape[0]
    ff = w_ffin.shape[1] // 2
    ff_shard = w_ffdown.shape[0]
    ff_own = ff_shard // TEAM
    per_peer = rows // devices
    span = rows * TEAM

    by_device = deal_order.reshape(n_zh, n_shard, TEAM, rows).transpose(0, 2, 1, 3).reshape(-1)
    row_ids = jnp.arange(rows, dtype=jnp.int32)
    key = jnp.sum(
        jnp.where(
            by_device[:, None] == device * rows + row_ids[None, :],
            jnp.arange(by_device.shape[0], dtype=jnp.int32)[:, None],
            0,
        ),
        axis=0,
    )
    rank = jnp.sum((key[:, None] < key[None, :]).astype(jnp.int32), axis=0)
    leave = (row_ids[:, None] == rank[None, :]).astype(BF)
    sent_x = dot(leave, tokens_in).astype(BF)
    sent_g = dot(leave, cotangent).astype(BF)
    got_x = lax.all_to_all(sent_x, ALL, split_axis=0, concat_axis=0, tiled=True)
    own_block = lax.dynamic_slice_in_dim(by_device, device * rows, rows)
    source = own_block // rows
    earlier = row_ids[None, :] < row_ids[:, None]
    own_rank = jnp.sum(((source[:, None] == source[None, :]) & earlier).astype(jnp.int32), axis=1)
    slot = source * per_peer + own_rank
    enter = (slot[:, None] == row_ids[None, :]).astype(BF)
    x_own = dot(enter, got_x).astype(BF)
    got_g = lax.all_to_all(after(sent_g, got_x), ALL, split_axis=0, concat_axis=0, tiled=True)
    g_own = dot(enter, got_g).astype(BF)

    def quarter(w):
        return lax.dynamic_slice_in_dim(w, me * cols, cols, axis=1)

    qkvu_part = jnp.concatenate([quarter(w) for w in (w_query, w_key, w_value, w_ugate)], 1)
    w_qkvu = jnp.concatenate(gather_shard(qkvu_part), 0)
    out_all = jnp.concatenate(gather_shard(after(w_out, w_qkvu)), 0)
    w_o = lax.dynamic_slice_in_dim(out_all, me * cols, cols)
    fin = w_ffin.reshape(depth, 2, n_shard, TEAM, ff_own)
    fin = lax.dynamic_index_in_dim(fin, me, 3, keepdims=False)
    fin = fin.transpose(1, 0, 2, 3).reshape(2 * depth, n_shard * ff_own)
    fin_parts = gather_shard(after(fin, out_all))
    w_gate = jnp.concatenate([p[:depth] for p in fin_parts], 0)
    w_up = jnp.concatenate([p[depth:] for p in fin_parts], 0)
    fdown = lax.dynamic_slice_in_dim(w_ffdown, me * ff_own, ff_own)
    w_down = jnp.concatenate(gather_shard(after(fdown, w_up)), 0)

    ends = jnp.sum(jnp.where(jnp.arange(8)[None, :] <= jnp.arange(8)[:, None], lengths[None, :], 0), axis=1)
    all_last = jnp.arange(1, groups + 1) * span - 1
    last_seg = jnp.sum((all_last[:, None] >= ends[None, :]).astype(jnp.int32), axis=1)
    before_seg = jnp.concatenate([jnp.full((1,), -1, jnp.int32), last_seg[:-1]])
    positions = group * span + jnp.arange(span)
    seg = jnp.sum((positions[:, None] >= ends[None, :]).astype(jnp.int32), axis=1)
    seg_before = before_seg[group]
    blocks = span // BLOCK
    seg_b = seg.reshape(blocks, BLOCK)
    prev_b = jnp.concatenate([seg_before[None], seg_b[:-1, -1]])
    rates = lax.dynamic_slice_in_dim(decay_rates, me * heads, heads)
    idx = jnp.arange(BLOCK).astype(F32)
    dist = idx[:, None] - idx[None, :]
    decay = jnp.where(dist >= 0, jnp.exp(-rates[:, None, None] * jnp.maximum(dist, 0.0)), 0.0)
    same = (seg_b[:, :, None] == seg_b[:, None, :]).astype(F32)
    mask = same[:, None] * decay[None]
    carry = (seg_b == prev_b[:, None]).astype(F32)
    q_scale = jnp.exp(-(idx + 1.0)[None, :, None] * rates) * carry[:, :, None]
    k_scale = jnp.exp(-(BLOCK - 1.0 - idx)[None, :, None] * rates) * (seg_b == seg_b[:, -1:]).astype(F32)[:, :, None]
    passing = (seg_b[:, -1] == prev_b).astype(F32)[:, None] * jnp.exp(-rates * BLOCK)[None]
    ids = jnp.arange(groups)
    gap = jnp.maximum(jnp.abs(ids - group) - 1, 0).astype(F32) * span
    into = (ids < group) & (last_seg == seg_before)
    outof = (ids > group) & (before_seg == last_seg[group])
    fade = jnp.exp(-gap[:, None] * rates[None, :])
    w_into = jnp.where(into[:, None], fade, 0.0)
    w_outof = jnp.where(outof[:, None], fade, 0.0)

    x = in_order(team_gather(x_own), me)
    x_all = jnp.concatenate(x, 0)
    xf = x_all.astype(F32)
    normed = (xf * norm_scale(xf)).astype(BF)
    pre = dot(normed, w_qkvu)
    pre_q, pre_k, pre_v, pre_u = (pre[:, i * cols : (i + 1) * cols] for i in range(4))
    shape = (blocks, BLOCK, heads, HEAD)
    q = jax.nn.silu(pre_q).astype(BF).reshape(shape)
    k = jax.nn.silu(pre_k).astype(BF).reshape(shape)
    v = pre_v.astype(BF).reshape(shape)

    def ein(text, a, b):
        return jnp.einsum(text, a, b, preferred_element_type=F32)

    ks = (k.astype(F32) * k_scale[..., None]).astype(BF)
    qs = (q.astype(F32) * q_scale[..., None]).astype(BF)
    kv = ein("bjhe,bjhf->bhef", ks, v)
    state = jnp.zeros((heads, HEAD, HEAD), F32)
    for b in range(blocks):
        state = passing[b][:, None, None] * state + kv[b]
    state_in = place_mix(state, w_into)
    scores = ein("bihe,bjhe->bhij", q, k)
    mixing = (scores * mask).astype(BF)
    mixed = ein("bhij,bjhf->bihf", mixing, v)
    states = []
    state = state_in
    for b in range(blocks):
        states.append(state)
        state = passing[b][:, None, None] * state + kv[b]
    states = jnp.stack(states).astype(BF)
    mixed = mixed + ein("bihe,bhef->bihf", qs, states)
    m_norm = (mixed * norm_scale(mixed)).reshape(span, cols)
    gated = (pre_u * m_norm).astype(BF)
    part = dot(gated, w_o).reshape(TEAM, rows, width)
    att = team_reduce(in_order([part[j] for j in range(TEAM)], me))
    att = jnp.concatenate(in_order(team_gather(att.astype(BF)), me), 0)
    hidden = xf + att.astype(F32)

    g_all = jnp.concatenate(in_order(team_gather(g_own), me), 0)
    n2 = (hidden * norm_scale(hidden)).astype(BF)
    gate, up = dot(n2, w_gate), dot(n2, w_up)
    product = (gate * up).astype(BF)
    res = dot(product, w_down).reshape(TEAM, rows, width)
    g_product = dot(g_all, w_down, ((1,), (1,)))
    g_gate, g_up = (g_product * up).astype(BF), (g_product * gate).astype(BF)
    gn2 = dot(g_gate, w_gate, ((1,), (1,))) + dot(g_up, w_up, ((1,), (1,)))
    gn2 = gn2.reshape(TEAM, rows, width)
    gn2 = team_reduce(in_order([gn2[j] for j in range(TEAM)], me))
    gn2 = jnp.concatenate(in_order(team_gather(gn2.astype(BF)), me), 0)
    g_hidden = g_all.astype(F32) + norm_back(hidden, gn2.astype(F32))
    ga = g_hidden.astype(BF)

    res = team_reduce(in_order([res[j] for j in range(TEAM)], me))
    my_rows = lambda a: lax.dynamic_slice_in_dim(a, me * rows, rows)
    result = (my_rows(hidden) + res).astype(BF)

    g_gated = dot(ga, w_o, ((1,), (1,)))
    g_pre_u = (g_gated * m_norm).astype(BF)
    gm = norm_back(mixed, (g_gated * pre_u).reshape(shape)).astype(BF)
    qg = ein("bihe,bihf->bhef", qs, gm)
    gs = jnp.zeros((heads, HEAD, HEAD), F32)
    for b in reversed(range(blocks)):
        gs = passing[b][:, None, None] * gs + qg[b]
    gs = place_mix(gs, w_outof)
    g_states = [None] * blocks
    for b in reversed(range(blocks)):
        g_states[b] = gs
        gs = passing[b][:, None, None] * gs + qg[b]
    g_states = jnp.stack(g_states).astype(BF)
    g_mixing = ein("bihf,bjhf->bhij", gm, v)
    g_scores = (g_mixing * mask).astype(BF)
    g_q = ein("bhij,bjhe->bihe", g_scores, k) + q_scale[..., None] * ein("bihf,bhef->bihe", gm, states)
    g_k = ein("bhij,bihe->bjhe", g_scores, q) + k_scale[..., None] * ein("bhef,bjhf->bjhe", g_states, v)
    g_v = ein("bhij,bihf->bjhf", mixing, gm) + ein("bjhe,bhef->bjhf", ks, g_states)

    def silu_back(pre_rows, grad):
        sig = jax.nn.sigmoid(pre_rows)
        return (grad * (sig * (1.0 + pre_rows * (1.0 - sig)))).astype(BF)

    g_pre = jnp.concatenate(
        [
            silu_back(pre_q, g_q.reshape(span, cols)),
            silu_back(pre_k, g_k.reshape(span, cols)),
            g_v.reshape(span, cols).astype(BF),
            g_pre_u,
        ],
        1,
    )
    gn = dot(g_pre, w_qkvu, ((1,), (1,))).reshape(TEAM, rows, width)
    gn = team_reduce(in_order([gn[j] for j in range(TEAM)], me))
    grad_x = (my_rows(g_hidden) + norm_back(x_own.astype(F32), gn)).astype(BF)

    def give_back(rows_own):
        ordered = dot(enter, rows_own, ((0,), (0,))).astype(BF)
        back = lax.all_to_all(ordered, ALL, split_axis=0, concat_axis=0, tiled=True)
        return dot(leave, back, ((0,), (0,))).astype(BF)

    output, input_grad = give_back(result), give_back(grad_x)

    def by_place(grad):
        return list(grad.astype(BF).reshape(n_shard, -1, grad.shape[-1]))

    d_down = dot(product, g_all, ((0,), (0,)))
    d_gate, d_up = dot(n2, g_gate, ((0,), (0,))), dot(n2, g_up, ((0,), (0,)))
    d_out = dot(gated, ga, ((0,), (0,)))
    d_qkvu = dot(normed, g_pre, ((0,), (0,)))

    def collect(parts):
        return in_order(team_gather(sum_zh(scatter_shard(parts))), me)

    down = collect(by_place(d_down))
    grad_down = jnp.concatenate(down, 0).astype(F32)
    fin_grad = [jnp.concatenate([a, b], 0) for a, b in zip(by_place(d_gate), by_place(d_up))]
    fin_grad = jnp.stack(collect(fin_grad), 0).reshape(TEAM, 2, depth, n_shard, ff_own)
    grad_fin = fin_grad.transpose(2, 1, 3, 0, 4).reshape(depth, 2 * ff).astype(F32)
    out_cols = width // n_shard
    d_out_cols = [d_out[:, j * out_cols : (j + 1) * out_cols].astype(BF) for j in range(n_shard)]
    d_out_rows = jnp.concatenate(collect(d_out_cols), 0)
    d_out_rows = lax.all_to_all(
        d_out_rows.reshape(n_shard, depth, out_cols), "shard", split_axis=0, concat_axis=0, tiled=True
    )
    grad_out = d_out_rows.transpose(1, 0, 2).reshape(depth, width).astype(F32)
    qkvu = collect(by_place(d_qkvu))
    grads = [
        jnp.concatenate([p[:, i * cols : (i + 1) * cols] for p in qkvu], 1).astype(F32) for i in range(4)
    ]
    return (output, input_grad, *grads, grad_out, grad_fin, grad_down)


def solution(mesh):
    rep, shard = mesh.shape["rep"], mesh.shape["shard"]
    team = Mesh(mesh.devices.reshape(rep // TEAM, 2, 2, shard), ALL)
    token, weight = P(ALL, None), P("shard", None)
    return jax.shard_map(
        body,
        mesh=team,
        in_specs=(token, token, P(), P(), P(), *([weight] * 7)),
        out_specs=(token, token, *([weight] * 7)),
        check_vma=False,
    )
```

time: 1140 us -> 452 us (0.40)
  waiting for transfers between devices: 807 us -> 162 us
  starting transfers between devices: 20.8 us -> 96.9 us
  matrix products: 97.4 us -> 51.2 us
  blocking collectives: 42.3 us -> 0 us
  other arithmetic: 104 us -> 69.7 us
  local copies, waits for them, and re-layouts: 39.5 us -> 61.9 us
  between operations: 17.5 us -> 3.81 us
    all_gather x9 -> x0, waiting for transfers between devices: 368 us -> none  [the longest x3 199 us: project_single(): lax.all_gather(weight, 'shard', axis=0, tiled=True)]
    reduce_scatter x4 -> x0, waiting for transfers between devices: 283 us -> none  [reduce_grad(): lax.psum_scatter(lax.dot_general(inputs, grad_pre, (((0,), (0,)), ((), ()...]
    ppermute x0 -> x82, waiting for transfers between devices: none -> 157 us  [the longest x68 156 us: send(): return lax.ppermute(value, axis, [(i, i ^ mask) for i in range(size)])]
    psum x1 -> x0, waiting for transfers between devices: 115 us -> none  [body(): lax.psum(sum_qkvu[:, :model_cols].astype(jnp.bfloat16), 'rep')]
    ppermute x0 -> x82, starting transfers between devices: none -> 73.4 us  [the longest x68 49.4 us: send(): return lax.ppermute(value, axis, [(i, i ^ mask) for i in range(size)])]
    select_n x69 -> x21, other arithmetic: 72.3 us -> 16.8 us  [the longest x18 14.4 us: in_order(): jnp.where(flip, pieces[j ^ bit], pieces[j])]
    dot_general x32 -> x35, matrix products: 97.4 us -> 51.2 us  [the longest x23 45.5 us: dot(): return lax.dot_general(a, b, (dims, ((), ())), preferred_element_type=F32)]
    unnamed x1 -> x0, blocking collectives: 42.3 us -> none
  transfers between devices with their start and end apart: 18 -> 87, of which waited for: 15 -> 24; matrix products, arithmetic and copies ran while one was open for 13% -> 34% of each run, Pallas kernels for 0% -> 0%
where the time goes in v1:
time: 452 us; the launch traced here: 446 us
  waiting for transfers between devices  162 us (36%)
  starting transfers between devices  96.9 us (21%)
  other arithmetic  69.7 us (15%)
  local copies, waits for them, and re-layouts  61.9 us (14%)
  matrix products  51.2 us (11%)
    ppermute x68, waiting for transfers between devices, send(): return lax.ppermute(value, axis, [(i, i ^ mask) for i in range(size)])  156 us
    ppermute x68, starting transfers between devices, send(): return lax.ppermute(value, axis, [(i, i ^ mask) for i in range(size)])  49.4 us
    dot_general x23, matrix products, dot(): return lax.dot_general(a, b, (dims, ((), ())), preferred_element_type=F32)  45.5 us
    ppermute x14, starting transfers between devices, place_mix(): lax.ppermute(low, ('zh', 'shard'), [(i, i ^ j) for i in range(groups)])  24 us
    unnamed x244, local copies, waits for them, and re-layouts  23.9 us
    select_n x18, other arithmetic, in_order(): jnp.where(flip, pieces[j ^ bit], pieces[j])  14.4 us
  transfers between devices with their start and end apart: 87, of which 24 were waited for; matrix products, arithmetic and copies ran while one was open for 34% of the time, Pallas kernels for 0%

profile of v1, /device:TPU:0, one launch (start us, length us, event | category | flops | bytes accessed | tf_op | source)
XLA Modules:
  0.0 445.9 jit_solution(5337195153170267022)
XLA Ops:
  3.8 3.0 collective-permute-start.5
  9.7 3.7 select_reduce_fusion
  13.6 2.1 fusion.14
  15.7 6.4 %all-to-all-start = ((bf16[32,8,1024]{2,1,0:T(8,128)(2,1)}), bf16[32,8,1024]{2,1,0:T(8,128)(2,1)}, u32[]{:S(2)}, u32[]{:S(2)}) async-start(bf16[32,8,1024]{2,1,0:T(8,128)(2,1)} %fusion.14), calls=%async_computation | async-start | bytes 1048576 | tf_op jit(solution)/shard_map/all_to_all | solution.py:136
  22.9 1.7 collective-permute-start.28
  29.4 2.1 convolution_convert_fusion.8
  42.2 4.5 %copy.181 = bf16[256,5632]{0,1:T(8,128)(2,1)} copy(bf16[256,5632]{1,0:T(8,128)(2,1)} %param.22) | data formatting | bytes 5767168 | tf_op args[10]
  62.3 6.2 %all-to-all-start.2 = ((bf16[32,8,1024]{2,1,0:T(8,128)(2,1)}), bf16[32,8,1024]{2,1,0:T(8,128)(2,1)}, u32[]{:S(2)}, u32[]{:S(2)}) async-start(bf16[32,8,1024]{2,1,0:T(8,128)(2,1)} %bitcast.257), calls=%async_computation.2 | async-start | bytes 1048576 | tf_op jit(solution)/shard_map/all_to_all | solution.py:144
  70.0 1.8 collective-permute-start
  76.8 13.9 %collective-permute-done = bf16[256,1024]{1,0:T(8,128)(2,1)S(1)} collective-permute-done((bf16[256,1024]{1,0:T(8,128)(2,1)S(1)}, bf16[256,1024]{1,0:T(8,128)(2,1)S(1)}, u32[]{:S(2)}, u32[]{:S(2)}) %collective-permute-start) | collective-permute-done | bytes 524320 | tf_op jit(solution)/shard_map/ppermute | solution.py:17
  93.4 2.6 fusion.27
  96.1 1.9 copy-done.8
  102.3 4.3 collective-permute-start.13
  107.1 2.4 collective-permute-start.11
  110.0 2.4 collective-permute-start.9
  127.8 1.8 fusion.38
  129.6 2.0 copy-done.4
  135.0 6.2 %collective-permute-done.24 = bf16[512,704]{0,1:T(8,128)(2,1)} collective-permute-done((bf16[512,704]{0,1:T(8,128)(2,1)}, bf16[512,704]{0,1:T(8,128)(2,1)}, u32[]{:S(2)}, u32[]{:S(2)}) %collective-permute-start.24) | collective-permute-done | bytes 720928 | tf_op jit(solution)/shard_map/ppermute | solution.py:17
  145.2 2.8 add_convert_fusion.10
  152.7 9.8 %collective-permute-done.20 = bf16[256,1024]{1,0:T(8,128)(2,1)S(1)} collective-permute-done((bf16[256,1024]{1,0:T(8,128)(2,1)S(1)}, bf16[256,1024]{1,0:T(8,128)(2,1)S(1)}, u32[]{:S(2)}, u32[]{:S(2)}) %collective-permute-start.20) | collective-permute-done | bytes 524320 | tf_op jit(solution)/shard_map/ppermute | solution.py:17
  163.5 1.8 broadcast_select_fusion.22
  165.4 11.3 %collective-permute-done.21 = bf16[256,1024]{1,0:T(8,128)(2,1)S(1)} collective-permute-done((bf16[256,1024]{1,0:T(8,128)(2,1)S(1)}, bf16[256,1024]{1,0:T(8,128)(2,1)S(1)}, u32[]{:S(2)}, u32[]{:S(2)}) %collective-permute-start.21) | collective-permute-done | bytes 524320 | tf_op jit(solution)/shard_map/ppermute | solution.py:17
  183.9 1.8 multiply_convert_fusion.1
  185.7 1.9 fusion.54
  189.3 1.9 fusion.53
  195.3 2.1 convolution_add_fusion
  197.9 1.7 collective-permute-start.77
  203.1 7.0 %collective-permute-done.77 = bf16[176,1024]{1,0:T(8,128)(2,1)S(1)} collective-permute-done((bf16[176,1024]{1,0:T(8,128)(2,1)S(1)}, bf16[176,1024]{1,0:T(8,128)(2,1)S(1)}, u32[]{:S(2)}, u32[]{:S(2)}) %collective-permute-start.77) | collective-permute-done | bytes 360480 | tf_op jit(solution)/shard_map/ppermute | solution.py:17
  211.8 6.0 %collective-permute-done.76 = bf16[176,1024]{1,0:T(8,128)(2,1)S(1)} collective-permute-done((bf16[176,1024]{1,0:T(8,128)(2,1)S(1)}, bf16[176,1024]{1,0:T(8,128)(2,1)S(1)}, u32[]{:S(2)}, u32[]{:S(2)}) %collective-permute-start.76) | collective-permute-done | bytes 360480 | tf_op jit(solution)/shard_map/ppermute | solution.py:17
  221.6 11.7 %collective-permute-done.40 = bf16[256,1024]{1,0:T(8,128)(2,1)S(1)} collective-permute-done((bf16[256,1024]{1,0:T(8,128)(2,1)S(1)}, bf16[256,1024]{1,0:T(8,128)(2,1)S(1)}, u32[]{:S(2)}, u32[]{:S(2)}) %collective-permute-start.40) | collective-permute-done | bytes 524320 | tf_op jit(solution)/shard_map/ppermute | solution.py:17
  235.4 1.7 collective-permute-start.34
  237.2 11.1 %collective-permute-done.69 = bf16[512,704]{0,1:T(8,128)(2,1)S(1)} collective-permute-done((bf16[512,704]{0,1:T(8,128)(2,1)S(1)}, bf16[512,704]{0,1:T(8,128)(2,1)S(1)}, u32[]{:S(2)}, u32[]{:S(2)}) %collective-permute-start.69) | collective-permute-done | bytes 720928 | tf_op jit(solution)/shard_map/ppermute | solution.py:17
  250.3 2.2 collective-permute-start.71
  253.6 29.6 %collective-permute-done.41 = bf16[256,1024]{1,0:T(8,128)(2,1)} collective-permute-done((bf16[256,1024]{1,0:T(8,128)(2,1)}, bf16[256,1024]{1,0:T(8,128)(2,1)}, u32[]{:S(2)}, u32[]{:S(2)}) %collective-permute-start.41) | collective-permute-done | bytes 524320 | tf_op jit(solution)/shard_map/ppermute | solution.py:17
  284.6 3.5 all-to-all-start.1
  288.2 2.5 add_convert_fusion
  293.9 3.9 fusion.1
  297.9 4.6 %slice_multiply_fusion = (f32[1024,256]{0,1:T(8,128)}, bf16[1024,256]{0,1:T(8,128)(2,1)}) fusion(f32[1024,1024]{0,1:T(8,128)} %copy-done.8, f32[1024,256]{0,1:T(8,128)S(1)} %bitcast.249, bf16[1024,1024]{1,0:T(8,128)(2,1)} %pad_maximum_fusion.2, s32[]{:T(128)S(6)} %select_n.780, f32[1024,1024]{1,0:T(8,128)S(1)} %fusion.1), kind=kOutput, calls=%fused_computation.125 | convolution fusion | flops 538705920 | bytes 8388612 | tf_op jit(solution)/shard_map/dot_general | solution.py:21
  302.5 2.7 reshape.486
  308.8 4.5 %collective-permute-start.50 = (bf16[2,128,128]{2,1,0:T(8,128)(2,1)S(1)}, bf16[2,128,128]{2,1,0:T(8,128)(2,1)S(1)}, u32[]{:S(2)}, u32[]{:S(2)}) collective-permute-start(bf16[2,128,128]{2,1,0:T(8,128)(2,1)S(1)} %fusion.57), channel_id=1, source_target_pairs={{0,19},{1,18},{2,17},{3,16},{16,3},{17,2},{18,1},{19,0},{4,23},{5,... | collective-permute-start | bytes 196616 | tf_op jit(solution)/shard_map/ppermute | solution.py:94
  314.4 1.8 collective-permute-start.48
  319.8 2.7 collective-permute-start.46
  326.1 2.3 collective-permute-start.63
  334.2 2.4 fusion.42
  336.6 3.0 convolution_convert_fusion
  340.0 1.7 collective-permute-start.64
  341.9 2.2 collective-permute-start.56
  344.8 3.6 collective-permute-done.64
  351.3 4.7 %collective-permute-done.65 = bf16[256,256]{1,0:T(8,128)(2,1)S(1)} collective-permute-done((bf16[256,256]{1,0:T(8,128)(2,1)S(1)}, bf16[256,256]{1,0:T(8,128)(2,1)S(1)}, u32[]{:S(2)}, u32[]{:S(2)}) %collective-permute-start.65) | collective-permute-done | bytes 131104 | tf_op jit(solution)/shard_map/ppermute | solution.py:17
  356.3 1.9 maximum_convert_fusion.1
  358.2 8.2 %collective-permute-done.55 = bf16[256,1024]{1,0:T(8,128)(2,1)S(1)} collective-permute-done((bf16[256,1024]{1,0:T(8,128)(2,1)S(1)}, bf16[256,1024]{1,0:T(8,128)(2,1)S(1)}, u32[]{:S(2)}, u32[]{:S(2)}) %collective-permute-start.55) | collective-permute-done | bytes 524320 | tf_op jit(solution)/shard_map/ppermute | solution.py:17
  367.7 1.8 collective-permute-start.57
  370.0 6.6 %collective-permute-done.72 = bf16[512,704]{0,1:T(8,128)(2,1)} collective-permute-done((bf16[512,704]{0,1:T(8,128)(2,1)S(1)}, bf16[512,704]{0,1:T(8,128)(2,1)}, u32[]{:S(2)}, u32[]{:S(2)}) %collective-permute-start.72) | collective-permute-done | bytes 720928 | tf_op jit(solution)/shard_map/ppermute | solution.py:17
  378.1 15.9 %collective-permute-done.57 = bf16[256,1024]{1,0:T(8,128)(2,1)S(1)} collective-permute-done((bf16[256,1024]{1,0:T(8,128)(2,1)S(1)}, bf16[256,1024]{1,0:T(8,128)(2,1)S(1)}, u32[]{:S(2)}, u32[]{:S(2)}) %collective-permute-start.57) | collective-permute-done | bytes 524320 | tf_op jit(solution)/shard_map/ppermute | solution.py:17
  395.0 4.5 %collective-permute-done.53 = bf16[256,1024]{1,0:T(8,128)(2,1)S(1)} collective-permute-done((bf16[256,1024]{1,0:T(8,128)(2,1)S(1)}, bf16[256,1024]{1,0:T(8,128)(2,1)S(1)}, u32[]{:S(2)}, u32[]{:S(2)}) %collective-permute-start.53) | collective-permute-done | bytes 524320 | tf_op jit(solution)/shard_map/ppermute | solution.py:17
  400.2 3.5 all-to-all-start.4
  403.7 2.6 fusion.16
  406.3 5.0 %all-to-all-done.4 = bf16[4,256,256]{2,1,0:T(8,128)(2,1)S(1)} async-done(((bf16[4,256,256]{2,1,0:T(8,128)(2,1)}), bf16[4,256,256]{2,1,0:T(8,128)(2,1)S(1)}, u32[]{:S(2)}, u32[]{:S(2)}) %all-to-all-start.4) | async-done | bytes 524320 | tf_op jit(solution)/shard_map/all_to_all | solution.py:309
  411.3 3.8 all-to-all-start.3
  415.2 2.2 convolution_convert_fusion.9
  417.4 2.6 broadcast_select_fusion.7
  420.0 2.1 stack.68
  426.5 4.1 maximum_convert_fusion
  430.5 6.3 %copy.208 = f32[256,5632]{1,0:T(8,128)} copy(f32[256,5632]{0,1:T(8,128)} %bitcast.247) | data formatting | bytes 11534336
  (547 shorter events, 151.3 us)
Async XLA Ops:
  3.8 55.2 %collective-permute-start.5 = (bf16[256,1024]{1,0:T(8,128)(2,1)}, bf16[256,1024]{1,0:T(8,128)(2,1)S(1)}, u32[]{:S(2)}, u32[]{:S(2)}) collective-permute-start(bf16[256,1024]{1,0:T(8,128)(2,1)} %pad_maximum_fusion.13), channel_id=1, source_target_pairs={{0,2},{1,3},{2,0},{3,1},{4,6},{5,7},{6,4},{7,5},{8,10},{9,11},{10,... | collective-permute-start | bytes 1572872 | tf_op jit(solution)/shard_map/ppermute | solution.py:17
  6.8 51.1 %collective-permute-start.3 = (bf16[256,1024]{1,0:T(8,128)(2,1)}, bf16[256,1024]{1,0:T(8,128)(2,1)S(1)}, u32[]{:S(2)}, u32[]{:S(2)}) collective-permute-start(bf16[256,1024]{1,0:T(8,128)(2,1)} %pad_maximum_fusion.13), channel_id=1, source_target_pairs={{0,1},{1,0},{2,3},{3,2},{4,5},{5,4},{6,7},{7,6},{8,9},{9,8},{10,11... | collective-permute-start | bytes 1572872 | tf_op jit(solution)/shard_map/ppermute | solution.py:17
  8.3 28.9 %collective-permute-start.14 = (bf16[256,1024]{1,0:T(8,128)(2,1)}, bf16[256,1024]{1,0:T(8,128)(2,1)}, u32[]{:S(2)}, u32[]{:S(2)}) collective-permute-start(bf16[256,1024]{1,0:T(8,128)(2,1)} %param.21), channel_id=1, source_target_pairs={{0,1},{1,0},{2,3},{3,2},{4,5},{5,4},{6,7},{7,6},{8,9},{9,8},{10,11... | collective-permute-start | bytes 1572872 | tf_op jit(solution)/shard_map/ppermute | solution.py:17
  8.8 30.8 %collective-permute-start.16 = (bf16[256,1024]{1,0:T(8,128)(2,1)}, bf16[256,1024]{1,0:T(8,128)(2,1)}, u32[]{:S(2)}, u32[]{:S(2)}) collective-permute-start(bf16[256,1024]{1,0:T(8,128)(2,1)} %param.21), channel_id=1, source_target_pairs={{0,2},{1,3},{2,0},{3,1},{4,6},{5,7},{6,4},{7,5},{8,10},{9,11},{10,... | collective-permute-start | bytes 1572872 | tf_op jit(solution)/shard_map/ppermute | solution.py:17
  15.7 46.6 %all-to-all-start = ((bf16[32,8,1024]{2,1,0:T(8,128)(2,1)}), bf16[32,8,1024]{2,1,0:T(8,128)(2,1)}, u32[]{:S(2)}, u32[]{:S(2)}) async-start(bf16[32,8,1024]{2,1,0:T(8,128)(2,1)} %fusion.14), calls=%async_computation | async-start | bytes 1048576 | tf_op jit(solution)/shard_map/all_to_all | solution.py:136
  22.9 25.5 %collective-permute-start.28 = (bf16[176,1024]{1,0:T(8,128)(2,1)}, bf16[176,1024]{1,0:T(8,128)(2,1)S(1)}, u32[]{:S(2)}, u32[]{:S(2)}) collective-permute-start(bf16[176,1024]{1,0:T(8,128)(2,1)} %constant_dynamic-slice_fusion.7), channel_id=1, source_target_pairs={{0,1},{1,0},{2,3},{3,2},{4,5},{5,4},{6,7},{7,6},{8,9},{9,8},{10,11... | collective-permute-start | bytes 1081352 | tf_op jit(solution)/shard_map/ppermute | solution.py:17
  37.2 19.0 %collective-permute-start.30 = (bf16[176,1024]{1,0:T(8,128)(2,1)}, bf16[176,1024]{1,0:T(8,128)(2,1)}, u32[]{:S(2)}, u32[]{:S(2)}) collective-permute-start(bf16[176,1024]{1,0:T(8,128)(2,1)} %constant_dynamic-slice_fusion.7), channel_id=1, source_target_pairs={{0,2},{1,3},{2,0},{3,1},{4,6},{5,7},{6,4},{7,5},{8,10},{9,11},{10,... | collective-permute-start | bytes 1081352 | tf_op jit(solution)/shard_map/ppermute | solution.py:17
  39.5 20.8 %collective-permute-start.15 = (bf16[128,1024]{1,0:T(8,128)(2,1)}, bf16[128,1024]{1,0:T(8,128)(2,1)}, u32[]{:S(2)}, u32[]{:S(2)}) collective-permute-start(bf16[128,1024]{1,0:T(8,128)(2,1)} %slice.353), channel_id=1, source_target_pairs={{0,2},{1,3},{2,0},{3,1},{4,6},{5,7},{6,4},{7,5},{8,10},{9,11},{10,... | collective-permute-start | bytes 786440 | tf_op jit(solution)/shard_map/ppermute | solution.py:17
  48.4 12.9 %collective-permute-start.17 = (bf16[128,1024]{1,0:T(8,128)(2,1)}, bf16[128,1024]{1,0:T(8,128)(2,1)}, u32[]{:S(2)}, u32[]{:S(2)}) collective-permute-start(bf16[128,1024]{1,0:T(8,128)(2,1)} %slice.354), channel_id=1, source_target_pairs={{0,1},{1,0},{2,3},{3,2},{4,5},{5,4},{6,7},{7,6},{8,9},{9,8},{10,11... | collective-permute-start | bytes 786440 | tf_op jit(solution)/shard_map/ppermute | solution.py:17
  58.6 16.2 %collective-permute-start.4 = (bf16[128,1024]{1,0:T(8,128)(2,1)}, bf16[128,1024]{1,0:T(8,128)(2,1)}, u32[]{:S(2)}, u32[]{:S(2)}) collective-permute-start(bf16[128,1024]{1,0:T(8,128)(2,1)} %slice.341), channel_id=1, source_target_pairs={{0,2},{1,3},{2,0},{3,1},{4,6},{5,7},{6,4},{7,5},{8,10},{9,11},{10,... | collective-permute-start | bytes 786440 | tf_op jit(solution)/shard_map/ppermute | solution.py:17
  59.7 16.1 %collective-permute-start.6 = (bf16[128,1024]{1,0:T(8,128)(2,1)}, bf16[128,1024]{1,0:T(8,128)(2,1)}, u32[]{:S(2)}, u32[]{:S(2)}) collective-permute-start(bf16[128,1024]{1,0:T(8,128)(2,1)} %slice.342), channel_id=1, source_target_pairs={{0,1},{1,0},{2,3},{3,2},{4,5},{5,4},{6,7},{7,6},{8,9},{9,8},{10,11... | collective-permute-start | bytes 786440 | tf_op jit(solution)/shard_map/ppermute | solution.py:17
  62.3 71.0 %all-to-all-start.2 = ((bf16[32,8,1024]{2,1,0:T(8,128)(2,1)}), bf16[32,8,1024]{2,1,0:T(8,128)(2,1)}, u32[]{:S(2)}, u32[]{:S(2)}) async-start(bf16[32,8,1024]{2,1,0:T(8,128)(2,1)} %bitcast.257), calls=%async_computation.2 | async-start | bytes 1048576 | tf_op jit(solution)/shard_map/all_to_all | solution.py:144
  70.0 20.8 %collective-permute-start = (bf16[256,1024]{1,0:T(8,128)(2,1)S(1)}, bf16[256,1024]{1,0:T(8,128)(2,1)S(1)}, u32[]{:S(2)}, u32[]{:S(2)}) collective-permute-start(bf16[256,1024]{1,0:T(8,128)(2,1)S(1)} %convolution_convert_fusion.11), channel_id=1, source_target_pairs={{0,8},{8,0},{1,9},{9,1},{2,10},{10,2},{3,11},{11,3},{4,12},{12,4},... | collective-permute-start | bytes 1572872 | tf_op jit(solution)/shard_map/ppermute | solution.py:17
  76.8 14.9 %collective-permute-start.2 = (bf16[256,1024]{1,0:T(8,128)(2,1)S(1)}, bf16[256,1024]{1,0:T(8,128)(2,1)S(1)}, u32[]{:S(2)}, u32[]{:S(2)}) collective-permute-start(bf16[256,1024]{1,0:T(8,128)(2,1)S(1)} %convolution_convert_fusion.11), channel_id=1, source_target_pairs={{0,4},{4,0},{1,5},{5,1},{2,6},{6,2},{3,7},{7,3},{8,12},{12,8},{9,1... | collective-permute-start | bytes 1572872 | tf_op jit(solution)/shard_map/ppermute | solution.py:17
  102.3 13.3 %collective-permute-start.13 = (bf16[2,128,128]{2,1,0:T(8,128)(2,1)S(1)}, bf16[2,128,128]{2,1,0:T(8,128)(2,1)S(1)}, u32[]{:S(2)}, u32[]{:S(2)}) collective-permute-start(bf16[2,128,128]{2,1,0:T(8,128)(2,1)S(1)} %fusion.59), channel_id=1, source_target_pairs={{0,19},{1,18},{2,17},{3,16},{16,3},{17,2},{18,1},{19,0},{4,23},{5,... | collective-permute-start | bytes 196616 | tf_op jit(solution)/shard_map/ppermute | solution.py:94
  107.1 11.5 %collective-permute-start.11 = (bf16[2,128,128]{2,1,0:T(8,128)(2,1)S(1)}, bf16[2,128,128]{2,1,0:T(8,128)(2,1)S(1)}, u32[]{:S(2)}, u32[]{:S(2)}) collective-permute-start(bf16[2,128,128]{2,1,0:T(8,128)(2,1)S(1)} %fusion.59), channel_id=1, source_target_pairs={{0,17},{1,16},{2,19},{3,18},{16,1},{17,0},{18,3},{19,2},{4,21},{5,... | collective-permute-start | bytes 196616 | tf_op jit(solution)/shard_map/ppermute | solution.py:94
  118.6 14.7 %collective-permute-start.29 = (bf16[88,1024]{1,0:T(8,128)(2,1)S(1)}, bf16[88,1024]{1,0:T(8,128)(2,1)S(1)}, u32[]{:S(2)}, u32[]{:S(2)}) collective-permute-start(bf16[88,1024]{1,0:T(8,128)(2,1)S(1)} %copy-done.78), channel_id=1, source_target_pairs={{0,2},{1,3},{2,0},{3,1},{4,6},{5,7},{6,4},{7,5},{8,10},{9,11},{10,... | collective-permute-start | bytes 540680 | tf_op jit(solution)/shard_map/ppermute | solution.py:17
  119.5 13.8 %collective-permute-start.31 = (bf16[88,1024]{1,0:T(8,128)(2,1)S(1)}, bf16[88,1024]{1,0:T(8,128)(2,1)S(1)}, u32[]{:S(2)}, u32[]{:S(2)}) collective-permute-start(bf16[88,1024]{1,0:T(8,128)(2,1)S(1)} %copy-done.77), channel_id=1, source_target_pairs={{0,1},{1,0},{2,3},{3,2},{4,5},{5,4},{6,7},{7,6},{8,9},{9,8},{10,11... | collective-permute-start | bytes 540680 | tf_op jit(solution)/shard_map/ppermute | solution.py:17
  120.7 20.5 %collective-permute-start.24 = (bf16[512,704]{0,1:T(8,128)(2,1)}, bf16[512,704]{0,1:T(8,128)(2,1)}, u32[]{:S(2)}, u32[]{:S(2)}) collective-permute-start(bf16[512,704]{0,1:T(8,128)(2,1)} %bitcast.77), channel_id=1, source_target_pairs={{0,1},{1,0},{2,3},{3,2},{4,5},{5,4},{6,7},{7,6},{8,9},{9,8},{10,11... | collective-permute-start | bytes 2162696 | tf_op jit(solution)/shard_map/ppermute | solution.py:17
  121.5 21.4 %collective-permute-start.26 = (bf16[512,704]{0,1:T(8,128)(2,1)}, bf16[512,704]{0,1:T(8,128)(2,1)}, u32[]{:S(2)}, u32[]{:S(2)}) collective-permute-start(bf16[512,704]{0,1:T(8,128)(2,1)} %bitcast.77), channel_id=1, source_target_pairs={{0,2},{1,3},{2,0},{3,1},{4,6},{5,7},{6,4},{7,5},{8,10},{9,11},{10,... | collective-permute-start | bytes 2162696 | tf_op jit(solution)/shard_map/ppermute | solution.py:17
  132.8 12.4 %collective-permute-start.19 = (bf16[256,1024]{1,0:T(8,128)(2,1)}, bf16[256,1024]{1,0:T(8,128)(2,1)}, u32[]{:S(2)}, u32[]{:S(2)}) collective-permute-start(bf16[256,1024]{1,0:T(8,128)(2,1)} %get-tuple-element.76), channel_id=1, source_target_pairs={{0,4},{4,0},{1,5},{5,1},{2,6},{6,2},{3,7},{7,3},{8,12},{12,8},{9,1... | collective-permute-start | bytes 1572872 | tf_op jit(solution)/shard_map/ppermute | solution.py:17
  134.9 14.6 %collective-permute-start.35 = (bf16[256,1024]{1,0:T(8,128)(2,1)S(1)}, bf16[256,1024]{1,0:T(8,128)(2,1)S(1)}, u32[]{:S(2)}, u32[]{:S(2)}) collective-permute-start(bf16[256,1024]{1,0:T(8,128)(2,1)S(1)} %convolution_convert_fusion.7), channel_id=1, source_target_pairs={{0,8},{8,0},{1,9},{9,1},{2,10},{10,2},{3,11},{11,3},{4,12},{12,4},... | collective-permute-start | bytes 1572872 | tf_op jit(solution)/shard_map/ppermute | solution.py:17
  148.1 14.4 %collective-permute-start.20 = (bf16[256,1024]{1,0:T(8,128)(2,1)S(1)}, bf16[256,1024]{1,0:T(8,128)(2,1)S(1)}, u32[]{:S(2)}, u32[]{:S(2)}) collective-permute-start(bf16[256,1024]{1,0:T(8,128)(2,1)S(1)} %add_convert_fusion.10), channel_id=1, source_target_pairs={{0,8},{8,0},{1,9},{9,1},{2,10},{10,2},{3,11},{11,3},{4,12},{12,4},... | collective-permute-start | bytes 1572872 | tf_op jit(solution)/shard_map/ppermute | solution.py:17
  149.6 27.3 %collective-permute-start.37 = (bf16[256,1024]{1,0:T(8,128)(2,1)S(1)}, bf16[256,1024]{1,0:T(8,128)(2,1)S(1)}, u32[]{:S(2)}, u32[]{:S(2)}) collective-permute-start(bf16[256,1024]{1,0:T(8,128)(2,1)S(1)} %convolution_convert_fusion.7), channel_id=1, source_target_pairs={{0,4},{4,0},{1,5},{5,1},{2,6},{6,2},{3,7},{7,3},{8,12},{12,8},{9,1... | collective-permute-start | bytes 1572872 | tf_op jit(solution)/shard_map/ppermute | solution.py:17
  151.5 25.4 %collective-permute-start.36 = (bf16[256,1024]{1,0:T(8,128)(2,1)S(1)}, bf16[256,1024]{1,0:T(8,128)(2,1)S(1)}, u32[]{:S(2)}, u32[]{:S(2)}) collective-permute-start(bf16[256,1024]{1,0:T(8,128)(2,1)S(1)} %collective-permute-done.35), channel_id=1, source_target_pairs={{0,4},{4,0},{1,5},{5,1},{2,6},{6,2},{3,7},{7,3},{8,12},{12,8},{9,1... | collective-permute-start | bytes 1572872 | tf_op jit(solution)/shard_map/ppermute | solution.py:17
  163.1 13.6 %collective-permute-start.21 = (bf16[256,1024]{1,0:T(8,128)(2,1)S(1)}, bf16[256,1024]{1,0:T(8,128)(2,1)S(1)}, u32[]{:S(2)}, u32[]{:S(2)}) collective-permute-start(bf16[256,1024]{1,0:T(8,128)(2,1)S(1)} %add_convert_fusion.9), channel_id=1, source_target_pairs={{0,8},{8,0},{1,9},{9,1},{2,10},{10,2},{3,11},{11,3},{4,12},{12,4},... | collective-permute-start | bytes 1572872 | tf_op jit(solution)/shard_map/ppermute | solution.py:17
  165.4 11.8 %collective-permute-start.23 = (bf16[256,1024]{1,0:T(8,128)(2,1)S(1)}, bf16[256,1024]{1,0:T(8,128)(2,1)S(1)}, u32[]{:S(2)}, u32[]{:S(2)}) collective-permute-start(bf16[256,1024]{1,0:T(8,128)(2,1)S(1)} %add_convert_fusion.9), channel_id=1, source_target_pairs={{0,4},{4,0},{1,5},{5,1},{2,6},{6,2},{3,7},{7,3},{8,12},{12,8},{9,1... | collective-permute-start | bytes 1572872 | tf_op jit(solution)/shard_map/ppermute | solution.py:17
  193.1 26.9 %collective-permute-start.33 = (bf16[256,1024]{1,0:T(8,128)(2,1)S(1)}, bf16[256,1024]{1,0:T(8,128)(2,1)S(1)}, u32[]{:S(2)}, u32[]{:S(2)}) collective-permute-start(bf16[256,1024]{1,0:T(8,128)(2,1)S(1)} %get-tuple-element.74), channel_id=1, source_target_pairs={{0,4},{4,0},{1,5},{5,1},{2,6},{6,2},{3,7},{7,3},{8,12},{12,8},{9,1... | collective-permute-start | bytes 1572872 | tf_op jit(solution)/shard_map/ppermute | solution.py:17
  197.9 12.2 %collective-permute-start.77 = (bf16[176,1024]{1,0:T(8,128)(2,1)S(1)}, bf16[176,1024]{1,0:T(8,128)(2,1)S(1)}, u32[]{:S(2)}, u32[]{:S(2)}) collective-permute-start(bf16[176,1024]{1,0:T(8,128)(2,1)S(1)} %get-tuple-element.128), channel_id=1, source_target_pairs={{0,3},{1,2},{2,1},{3,0},{4,7},{5,6},{6,5},{7,4},{8,11},{9,10},{10,... | collective-permute-start | bytes 1081352 | tf_op jit(solution)/shard_map/ppermute | solution.py:17
  199.6 18.1 %collective-permute-start.76 = (bf16[176,1024]{1,0:T(8,128)(2,1)S(1)}, bf16[176,1024]{1,0:T(8,128)(2,1)S(1)}, u32[]{:S(2)}, u32[]{:S(2)}) collective-permute-start(bf16[176,1024]{1,0:T(8,128)(2,1)S(1)} %get-tuple-element.127), channel_id=1, source_target_pairs={{0,2},{1,3},{2,0},{3,1},{4,6},{5,7},{6,4},{7,5},{8,10},{9,11},{10,... | collective-permute-start | bytes 1081352 | tf_op jit(solution)/shard_map/ppermute | solution.py:17
  200.2 18.3 %collective-permute-start.75 = (bf16[176,1024]{1,0:T(8,128)(2,1)S(1)}, bf16[176,1024]{1,0:T(8,128)(2,1)S(1)}, u32[]{:S(2)}, u32[]{:S(2)}) collective-permute-start(bf16[176,1024]{1,0:T(8,128)(2,1)S(1)} %get-tuple-element.126), channel_id=1, source_target_pairs={{0,1},{1,0},{2,3},{3,2},{4,5},{5,4},{6,7},{7,6},{8,9},{9,8},{10,11... | collective-permute-start | bytes 1081352 | tf_op jit(solution)/shard_map/ppermute | solution.py:17
  202.5 19.0 %collective-permute-start.38 = (bf16[256,1024]{1,0:T(8,128)(2,1)S(1)}, bf16[256,1024]{1,0:T(8,128)(2,1)S(1)}, u32[]{:S(2)}, u32[]{:S(2)}) collective-permute-start(bf16[256,1024]{1,0:T(8,128)(2,1)S(1)} %get-tuple-element.71), channel_id=1, source_target_pairs={{0,4},{4,0},{1,5},{5,1},{2,6},{6,2},{3,7},{7,3},{8,12},{12,8},{9,1... | collective-permute-start | bytes 1572872 | tf_op jit(solution)/shard_map/ppermute | solution.py:17
  210.1 25.3 %collective-permute-start.70 = (bf16[512,704]{0,1:T(8,128)(2,1)S(1)}, bf16[512,704]{0,1:T(8,128)(2,1)S(1)}, u32[]{:S(2)}, u32[]{:S(2)}) collective-permute-start(bf16[512,704]{0,1:T(8,128)(2,1)S(1)} %broadcast_select_fusion.16), channel_id=1, source_target_pairs={{0,3},{1,2},{2,1},{3,0},{4,7},{5,6},{6,5},{7,4},{8,11},{9,10},{10,... | collective-permute-start | bytes 2162696 | tf_op jit(solution)/shard_map/ppermute | solution.py:17
  217.7 30.6 %collective-permute-start.69 = (bf16[512,704]{0,1:T(8,128)(2,1)S(1)}, bf16[512,704]{0,1:T(8,128)(2,1)S(1)}, u32[]{:S(2)}, u32[]{:S(2)}) collective-permute-start(bf16[512,704]{0,1:T(8,128)(2,1)S(1)} %get-tuple-element.84), channel_id=1, source_target_pairs={{0,2},{1,3},{2,0},{3,1},{4,6},{5,7},{6,4},{7,5},{8,10},{9,11},{10,... | collective-permute-start | bytes 2162696 | tf_op jit(solution)/shard_map/ppermute | solution.py:17
  218.5 30.3 %collective-permute-start.68 = (bf16[512,704]{0,1:T(8,128)(2,1)S(1)}, bf16[512,704]{0,1:T(8,128)(2,1)S(1)}, u32[]{:S(2)}, u32[]{:S(2)}) collective-permute-start(bf16[512,704]{0,1:T(8,128)(2,1)S(1)} %get-tuple-element.83), channel_id=1, source_target_pairs={{0,1},{1,0},{2,3},{3,2},{4,5},{5,4},{6,7},{7,6},{8,9},{9,8},{10,11... | collective-permute-start | bytes 2162696 | tf_op jit(solution)/shard_map/ppermute | solution.py:17
  220.0 13.2 %collective-permute-start.40 = (bf16[256,1024]{1,0:T(8,128)(2,1)S(1)}, bf16[256,1024]{1,0:T(8,128)(2,1)S(1)}, u32[]{:S(2)}, u32[]{:S(2)}) collective-permute-start(bf16[256,1024]{1,0:T(8,128)(2,1)S(1)} %add_convert_fusion.6), channel_id=1, source_target_pairs={{0,8},{8,0},{1,9},{9,1},{2,10},{10,2},{3,11},{11,3},{4,12},{12,4},... | collective-permute-start | bytes 1572872 | tf_op jit(solution)/shard_map/ppermute | solution.py:17
  221.5 32.1 %collective-permute-start.32 = (bf16[256,1024]{1,0:T(8,128)(2,1)S(1)}, bf16[256,1024]{1,0:T(8,128)(2,1)S(1)}, u32[]{:S(2)}, u32[]{:S(2)}) collective-permute-start(bf16[256,1024]{1,0:T(8,128)(2,1)S(1)} %get-tuple-element.73), channel_id=1, source_target_pairs={{0,4},{4,0},{1,5},{5,1},{2,6},{6,2},{3,7},{7,3},{8,12},{12,8},{9,1... | collective-permute-start | bytes 1572872 | tf_op jit(solution)/shard_map/ppermute | solution.py:17
  233.2 19.9 %collective-permute-start.78 = (bf16[176,1024]{1,0:T(8,128)(2,1)S(1)}, bf16[176,1024]{1,0:T(8,128)(2,1)S(1)}, u32[]{:S(2)}, u32[]{:S(2)}) collective-permute-start(bf16[176,1024]{1,0:T(8,128)(2,1)S(1)} %add_convert_fusion.12), channel_id=1, source_target_pairs={{0,16},{16,0},{1,17},{17,1},{2,18},{18,2},{3,19},{19,3},{4,20},{20... | collective-permute-start | bytes 1081352 | tf_op jit(solution)/shard_map/ppermute | solution.py:17
  235.4 47.8 %collective-permute-start.34 = (bf16[256,1024]{1,0:T(8,128)(2,1)S(1)}, bf16[256,1024]{1,0:T(8,128)(2,1)S(1)}, u32[]{:S(2)}, u32[]{:S(2)}) collective-permute-start(bf16[256,1024]{1,0:T(8,128)(2,1)S(1)} %add_convert_fusion.8), channel_id=1, source_target_pairs={{0,8},{8,0},{1,9},{9,1},{2,10},{10,2},{3,11},{11,3},{4,12},{12,4},... | collective-permute-start | bytes 1572872 | tf_op jit(solution)/shard_map/ppermute | solution.py:17
  248.3 34.9 %collective-permute-start.41 = (bf16[256,1024]{1,0:T(8,128)(2,1)}, bf16[256,1024]{1,0:T(8,128)(2,1)}, u32[]{:S(2)}, u32[]{:S(2)}) collective-permute-start(bf16[256,1024]{1,0:T(8,128)(2,1)} %add_convert_fusion.5), channel_id=1, source_target_pairs={{0,8},{8,0},{1,9},{9,1},{2,10},{10,2},{3,11},{11,3},{4,12},{12,4},... | collective-permute-start | bytes 1572872 | tf_op jit(solution)/shard_map/ppermute | solution.py:17
  250.3 37.8 %collective-permute-start.71 = (bf16[512,704]{0,1:T(8,128)(2,1)}, bf16[512,704]{0,1:T(8,128)(2,1)}, u32[]{:S(2)}, u32[]{:S(2)}) collective-permute-start(bf16[512,704]{0,1:T(8,128)(2,1)} %add_convert_fusion.1), channel_id=1, source_target_pairs={{0,16},{16,0},{1,17},{17,1},{2,18},{18,2},{3,19},{19,3},{4,20},{20... | collective-permute-start | bytes 2162696 | tf_op jit(solution)/shard_map/ppermute | solution.py:17
  253.3 66.5 %collective-permute-start.79 = (bf16[176,1024]{1,0:T(8,128)(2,1)S(1)}, bf16[176,1024]{1,0:T(8,128)(2,1)}, u32[]{:S(2)}, u32[]{:S(2)}) collective-permute-start(bf16[176,1024]{1,0:T(8,128)(2,1)S(1)} %add_convert_fusion.11), channel_id=1, source_target_pairs={{0,8},{8,0},{1,9},{9,1},{2,10},{10,2},{3,11},{11,3},{4,12},{12,4},... | collective-permute-start | bytes 1081352 | tf_op jit(solution)/shard_map/ppermute | solution.py:17
  253.6 37.1 %collective-permute-start.43 = (bf16[256,1024]{1,0:T(8,128)(2,1)}, bf16[256,1024]{1,0:T(8,128)(2,1)}, u32[]{:S(2)}, u32[]{:S(2)}) collective-permute-start(bf16[256,1024]{1,0:T(8,128)(2,1)} %add_convert_fusion.5), channel_id=1, source_target_pairs={{0,4},{4,0},{1,5},{5,1},{2,6},{6,2},{3,7},{7,3},{8,12},{12,8},{9,1... | collective-permute-start | bytes 1572872 | tf_op jit(solution)/shard_map/ppermute | solution.py:17
  284.6 115.6 %all-to-all-start.1 = ((bf16[32,8,1024]{2,1,0:T(8,128)(2,1)}), bf16[32,8,1024]{2,1,0:T(8,128)(2,1)}, u32[]{:S(2)}, u32[]{:S(2)}) async-start(bf16[32,8,1024]{2,1,0:T(8,128)(2,1)} %fusion.15), calls=%async_computation.1 | async-start | bytes 1048576 | tf_op jit(solution)/shard_map/all_to_all | solution.py:285
  308.8 13.7 %collective-permute-start.50 = (bf16[2,128,128]{2,1,0:T(8,128)(2,1)S(1)}, bf16[2,128,128]{2,1,0:T(8,128)(2,1)S(1)}, u32[]{:S(2)}, u32[]{:S(2)}) collective-permute-start(bf16[2,128,128]{2,1,0:T(8,128)(2,1)S(1)} %fusion.57), channel_id=1, source_target_pairs={{0,19},{1,18},{2,17},{3,16},{16,3},{17,2},{18,1},{19,0},{4,23},{5,... | collective-permute-start | bytes 196616 | tf_op jit(solution)/shard_map/ppermute | solution.py:94
  325.5 24.5 %collective-permute-start.81 = (bf16[176,1024]{1,0:T(8,128)(2,1)S(1)}, bf16[176,1024]{1,0:T(8,128)(2,1)S(1)}, u32[]{:S(2)}, u32[]{:S(2)}) collective-permute-start(bf16[176,1024]{1,0:T(8,128)(2,1)S(1)} %add_convert_fusion.11), channel_id=1, source_target_pairs={{0,4},{4,0},{1,5},{5,1},{2,6},{6,2},{3,7},{7,3},{8,12},{12,8},{9,1... | collective-permute-start | bytes 1081352 | tf_op jit(solution)/shard_map/ppermute | solution.py:17
  325.9 24.2 %collective-permute-start.80 = (bf16[176,1024]{1,0:T(8,128)(2,1)}, bf16[176,1024]{1,0:T(8,128)(2,1)S(1)}, u32[]{:S(2)}, u32[]{:S(2)}) collective-permute-start(bf16[176,1024]{1,0:T(8,128)(2,1)} %collective-permute-done.79), channel_id=1, source_target_pairs={{0,4},{4,0},{1,5},{5,1},{2,6},{6,2},{3,7},{7,3},{8,12},{12,8},{9,1... | collective-permute-start | bytes 1081352 | tf_op jit(solution)/shard_map/ppermute | solution.py:17
  326.1 13.7 %collective-permute-start.63 = (bf16[256,256]{1,0:T(8,128)(2,1)S(1)}, bf16[256,256]{1,0:T(8,128)(2,1)S(1)}, u32[]{:S(2)}, u32[]{:S(2)}) collective-permute-start(bf16[256,256]{1,0:T(8,128)(2,1)S(1)} %get-tuple-element.158), channel_id=1, source_target_pairs={{0,3},{1,2},{2,1},{3,0},{4,7},{5,6},{6,5},{7,4},{8,11},{9,10},{10,... | collective-permute-start | bytes 393224 | tf_op jit(solution)/shard_map/ppermute | solution.py:17
  328.3 11.5 %collective-permute-start.62 = (bf16[256,256]{1,0:T(8,128)(2,1)S(1)}, bf16[256,256]{1,0:T(8,128)(2,1)S(1)}, u32[]{:S(2)}, u32[]{:S(2)}) collective-permute-start(bf16[256,256]{1,0:T(8,128)(2,1)S(1)} %get-tuple-element.157), channel_id=1, source_target_pairs={{0,2},{1,3},{2,0},{3,1},{4,6},{5,7},{6,4},{7,5},{8,10},{9,11},{10,... | collective-permute-start | bytes 393224 | tf_op jit(solution)/shard_map/ppermute | solution.py:17
  341.9 16.4 %collective-permute-start.56 = (bf16[256,1024]{1,0:T(8,128)(2,1)S(1)}, bf16[256,1024]{1,0:T(8,128)(2,1)S(1)}, u32[]{:S(2)}, u32[]{:S(2)}) collective-permute-start(bf16[256,1024]{1,0:T(8,128)(2,1)S(1)} %get-tuple-element.98), channel_id=1, source_target_pairs={{0,3},{1,2},{2,1},{3,0},{4,7},{5,6},{6,5},{7,4},{8,11},{9,10},{10,... | collective-permute-start | bytes 1572872 | tf_op jit(solution)/shard_map/ppermute | solution.py:17
  344.1 22.3 %collective-permute-start.55 = (bf16[256,1024]{1,0:T(8,128)(2,1)S(1)}, bf16[256,1024]{1,0:T(8,128)(2,1)S(1)}, u32[]{:S(2)}, u32[]{:S(2)}) collective-permute-start(bf16[256,1024]{1,0:T(8,128)(2,1)S(1)} %get-tuple-element.97), channel_id=1, source_target_pairs={{0,2},{1,3},{2,0},{3,1},{4,6},{5,7},{6,4},{7,5},{8,10},{9,11},{10,... | collective-permute-start | bytes 1572872 | tf_op jit(solution)/shard_map/ppermute | solution.py:17
  348.4 18.1 %collective-permute-start.54 = (bf16[256,1024]{1,0:T(8,128)(2,1)S(1)}, bf16[256,1024]{1,0:T(8,128)(2,1)S(1)}, u32[]{:S(2)}, u32[]{:S(2)}) collective-permute-start(bf16[256,1024]{1,0:T(8,128)(2,1)S(1)} %get-tuple-element.96), channel_id=1, source_target_pairs={{0,1},{1,0},{2,3},{3,2},{4,5},{5,4},{6,7},{7,6},{8,9},{9,8},{10,11... | collective-permute-start | bytes 1572872 | tf_op jit(solution)/shard_map/ppermute | solution.py:17
  350.0 17.7 %collective-permute-start.52 = (bf16[256,1024]{1,0:T(8,128)(2,1)S(1)}, bf16[256,1024]{1,0:T(8,128)(2,1)S(1)}, u32[]{:S(2)}, u32[]{:S(2)}) collective-permute-start(bf16[256,1024]{1,0:T(8,128)(2,1)S(1)} %get-tuple-element.68), channel_id=1, source_target_pairs={{0,4},{4,0},{1,5},{5,1},{2,6},{6,2},{3,7},{7,3},{8,12},{12,8},{9,1... | collective-permute-start | bytes 1572872 | tf_op jit(solution)/shard_map/ppermute | solution.py:17
  356.0 20.7 %collective-permute-start.72 = (bf16[512,704]{0,1:T(8,128)(2,1)S(1)}, bf16[512,704]{0,1:T(8,128)(2,1)}, u32[]{:S(2)}, u32[]{:S(2)}) collective-permute-start(bf16[512,704]{0,1:T(8,128)(2,1)S(1)} %copy-done.35), channel_id=1, source_target_pairs={{0,8},{8,0},{1,9},{9,1},{2,10},{10,2},{3,11},{11,3},{4,12},{12,4},... | collective-permute-start | bytes 2162696 | tf_op jit(solution)/shard_map/ppermute | solution.py:17
  358.2 59.2 %collective-permute-start.74 = (bf16[512,704]{0,1:T(8,128)(2,1)S(1)}, bf16[512,704]{0,1:T(8,128)(2,1)}, u32[]{:S(2)}, u32[]{:S(2)}) collective-permute-start(bf16[512,704]{0,1:T(8,128)(2,1)S(1)} %copy-done.35), channel_id=1, source_target_pairs={{0,4},{4,0},{1,5},{5,1},{2,6},{6,2},{3,7},{7,3},{8,12},{12,8},{9,1... | collective-permute-start | bytes 2162696 | tf_op jit(solution)/shard_map/ppermute | solution.py:17
  367.7 26.3 %collective-permute-start.57 = (bf16[256,1024]{1,0:T(8,128)(2,1)S(1)}, bf16[256,1024]{1,0:T(8,128)(2,1)S(1)}, u32[]{:S(2)}, u32[]{:S(2)}) collective-permute-start(bf16[256,1024]{1,0:T(8,128)(2,1)S(1)} %add_convert_fusion.3), channel_id=1, source_target_pairs={{0,16},{16,0},{1,17},{17,1},{2,18},{18,2},{3,19},{19,3},{4,20},{20... | collective-permute-start | bytes 1572872 | tf_op jit(solution)/shard_map/ppermute | solution.py:17
  376.7 18.3 %collective-permute-start.51 = (bf16[256,1024]{1,0:T(8,128)(2,1)S(1)}, bf16[256,1024]{1,0:T(8,128)(2,1)S(1)}, u32[]{:S(2)}, u32[]{:S(2)}) collective-permute-start(bf16[256,1024]{1,0:T(8,128)(2,1)S(1)} %get-tuple-element.67), channel_id=1, source_target_pairs={{0,4},{4,0},{1,5},{5,1},{2,6},{6,2},{3,7},{7,3},{8,12},{12,8},{9,1... | collective-permute-start | bytes 1572872 | tf_op jit(solution)/shard_map/ppermute | solution.py:17
  376.7 40.7 %collective-permute-start.73 = (bf16[512,704]{0,1:T(8,128)(2,1)}, bf16[512,704]{0,1:T(8,128)(2,1)}, u32[]{:S(2)}, u32[]{:S(2)}) collective-permute-start(bf16[512,704]{0,1:T(8,128)(2,1)} %collective-permute-done.72), channel_id=1, source_target_pairs={{0,4},{4,0},{1,5},{5,1},{2,6},{6,2},{3,7},{7,3},{8,12},{12,8},{9,1... | collective-permute-start | bytes 2162696 | tf_op jit(solution)/shard_map/ppermute | solution.py:17
  377.2 22.3 %collective-permute-start.53 = (bf16[256,1024]{1,0:T(8,128)(2,1)S(1)}, bf16[256,1024]{1,0:T(8,128)(2,1)S(1)}, u32[]{:S(2)}, u32[]{:S(2)}) collective-permute-start(bf16[256,1024]{1,0:T(8,128)(2,1)S(1)} %add_convert_fusion.4), channel_id=1, source_target_pairs={{0,8},{8,0},{1,9},{9,1},{2,10},{10,2},{3,11},{11,3},{4,12},{12,4},... | collective-permute-start | bytes 1572872 | tf_op jit(solution)/shard_map/ppermute | solution.py:17
  400.1 26.0 %collective-permute-start.58 = (bf16[256,1024]{1,0:T(8,128)(2,1)}, bf16[256,1024]{1,0:T(8,128)(2,1)}, u32[]{:S(2)}, u32[]{:S(2)}) collective-permute-start(bf16[256,1024]{1,0:T(8,128)(2,1)} %add_convert_fusion.2), channel_id=1, source_target_pairs={{0,8},{8,0},{1,9},{9,1},{2,10},{10,2},{3,11},{11,3},{4,12},{12,4},... | collective-permute-start | bytes 1572872 | tf_op jit(solution)/shard_map/ppermute | solution.py:17
  400.2 11.1 %all-to-all-start.4 = ((bf16[4,256,256]{2,1,0:T(8,128)(2,1)}), bf16[4,256,256]{2,1,0:T(8,128)(2,1)S(1)}, u32[]{:S(2)}, u32[]{:S(2)}) async-start(bf16[4,256,256]{2,1,0:T(8,128)(2,1)} %bitcast.258), calls=%async_computation.4 | async-start | bytes 1048576 | tf_op jit(solution)/shard_map/all_to_all | solution.py:309
  411.3 26.7 %all-to-all-start.3 = ((bf16[32,8,1024]{2,1,0:T(8,128)(2,1)}), bf16[32,8,1024]{2,1,0:T(8,128)(2,1)S(1)}, u32[]{:S(2)}, u32[]{:S(2)}) async-start(bf16[32,8,1024]{2,1,0:T(8,128)(2,1)} %fusion.16), calls=%async_computation.3 | async-start | bytes 1048576 | tf_op jit(solution)/shard_map/all_to_all | solution.py:285
  425.6 13.5 %collective-permute-start.60 = (bf16[256,1024]{1,0:T(8,128)(2,1)}, bf16[256,1024]{1,0:T(8,128)(2,1)}, u32[]{:S(2)}, u32[]{:S(2)}) collective-permute-start(bf16[256,1024]{1,0:T(8,128)(2,1)} %add_convert_fusion.2), channel_id=1, source_target_pairs={{0,4},{4,0},{1,5},{5,1},{2,6},{6,2},{3,7},{7,3},{8,12},{12,8},{9,1... | collective-permute-start | bytes 1572872 | tf_op jit(solution)/shard_map/ppermute | solution.py:17
  426.1 13.1 %collective-permute-start.59 = (bf16[256,1024]{1,0:T(8,128)(2,1)}, bf16[256,1024]{1,0:T(8,128)(2,1)}, u32[]{:S(2)}, u32[]{:S(2)}) collective-permute-start(bf16[256,1024]{1,0:T(8,128)(2,1)} %collective-permute-done.58), channel_id=1, source_target_pairs={{0,4},{4,0},{1,5},{5,1},{2,6},{6,2},{3,7},{7,3},{8,12},{12,8},{9,1... | collective-permute-start | bytes 1572872 | tf_op jit(solution)/shard_map/ppermute | solution.py:17
  (139 other events, 1127.6 us)

commit v2 on v1

--- a/solution.py
+++ b/solution.py
@@ -1,6 +1,10 @@
+import functools
+
 import jax
 import jax.numpy as jnp
 from jax import lax
+from jax.experimental import pallas as pl
+from jax.experimental.pallas import tpu as pltpu
 from jax.sharding import Mesh, PartitionSpec as P
 
 HEAD = 128
@@ -101,7 +105,7 @@
     return lax.optimization_barrier((value, *others))[0]
 
 
-def body(tokens_in, cotangent, deal_order, lengths, decay_rates, w_query, w_key, w_value, w_ugate, w_out, w_ffin, w_ffdown):
+def general_body(tokens_in, cotangent, deal_order, lengths, decay_rates, w_query, w_key, w_value, w_ugate, w_out, w_ffin, w_ffdown):
     rows, width = tokens_in.shape
     n_zh, n_shard = lax.axis_size("zh"), lax.axis_size("shard")
     groups = n_zh * n_shard
@@ -317,12 +321,995 @@
     return (output, input_grad, *grads, grad_out, grad_fin, grad_down)
 
 
+N_SHARD = 4
+ROWS = 256
+WIDTH = 1024
+COLS = 256
+HEADS_OWN = 2
+FF_PART = 176
+FF_OWN = 704
+SLOTS = 8
+DEVICES = 32
+TN = ((0,), (0,))
+NT = ((1,), (1,))
+NN = ((1,), (0,))
+GLOBAL = pl.BlockSpec(memory_space=pltpu.VMEM)
+
+
+def far(*values):
+    return tuple(pltpu.with_memory_space_constraint(v, pltpu.HBM) for v in values)
+
+
+def rel_of(i):
+    return (i & 1) * 2 + (i >> 1)
+
+
+def hbm(shape, dtype=BF):
+    return pltpu.HBM(shape, dtype)
+
+
+def sds(shape, dtype=BF):
+    return jax.ShapeDtypeStruct(shape, dtype)
+
+
+def run(kernel, out, prefetch, args, grid=None, in_specs=None, out_specs=None, scratch=(), mib=16, flops=0, nbytes=0):
+    return pl.pallas_call(
+        kernel,
+        out_shape=out,
+        grid_spec=pltpu.PrefetchScalarGridSpec(
+            num_scalar_prefetch=len(prefetch),
+            grid=grid or (1,),
+            in_specs=in_specs,
+            out_specs=out_specs,
+            scratch_shapes=list(scratch),
+        ),
+        compiler_params=pltpu.CompilerParams(
+            vmem_limit_bytes=mib << 20, dimension_semantics=("arbitrary",) * len(grid or (1,))
+        ),
+        cost_estimate=pl.CostEstimate(flops=0, bytes_accessed=0, transcendentals=0),
+    )(*prefetch, *args)
+
+
+def full(*shape):
+    return pl.BlockSpec(shape, lambda *_: (0,) * len(shape))
+
+
+def place(info, j):
+    return info[1] ^ j
+
+
+def block_abs(i, info):
+    return info[0] ^ rel_of(i)
+
+
+def seg_scalar(p, ends):
+    total = jnp.int32(0)
+    for n in range(8):
+        total = total + jnp.where(p >= ends[n], 1, 0)
+    return jnp.where(p < 0, -1, total)
+
+
+def seg_vector(base, shape, dim, ends):
+    p = base + lax.broadcasted_iota(jnp.int32, shape, dim)
+    total = jnp.zeros(shape, jnp.int32)
+    for n in range(8):
+        total = total + jnp.where(p >= ends[n], 1, 0)
+    return total
+
+
+def scales(a, info, ends, rates, h):
+    base = info[2] + a * BLOCK
+    prev = seg_scalar(base - 1, ends)
+    last = seg_scalar(base + BLOCK - 1, ends)
+    seg = seg_vector(base, (BLOCK, HEAD), 0, ends)
+    idx = lax.broadcasted_iota(jnp.int32, (BLOCK, HEAD), 0).astype(F32)
+    r = rates[info[0] * HEADS_OWN + h]
+    q_scale = jnp.where(seg == prev, jnp.exp(-(idx + 1.0) * r), 0.0)
+    k_scale = jnp.where(seg == last, jnp.exp(-(BLOCK - 1.0 - idx) * r), 0.0)
+    return q_scale, k_scale, passing(a, info, ends, rates, h)
+
+
+def passing(a, info, ends, rates, h):
+    base = info[2] + a * BLOCK
+    same = seg_scalar(base - 1, ends) == seg_scalar(base + BLOCK - 1, ends)
+    r = rates[info[0] * HEADS_OWN + h]
+    return jnp.exp(jnp.full((1, HEAD), -float(BLOCK), F32) * r) * jnp.where(same, 1.0, 0.0)
+
+
+def decay_masks(info, rates, out):
+    dist = lax.broadcasted_iota(jnp.int32, (BLOCK, BLOCK), 0) - lax.broadcasted_iota(jnp.int32, (BLOCK, BLOCK), 1)
+    away = jnp.maximum(dist, 0).astype(F32)
+    for h in range(HEADS_OWN):
+        r = rates[info[0] * HEADS_OWN + h]
+        out[h] = jnp.where(dist >= 0, jnp.exp(-away * r), 0.0)
+
+
+def same_seg(a, info, ends):
+    base = info[2] + a * BLOCK
+    return seg_vector(base, (BLOCK, 1), 0, ends) == seg_vector(base, (1, BLOCK), 1, ends)
+
+
+def rms(v):
+    return v * lax.rsqrt(jnp.mean(v * v, axis=-1, keepdims=True) + EPS)
+
+
+def rms_back(v, g):
+    s = lax.rsqrt(jnp.mean(v * v, axis=-1, keepdims=True) + EPS)
+    return s * g - v * ((s * s * s) * jnp.mean(v * g, axis=-1, keepdims=True))
+
+
+def lanes(j, info):
+    return pl.ds(pl.multiple_of(place(info, j) * 256, 256), 256)
+
+
+def rows_kernel(info, deal, tok, cot, leave, enter, sent_x, sent_g):
+    dev = info[3]
+    d = deal[...]
+    owner = lax.shift_right_logical(d, 8)
+    mine = owner == dev
+    r_i = lax.broadcasted_iota(jnp.int32, (ROWS, ROWS), 0)
+    c_i = lax.broadcasted_iota(jnp.int32, (ROWS, ROWS), 1)
+    upper = jnp.where(r_i < c_i, 1.0, 0.0).astype(BF)
+    count = dot(jnp.where(mine, 1.0, 0.0).astype(BF), upper)
+    local = (d - dev * ROWS).astype(F32)
+    lane8 = lax.broadcasted_iota(jnp.int32, (DEVICES, 128), 1)
+    picked = jnp.zeros((DEVICES, 128), F32)
+    for slot in range(SLOTS):
+        row = jnp.sum(jnp.where(mine & (count == float(slot)), local, 0.0), axis=1, keepdims=True)
+        picked = jnp.where(lane8 == slot, row, picked)
+    k_r = lax.broadcasted_iota(jnp.int32, (ROWS, DEVICES), 0)
+    k_c = lax.broadcasted_iota(jnp.int32, (ROWS, DEVICES), 1)
+    spread = jnp.where(lax.shift_right_logical(k_r, 3) == k_c, 1.0, 0.0).astype(BF)
+    wide = dot(spread, picked.astype(BF))
+    k8 = lax.broadcasted_iota(jnp.int32, (ROWS, 128), 0) & 7
+    l8 = lax.broadcasted_iota(jnp.int32, (ROWS, 128), 1)
+    column = jnp.sum(jnp.where(k8 == l8, wide, 0.0), axis=1, keepdims=True)
+    lv = jnp.where(column == c_i.astype(F32), 1.0, 0.0).astype(BF)
+    leave[...] = lv
+    sent_x[...] = dot(lv, tok[...]).astype(BF)
+    sent_g[...] = dot(lv, cot[...]).astype(BF)
+    for i in range(TEAM):
+        a = info[0] ^ rel_of(i)
+        at = (info[4] * TEAM + a) * N_SHARD + info[1]
+        src = lax.shift_right_logical(deal[pl.ds(at, 1), :], 8)
+        src_f = src.astype(F32)
+        src_col = jnp.sum(jnp.where(r_i == c_i, src_f, 0.0), axis=1, keepdims=True)
+        alike = jnp.where((src_col == src_f) & (c_i < r_i), 1.0, 0.0)
+        rank = jnp.sum(alike, axis=1, keepdims=True)
+        slot = src_col * float(SLOTS) + rank
+        enter[i] = jnp.where(slot == c_i.astype(F32), 1.0, 0.0).astype(BF)
+
+
+def exchange_rows(info, by_device, tokens_in, cotangent):
+    return run(
+        rows_kernel,
+        (sds((ROWS, ROWS)), sds((TEAM, ROWS, ROWS)), sds((ROWS, WIDTH)), sds((ROWS, WIDTH))),
+        (info,),
+        (by_device, tokens_in, cotangent),
+        in_specs=[full(DEVICES, ROWS), full(ROWS, WIDTH), full(ROWS, WIDTH)],
+        out_specs=[full(ROWS, ROWS), full(TEAM, ROWS, ROWS), full(ROWS, WIDTH), full(ROWS, WIDTH)],
+        flops=4 << 28,
+        nbytes=3 << 20,
+    )
+
+
+def quarter_kernel(info, wq, wk, wv, wu, out):
+    for t, w in enumerate((wq, wk, wv, wu)):
+        out[t * COLS : (t + 1) * COLS] = w[...]
+
+
+def take_quarter(info, *weights):
+    spec = pl.BlockSpec((256, COLS), lambda i, info: (0, info[0]))
+    return run(
+        quarter_kernel,
+        sds((4 * COLS, COLS)),
+        (info,),
+        weights,
+        in_specs=[spec] * 4,
+        out_specs=full(4 * COLS, COLS),
+        nbytes=1 << 20,
+    )
+
+
+def ff_bundle_kernel(info, fin, down, out, turned):
+    me = info[0]
+    unit = jnp.where(
+        lax.broadcasted_iota(jnp.int32, (256, 256), 0) == lax.broadcasted_iota(jnp.int32, (256, 256), 1), 1.0, 0.0
+    ).astype(BF)
+    for n in range(11):
+        turned[n * 512 : (n + 1) * 512] = dot(fin[:, n * 512 : (n + 1) * 512], unit, TN).astype(BF)
+    for n in range(2 * N_SHARD):
+        start = pl.multiple_of(n * FF_OWN + me * FF_PART, 16)
+        out[n * FF_PART : (n + 1) * FF_PART] = turned[pl.ds(start, FF_PART)]
+    for c in range(4):
+        rows = pl.ds(pl.multiple_of(me * FF_PART, 16), FF_PART)
+        at = 2 * FF_OWN + c * FF_PART
+        out[at : at + FF_PART] = down[rows, c * 256 : (c + 1) * 256]
+
+
+def ff_bundle(info, fin, down):
+    return run(
+        ff_bundle_kernel,
+        sds((3 * FF_OWN, 256)),
+        (info,),
+        (fin, down),
+        in_specs=[full(*fin.shape), full(*down.shape)],
+        out_specs=full(3 * FF_OWN, 256),
+        scratch=[pltpu.VMEM((8 * FF_OWN, 256), BF)],
+        flops=1 << 30,
+        nbytes=6 << 20,
+    )
+
+
+def gather_pieces(part):
+    return [part] + [send(part, "shard", j) for j in (1, 2, 3)]
+
+
+def gather_out(w_out, me, shard):
+    axes = ("zl", "core", "shard")
+    rel = me ^ shard
+    wo = w_out
+    for j in (1, 2, 3):
+        pairs = [(m * N_SHARD + m, m * N_SHARD + (m ^ j)) for m in range(TEAM)]
+        wo = jnp.where(rel == j, lax.ppermute(w_out, axes, pairs), wo)
+    return wo
+
+
+def weight_at(refs, j, t):
+    return refs[j][t * 256 : (t + 1) * 256]
+
+
+def project_kernel(info, ends, rates, enter, r0, r1, r2, r3, w0, w1, w2, w3,
+                   x, normed, pq, pk, pu, q, k, v, kv, state, scr):
+    i = pl.program_id(0)
+    a = block_abs(i, info)
+    for t, raw in enumerate((r0, r1, r2, r3)):
+
+        @pl.when(i == t)
+        def _():
+            x[0] = dot(enter[0], raw[...]).astype(BF)
+
+    scr[...] = rms(x[0].astype(F32)).astype(BF)
+    normed[0] = scr[...]
+    refs = (w0, w1, w2, w3)
+    pre = []
+    for t in range(4):
+        total = dot(scr[:, lanes(0, info)], weight_at(refs, 0, t))
+        for j in (1, 2, 3):
+            total = total + dot(scr[:, lanes(j, info)], weight_at(refs, j, t))
+        pre.append(total)
+    pq[0], pk[0], pu[0] = pre[0], pre[1], pre[3]
+    qb = (pre[0] * jax.nn.sigmoid(pre[0])).astype(BF)
+    kb = (pre[1] * jax.nn.sigmoid(pre[1])).astype(BF)
+    vb = pre[2].astype(BF)
+    q[0], k[0], v[0] = qb, kb, vb
+    for h in range(HEADS_OWN):
+        at = slice(h * HEAD, (h + 1) * HEAD)
+        _, k_scale, _ = scales(a, info, ends, rates, h)
+        ks = (kb[:, at].astype(F32) * k_scale).astype(BF)
+        kv[a, h] = dot(ks, vb[:, at], TN)
+
+    @pl.when(i == TEAM - 1)
+    def _():
+        for h in range(HEADS_OWN):
+            total = kv[0, h]
+            for b in range(1, TEAM):
+                total = passing(b, info, ends, rates, h) * total + kv[b, h]
+            state[h] = total.astype(BF)
+
+
+def project(scal, enter, raws, pieces):
+    info = scal[0]
+    by_abs = pl.BlockSpec((1, ROWS, COLS), lambda i, info, *_: (block_abs(i, info), 0, 0))
+    by_abs_wide = pl.BlockSpec((1, ROWS, WIDTH), lambda i, info, *_: (block_abs(i, info), 0, 0))
+    by_i = pl.BlockSpec((1, ROWS, ROWS), lambda i, *_: (i, 0, 0))
+    by_i_wide = pl.BlockSpec((1, ROWS, WIDTH), lambda i, *_: (i, 0, 0))
+    f32_block, bf_block = sds((TEAM, ROWS, COLS), F32), sds((TEAM, ROWS, COLS))
+    return run(
+        project_kernel,
+        (
+            hbm((TEAM, ROWS, WIDTH)), hbm((TEAM, ROWS, WIDTH)), hbm((TEAM, ROWS, COLS), F32), hbm((TEAM, ROWS, COLS), F32),
+            f32_block, bf_block, bf_block,
+            bf_block, sds((TEAM, HEADS_OWN, HEAD, HEAD), F32), sds((HEADS_OWN, HEAD, HEAD)),
+        ),
+        scal,
+        (enter, *raws, *pieces),
+        grid=(TEAM,),
+        in_specs=[by_i, *[full(ROWS, WIDTH)] * 4, *[full(*p.shape) for p in pieces]],
+        out_specs=[
+            by_i_wide, by_abs_wide, *[by_abs] * 6, full(TEAM, HEADS_OWN, HEAD, HEAD), full(HEADS_OWN, HEAD, HEAD),
+        ],
+        scratch=[pltpu.VMEM((ROWS, WIDTH), BF)],
+        flops=3 << 30,
+        nbytes=14 << 20,
+    )
+
+
+def local_kernel(info, ends, rates, q, k, v, mixed, dec):
+    b = pl.program_id(0)
+
+    @pl.when(b == 0)
+    def _():
+        decay_masks(info, rates, dec)
+
+    same = same_seg(b, info, ends)
+    for h in range(HEADS_OWN):
+        at = slice(h * HEAD, (h + 1) * HEAD)
+        scores = dot(q[0, :, at], k[0, :, at], NT)
+        mixing = jnp.where(same, scores * dec[h], 0.0).astype(BF)
+        mixed[0, :, at] = dot(mixing, v[0, :, at])
+
+
+BLOCK_SPEC = pl.BlockSpec((1, ROWS, COLS), lambda i, *_: (i, 0, 0))
+
+
+def attend_local(scal, q, k, v):
+    return run(
+        local_kernel,
+        sds((TEAM, ROWS, COLS), F32),
+        scal,
+        (q, k, v),
+        grid=(TEAM,),
+        in_specs=[BLOCK_SPEC] * 3,
+        out_specs=BLOCK_SPEC,
+        scratch=[pltpu.VMEM((HEADS_OWN, BLOCK, BLOCK), F32)],
+        flops=1 << 28,
+        nbytes=3 << 20,
+    )
+
+
+def run_states(start, step, out, info, ends, rates, order):
+    for h in range(HEADS_OWN):
+        now = start[h]
+        for b in order:
+            out[b, h] = now.astype(BF)
+            now = passing(b, info, ends, rates, h) * now + step[b, h]
+
+
+def halves(i, value, keep, give):
+    @pl.when(i < 2)
+    def _():
+        keep[0] = value
+
+    @pl.when(i >= 2)
+    def _():
+        give[0] = value
+
+
+def carry_kernel(info, ends, rates, local, q, pu, kv, s_in, wo, mixed, gated, keep, give, states):
+    i = pl.program_id(0)
+    a = block_abs(i, info)
+
+    @pl.when(i == 0)
+    def _():
+        run_states(s_in, kv, states, info, ends, rates, range(TEAM))
+
+    for h in range(HEADS_OWN):
+        at = slice(h * HEAD, (h + 1) * HEAD)
+        q_scale, _, _ = scales(a, info, ends, rates, h)
+        qs = (q[0, :, at].astype(F32) * q_scale).astype(BF)
+        m = local[0, :, at] + dot(qs, states[a, h])
+        mixed[0, :, at] = m
+        gated[0, :, at] = (pu[0, :, at] * rms(m)).astype(BF)
+    halves(i, dot(gated[0], wo[...]).astype(BF), keep, give)
+
+
+KEEP = pl.BlockSpec((1, ROWS, WIDTH), lambda i, *_: (jnp.minimum(i, 1), 0, 0))
+GIVE = pl.BlockSpec((1, ROWS, WIDTH), lambda i, *_: (jnp.maximum(i - 2, 0), 0, 0))
+BY_ABS = pl.BlockSpec((1, ROWS, COLS), lambda i, info, *_: (block_abs(i, info), 0, 0))
+BY_ABS_WIDE = pl.BlockSpec((1, ROWS, WIDTH), lambda i, info, *_: (block_abs(i, info), 0, 0))
+BY_I = pl.BlockSpec((1, ROWS, ROWS), lambda i, *_: (i, 0, 0))
+BY_I_WIDE = pl.BlockSpec((1, ROWS, WIDTH), lambda i, *_: (i, 0, 0))
+PAIR = sds((2, ROWS, WIDTH))
+
+
+def carry_in(scal, local, q, pu, kv, s_in, wo):
+    return run(
+        carry_kernel,
+        (sds((TEAM, ROWS, COLS), F32), sds((TEAM, ROWS, COLS)), PAIR, PAIR),
+        scal,
+        (local, q, pu, kv, s_in, wo),
+        grid=(TEAM,),
+        in_specs=[BY_ABS, BY_ABS, BY_ABS, full(*kv.shape), full(*s_in.shape), full(*wo.shape)],
+        out_specs=[BY_ABS, BY_ABS, KEEP, GIVE],
+        scratch=[pltpu.VMEM((TEAM, HEADS_OWN, HEAD, HEAD), BF)],
+        flops=1 << 29,
+        nbytes=8 << 20,
+    )
+
+
+def sglu_kernel(info, enter, x, ta, tb, g0, g1, g2, g3, w,
+                g, n2, product, gg, gu, r_keep, r_give, n_keep, n_give, wd, scr, back):
+    i = pl.program_id(0)
+    pieces = [w.at[p] for p in range(N_SHARD)]
+
+    @pl.when(i == 0)
+    def _():
+        for p in range(N_SHARD):
+            for c in range(4):
+                at = 2 * FF_OWN + c * FF_PART
+                wd[p * FF_PART : (p + 1) * FF_PART, c * 256 : (c + 1) * 256] = w[p, at : at + FF_PART]
+
+    for t, raw in enumerate((g0, g1, g2, g3)):
+
+        @pl.when(i == t)
+        def _():
+            g[0] = dot(enter[0], raw[...]).astype(BF)
+
+    att = jnp.where(i < 2, ta[0].astype(F32), tb[0].astype(F32))
+    scr[...] = rms(x[0].astype(F32) + att).astype(BF)
+    n2[0] = scr[...]
+    gate = up = None
+    for j in range(N_SHARD):
+        rows = scr[:, j * 256 : (j + 1) * 256]
+        one, two = dot(rows, pieces[j][:FF_OWN], NT), dot(rows, pieces[j][FF_OWN : 2 * FF_OWN], NT)
+        gate, up = (one, two) if j == 0 else (gate + one, up + two)
+    prod = (gate * up).astype(BF)
+    product[0] = prod
+    g_prod = dot(g[0], wd[...], NT)
+    one, two = (g_prod * up).astype(BF), (g_prod * gate).astype(BF)
+    gg[0], gu[0] = one, two
+    for j in range(N_SHARD):
+        back[:, j * 256 : (j + 1) * 256] = (dot(one, pieces[j][:FF_OWN]) + dot(two, pieces[j][FF_OWN : 2 * FF_OWN])).astype(BF)
+    halves(i, back[...], n_keep, n_give)
+    halves(i, dot(prod, wd[...]).astype(BF), r_keep, r_give)
+
+
+def sglu(info, enter, x, ta, tb, raws, w_ff):
+    hid = pl.BlockSpec((1, ROWS, FF_OWN), lambda i, *_: (i, 0, 0))
+    hid_out = sds((TEAM, ROWS, FF_OWN))
+    wide = sds((TEAM, ROWS, WIDTH))
+    return run(
+        sglu_kernel,
+        (wide, wide, hid_out, hid_out, hid_out, PAIR, PAIR, PAIR, PAIR),
+        (info,),
+        (enter, x, ta, tb, *raws, w_ff),
+        grid=(TEAM,),
+        in_specs=[BY_I, BY_I_WIDE, KEEP, GIVE, *[full(ROWS, WIDTH)] * 4, full(*w_ff.shape)],
+        out_specs=[BY_I_WIDE, BY_I_WIDE, hid, hid, hid, KEEP, GIVE, KEEP, GIVE],
+        scratch=[
+            pltpu.VMEM((FF_OWN, WIDTH), BF),
+            pltpu.VMEM((ROWS, WIDTH), BF),
+            pltpu.VMEM((ROWS, WIDTH), BF),
+        ],
+        mib=34,
+        flops=12 << 30,
+        nbytes=28 << 20,
+    )
+
+
+def flat(v):
+    return v.reshape(-1, v.shape[-1])
+
+
+def turn(i, first):
+    return rel_of(i) if first == 1 else i
+
+
+def grads_call(kernel, info, rows, args, specs, scratch=(), nbytes=0):
+    shape = (2, rows, 256)
+    return run(
+        kernel,
+        (sds(shape), sds(shape)),
+        (info,),
+        args,
+        grid=(N_SHARD,),
+        in_specs=specs,
+        out_specs=[
+            pl.BlockSpec((1, rows, 256), lambda i, *_: (jnp.minimum(i, 1), 0, 0)),
+            pl.BlockSpec((1, rows, 256), lambda i, *_: (jnp.maximum(i - 2, 0), 0, 0)),
+        ],
+        scratch=scratch,
+        nbytes=nbytes,
+    )
+
+
+def hidden_grads_kernel(info, n2, grad, keep, give):
+    halves(pl.program_id(0), dot(grad[...], n2[...], TN).astype(BF), keep, give)
+
+
+def hidden_grads(info, n2, grad, first):
+    span = TEAM * ROWS
+    specs = [
+        pl.BlockSpec((span, 256), lambda i, info: (0, place(info, turn(i, first)))),
+        full(span, FF_OWN),
+    ]
+    return grads_call(hidden_grads_kernel, info, FF_OWN, (flat(n2), flat(grad)), specs)
+
+
+def down_grads(info, g, product, first):
+    span = TEAM * ROWS
+
+    def kernel(info, g, product, keep, give, dd):
+        i = pl.program_id(0)
+
+        @pl.when(i == 0)
+        def _():
+            for c in range(4):
+                dd[c] = dot(product[...], g[:, c * 256 : (c + 1) * 256], TN).astype(BF)
+
+        rows = pl.ds(pl.multiple_of(place(info, turn(i, first)) * FF_PART, 16), FF_PART)
+        for c in range(4):
+            at = slice(c * FF_PART, (c + 1) * FF_PART)
+
+            @pl.when(i < 2)
+            def _():
+                keep[0, at] = dd[c, rows]
+
+            @pl.when(i >= 2)
+            def _():
+                give[0, at] = dd[c, rows]
+
+    specs = [full(span, WIDTH), full(span, FF_OWN)]
+    return grads_call(
+        kernel, info, FF_OWN, (flat(g), flat(product)), specs, scratch=[pltpu.VMEM((4, FF_OWN, 256), BF)]
+    )
+
+
+def hidden_back_kernel(info, ends, rates, x, ta, tb, ua, ub, g, wo, mixed, pu, q,
+                       ga, gpu, gm, qg, gh, state):
+    i = pl.program_id(0)
+    a = block_abs(i, info)
+    att = jnp.where(i < 2, ta[0].astype(F32), tb[0].astype(F32))
+    gn2 = jnp.where(i < 2, ua[0].astype(F32), ub[0].astype(F32))
+    grad = g[0].astype(F32) + rms_back(x[0].astype(F32) + att, gn2)
+    ga[0] = grad.astype(BF)
+
+    @pl.when(i == 0)
+    def _():
+        gh[...] = grad
+
+    g_gated = dot(ga[0], wo[...], NT)
+    for h in range(HEADS_OWN):
+        at = slice(h * HEAD, (h + 1) * HEAD)
+        m = mixed[0, :, at]
+        gpu[0, :, at] = (g_gated[:, at] * rms(m)).astype(BF)
+        gmb = rms_back(m, g_gated[:, at] * pu[0, :, at]).astype(BF)
+        gm[0, :, at] = gmb
+        q_scale, _, _ = scales(a, info, ends, rates, h)
+        qs = (q[0, :, at].astype(F32) * q_scale).astype(BF)
+        qg[a, h] = dot(qs, gmb, TN)
+
+    @pl.when(i == TEAM - 1)
+    def _():
+        for h in range(HEADS_OWN):
+            total = qg[TEAM - 1, h]
+            for b in reversed(range(TEAM - 1)):
+                total = passing(b, info, ends, rates, h) * total + qg[b, h]
+            state[h] = total.astype(BF)
+
+
+def hidden_back(scal, x, ta, tb, ua, ub, g, wo, mixed, pu, q):
+    block = sds((TEAM, ROWS, COLS))
+    return run(
+        hidden_back_kernel,
+        (
+            sds((TEAM, ROWS, WIDTH)), block, block, sds((TEAM, HEADS_OWN, HEAD, HEAD), F32), sds((ROWS, WIDTH), F32),
+            sds((HEADS_OWN, HEAD, HEAD)),
+        ),
+        scal,
+        (x, ta, tb, ua, ub, g, wo, mixed, pu, q),
+        grid=(TEAM,),
+        in_specs=[BY_I_WIDE, KEEP, GIVE, KEEP, GIVE, BY_I_WIDE, full(*wo.shape), BY_ABS, BY_ABS, BY_ABS],
+        out_specs=[
+            BY_ABS_WIDE, BY_ABS, BY_ABS, full(TEAM, HEADS_OWN, HEAD, HEAD), full(ROWS, WIDTH), full(HEADS_OWN, HEAD, HEAD),
+        ],
+        flops=1 << 30,
+        nbytes=14 << 20,
+    )
+
+
+def scores_back_kernel(info, ends, rates, q, k, v, gm, kv, s_in, gq, gk, gv, dec, states):
+    b = pl.program_id(0)
+
+    @pl.when(b == 0)
+    def _():
+        decay_masks(info, rates, dec)
+        run_states(s_in, kv, states, info, ends, rates, range(TEAM))
+
+    same = same_seg(b, info, ends)
+    for h in range(HEADS_OWN):
+        at = slice(h * HEAD, (h + 1) * HEAD)
+        qh, kh, vh, gh = q[0, :, at], k[0, :, at], v[0, :, at], gm[0, :, at]
+        q_scale, _, _ = scales(b, info, ends, rates, h)
+        mixing = jnp.where(same, dot(qh, kh, NT) * dec[h], 0.0).astype(BF)
+        g_scores = jnp.where(same, dot(gh, vh, NT) * dec[h], 0.0).astype(BF)
+        gq[0, :, at] = dot(g_scores, kh) + q_scale * dot(gh, states[b, h], NT)
+        gk[0, :, at] = dot(g_scores, qh, TN)
+        gv[0, :, at] = dot(mixing, gh, TN)
+
+
+def scores_back(scal, q, k, v, gm, kv, s_in):
+    block = sds((TEAM, ROWS, COLS), F32)
+    return run(
+        scores_back_kernel,
+        (block, block, block),
+        scal,
+        (q, k, v, gm, kv, s_in),
+        grid=(TEAM,),
+        in_specs=[*[BLOCK_SPEC] * 4, full(*kv.shape), full(*s_in.shape)],
+        out_specs=[BLOCK_SPEC] * 3,
+        scratch=[
+            pltpu.VMEM((HEADS_OWN, BLOCK, BLOCK), F32),
+            pltpu.VMEM((TEAM, HEADS_OWN, HEAD, HEAD), BF),
+        ],
+        flops=3 << 28,
+        nbytes=6 << 20,
+    )
+
+
+def silu_slope(p):
+    s = jax.nn.sigmoid(p)
+    return s * (1.0 + p * (1.0 - s))
+
+
+def project_back_kernel(info, ends, rates, gq, gk, gv, pq, pk, k, v, gpu, qg, g_in, w0, w1, w2, w3,
+                        dqkv, keep, give, states, back):
+    i = pl.program_id(0)
+    a = block_abs(i, info)
+
+    @pl.when(i == 0)
+    def _():
+        run_states(g_in, qg, states, info, ends, rates, (3, 2, 1, 0))
+
+    dqkv[0, :, :COLS] = (gq[0] * silu_slope(pq[0])).astype(BF)
+    for h in range(HEADS_OWN):
+        at = slice(h * HEAD, (h + 1) * HEAD)
+        _, k_scale, _ = scales(a, info, ends, rates, h)
+        kh, vh = k[0, :, at], v[0, :, at]
+        ks = (kh.astype(F32) * k_scale).astype(BF)
+        g_k = gk[0, :, at] + k_scale * dot(vh, states[a, h], NT)
+        to_k = slice(COLS + h * HEAD, COLS + (h + 1) * HEAD)
+        to_v = slice(2 * COLS + h * HEAD, 2 * COLS + (h + 1) * HEAD)
+        dqkv[0, :, to_k] = (g_k * silu_slope(pk[0, :, at])).astype(BF)
+        dqkv[0, :, to_v] = (gv[0, :, at] + dot(ks, states[a, h])).astype(BF)
+    refs = (w0, w1, w2, w3)
+    grads = (dqkv[0, :, :COLS], dqkv[0, :, COLS : 2 * COLS], dqkv[0, :, 2 * COLS :], gpu[0])
+    for j in range(N_SHARD):
+        total = dot(grads[0], weight_at(refs, j, 0), NT)
+        for t in (1, 2, 3):
+            total = total + dot(grads[t], weight_at(refs, j, t), NT)
+        back[:, lanes(j, info)] = total.astype(BF)
+    halves(i, back[...], keep, give)
+
+
+def project_back(scal, gq, gk, gv, pq, pk, k, v, gpu, qg, g_in, pieces):
+    return run(
+        project_back_kernel,
+        (sds((TEAM, ROWS, 3 * COLS)), PAIR, PAIR),
+        scal,
+        (gq, gk, gv, pq, pk, k, v, gpu, qg, g_in, *pieces),
+        grid=(TEAM,),
+        in_specs=[*[BY_ABS] * 8, full(*qg.shape), full(*g_in.shape), *[full(*p.shape) for p in pieces]],
+        out_specs=[pl.BlockSpec((1, ROWS, 3 * COLS), lambda i, info, *_: (block_abs(i, info), 0, 0)), KEEP, GIVE],
+        scratch=[pltpu.VMEM((TEAM, HEADS_OWN, HEAD, HEAD), BF), pltpu.VMEM((ROWS, WIDTH), BF)],
+        flops=5 << 29,
+        nbytes=14 << 20,
+    )
+
+
+def column_grads(info, pairs, first):
+    span = TEAM * ROWS
+    args, specs = [], []
+    for pair in pairs:
+        for v in pair:
+            args.append(v.reshape(span, v.shape[-1]))
+            wide = v.shape[-1] == WIDTH
+            cut = (lambda i, info: (0, place(info, turn(i, first)))) if wide else (lambda i, info: (0, 0))
+            specs.append(pl.BlockSpec((span, 256 if wide else v.shape[-1]), cut))
+    n = sum(1 if b.shape[-1] == WIDTH else b.shape[-1] // 256 for _, b in pairs)
+
+    def kernel(info, *refs):
+        i = pl.program_id(0)
+        values = []
+        for t in range(len(pairs)):
+            value = dot(refs[2 * t][...], refs[2 * t + 1][...], TN).astype(BF)
+            values += [value[:, c * 256 : (c + 1) * 256] for c in range(value.shape[1] // 256)]
+        for t, value in enumerate(values):
+            at = slice(t * 256, (t + 1) * 256)
+
+            @pl.when(i < 2)
+            def _():
+                refs[-2][0, at] = value
+
+            @pl.when(i >= 2)
+            def _():
+                refs[-1][0, at] = value
+
+    return grads_call(kernel, info, n * 256, tuple(args), specs)
+
+
+def hop(parts, first, hold=()):
+    keep, give = parts
+    got = send(give, "shard", first)
+    if hold:
+        got = after(got, *hold)
+    total = keep.astype(F32) + got.astype(F32)
+    return total[0].astype(BF), total[1].astype(BF)
+
+
+def hop_two(own, other, first, hold=(), hold_send=()):
+    got = send(after(other, *hold_send) if hold_send else other, "shard", 3 - first)
+    if hold:
+        got = after(got, *hold)
+    return (own.astype(F32) + got.astype(F32)).astype(BF)
+
+
+def over_zh(part, hold=(), hold_send=()):
+    if hold_send:
+        part = after(part, *hold_send)
+    got = send(part, "zh", 1)
+    if hold:
+        got = after(got, *hold)
+    return (part.astype(F32) + got.astype(F32)).astype(BF)
+
+
+def fin_out_kernel(info, p0, p1, p2, p3, u0, u1, u2, u3, fin, stack):
+    unit = jnp.where(
+        lax.broadcasted_iota(jnp.int32, (256, 256), 0) == lax.broadcasted_iota(jnp.int32, (256, 256), 1), 1.0, 0.0
+    ).astype(BF)
+    for j, both in enumerate(((p0, u0), (p1, u1), (p2, u2), (p3, u3))):
+        q = info[0] ^ j
+        for n in range(2 * N_SHARD):
+            start = pl.multiple_of(n * FF_OWN + q * FF_PART, 16)
+            m = n % N_SHARD
+            stack[pl.ds(start, FF_PART)] = both[n // N_SHARD][m * FF_PART : (m + 1) * FF_PART]
+    for n in range(11):
+        fin[:, n * 512 : (n + 1) * 512] = dot(unit, stack[n * 512 : (n + 1) * 512], NT)
+
+
+def fin_out(info, pieces):
+    return run(
+        fin_out_kernel,
+        sds((256, 8 * FF_OWN), F32),
+        (info,),
+        tuple(pieces),
+        in_specs=[full(FF_OWN, 256)] * 8,
+        out_specs=full(256, 8 * FF_OWN),
+        scratch=[pltpu.VMEM((8 * FF_OWN, 256), BF)],
+        mib=24,
+        flops=1 << 30,
+        nbytes=9 << 20,
+    )
+
+
+def down_out_kernel(info, p0, p1, p2, p3, down):
+    for j, p in enumerate((p0, p1, p2, p3)):
+        rows = pl.ds(pl.multiple_of((info[0] ^ j) * FF_PART, 16), FF_PART)
+        for c in range(4):
+            down[rows, c * 256 : (c + 1) * 256] = p[c * FF_PART : (c + 1) * FF_PART].astype(F32)
+
+
+def down_out(info, pieces):
+    return run(
+        down_out_kernel,
+        sds((FF_OWN, WIDTH), F32),
+        (info,),
+        tuple(pieces),
+        in_specs=[full(FF_OWN, 256)] * 4,
+        out_specs=full(FF_OWN, WIDTH),
+        nbytes=5 << 20,
+    )
+
+
+def columns_out_kernel(info, *refs):
+    pieces, outs = refs[:4], refs[4:]
+    for j, p in enumerate(pieces):
+        at = pl.ds(pl.multiple_of((info[0] ^ j) * 256, 256), 256)
+        for t, out in enumerate(outs):
+            out[:, at] = p[t * 256 : (t + 1) * 256].astype(F32)
+
+
+def columns_out(info, pieces, n):
+    return run(
+        columns_out_kernel,
+        (sds((256, WIDTH), F32),) * n,
+        (info,),
+        tuple(pieces),
+        in_specs=[full(*p.shape) for p in pieces],
+        out_specs=[full(256, WIDTH)] * n,
+        nbytes=(3 * n) << 19,
+    )
+
+
+def out_grad_kernel(info, o0, o1, o2, o3, p0, p1, p2, p3, g_out, g_u):
+    for j, (o, p) in enumerate(zip((o0, o1, o2, o3), (p0, p1, p2, p3))):
+        g_out[:, lanes(j, info)] = o[...].astype(F32)
+        g_u[:, pl.ds(pl.multiple_of((info[0] ^ j) * 256, 256), 256)] = p[256:].astype(F32)
+
+
+def finish_kernel(x, gh, here, got, enter, out):
+    gn = here[...] + got[...].astype(F32)
+    grad = (gh[...] + rms_back(x[0].astype(F32), gn)).astype(BF)
+    out[...] = dot(enter[0], grad, TN).astype(BF)
+
+
+def result_kernel(x, att, here, got, enter, out):
+    result = (x[0].astype(F32) + att[0].astype(F32) + here[...] + got[...].astype(F32)).astype(BF)
+    out[...] = dot(enter[0], result, TN).astype(BF)
+
+
+def finish(kernel, x, second, here, got, enter):
+    first = lambda v: pl.BlockSpec((1, *v.shape[1:]), lambda _: (0,) * v.ndim) if v.ndim == 3 else full(*v.shape)
+    args = (x, second, here, got, enter)
+    return run(
+        kernel,
+        sds((ROWS, WIDTH)),
+        (),
+        args,
+        in_specs=[first(v) for v in args],
+        out_specs=full(ROWS, WIDTH),
+        flops=1 << 28,
+        nbytes=4 << 20,
+    )
+
+
+def unsort_kernel(leave, rows, out):
+    out[...] = dot(leave[...], rows[...], TN).astype(BF)
+
+
+def unsort(leave, rows):
+    return run(
+        unsort_kernel,
+        sds((ROWS, WIDTH)),
+        (),
+        (leave, rows),
+        in_specs=[full(ROWS, ROWS), full(ROWS, WIDTH)],
+        out_specs=full(ROWS, WIDTH),
+        flops=1 << 28,
+        nbytes=2 << 20,
+    )
+
+
+def exchange(rows):
+    return lax.all_to_all(rows, ALL, split_axis=0, concat_axis=0, tiled=True)
+
+
+def team_raw(own):
+    pair = send(own, "zl", 1)
+    return [own, pair, send(own, "core", 1), send(pair, "core", 1)]
+
+
+def team_sum(keep, give, hold=()):
+    got = send(give, "core", 1)
+    half = (keep.astype(F32) + got.astype(F32)).astype(BF)
+    other = send(half, "zl", 1)
+    if hold:
+        other = after(other, *hold)
+    ours = (half.astype(F32) + other[::-1].astype(F32)).astype(BF)
+    return ours, send(ours, "core", 1), half
+
+
+def team_own(keep, give, *behind):
+    got = send(give, "core", 1)
+    here = keep[0].astype(F32) + got[0].astype(F32)
+    there = (keep[1].astype(F32) + got[1].astype(F32)).astype(BF)
+    if behind:
+        there = after(there, *behind)
+    return here, send(there, "zl", 1), there
+
+
+def state_in(state, near, whole, cross):
+    low = [state] + [lax.ppermute(state, "shard", [(i, i ^ j) for i in range(4)]) for j in (1, 2, 3)]
+    wide = [v.astype(F32) for v in low]
+    hand = sum(whole[j][:, None, None] * wide[j] for j in range(4)).astype(BF)
+    got = send(hand, "zh", 1)
+    here = sum(near[j][:, None, None] * wide[j] for j in (1, 2, 3))
+    return here + cross[:, None, None] * got.astype(F32), hand
+
+
+def fast_body(tokens_in, cotangent, deal_order, lengths, decay_rates, w_query, w_key, w_value, w_ugate, w_out, w_ffin, w_ffdown):
+    zh, zl, core, shard = (lax.axis_index(a) for a in ALL)
+    me = zl * 2 + core
+    group = zh * N_SHARD + shard
+    device = (zh * TEAM + me) * N_SHARD + shard
+    span = TEAM * ROWS
+    info = jnp.stack([me, shard, group * span, device, zh, jnp.int32(0), jnp.int32(0), jnp.int32(0)]).astype(jnp.int32)
+    ends = jnp.sum(jnp.where(jnp.arange(8)[None, :] <= jnp.arange(8)[:, None], lengths[None, :], 0), axis=1).astype(jnp.int32)
+    scal = (info, ends, decay_rates)
+    by_device = deal_order.reshape(2, N_SHARD, TEAM, ROWS).transpose(0, 2, 1, 3).reshape(DEVICES, ROWS)
+
+    leave, enter, sent_x, sent_g = exchange_rows(info, by_device, *far(tokens_in, cotangent))
+    raw_x = exchange(sent_x)
+    quarter = take_quarter(after(info, sent_x), *far(w_query, w_key, w_value, w_ugate))
+    w_proj = gather_pieces(quarter)
+    w_ff = lax.all_gather(after(ff_bundle(after(info, quarter), *far(w_ffin, w_ffdown)), raw_x), "shard", axis=0)
+    wo = gather_out(w_out, me, shard)
+    x_raws = team_raw(raw_x)
+    raw_g = exchange(after(sent_g, raw_x))
+    g_raws = team_raw(raw_g)
+
+    ids = jnp.arange(8)
+    last = jnp.sum(((ids[:, None] + 1) * span - 1 >= ends[None, :]).astype(jnp.int32), axis=1)
+    before = jnp.where(ids == 0, -1, jnp.sum((ids[:, None] * span - 1 >= ends[None, :]).astype(jnp.int32), axis=1))
+    rates = lax.dynamic_slice_in_dim(decay_rates, me * HEADS_OWN, HEADS_OWN)
+
+    def weigh(flag, gap):
+        return jnp.where(flag[..., None], jnp.exp(-(jnp.maximum(gap, 0) * span).astype(F32)[..., None] * rates), 0.0)
+
+    js = jnp.arange(4)
+    peers = zh * N_SHARD + (shard ^ js)
+    my_last, my_before = last[group], before[group]
+    f_near = weigh((peers < group) & (last[peers] == my_before), group - 1 - peers)
+    end = zh * N_SHARD + 3
+    f_whole = weigh(last[peers] == last[end], end - peers)
+    f_cross = weigh((zh == 1) & (last[3] == my_before), shard)
+    b_near = weigh((peers > group) & (before[peers] == my_last), peers - 1 - group)
+    start = zh * N_SHARD
+    b_whole = weigh(before[peers] == before[start], peers - start)
+    b_cross = weigh((zh == 0) & (before[4] == my_last), 3 - shard)
+
+    x, normed, pq, pk, pu, q, k, v, kv, state = project(scal, enter, far(*x_raws), far(*w_proj))
+    s_in, _ = state_in(state, f_near, f_whole, f_cross)
+    local = attend_local(scal, q, k, v)
+    mixed, gated, a_keep, a_give = carry_in((after(info, g_raws[1]), *scal[1:]), local, q, pu, kv, s_in, wo)
+    ta, tb, _ = team_sum(a_keep, a_give)
+    g, n2, product, gg, gu, r_keep, r_give, n_keep, n_give = sglu(info, enter, x, ta, tb, far(*g_raws), *far(w_ff))
+    n_got = send(n_give, "core", 1)
+    n_half = (n_keep.astype(F32) + n_got.astype(F32)).astype(BF)
+    n_other = send(n_half, "zl", 1)
+    d_gate = hidden_grads(after(info, n_half), n2, gg, 1)
+    d_up = hidden_grads(after(info, d_gate[1]), n2, gu, 2)
+    d_down = down_grads(after(info, d_up[1]), g, product, 1)
+    n_other = after(n_other, d_down[1])
+    ua = (n_half.astype(F32) + n_other[::-1].astype(F32)).astype(BF)
+    ub = send(ua, "core", 1)
+    gate_own, gate_other = hop(d_gate, 1, hold=(ua,))
+    up_own, up_other = hop(d_up, 2, hold=(ua,))
+    gate = hop_two(gate_own, gate_other, 1, hold=(gate_other,))
+
+    ga, gpu, gm, qg, gh, g_state = hidden_back((after(info, gate_other, up_other), *scal[1:]), x, ta, tb, ua, ub, g, wo, mixed, pu, q)
+    g_in, handed = state_in(g_state, b_near, b_whole, b_cross)
+    gq, gk, gv = scores_back((after(info, gate), *scal[1:]), q, k, v, gm, kv, s_in)
+    d_ou = column_grads(after(info, gq), [(gated, ga), (normed, gpu)], 2)
+    up = hop_two(up_own, up_other, 2, hold=(handed,))
+    r_here, r_there, r_sent = team_own(r_keep, r_give, ub)
+    sent_back = finish(result_kernel, x, ta, r_here, r_there, after(enter, gq))
+    dqkv, p_keep, p_give = project_back(
+        (after(info, d_ou[1], sent_back), *scal[1:]), gq, gk, gv, pq, pk, k, v, gpu, qg, g_in, far(*w_proj)
+    )
+    here, there, p_sent = team_own(p_keep, p_give)
+    d_qkv = column_grads(after(info, p_sent), [(normed, dqkv)], 1)
+    qkv_own, qkv_other = hop(d_qkv, 1, hold=(p_sent,))
+    last_sent = finish(finish_kernel, x, gh, here, there, enter)
+    input_grad = unsort(leave, exchange(last_sent))
+    output = unsort(leave, exchange(after(sent_back, last_sent)))
+
+    gate_sum = over_zh(gate, hold=(p_sent,), hold_send=(gq,))
+    up_sum = over_zh(up, hold=(p_sent,), hold_send=(gq,))
+    down = hop_two(*hop(d_down, 1, hold=(p_sent,)), 1, hold=(p_sent,))
+    ou = hop_two(*hop(d_ou, 2, hold=(p_sent,)), 2, hold=(p_sent,))
+    down_sum = over_zh(down)
+    ou_sum = over_zh(ou)
+    qkv_sum = over_zh(hop_two(qkv_own, qkv_other, 1))
+    grad_fin = fin_out(info, (*far(*team_gather(gate_sum)), *far(*team_gather(up_sum))))
+    grad_down = down_out(info, far(*team_gather(down_sum)))
+    ou = team_gather(ou_sum)
+    outs = []
+    for j in range(4):
+        pick = me ^ shard ^ j
+        top = [p[:256] for p in ou]
+        piece = jnp.where(pick < 2, jnp.where(pick == 0, top[0], top[1]), jnp.where(pick == 2, top[2], top[3]))
+        outs.append(piece if j == 0 else send(piece, "shard", j))
+    grad_out, grad_u = run(
+        out_grad_kernel,
+        (sds((256, WIDTH), F32),) * 2,
+        (info,),
+        far(*outs, *ou),
+        in_specs=[*[full(256, 256)] * 4, *[full(512, 256)] * 4],
+        out_specs=[full(256, WIDTH)] * 2,
+        nbytes=3 << 20,
+    )
+    grad_q, grad_k, grad_v = columns_out(info, far(*team_gather(qkv_sum)), 3)
+    return (output, input_grad, grad_q, grad_k, grad_v, grad_u, grad_out, grad_fin, grad_down)
+
+
 def solution(mesh):
     rep, shard = mesh.shape["rep"], mesh.shape["shard"]
     team = Mesh(mesh.devices.reshape(rep // TEAM, 2, 2, shard), ALL)
     token, weight = P(ALL, None), P("shard", None)
     return jax.shard_map(
-        body,
+        fast_body if (rep, shard) == (8, 4) else general_body,
         mesh=team,
         in_specs=(token, token, P(), P(), P(), *([weight] * 7)),
         out_specs=(token, token, *([weight] * 7)),

time: 452 us -> 404 us (0.89); the launches traced: 446 us -> 403 us
  Pallas kernels: 0 us -> 102 us
  other arithmetic: 69.7 us -> 16.8 us
  matrix products: 51.2 us -> 0 us
  local copies, waits for them, and re-layouts: 61.9 us -> 14.4 us
  starting transfers between devices: 96.9 us -> 70.8 us
  waiting for transfers between devices: 162 us -> 181 us
  between operations: 3.81 us -> 17.6 us
    pallas_call x0 -> x23, Pallas kernels: none -> 102 us  [run(): pl.pallas_call(kernel, out_shape=out, grid_spec=pltpu.PrefetchScalarGridS...]
    dot_general x35 -> x0, matrix products: 51.2 us -> none  [the longest x23 45.5 us: dot(): return lax.dot_general(a, b, (dims, ((), ())), preferred_element_type=F32)]
    convert_element_type x34 -> x18, other arithmetic: 31.3 us -> 8.66 us  [the longest x5 3.94 us: over_zh(): return (part.astype(F32) + got.astype(F32)).astype(BF)]
    unnamed x244 -> x106, local copies, waits for them, and re-layouts: 23.9 us -> 10 us
    select_n x21 -> x8, other arithmetic: 16.8 us -> 4.06 us  [the longest x2 2.72 us: fast_body(): jnp.where(pick < 2, jnp.where(pick == 0, top[0], top[1]), jnp.where(pick...]
    ppermute x14 -> x9, starting transfers between devices: 24 us -> 11.3 us  [the longest x3 7.62 us: gather_out(): wo = jnp.where(rel == j, lax.ppermute(w_out, axes, pairs), wo)]
    ppermute x14 -> x9, waiting for transfers between devices: 1.28 us -> 13.3 us  [the longest x6 13.3 us: state_in(): lax.ppermute(state, 'shard', [(i, i ^ j) for i in range(4)])]
    slice x17 -> x1, local copies, waits for them, and re-layouts: 10.8 us -> 0.65 us  [fast_body(): f_cross = weigh((zh == 1) & (last[3] == my_before), shard)]
  transfers between devices with their start and end apart: 87 -> 68, of which waited for: 24 -> 27; matrix products, arithmetic and copies ran while one was open for 34% -> 5% of each run, Pallas kernels for 0% -> 17%
where the time goes in v2:
time: 404 us; the launch traced here: 403 us
  waiting for transfers between devices  181 us (45%)
  Pallas kernels  102 us (25%)
  starting transfers between devices  70.8 us (18%)
  between operations  17.6 us (4%)
  other arithmetic  16.8 us (4%)
  local copies, waits for them, and re-layouts  14.4 us (4%)
    ppermute x54, waiting for transfers between devices, send(): return lax.ppermute(value, axis, [(i, i ^ mask) for i in range(size)])  163 us
    pallas_call x23, Pallas kernels, run(): pl.pallas_call(kernel, out_shape=out, grid_spec=pltpu.PrefetchScalarGridS...  102 us
    ppermute x54, starting transfers between devices, send(): return lax.ppermute(value, axis, [(i, i ^ mask) for i in range(size)])  42.2 us
    all_to_all x4, starting transfers between devices, exchange(): return lax.all_to_all(rows, ALL, split_axis=0, concat_axis=0, tiled=True)  17.2 us
    ppermute x6, waiting for transfers between devices, state_in(): lax.ppermute(state, 'shard', [(i, i ^ j) for i in range(4)])  13.3 us
    unnamed x106, local copies, waits for them, and re-layouts  10 us
  transfers between devices with their start and end apart: 68, of which 27 were waited for; matrix products, arithmetic and copies ran while one was open for 5% of the time, Pallas kernels for 17%

profile of v2, /device:TPU:0, one launch (start us, length us, event | category | flops | bytes accessed | tf_op | source)
XLA Modules:
  0.0 402.9 jit_solution(8608807135846344565)
XLA Ops:
  8.1 3.5 shard_map.187
  11.6 7.4 %all-to-all-start = ((bf16[32,8,1024]{2,1,0:T(8,128)(2,1)}), bf16[32,8,1024]{2,1,0:T(8,128)(2,1)}, u32[]{:S(2)}, u32[]{:S(2)}) async-start(bf16[32,8,1024]{2,1,0:T(8,128)(2,1)} %bitcast.6), calls=%async_computation | async-start | bytes 1048576 | tf_op jit(solution)/shard_map/all_to_all | solution.py:1165
  19.0 1.7 shard_map.188.w0
  20.7 1.8 collective-permute-start.3
  22.5 1.5 collective-permute-start.4
  26.0 3.8 shard_map.192
  30.7 4.5 %all-to-all-done = bf16[32,8,1024]{2,1,0:T(8,128)(2,1)} async-done(((bf16[32,8,1024]{2,1,0:T(8,128)(2,1)}), bf16[32,8,1024]{2,1,0:T(8,128)(2,1)}, u32[]{:S(2)}, u32[]{:S(2)}) %all-to-all-start) | async-done | bytes 524320 | tf_op jit(solution)/shard_map/all_to_all | solution.py:1165
  41.6 3.4 all-to-all-start.1
  45.1 14.0 %collective-permute-done.r1 = bf16[256,1024]{1,0:T(8,128)(2,1)S(1)} collective-permute-done((bf16[256,1024]{1,0:T(8,128)(2,1)}, bf16[256,1024]{1,0:T(8,128)(2,1)S(1)}, u32[]{:S(2)}, u32[]{:S(2)}) %collective-permute-start) | collective-permute-done | bytes 524320 | tf_op jit(solution)/shard_map/ppermute | solution.py:21
  59.3 3.4 collective-permute-start.11
  62.7 2.1 collective-permute-start.12
  64.8 2.1 collective-permute-start.13
  67.9 10.1 %shard_map.189 = (bf16[4,256,1024]{2,1,0:T(8,128)(2,1)}, bf16[4,256,1024]{2,1,0:T(8,128)(2,1)}, f32[4,256,256]{2,1,0:T(8,128)}, f32[4,256,256]{2,1,0:T(8,128)}, ...) custom-call(s32[8]{0:T(128)S(1)} %stack.23.info, ...), custom_call_target="tpu_custom_call" | custom-call | tf_op jit(solution)/shard_map/pallas_call | solution.py:356
  80.3 4.4 %collective-permute-done.7 = bf16[2,128,128]{2,1,0:T(8,128)(2,1)S(1)} collective-permute-done((bf16[2,128,128]{2,1,0:T(8,128)(2,1)S(1)}, bf16[2,128,128]{2,1,0:T(8,128)(2,1)S(1)}, u32[]{:S(2)}, u32[]{:S(2)}) %collective-permute-start.7) | collective-permute-done | bytes 65568 | tf_op jit(solution)/shard_map/ppermute | solution.py:1193
  84.7 2.1 collective-permute-done.8
  86.7 4.5 %collective-permute-done.9 = bf16[2,128,128]{2,1,0:T(8,128)(2,1)S(1)} collective-permute-done((bf16[2,128,128]{2,1,0:T(8,128)(2,1)S(1)}, bf16[2,128,128]{2,1,0:T(8,128)(2,1)S(1)}, u32[]{:S(2)}, u32[]{:S(2)}) %collective-permute-start.9) | collective-permute-done | bytes 65568 | tf_op jit(solution)/shard_map/ppermute | solution.py:1193
  93.4 2.8 shard_map.190.local
  96.3 3.0 collective-permute-done.10
  99.5 2.1 collective-permute-done.6.g1
  101.5 3.8 shard_map.191
  105.4 2.6 collective-permute-done.14
  108.6 25.2 %collective-permute-done.15 = bf16[2,256,1024]{2,1,0:T(8,128)(2,1)S(1)} collective-permute-done((bf16[2,256,1024]{2,1,0:T(8,128)(2,1)S(1)}, bf16[2,256,1024]{2,1,0:T(8,128)(2,1)S(1)}, u32[]{:S(2)}, u32[]{:S(2)}) %collective-permute-start.15) | collective-permute-done | bytes 1048608 | tf_op jit(solution)/shard_map/ppermute | solution.py:21
  134.8 3.4 collective-permute-done.17.g2
  143.1 19.1 %shard_map.193 = (bf16[4,256,1024]{2,1,0:T(8,128)(2,1)S(1)}, bf16[4,256,1024]{2,1,0:T(8,128)(2,1)S(1)}, bf16[4,256,704]{2,1,0:T(8,128)(2,1)S(1)}, bf16[4,256,704...) custom-call(s32[8]{0:T(128)S(1)} %stack.23.info, ...), custom_call_target="tpu_custom_call" | custom-call | tf_op jit(solution)/shard_map/pallas_call | solution.py:356
  162.6 2.3 collective-permute-done.20
  165.7 3.6 shard_map.194
  169.5 3.5 shard_map.195
  173.1 1.4 collective-permute-start.26
  174.5 3.0 shard_map.196
  177.5 13.3 %collective-permute-done.21 = bf16[2,256,1024]{2,1,0:T(8,128)(2,1)S(1)} collective-permute-done((bf16[2,256,1024]{2,1,0:T(8,128)(2,1)S(1)}, bf16[2,256,1024]{2,1,0:T(8,128)(2,1)S(1)}, u32[]{:S(2)}, u32[]{:S(2)}) %collective-permute-start.21) | collective-permute-done | bytes 1048608 | tf_op jit(solution)/shard_map/ppermute | solution.py:21
  192.5 1.5 collective-permute-done.22.ub
  194.0 6.8 %shard_map.197 = (bf16[4,256,1024]{2,1,0:T(8,128)(2,1)S(1)}, bf16[4,256,256]{2,1,0:T(8,128)(2,1)S(1)}, bf16[4,256,256]{2,1,0:T(8,128)(2,1)S(1)}, f32[4,2,128,128...) custom-call(s32[8]{0:T(128)S(1)} %stack.23.info, s32[8]{0:T(128)S(1)} %select_reduce_fusion.ends, ...), custom_call_target="tpu_custom_call" | custom-call | tf_op jit(solution)/shard_map/pallas_call | solution.py:356
  202.5 2.0 collective-permute-start.29
  206.1 1.5 collective-permute-done.29
  207.7 2.1 collective-permute-start.30
  210.0 4.2 %shard_map.198 = (f32[4,256,256]{2,1,0:T(8,128)S(1)}, f32[4,256,256]{2,1,0:T(8,128)S(1)}, f32[4,256,256]{2,1,0:T(8,128)S(1)}) custom-call(s32[8]{0:T(128)S(1)} %stack.23.info, s32[8]{0:T(128)S(1)} %select_reduce_fusion.ends, f32[8]{0:T(128)S(1)} %copy-done.27, bf16[4,256,256]{2,1,0:T(8,128)(2,1)S(1)} %copy-done.3, bf16[4,256,256]{2,1,0:T(8,128)(2,1)S(1)} %copy-done.7, ...), custom_call_target="tpu_custom_call" | custom-call | tf_op jit(solution)/shard_map/pallas_call | solution.py:356
  214.2 3.3 shard_map.200
  217.7 1.7 collective-permute-done.23.got
  221.1 7.2 %shard_map.201 = (bf16[4,256,768]{2,1,0:T(8,128)(2,1)S(1)}, bf16[2,256,1024]{2,1,0:T(8,128)(2,1)S(1)}, bf16[2,256,1024]{2,1,0:T(8,128)(2,1)S(1)}) custom-call(s32[8]{0:T(128)S(1)} %stack.23.info, s32[8]{0:T(128)S(1)} %select_reduce_fusion.ends, f32[8]{0:T(128)S(1)} %copy-done.27, f32[4,256,256]{2,1,0:T(8,128)S(1)} %get-tuple-element.137.gq, ...), custom_call_target="tpu_custom_call" | custom-call | tf_op jit(solution)/shard_map/pallas_call | solution.py:356
  228.9 1.7 collective-permute-start.57
  231.1 2.1 collective-permute-start.48
  233.2 6.5 %collective-permute-done.52 = bf16[704,256]{1,0:T(8,128)(2,1)S(1)} collective-permute-done((bf16[704,256]{1,0:T(8,128)(2,1)S(1)}, bf16[704,256]{1,0:T(8,128)(2,1)S(1)}, u32[]{:S(2)}, u32[]{:S(2)}) %collective-permute-start.52) | collective-permute-done | bytes 360480 | tf_op jit(solution)/shard_map/ppermute | solution.py:21
  239.8 1.4 collective-permute-start.53
  242.2 3.9 shard_map.205
  247.4 11.4 %collective-permute-done.48 = bf16[704,256]{1,0:T(8,128)(2,1)S(1)} collective-permute-done((bf16[704,256]{1,0:T(8,128)(2,1)S(1)}, bf16[704,256]{1,0:T(8,128)(2,1)S(1)}, u32[]{:S(2)}, u32[]{:S(2)}) %collective-permute-start.48) | collective-permute-done | bytes 360480 | tf_op jit(solution)/shard_map/ppermute | solution.py:21
  260.3 4.9 %collective-permute-done.53 = bf16[704,256]{1,0:T(8,128)(2,1)S(1)} collective-permute-done((bf16[704,256]{1,0:T(8,128)(2,1)S(1)}, bf16[704,256]{1,0:T(8,128)(2,1)S(1)}, u32[]{:S(2)}, u32[]{:S(2)}) %collective-permute-start.53) | collective-permute-done | bytes 360480 | tf_op jit(solution)/shard_map/ppermute | solution.py:21
  265.2 1.5 collective-permute-start.58
  266.8 10.4 %collective-permute-done.40 = bf16[512,256]{1,0:T(8,128)(2,1)S(1)} collective-permute-done((bf16[512,256]{1,0:T(8,128)(2,1)S(1)}, bf16[512,256]{1,0:T(8,128)(2,1)S(1)}, u32[]{:S(2)}, u32[]{:S(2)}) %collective-permute-start.40) | collective-permute-done | bytes 262176 | tf_op jit(solution)/shard_map/ppermute | solution.py:21
  279.5 2.1 collective-permute-start.41
  284.5 1.5 shard_map.202
  286.0 3.6 all-to-all-start.2
  290.7 2.7 collective-permute-start.35
  296.2 2.9 collective-permute-start.59
  299.1 33.7 %collective-permute-done.43.p2 = bf16[512,256]{1,0:T(8,128)(2,1)S(1)} collective-permute-done((bf16[512,256]{1,0:T(8,128)(2,1)S(1)}, bf16[512,256]{1,0:T(8,128)(2,1)S(1)}, u32[]{:S(2)}, u32[]{:S(2)}) %collective-permute-start.43) | collective-permute-done | bytes 262176 | tf_op jit(solution)/shard_map/ppermute | solution.py:21
  334.0 2.9 all-to-all-start.3
  343.5 20.9 %collective-permute-done.61.p2 = bf16[704,256]{1,0:T(8,128)(2,1)} collective-permute-done((bf16[704,256]{1,0:T(8,128)(2,1)S(1)}, bf16[704,256]{1,0:T(8,128)(2,1)}, u32[]{:S(2)}, u32[]{:S(2)}) %collective-permute-start.61) | collective-permute-done | bytes 360480 | tf_op jit(solution)/shard_map/ppermute | solution.py:21
  365.0 1.7 select_select_fusion.2
  366.8 1.5 collective-permute-start.46
  368.3 4.3 %collective-permute-done.46.o2 = bf16[256,256]{1,0:T(8,128)(2,1)S(1)} collective-permute-done((bf16[256,256]{1,0:T(8,128)(2,1)S(1)}, bf16[256,256]{1,0:T(8,128)(2,1)S(1)}, u32[]{:S(2)}, u32[]{:S(2)}) %collective-permute-start.46) | collective-permute-done | bytes 131104 | tf_op jit(solution)/shard_map/ppermute | solution.py:21
  372.6 2.4 collective-permute-start.47
  375.0 6.0 %shard_map.208 = f32[256,5632]{1,0:T(8,128)} custom-call(s32[8]{0:T(128)S(1)} %stack.23.info, bf16[704,256]{1,0:T(8,128)(2,1)} %add_convert_fusion.14.p0, bf16[704,256]{1,0:T(8,128)(2,1)} %collective-permute-done.49.p1, bf16[704,256]{1,0:T(8,128)(2,1)} %collective-permute-done.50.p2, bf16[704,256]{1,0:T(8,128)(2,1)} %collective-permute-done.51.p3, ...), custom_call_target="tpu_custom_call" | custom-call | tf_op jit(solution)/shard_map/pallas_call | solution.py:356
  381.6 3.4 shard_map.207
  386.5 3.6 shard_map.209
  392.3 3.7 shard_map.206
  (261 shorter events, 54.8 us)
Async XLA Ops:
  11.6 23.7 %all-to-all-start = ((bf16[32,8,1024]{2,1,0:T(8,128)(2,1)}), bf16[32,8,1024]{2,1,0:T(8,128)(2,1)}, u32[]{:S(2)}, u32[]{:S(2)}) async-start(bf16[32,8,1024]{2,1,0:T(8,128)(2,1)} %bitcast.6), calls=%async_computation | async-start | bytes 1048576 | tf_op jit(solution)/shard_map/all_to_all | solution.py:1165
  19.0 121.8 %all-gather.3.cloned.1.call-start = ((), (), s32[]{:S(2)}) async-start(), calls=%async_computation.4 | async-start | bytes 5406720 | tf_op jit(solution)/shard_map/all_gather | solution.py:1216
  20.7 38.5 %collective-permute-start.3 = (bf16[1024,256]{1,0:T(8,128)(2,1)S(1)}, bf16[1024,256]{1,0:T(8,128)(2,1)S(1)}, u32[]{:S(2)}, u32[]{:S(2)}) collective-permute-start(bf16[1024,256]{1,0:T(8,128)(2,1)S(1)} %shard_map.188.w0), channel_id=1, source_target_pairs={{0,1},{1,0},{2,3},{3,2},{4,5},{5,4},{6,7},{7,6},{8,9},{9,8},{10,11... | collective-permute-start | bytes 1572872 | tf_op jit(solution)/shard_map/ppermute | solution.py:21
  22.5 40.2 %collective-permute-start.4 = (bf16[1024,256]{1,0:T(8,128)(2,1)S(1)}, bf16[1024,256]{1,0:T(8,128)(2,1)S(1)}, u32[]{:S(2)}, u32[]{:S(2)}) collective-permute-start(bf16[1024,256]{1,0:T(8,128)(2,1)S(1)} %shard_map.188.w0), channel_id=1, source_target_pairs={{0,2},{1,3},{2,0},{3,1},{4,6},{5,7},{6,4},{7,5},{8,10},{9,11},{10,... | collective-permute-start | bytes 1572872 | tf_op jit(solution)/shard_map/ppermute | solution.py:21
  24.0 40.8 %collective-permute-start.5 = (bf16[1024,256]{1,0:T(8,128)(2,1)S(1)}, bf16[1024,256]{1,0:T(8,128)(2,1)S(1)}, u32[]{:S(2)}, u32[]{:S(2)}) collective-permute-start(bf16[1024,256]{1,0:T(8,128)(2,1)S(1)} %shard_map.188.w0), channel_id=1, source_target_pairs={{0,3},{1,2},{2,1},{3,0},{4,7},{5,6},{6,5},{7,4},{8,11},{9,10},{10,... | collective-permute-start | bytes 1572872 | tf_op jit(solution)/shard_map/ppermute | solution.py:21
  39.1 20.0 %collective-permute-start = (bf16[256,1024]{1,0:T(8,128)(2,1)}, bf16[256,1024]{1,0:T(8,128)(2,1)S(1)}, u32[]{:S(2)}, u32[]{:S(2)}) collective-permute-start(bf16[256,1024]{1,0:T(8,128)(2,1)} %bitcast.7.r0), channel_id=1, source_target_pairs={{0,8},{8,0},{1,9},{9,1},{2,10},{10,2},{3,11},{11,3},{4,12},{12,4},... | collective-permute-start | bytes 1572872 | tf_op jit(solution)/shard_map/ppermute | solution.py:21
  41.6 43.1 %all-to-all-start.1 = ((bf16[32,8,1024]{2,1,0:T(8,128)(2,1)}), bf16[32,8,1024]{2,1,0:T(8,128)(2,1)}, u32[]{:S(2)}, u32[]{:S(2)}) async-start(bf16[32,8,1024]{2,1,0:T(8,128)(2,1)} %bitcast.8), calls=%async_computation.1 | async-start | bytes 1048576 | tf_op jit(solution)/shard_map/all_to_all | solution.py:1165
  45.0 21.8 %collective-permute-start.1 = (bf16[256,1024]{1,0:T(8,128)(2,1)}, bf16[256,1024]{1,0:T(8,128)(2,1)S(1)}, u32[]{:S(2)}, u32[]{:S(2)}) collective-permute-start(bf16[256,1024]{1,0:T(8,128)(2,1)} %bitcast.7.r0), channel_id=1, source_target_pairs={{0,4},{4,0},{1,5},{5,1},{2,6},{6,2},{3,7},{7,3},{8,12},{12,8},{9,1... | collective-permute-start | bytes 1572872 | tf_op jit(solution)/shard_map/ppermute | solution.py:21
  59.1 7.8 %collective-permute-start.2 = (bf16[256,1024]{1,0:T(8,128)(2,1)S(1)}, bf16[256,1024]{1,0:T(8,128)(2,1)S(1)}, u32[]{:S(2)}, u32[]{:S(2)}) collective-permute-start(bf16[256,1024]{1,0:T(8,128)(2,1)S(1)} %collective-permute-done.r1), channel_id=1, source_target_pairs={{0,4},{4,0},{1,5},{5,1},{2,6},{6,2},{3,7},{7,3},{8,12},{12,8},{9,1... | collective-permute-start | bytes 1572872 | tf_op jit(solution)/shard_map/ppermute | solution.py:21
  59.3 33.0 %collective-permute-start.11 = (bf16[256,1024]{1,0:T(8,128)(2,1)}, bf16[256,1024]{1,0:T(8,128)(2,1)}, u32[]{:S(2)}, u32[]{:S(2)}) collective-permute-start(bf16[256,1024]{1,0:T(8,128)(2,1)} %param.21), channel_id=1, source_target_pairs={{0,3},{5,6},{10,9},{15,12},{16,19},{21,22},{26,25},{31,28}} | collective-permute-start | bytes 1572872 | tf_op jit(solution)/shard_map/ppermute | solution.py:554
  62.7 29.6 %collective-permute-start.12 = (bf16[256,1024]{1,0:T(8,128)(2,1)}, bf16[256,1024]{1,0:T(8,128)(2,1)}, u32[]{:S(2)}, u32[]{:S(2)}) collective-permute-start(bf16[256,1024]{1,0:T(8,128)(2,1)} %param.21), channel_id=1, source_target_pairs={{0,2},{5,7},{10,8},{15,13},{16,18},{21,23},{26,24},{31,29}} | collective-permute-start | bytes 1572872 | tf_op jit(solution)/shard_map/ppermute | solution.py:554
  64.8 27.4 %collective-permute-start.13 = (bf16[256,1024]{1,0:T(8,128)(2,1)}, bf16[256,1024]{1,0:T(8,128)(2,1)}, u32[]{:S(2)}, u32[]{:S(2)}) collective-permute-start(bf16[256,1024]{1,0:T(8,128)(2,1)} %param.21), channel_id=1, source_target_pairs={{0,1},{5,4},{10,11},{15,14},{16,17},{21,20},{26,27},{31,30}} | collective-permute-start | bytes 1572872 | tf_op jit(solution)/shard_map/ppermute | solution.py:554
  78.8 5.8 %collective-permute-start.7 = (bf16[2,128,128]{2,1,0:T(8,128)(2,1)S(1)}, bf16[2,128,128]{2,1,0:T(8,128)(2,1)S(1)}, u32[]{:S(2)}, u32[]{:S(2)}) collective-permute-start(bf16[2,128,128]{2,1,0:T(8,128)(2,1)S(1)} %get-tuple-element.106), channel_id=1, source_target_pairs={{0,1},{1,0},{2,3},{3,2},{4,5},{5,4},{6,7},{7,6},{8,9},{9,8},{10,11... | collective-permute-start | bytes 196616 | tf_op jit(solution)/shard_map/ppermute | solution.py:1193
  80.2 6.5 %collective-permute-start.8 = (bf16[2,128,128]{2,1,0:T(8,128)(2,1)S(1)}, bf16[2,128,128]{2,1,0:T(8,128)(2,1)S(1)}, u32[]{:S(2)}, u32[]{:S(2)}) collective-permute-start(bf16[2,128,128]{2,1,0:T(8,128)(2,1)S(1)} %get-tuple-element.106), channel_id=1, source_target_pairs={{0,2},{1,3},{2,0},{3,1},{4,6},{5,7},{6,4},{7,5},{8,10},{9,11},{10,... | collective-permute-start | bytes 196616 | tf_op jit(solution)/shard_map/ppermute | solution.py:1193
  84.6 6.5 %collective-permute-start.9 = (bf16[2,128,128]{2,1,0:T(8,128)(2,1)S(1)}, bf16[2,128,128]{2,1,0:T(8,128)(2,1)S(1)}, u32[]{:S(2)}, u32[]{:S(2)}) collective-permute-start(bf16[2,128,128]{2,1,0:T(8,128)(2,1)S(1)} %get-tuple-element.106), channel_id=1, source_target_pairs={{0,3},{1,2},{2,1},{3,0},{4,7},{5,6},{6,5},{7,4},{8,11},{9,10},{10,... | collective-permute-start | bytes 196616 | tf_op jit(solution)/shard_map/ppermute | solution.py:1193
  86.7 14.8 %collective-permute-start.6 = (bf16[256,1024]{1,0:T(8,128)(2,1)}, bf16[256,1024]{1,0:T(8,128)(2,1)S(1)}, u32[]{:S(2)}, u32[]{:S(2)}) collective-permute-start(bf16[256,1024]{1,0:T(8,128)(2,1)} %bitcast.9.g0), channel_id=1, source_target_pairs={{0,8},{8,0},{1,9},{9,1},{2,10},{10,2},{3,11},{11,3},{4,12},{12,4},... | collective-permute-start | bytes 1572872 | tf_op jit(solution)/shard_map/ppermute | solution.py:21
  91.3 8.0 %collective-permute-start.10 = (bf16[2,128,128]{2,1,0:T(8,128)(2,1)S(1)}, bf16[2,128,128]{2,1,0:T(8,128)(2,1)S(1)}, u32[]{:S(2)}, u32[]{:S(2)}) collective-permute-start(bf16[2,128,128]{2,1,0:T(8,128)(2,1)S(1)} %fusion.13), channel_id=1, source_target_pairs={{0,16},{16,0},{1,17},{17,1},{2,18},{18,2},{3,19},{19,3},{4,20},{20... | collective-permute-start | bytes 196616 | tf_op jit(solution)/shard_map/ppermute | solution.py:21
  108.5 25.3 %collective-permute-start.15 = (bf16[2,256,1024]{2,1,0:T(8,128)(2,1)S(1)}, bf16[2,256,1024]{2,1,0:T(8,128)(2,1)S(1)}, u32[]{:S(2)}, u32[]{:S(2)}) collective-permute-start(bf16[2,256,1024]{2,1,0:T(8,128)(2,1)S(1)} %add_convert_fusion.3), channel_id=1, source_target_pairs={{0,8},{8,0},{1,9},{9,1},{2,10},{10,2},{3,11},{11,3},{4,12},{12,4},... | collective-permute-start | bytes 3145736 | tf_op jit(solution)/shard_map/ppermute | solution.py:21
  134.2 5.6 %collective-permute-start.16 = (bf16[2,256,1024]{2,1,0:T(8,128)(2,1)S(1)}, bf16[2,256,1024]{2,1,0:T(8,128)(2,1)S(1)}, u32[]{:S(2)}, u32[]{:S(2)}) collective-permute-start(bf16[2,256,1024]{2,1,0:T(8,128)(2,1)S(1)} %add_convert_fusion.2.ta.att), channel_id=1, source_target_pairs={{0,4},{4,0},{1,5},{5,1},{2,6},{6,2},{3,7},{7,3},{8,12},{12,8},{9,1... | collective-permute-start | bytes 3145736 | tf_op jit(solution)/shard_map/ppermute | solution.py:21
  134.3 4.0 collective-permute-start.17
  165.3 25.5 %collective-permute-start.21 = (bf16[2,256,1024]{2,1,0:T(8,128)(2,1)S(1)}, bf16[2,256,1024]{2,1,0:T(8,128)(2,1)S(1)}, u32[]{:S(2)}, u32[]{:S(2)}) collective-permute-start(bf16[2,256,1024]{2,1,0:T(8,128)(2,1)S(1)} %add_convert_fusion.1), channel_id=1, source_target_pairs={{0,8},{8,0},{1,9},{9,1},{2,10},{10,2},{3,11},{11,3},{4,12},{12,4},... | collective-permute-start | bytes 3145736 | tf_op jit(solution)/shard_map/ppermute | solution.py:21
  169.3 22.1 %collective-permute-start.24 = (bf16[2,704,256]{2,1,0:T(8,128)(2,1)S(1)}, bf16[2,704,256]{2,1,0:T(8,128)(2,1)S(1)}, u32[]{:S(2)}, u32[]{:S(2)}) collective-permute-start(bf16[2,704,256]{2,1,0:T(8,128)(2,1)S(1)} %get-tuple-element.118), channel_id=1, source_target_pairs={{0,1},{1,0},{2,3},{3,2},{4,5},{5,4},{6,7},{7,6},{8,9},{9,8},{10,11... | collective-permute-start | bytes 2162696 | tf_op jit(solution)/shard_map/ppermute | solution.py:21
  169.4 35.0 %collective-permute-start.19 = (bf16[2,256,1024]{2,1,0:T(8,128)(2,1)S(1)}, bf16[2,256,1024]{2,1,0:T(8,128)(2,1)S(1)}, u32[]{:S(2)}, u32[]{:S(2)}) collective-permute-start(bf16[2,256,1024]{2,1,0:T(8,128)(2,1)S(1)} %get-tuple-element.112), channel_id=1, source_target_pairs={{0,4},{4,0},{1,5},{5,1},{2,6},{6,2},{3,7},{7,3},{8,12},{12,8},{9,1... | collective-permute-start | bytes 3145736 | tf_op jit(solution)/shard_map/ppermute | solution.py:21
  173.1 19.2 %collective-permute-start.26 = (bf16[2,704,256]{2,1,0:T(8,128)(2,1)S(1)}, bf16[2,704,256]{2,1,0:T(8,128)(2,1)S(1)}, u32[]{:S(2)}, u32[]{:S(2)}) collective-permute-start(bf16[2,704,256]{2,1,0:T(8,128)(2,1)S(1)} %get-tuple-element.121), channel_id=1, source_target_pairs={{0,2},{1,3},{2,0},{3,1},{4,6},{5,7},{6,4},{7,5},{8,10},{9,11},{10,... | collective-permute-start | bytes 2162696 | tf_op jit(solution)/shard_map/ppermute | solution.py:21
  191.6 13.2 %collective-permute-start.25 = (bf16[704,256]{1,0:T(8,128)(2,1)S(1)}, bf16[704,256]{1,0:T(8,128)(2,1)S(1)}, u32[]{:S(2)}, u32[]{:S(2)}) collective-permute-start(bf16[704,256]{1,0:T(8,128)(2,1)S(1)} %slice_bitcast_fusion.6), channel_id=1, source_target_pairs={{0,2},{1,3},{2,0},{3,1},{4,6},{5,7},{6,4},{7,5},{8,10},{9,11},{10,... | collective-permute-start | bytes 1081352 | tf_op jit(solution)/shard_map/ppermute | solution.py:21
  200.9 4.7 %collective-permute-start.27 = (bf16[2,128,128]{2,1,0:T(8,128)(2,1)S(1)}, bf16[2,128,128]{2,1,0:T(8,128)(2,1)S(1)}, u32[]{:S(2)}, u32[]{:S(2)}) collective-permute-start(bf16[2,128,128]{2,1,0:T(8,128)(2,1)S(1)} %get-tuple-element.152), channel_id=1, source_target_pairs={{0,1},{1,0},{2,3},{3,2},{4,5},{5,4},{6,7},{7,6},{8,9},{9,8},{10,11... | collective-permute-start | bytes 196616 | tf_op jit(solution)/shard_map/ppermute | solution.py:1193
  201.1 5.0 %collective-permute-start.28 = (bf16[2,128,128]{2,1,0:T(8,128)(2,1)S(1)}, bf16[2,128,128]{2,1,0:T(8,128)(2,1)S(1)}, u32[]{:S(2)}, u32[]{:S(2)}) collective-permute-start(bf16[2,128,128]{2,1,0:T(8,128)(2,1)S(1)} %get-tuple-element.152), channel_id=1, source_target_pairs={{0,2},{1,3},{2,0},{3,1},{4,6},{5,7},{6,4},{7,5},{8,10},{9,11},{10,... | collective-permute-start | bytes 196616 | tf_op jit(solution)/shard_map/ppermute | solution.py:1193
  202.5 5.2 %collective-permute-start.29 = (bf16[2,128,128]{2,1,0:T(8,128)(2,1)S(1)}, bf16[2,128,128]{2,1,0:T(8,128)(2,1)S(1)}, u32[]{:S(2)}, u32[]{:S(2)}) collective-permute-start(bf16[2,128,128]{2,1,0:T(8,128)(2,1)S(1)} %get-tuple-element.152), channel_id=1, source_target_pairs={{0,3},{1,2},{2,1},{3,0},{4,7},{5,6},{6,5},{7,4},{8,11},{9,10},{10,... | collective-permute-start | bytes 196616 | tf_op jit(solution)/shard_map/ppermute | solution.py:1193
  204.8 14.6 %collective-permute-start.23 = (bf16[256,1024]{1,0:T(8,128)(2,1)S(1)}, bf16[256,1024]{1,0:T(8,128)(2,1)S(1)}, u32[]{:S(2)}, u32[]{:S(2)}) collective-permute-start(bf16[256,1024]{1,0:T(8,128)(2,1)S(1)} %get-tuple-element.127), channel_id=1, source_target_pairs={{0,8},{8,0},{1,9},{9,1},{2,10},{10,2},{3,11},{11,3},{4,12},{12,4},... | collective-permute-start | bytes 1572872 | tf_op jit(solution)/shard_map/ppermute | solution.py:21
  207.7 9.8 %collective-permute-start.30 = (bf16[2,128,128]{2,1,0:T(8,128)(2,1)S(1)}, bf16[2,128,128]{2,1,0:T(8,128)(2,1)S(1)}, u32[]{:S(2)}, u32[]{:S(2)}) collective-permute-start(bf16[2,128,128]{2,1,0:T(8,128)(2,1)S(1)} %fusion.20), channel_id=1, source_target_pairs={{0,16},{16,0},{1,17},{17,1},{2,18},{18,2},{3,19},{19,3},{4,20},{20... | collective-permute-start | bytes 196616 | tf_op jit(solution)/shard_map/ppermute | solution.py:21
  228.4 12.8 %collective-permute-start.31 = (bf16[2,256,1024]{2,1,0:T(8,128)(2,1)S(1)}, bf16[2,256,1024]{2,1,0:T(8,128)(2,1)S(1)}, u32[]{:S(2)}, u32[]{:S(2)}) collective-permute-start(bf16[2,256,1024]{2,1,0:T(8,128)(2,1)S(1)} %get-tuple-element.154), channel_id=1, source_target_pairs={{0,4},{4,0},{1,5},{5,1},{2,6},{6,2},{3,7},{7,3},{8,12},{12,8},{9,1... | collective-permute-start | bytes 3145736 | tf_op jit(solution)/shard_map/ppermute | solution.py:21
  228.4 11.3 %collective-permute-start.52 = (bf16[704,256]{1,0:T(8,128)(2,1)S(1)}, bf16[704,256]{1,0:T(8,128)(2,1)S(1)}, u32[]{:S(2)}, u32[]{:S(2)}) collective-permute-start(bf16[704,256]{1,0:T(8,128)(2,1)S(1)} %slice_bitcast_fusion.5), channel_id=1, source_target_pairs={{0,1},{1,0},{2,3},{3,2},{4,5},{5,4},{6,7},{7,6},{8,9},{9,8},{10,11... | collective-permute-start | bytes 1081352 | tf_op jit(solution)/shard_map/ppermute | solution.py:21
  228.9 31.2 %collective-permute-start.57 = (bf16[2,704,256]{2,1,0:T(8,128)(2,1)S(1)}, bf16[2,704,256]{2,1,0:T(8,128)(2,1)S(1)}, u32[]{:S(2)}, u32[]{:S(2)}) collective-permute-start(bf16[2,704,256]{2,1,0:T(8,128)(2,1)S(1)} %get-tuple-element.125), channel_id=1, source_target_pairs={{0,1},{1,0},{2,3},{3,2},{4,5},{5,4},{6,7},{7,6},{8,9},{9,8},{10,11... | collective-permute-start | bytes 2162696 | tf_op jit(solution)/shard_map/ppermute | solution.py:21
  230.5 15.6 %collective-permute-start.39 = (bf16[2,512,256]{2,1,0:T(8,128)(2,1)S(1)}, bf16[2,512,256]{2,1,0:T(8,128)(2,1)S(1)}, u32[]{:S(2)}, u32[]{:S(2)}) collective-permute-start(bf16[2,512,256]{2,1,0:T(8,128)(2,1)S(1)} %get-tuple-element.145), channel_id=1, source_target_pairs={{0,2},{1,3},{2,0},{3,1},{4,6},{5,7},{6,4},{7,5},{8,10},{9,11},{10,... | collective-permute-start | bytes 1572872 | tf_op jit(solution)/shard_map/ppermute | solution.py:21
  231.1 27.8 %collective-permute-start.48 = (bf16[704,256]{1,0:T(8,128)(2,1)S(1)}, bf16[704,256]{1,0:T(8,128)(2,1)S(1)}, u32[]{:S(2)}, u32[]{:S(2)}) collective-permute-start(bf16[704,256]{1,0:T(8,128)(2,1)S(1)} %fusion.3), channel_id=1, source_target_pairs={{0,16},{16,0},{1,17},{17,1},{2,18},{18,2},{3,19},{19,3},{4,20},{20... | collective-permute-start | bytes 1081352 | tf_op jit(solution)/shard_map/ppermute | solution.py:21
  239.8 25.4 %collective-permute-start.53 = (bf16[704,256]{1,0:T(8,128)(2,1)S(1)}, bf16[704,256]{1,0:T(8,128)(2,1)S(1)}, u32[]{:S(2)}, u32[]{:S(2)}) collective-permute-start(bf16[704,256]{1,0:T(8,128)(2,1)S(1)} %fusion.2), channel_id=1, source_target_pairs={{0,16},{16,0},{1,17},{17,1},{2,18},{18,2},{3,19},{19,3},{4,20},{20... | collective-permute-start | bytes 1081352 | tf_op jit(solution)/shard_map/ppermute | solution.py:21
  241.6 41.9 %collective-permute-start.32 = (bf16[256,1024]{1,0:T(8,128)(2,1)S(1)}, bf16[256,1024]{1,0:T(8,128)(2,1)S(1)}, u32[]{:S(2)}, u32[]{:S(2)}) collective-permute-start(bf16[256,1024]{1,0:T(8,128)(2,1)S(1)} %get-tuple-element.183), channel_id=1, source_target_pairs={{0,8},{8,0},{1,9},{9,1},{2,10},{10,2},{3,11},{11,3},{4,12},{12,4},... | collective-permute-start | bytes 1572872 | tf_op jit(solution)/shard_map/ppermute | solution.py:21
  246.1 31.1 %collective-permute-start.33 = (bf16[2,768,256]{2,1,0:T(8,128)(2,1)S(1)}, bf16[2,768,256]{2,1,0:T(8,128)(2,1)S(1)}, u32[]{:S(2)}, u32[]{:S(2)}) collective-permute-start(bf16[2,768,256]{2,1,0:T(8,128)(2,1)S(1)} %get-tuple-element.159), channel_id=1, source_target_pairs={{0,1},{1,0},{2,3},{3,2},{4,5},{5,4},{6,7},{7,6},{8,9},{9,8},{10,11... | collective-permute-start | bytes 2359304 | tf_op jit(solution)/shard_map/ppermute | solution.py:21
  258.9 18.3 %collective-permute-start.40 = (bf16[512,256]{1,0:T(8,128)(2,1)S(1)}, bf16[512,256]{1,0:T(8,128)(2,1)S(1)}, u32[]{:S(2)}, u32[]{:S(2)}) collective-permute-start(bf16[512,256]{1,0:T(8,128)(2,1)S(1)} %slice_bitcast_fusion.8), channel_id=1, source_target_pairs={{0,1},{1,0},{2,3},{3,2},{4,5},{5,4},{6,7},{7,6},{8,9},{9,8},{10,11... | collective-permute-start | bytes 786440 | tf_op jit(solution)/shard_map/ppermute | solution.py:21
  260.1 36.1 %collective-permute-start.49 = (bf16[704,256]{1,0:T(8,128)(2,1)}, bf16[704,256]{1,0:T(8,128)(2,1)}, u32[]{:S(2)}, u32[]{:S(2)}) collective-permute-start(bf16[704,256]{1,0:T(8,128)(2,1)} %add_convert_fusion.14.p0), channel_id=1, source_target_pairs={{0,4},{4,0},{1,5},{5,1},{2,6},{6,2},{3,7},{7,3},{8,12},{12,8},{9,1... | collective-permute-start | bytes 1081352 | tf_op jit(solution)/shard_map/ppermute | solution.py:21
  265.2 17.2 %collective-permute-start.58 = (bf16[704,256]{1,0:T(8,128)(2,1)S(1)}, bf16[704,256]{1,0:T(8,128)(2,1)S(1)}, u32[]{:S(2)}, u32[]{:S(2)}) collective-permute-start(bf16[704,256]{1,0:T(8,128)(2,1)S(1)} %slice_bitcast_fusion.2), channel_id=1, source_target_pairs={{0,2},{1,3},{2,0},{3,1},{4,6},{5,7},{6,4},{7,5},{8,10},{9,11},{10,... | collective-permute-start | bytes 1081352 | tf_op jit(solution)/shard_map/ppermute | solution.py:21
  278.2 11.4 %collective-permute-start.34 = (bf16[768,256]{1,0:T(8,128)(2,1)}, bf16[768,256]{1,0:T(8,128)(2,1)}, u32[]{:S(2)}, u32[]{:S(2)}) collective-permute-start(bf16[768,256]{1,0:T(8,128)(2,1)} %slice_bitcast_fusion), channel_id=1, source_target_pairs={{0,2},{1,3},{2,0},{3,1},{4,6},{5,7},{6,4},{7,5},{8,10},{9,11},{10,... | collective-permute-start | bytes 1179656 | tf_op jit(solution)/shard_map/ppermute | solution.py:21
  279.5 15.0 %collective-permute-start.41 = (bf16[512,256]{1,0:T(8,128)(2,1)}, bf16[512,256]{1,0:T(8,128)(2,1)}, u32[]{:S(2)}, u32[]{:S(2)}) collective-permute-start(bf16[512,256]{1,0:T(8,128)(2,1)} %fusion.6), channel_id=1, source_target_pairs={{0,16},{16,0},{1,17},{17,1},{2,18},{18,2},{3,19},{19,3},{4,20},{20... | collective-permute-start | bytes 786440 | tf_op jit(solution)/shard_map/ppermute | solution.py:21
  282.5 51.0 %collective-permute-start.50 = (bf16[704,256]{1,0:T(8,128)(2,1)}, bf16[704,256]{1,0:T(8,128)(2,1)}, u32[]{:S(2)}, u32[]{:S(2)}) collective-permute-start(bf16[704,256]{1,0:T(8,128)(2,1)} %add_convert_fusion.14.p0), channel_id=1, source_target_pairs={{0,8},{8,0},{1,9},{9,1},{2,10},{10,2},{3,11},{11,3},{4,12},{12,4},... | collective-permute-start | bytes 1081352 | tf_op jit(solution)/shard_map/ppermute | solution.py:21
  283.4 50.1 %collective-permute-start.55 = (bf16[704,256]{1,0:T(8,128)(2,1)}, bf16[704,256]{1,0:T(8,128)(2,1)}, u32[]{:S(2)}, u32[]{:S(2)}) collective-permute-start(bf16[704,256]{1,0:T(8,128)(2,1)} %add_convert_fusion.13.u0), channel_id=1, source_target_pairs={{0,8},{8,0},{1,9},{9,1},{2,10},{10,2},{3,11},{11,3},{4,12},{12,4},... | collective-permute-start | bytes 1081352 | tf_op jit(solution)/shard_map/ppermute | solution.py:21
  286.0 48.0 %all-to-all-start.2 = ((bf16[32,8,1024]{2,1,0:T(8,128)(2,1)}), bf16[32,8,1024]{2,1,0:T(8,128)(2,1)S(1)}, u32[]{:S(2)}, u32[]{:S(2)}) async-start(bf16[32,8,1024]{2,1,0:T(8,128)(2,1)} %bitcast.48), calls=%async_computation.2 | async-start | bytes 1048576 | tf_op jit(solution)/shard_map/all_to_all | solution.py:1165
  290.7 42.1 %collective-permute-start.35 = (bf16[768,256]{1,0:T(8,128)(2,1)S(1)}, bf16[768,256]{1,0:T(8,128)(2,1)S(1)}, u32[]{:S(2)}, u32[]{:S(2)}) collective-permute-start(bf16[768,256]{1,0:T(8,128)(2,1)S(1)} %fusion), channel_id=1, source_target_pairs={{0,16},{16,0},{1,17},{17,1},{2,18},{18,2},{3,19},{19,3},{4,20},{20... | collective-permute-start | bytes 1179656 | tf_op jit(solution)/shard_map/ppermute | solution.py:21
  295.6 37.2 %collective-permute-start.43 = (bf16[512,256]{1,0:T(8,128)(2,1)S(1)}, bf16[512,256]{1,0:T(8,128)(2,1)S(1)}, u32[]{:S(2)}, u32[]{:S(2)}) collective-permute-start(bf16[512,256]{1,0:T(8,128)(2,1)S(1)} %add_convert_fusion.15.p0), channel_id=1, source_target_pairs={{0,8},{8,0},{1,9},{9,1},{2,10},{10,2},{3,11},{11,3},{4,12},{12,4},... | collective-permute-start | bytes 786440 | tf_op jit(solution)/shard_map/ppermute | solution.py:21
  296.2 41.3 %collective-permute-start.59 = (bf16[704,256]{1,0:T(8,128)(2,1)S(1)}, bf16[704,256]{1,0:T(8,128)(2,1)}, u32[]{:S(2)}, u32[]{:S(2)}) collective-permute-start(bf16[704,256]{1,0:T(8,128)(2,1)S(1)} %fusion.1), channel_id=1, source_target_pairs={{0,16},{16,0},{1,17},{17,1},{2,18},{18,2},{3,19},{19,3},{4,20},{20... | collective-permute-start | bytes 1081352 | tf_op jit(solution)/shard_map/ppermute | solution.py:21
  332.8 7.0 %collective-permute-start.42 = (bf16[512,256]{1,0:T(8,128)(2,1)S(1)}, bf16[512,256]{1,0:T(8,128)(2,1)}, u32[]{:S(2)}, u32[]{:S(2)}) collective-permute-start(bf16[512,256]{1,0:T(8,128)(2,1)S(1)} %add_convert_fusion.15.p0), channel_id=1, source_target_pairs={{0,4},{4,0},{1,5},{5,1},{2,6},{6,2},{3,7},{7,3},{8,12},{12,8},{9,1... | collective-permute-start | bytes 786440 | tf_op jit(solution)/shard_map/ppermute | solution.py:21
  332.8 7.9 %collective-permute-start.44 = (bf16[512,256]{1,0:T(8,128)(2,1)S(1)}, bf16[512,256]{1,0:T(8,128)(2,1)}, u32[]{:S(2)}, u32[]{:S(2)}) collective-permute-start(bf16[512,256]{1,0:T(8,128)(2,1)S(1)} %collective-permute-done.43.p2), channel_id=1, source_target_pairs={{0,4},{4,0},{1,5},{5,1},{2,6},{6,2},{3,7},{7,3},{8,12},{12,8},{9,1... | collective-permute-start | bytes 786440 | tf_op jit(solution)/shard_map/ppermute | solution.py:21
  333.4 8.3 %collective-permute-start.54 = (bf16[704,256]{1,0:T(8,128)(2,1)}, bf16[704,256]{1,0:T(8,128)(2,1)}, u32[]{:S(2)}, u32[]{:S(2)}) collective-permute-start(bf16[704,256]{1,0:T(8,128)(2,1)} %add_convert_fusion.13.u0), channel_id=1, source_target_pairs={{0,4},{4,0},{1,5},{5,1},{2,6},{6,2},{3,7},{7,3},{8,12},{12,8},{9,1... | collective-permute-start | bytes 1081352 | tf_op jit(solution)/shard_map/ppermute | solution.py:21
  333.6 8.8 %collective-permute-start.51 = (bf16[704,256]{1,0:T(8,128)(2,1)}, bf16[704,256]{1,0:T(8,128)(2,1)}, u32[]{:S(2)}, u32[]{:S(2)}) collective-permute-start(bf16[704,256]{1,0:T(8,128)(2,1)} %collective-permute-done.50.p2), channel_id=1, source_target_pairs={{0,4},{4,0},{1,5},{5,1},{2,6},{6,2},{3,7},{7,3},{8,12},{12,8},{9,1... | collective-permute-start | bytes 1081352 | tf_op jit(solution)/shard_map/ppermute | solution.py:21
  334.0 57.2 %all-to-all-start.3 = ((bf16[32,8,1024]{2,1,0:T(8,128)(2,1)}), bf16[32,8,1024]{2,1,0:T(8,128)(2,1)S(1)}, u32[]{:S(2)}, u32[]{:S(2)}) async-start(bf16[32,8,1024]{2,1,0:T(8,128)(2,1)} %bitcast.50), calls=%async_computation.3 | async-start | bytes 1048576 | tf_op jit(solution)/shard_map/all_to_all | solution.py:1165
  337.5 27.4 %collective-permute-start.37 = (bf16[768,256]{1,0:T(8,128)(2,1)S(1)}, bf16[768,256]{1,0:T(8,128)(2,1)S(1)}, u32[]{:S(2)}, u32[]{:S(2)}) collective-permute-start(bf16[768,256]{1,0:T(8,128)(2,1)S(1)} %add_convert_fusion.11.refs_0_), channel_id=1, source_target_pairs={{0,8},{8,0},{1,9},{9,1},{2,10},{10,2},{3,11},{11,3},{4,12},{12,4},... | collective-permute-start | bytes 1179656 | tf_op jit(solution)/shard_map/ppermute | solution.py:21
  339.8 24.6 %collective-permute-start.61 = (bf16[704,256]{1,0:T(8,128)(2,1)S(1)}, bf16[704,256]{1,0:T(8,128)(2,1)}, u32[]{:S(2)}, u32[]{:S(2)}) collective-permute-start(bf16[704,256]{1,0:T(8,128)(2,1)S(1)} %add_convert_fusion.12.p0), channel_id=1, source_target_pairs={{0,8},{8,0},{1,9},{9,1},{2,10},{10,2},{3,11},{11,3},{4,12},{12,4},... | collective-permute-start | bytes 1081352 | tf_op jit(solution)/shard_map/ppermute | solution.py:21
  340.7 23.7 %collective-permute-start.56 = (bf16[704,256]{1,0:T(8,128)(2,1)}, bf16[704,256]{1,0:T(8,128)(2,1)S(1)}, u32[]{:S(2)}, u32[]{:S(2)}) collective-permute-start(bf16[704,256]{1,0:T(8,128)(2,1)} %collective-permute-done.55.u2), channel_id=1, source_target_pairs={{0,4},{4,0},{1,5},{5,1},{2,6},{6,2},{3,7},{7,3},{8,12},{12,8},{9,1... | collective-permute-start | bytes 1081352 | tf_op jit(solution)/shard_map/ppermute | solution.py:21
  341.7 43.2 %collective-permute-start.60 = (bf16[704,256]{1,0:T(8,128)(2,1)S(1)}, bf16[704,256]{1,0:T(8,128)(2,1)S(1)}, u32[]{:S(2)}, u32[]{:S(2)}) collective-permute-start(bf16[704,256]{1,0:T(8,128)(2,1)S(1)} %add_convert_fusion.12.p0), channel_id=1, source_target_pairs={{0,4},{4,0},{1,5},{5,1},{2,6},{6,2},{3,7},{7,3},{8,12},{12,8},{9,1... | collective-permute-start | bytes 1081352 | tf_op jit(solution)/shard_map/ppermute | solution.py:21
  342.3 24.4 %collective-permute-start.45 = (bf16[256,256]{1,0:T(8,128)(2,1)S(1)}, bf16[256,256]{1,0:T(8,128)(2,1)S(1)}, u32[]{:S(2)}, u32[]{:S(2)}) collective-permute-start(bf16[256,256]{1,0:T(8,128)(2,1)S(1)} %get-tuple-element.188), channel_id=1, source_target_pairs={{0,1},{1,0},{2,3},{3,2},{4,5},{5,4},{6,7},{7,6},{8,9},{9,8},{10,11... | collective-permute-start | bytes 393224 | tf_op jit(solution)/shard_map/ppermute | solution.py:21
  364.4 20.6 %collective-permute-start.62 = (bf16[704,256]{1,0:T(8,128)(2,1)}, bf16[704,256]{1,0:T(8,128)(2,1)S(1)}, u32[]{:S(2)}, u32[]{:S(2)}) collective-permute-start(bf16[704,256]{1,0:T(8,128)(2,1)} %collective-permute-done.61.p2), channel_id=1, source_target_pairs={{0,4},{4,0},{1,5},{5,1},{2,6},{6,2},{3,7},{7,3},{8,12},{12,8},{9,1... | collective-permute-start | bytes 1081352 | tf_op jit(solution)/shard_map/ppermute | solution.py:21
  364.4 27.9 %collective-permute-start.36 = (bf16[768,256]{1,0:T(8,128)(2,1)S(1)}, bf16[768,256]{1,0:T(8,128)(2,1)}, u32[]{:S(2)}, u32[]{:S(2)}) collective-permute-start(bf16[768,256]{1,0:T(8,128)(2,1)S(1)} %add_convert_fusion.11.refs_0_), channel_id=1, source_target_pairs={{0,4},{4,0},{1,5},{5,1},{2,6},{6,2},{3,7},{7,3},{8,12},{12,8},{9,1... | collective-permute-start | bytes 1179656 | tf_op jit(solution)/shard_map/ppermute | solution.py:21
  364.9 27.4 %collective-permute-start.38 = (bf16[768,256]{1,0:T(8,128)(2,1)S(1)}, bf16[768,256]{1,0:T(8,128)(2,1)}, u32[]{:S(2)}, u32[]{:S(2)}) collective-permute-start(bf16[768,256]{1,0:T(8,128)(2,1)S(1)} %collective-permute-done.37.refs_2_), channel_id=1, source_target_pairs={{0,4},{4,0},{1,5},{5,1},{2,6},{6,2},{3,7},{7,3},{8,12},{12,8},{9,1... | collective-permute-start | bytes 1179656 | tf_op jit(solution)/shard_map/ppermute | solution.py:21
  366.8 5.8 %collective-permute-start.46 = (bf16[256,256]{1,0:T(8,128)(2,1)S(1)}, bf16[256,256]{1,0:T(8,128)(2,1)S(1)}, u32[]{:S(2)}, u32[]{:S(2)}) collective-permute-start(bf16[256,256]{1,0:T(8,128)(2,1)S(1)} %get-tuple-element.189), channel_id=1, source_target_pairs={{0,2},{1,3},{2,0},{3,1},{4,6},{5,7},{6,4},{7,5},{8,10},{9,11},{10,... | collective-permute-start | bytes 393224 | tf_op jit(solution)/shard_map/ppermute | solution.py:21
  372.6 8.4 %collective-permute-start.47 = (bf16[256,256]{1,0:T(8,128)(2,1)S(1)}, bf16[256,256]{1,0:T(8,128)(2,1)S(1)}, u32[]{:S(2)}, u32[]{:S(2)}) collective-permute-start(bf16[256,256]{1,0:T(8,128)(2,1)S(1)} %get-tuple-element.187), channel_id=1, source_target_pairs={{0,3},{1,2},{2,1},{3,0},{4,7},{5,6},{6,5},{7,4},{8,11},{9,10},{10,... | collective-permute-start | bytes 393224 | tf_op jit(solution)/shard_map/ppermute | solution.py:21
  (57 other events, 691.4 us)
Sparse Core Ops, SparseCore 0:
  35.4 73.3 all-gather.2

commit v3 on v2

--- a/solution.py
+++ b/solution.py
@@ -1019,8 +1019,10 @@
     return grads_call(kernel, info, n * 256, tuple(args), specs)
 
 
-def hop(parts, first, hold=()):
+def hop(parts, first, hold=(), hold_send=()):
     keep, give = parts
+    if hold_send:
+        give = after(give, *hold_send)
     got = send(give, "shard", first)
     if hold:
         got = after(got, *hold)
@@ -1028,32 +1030,32 @@
     return total[0].astype(BF), total[1].astype(BF)
 
 
-def hop_two(own, other, first, hold=(), hold_send=()):
-    got = send(after(other, *hold_send) if hold_send else other, "shard", 3 - first)
+def hop_two(own, other, first):
+    return own, send(other, "shard", 3 - first)
+
+
+def joined(terms, hold=()):
     if hold:
-        got = after(got, *hold)
-    return (own.astype(F32) + got.astype(F32)).astype(BF)
-
-
-def over_zh(part, hold=(), hold_send=()):
-    if hold_send:
-        part = after(part, *hold_send)
+        terms = [(own, after(got, *hold)) for own, got in terms]
+    return jnp.concatenate([(own.astype(F32) + got.astype(F32)).astype(BF) for own, got in terms], 0)
+
+
+def over_zh(part, hold=()):
     got = send(part, "zh", 1)
     if hold:
         got = after(got, *hold)
     return (part.astype(F32) + got.astype(F32)).astype(BF)
 
 
-def fin_out_kernel(info, p0, p1, p2, p3, u0, u1, u2, u3, fin, stack):
+def fin_out_kernel(info, p0, p1, p2, p3, fin, stack):
     unit = jnp.where(
         lax.broadcasted_iota(jnp.int32, (256, 256), 0) == lax.broadcasted_iota(jnp.int32, (256, 256), 1), 1.0, 0.0
     ).astype(BF)
-    for j, both in enumerate(((p0, u0), (p1, u1), (p2, u2), (p3, u3))):
+    for j, p in enumerate((p0, p1, p2, p3)):
         q = info[0] ^ j
         for n in range(2 * N_SHARD):
             start = pl.multiple_of(n * FF_OWN + q * FF_PART, 16)
-            m = n % N_SHARD
-            stack[pl.ds(start, FF_PART)] = both[n // N_SHARD][m * FF_PART : (m + 1) * FF_PART]
+            stack[pl.ds(start, FF_PART)] = p[n * FF_PART : (n + 1) * FF_PART]
     for n in range(11):
         fin[:, n * 512 : (n + 1) * 512] = dot(unit, stack[n * 512 : (n + 1) * 512], NT)
 
@@ -1064,7 +1066,7 @@
         sds((256, 8 * FF_OWN), F32),
         (info,),
         tuple(pieces),
-        in_specs=[full(FF_OWN, 256)] * 8,
+        in_specs=[full(2 * FF_OWN, 256)] * 4,
         out_specs=full(256, 8 * FF_OWN),
         scratch=[pltpu.VMEM((8 * FF_OWN, 256), BF)],
         mib=24,
@@ -1086,36 +1088,30 @@
         sds((FF_OWN, WIDTH), F32),
         (info,),
         tuple(pieces),
-        in_specs=[full(FF_OWN, 256)] * 4,
+        in_specs=[full(*p.shape) for p in pieces],
         out_specs=full(FF_OWN, WIDTH),
         nbytes=5 << 20,
     )
 
 
-def columns_out_kernel(info, *refs):
-    pieces, outs = refs[:4], refs[4:]
-    for j, p in enumerate(pieces):
+def last_out_kernel(info, q0, q1, q2, q3, d0, d1, d2, d3, o0, o1, o2, o3, g_q, g_k, g_v, g_u, g_out):
+    for j, (p, d, o) in enumerate(zip((q0, q1, q2, q3), (d0, d1, d2, d3), (o0, o1, o2, o3))):
         at = pl.ds(pl.multiple_of((info[0] ^ j) * 256, 256), 256)
-        for t, out in enumerate(outs):
+        for t, out in enumerate((g_q, g_k, g_v)):
             out[:, at] = p[t * 256 : (t + 1) * 256].astype(F32)
-
-
-def columns_out(info, pieces, n):
-    return run(
-        columns_out_kernel,
-        (sds((256, WIDTH), F32),) * n,
+        g_u[:, at] = d[FF_OWN + 256 :].astype(F32)
+        g_out[:, lanes(j, info)] = o[...].astype(F32)
+
+
+def last_out(info, pieces):
+    return run(
+        last_out_kernel,
+        (sds((256, WIDTH), F32),) * 5,
         (info,),
         tuple(pieces),
         in_specs=[full(*p.shape) for p in pieces],
-        out_specs=[full(256, WIDTH)] * n,
-        nbytes=(3 * n) << 19,
-    )
-
-
-def out_grad_kernel(info, o0, o1, o2, o3, p0, p1, p2, p3, g_out, g_u):
-    for j, (o, p) in enumerate(zip((o0, o1, o2, o3), (p0, p1, p2, p3))):
-        g_out[:, lanes(j, info)] = o[...].astype(F32)
-        g_u[:, pl.ds(pl.multiple_of((info[0] ^ j) * 256, 256), 256)] = p[256:].astype(F32)
+        out_specs=[full(256, WIDTH)] * 5,
+    )
 
 
 def finish_kernel(x, gh, here, got, enter, out):
@@ -1181,21 +1177,23 @@
 
 
 def team_own(keep, give, *behind):
-    got = send(give, "core", 1)
-    here = keep[0].astype(F32) + got[0].astype(F32)
-    there = (keep[1].astype(F32) + got[1].astype(F32)).astype(BF)
+    there = keep[1].astype(F32) + send(give[1], "core", 1).astype(F32)
+    here = keep[0].astype(F32) + send(give[0], "core", 1).astype(F32)
+    there = there.astype(BF)
     if behind:
         there = after(there, *behind)
-    return here, send(there, "zl", 1), there
-
-
-def state_in(state, near, whole, cross):
+    return here, send(there, "zl", 1)
+
+
+def state_in(state, near, whole, cross, hold=()):
     low = [state] + [lax.ppermute(state, "shard", [(i, i ^ j) for i in range(4)]) for j in (1, 2, 3)]
     wide = [v.astype(F32) for v in low]
-    hand = sum(whole[j][:, None, None] * wide[j] for j in range(4)).astype(BF)
+    hand = sum(whole[j][:, None, None] * wide[j] for j in range(4))
+    if hold:
+        hand = after(hand, *hold)
     got = send(hand, "zh", 1)
     here = sum(near[j][:, None, None] * wide[j] for j in (1, 2, 3))
-    return here + cross[:, None, None] * got.astype(F32), hand
+    return here + cross[:, None, None] * got, hand
 
 
 def fast_body(tokens_in, cotangent, deal_order, lengths, decay_rates, w_query, w_key, w_value, w_ugate, w_out, w_ffin, w_ffdown):
@@ -1213,94 +1211,93 @@
     raw_x = exchange(sent_x)
     quarter = take_quarter(after(info, sent_x), *far(w_query, w_key, w_value, w_ugate))
     w_proj = gather_pieces(quarter)
-    w_ff = lax.all_gather(after(ff_bundle(after(info, quarter), *far(w_ffin, w_ffdown)), raw_x), "shard", axis=0)
+    bundle = ff_bundle(after(info, quarter), *far(w_ffin, w_ffdown))
+    w_ff = lax.all_gather(after(bundle, raw_x), "shard", axis=0)
     wo = gather_out(w_out, me, shard)
     x_raws = team_raw(raw_x)
-    raw_g = exchange(after(sent_g, raw_x))
-    g_raws = team_raw(raw_g)
-
-    ids = jnp.arange(8)
-    last = jnp.sum(((ids[:, None] + 1) * span - 1 >= ends[None, :]).astype(jnp.int32), axis=1)
-    before = jnp.where(ids == 0, -1, jnp.sum((ids[:, None] * span - 1 >= ends[None, :]).astype(jnp.int32), axis=1))
+    g_raws = team_raw(exchange(after(sent_g, raw_x)))
+
     rates = lax.dynamic_slice_in_dim(decay_rates, me * HEADS_OWN, HEADS_OWN)
+
+    def seg_at(p):
+        seg = jnp.sum((p[..., None] >= ends).astype(jnp.int32), axis=-1)
+        return jnp.where(p < 0, -1, seg)
 
     def weigh(flag, gap):
         return jnp.where(flag[..., None], jnp.exp(-(jnp.maximum(gap, 0) * span).astype(F32)[..., None] * rates), 0.0)
 
-    js = jnp.arange(4)
-    peers = zh * N_SHARD + (shard ^ js)
-    my_last, my_before = last[group], before[group]
-    f_near = weigh((peers < group) & (last[peers] == my_before), group - 1 - peers)
-    end = zh * N_SHARD + 3
-    f_whole = weigh(last[peers] == last[end], end - peers)
-    f_cross = weigh((zh == 1) & (last[3] == my_before), shard)
-    b_near = weigh((peers > group) & (before[peers] == my_last), peers - 1 - group)
-    start = zh * N_SHARD
-    b_whole = weigh(before[peers] == before[start], peers - start)
-    b_cross = weigh((zh == 0) & (before[4] == my_last), 3 - shard)
+    peers = zh * N_SHARD + (shard ^ jnp.arange(4))
+    peers_last, peers_before = seg_at((peers + 1) * span - 1), seg_at(peers * span - 1)
+    my_last, my_before = peers_last[0], peers_before[0]
+    end, start = zh * N_SHARD + 3, zh * N_SHARD
+    f_near = weigh((peers < group) & (peers_last == my_before), group - 1 - peers)
+    f_whole = weigh(peers_last == seg_at((end + 1) * span - 1), end - peers)
+    f_cross = weigh((zh == 1) & (seg_at(start * span - 1) == my_before), shard)
+    b_near = weigh((peers > group) & (peers_before == my_last), peers - 1 - group)
+    b_whole = weigh(peers_before == seg_at(start * span - 1), peers - start)
+    b_cross = weigh((zh == 0) & (seg_at((end + 1) * span - 1) == my_last), 3 - shard)
 
     x, normed, pq, pk, pu, q, k, v, kv, state = project(scal, enter, far(*x_raws), far(*w_proj))
     s_in, _ = state_in(state, f_near, f_whole, f_cross)
     local = attend_local(scal, q, k, v)
     mixed, gated, a_keep, a_give = carry_in((after(info, g_raws[1]), *scal[1:]), local, q, pu, kv, s_in, wo)
-    ta, tb, _ = team_sum(a_keep, a_give)
-    g, n2, product, gg, gu, r_keep, r_give, n_keep, n_give = sglu(info, enter, x, ta, tb, far(*g_raws), *far(w_ff))
+    ta, tb, _ = team_sum(a_keep, a_give, hold=(g_raws[2], g_raws[3]))
+    g, n2, product, gg, gu, r_keep, r_give, n_keep, n_give = sglu(info, *far(enter), x, ta, *far(tb), far(*g_raws), *far(w_ff))
     n_got = send(n_give, "core", 1)
+    d_gate = hidden_grads(info, n2, gg, 1)
     n_half = (n_keep.astype(F32) + n_got.astype(F32)).astype(BF)
     n_other = send(n_half, "zl", 1)
-    d_gate = hidden_grads(after(info, n_half), n2, gg, 1)
-    d_up = hidden_grads(after(info, d_gate[1]), n2, gu, 2)
+    d_up = hidden_grads(after(info, n_half), n2, gu, 2)
     d_down = down_grads(after(info, d_up[1]), g, product, 1)
-    n_other = after(n_other, d_down[1])
+    gate_own, gate_other = hop(d_gate, 1, hold=(d_down[1],))
+    n_other = after(n_other, d_down[1], gate_other)
     ua = (n_half.astype(F32) + n_other[::-1].astype(F32)).astype(BF)
     ub = send(ua, "core", 1)
-    gate_own, gate_other = hop(d_gate, 1, hold=(ua,))
     up_own, up_other = hop(d_up, 2, hold=(ua,))
-    gate = hop_two(gate_own, gate_other, 1, hold=(gate_other,))
-
-    ga, gpu, gm, qg, gh, g_state = hidden_back((after(info, gate_other, up_other), *scal[1:]), x, ta, tb, ua, ub, g, wo, mixed, pu, q)
-    g_in, handed = state_in(g_state, b_near, b_whole, b_cross)
-    gq, gk, gv = scores_back((after(info, gate), *scal[1:]), q, k, v, gm, kv, s_in)
-    d_ou = column_grads(after(info, gq), [(gated, ga), (normed, gpu)], 2)
-    up = hop_two(up_own, up_other, 2, hold=(handed,))
-    r_here, r_there, r_sent = team_own(r_keep, r_give, ub)
-    sent_back = finish(result_kernel, x, ta, r_here, r_there, after(enter, gq))
+
+    ga, gpu, gm, qg, gh, g_state = hidden_back(
+        (after(info, up_other), *scal[1:]), x, ta, *far(tb), ua, *far(ub), g, wo, mixed, pu, q
+    )
+    gate = hop_two(gate_own, gate_other, 1)
+    up = hop_two(up_own, up_other, 2)
+    gq, gk, gv = scores_back(scal, q, k, v, gm, kv, s_in)
+    r_here, r_there = team_own(r_keep, r_give, ua)
+    g_in, handed = state_in(g_state, b_near, b_whole, b_cross, hold=(r_there,))
+    d_ou = column_grads(after(info, handed), [(gated, ga), (normed, gpu)], 2)
+    fin = joined((gate, up), hold=(d_ou[1],))
     dqkv, p_keep, p_give = project_back(
-        (after(info, d_ou[1], sent_back), *scal[1:]), gq, gk, gv, pq, pk, k, v, gpu, qg, g_in, far(*w_proj)
-    )
-    here, there, p_sent = team_own(p_keep, p_give)
-    d_qkv = column_grads(after(info, p_sent), [(normed, dqkv)], 1)
-    qkv_own, qkv_other = hop(d_qkv, 1, hold=(p_sent,))
-    last_sent = finish(finish_kernel, x, gh, here, there, enter)
+        (after(info, fin), *scal[1:]), gq, gk, gv, pq, pk, k, v, gpu, qg, g_in, far(*w_proj)
+    )
+    here, there = team_own(p_keep, p_give)
+    d_qkv = column_grads(info, [(normed, dqkv)], 1)
+    last_sent = finish(finish_kernel, x, gh, here, there, after(enter, d_qkv[1]))
     input_grad = unsort(leave, exchange(last_sent))
-    output = unsort(leave, exchange(after(sent_back, last_sent)))
-
-    gate_sum = over_zh(gate, hold=(p_sent,), hold_send=(gq,))
-    up_sum = over_zh(up, hold=(p_sent,), hold_send=(gq,))
-    down = hop_two(*hop(d_down, 1, hold=(p_sent,)), 1, hold=(p_sent,))
-    ou = hop_two(*hop(d_ou, 2, hold=(p_sent,)), 2, hold=(p_sent,))
-    down_sum = over_zh(down)
-    ou_sum = over_zh(ou)
-    qkv_sum = over_zh(hop_two(qkv_own, qkv_other, 1))
-    grad_fin = fin_out(info, (*far(*team_gather(gate_sum)), *far(*team_gather(up_sum))))
-    grad_down = down_out(info, far(*team_gather(down_sum)))
-    ou = team_gather(ou_sum)
+    output = unsort(leave, exchange(finish(result_kernel, x, ta, r_here, r_there, after(enter, last_sent))))
+
+    down_own, down_other = hop(d_down, 1, hold=(last_sent,), hold_send=(handed,))
+    ou_own, ou_other = hop(d_ou, 2, hold=(down_other,))
+    fin_sum = over_zh(fin, hold=(ou_other,))
+    fin_pair = send(fin_sum, "zl", 1)
+    down_ou = joined((hop_two(down_own, down_other, 1), hop_two(ou_own, ou_other, 2)), hold=(fin_sum,))
+    qkv_own, qkv_other = hop(d_qkv, 1, hold=(last_sent,))
+    qkv = joined((hop_two(qkv_own, qkv_other, 1),))
+    down_sum = over_zh(down_ou, hold=(fin_pair, input_grad))
+    down_pair = send(down_sum, "zl", 1)
+    fin_all = [fin_sum, send(fin_sum, "core", 1), fin_pair, send(fin_pair, "core", 1)]
+    down_all = [down_sum, send(down_sum, "core", 1), down_pair, send(down_pair, "core", 1)]
+    grad_fin = fin_out(info, far(*fin_all))
+    grad_down = down_out(info, far(*down_all))
     outs = []
     for j in range(4):
         pick = me ^ shard ^ j
-        top = [p[:256] for p in ou]
+        top = [p[FF_OWN : FF_OWN + 256] for p in down_all]
         piece = jnp.where(pick < 2, jnp.where(pick == 0, top[0], top[1]), jnp.where(pick == 2, top[2], top[3]))
         outs.append(piece if j == 0 else send(piece, "shard", j))
-    grad_out, grad_u = run(
-        out_grad_kernel,
-        (sds((256, WIDTH), F32),) * 2,
-        (info,),
-        far(*outs, *ou),
-        in_specs=[*[full(256, 256)] * 4, *[full(512, 256)] * 4],
-        out_specs=[full(256, WIDTH)] * 2,
-        nbytes=3 << 20,
-    )
-    grad_q, grad_k, grad_v = columns_out(info, far(*team_gather(qkv_sum)), 3)
+    qkv_sum = over_zh(qkv, hold=(down_pair, output, grad_fin))
+    qkv_pair = send(qkv_sum, "zl", 1)
+    qkv_late = after(qkv_pair, grad_down, *outs[1:])
+    qkv_all = [qkv_sum, send(qkv_sum, "core", 1), qkv_late, send(qkv_late, "core", 1)]
+    grad_q, grad_k, grad_v, grad_u, grad_out = last_out(info, far(*qkv_all, *down_all, *outs))
     return (output, input_grad, grad_q, grad_k, grad_v, grad_u, grad_out, grad_fin, grad_down)
 
 

time: 404 us -> 370 us (0.916)
  waiting for transfers between devices: 181 us -> 145 us
    ppermute x54 -> x48, waiting for transfers between devices: 163 us -> 130 us  [send(): return lax.ppermute(value, axis, [(i, i ^ mask) for i in range(size)])]
    pallas_call x23 -> x22, Pallas kernels: 102 us -> 105 us  [run(): pl.pallas_call(kernel, out_shape=out, grid_spec=pltpu.PrefetchScalarGridS...]
    unnamed x106 -> x136, local copies, waits for them, and re-layouts: 10 us -> 8.54 us
    ppermute x54 -> x48, starting transfers between devices: 42.2 us -> 40.8 us  [send(): return lax.ppermute(value, axis, [(i, i ^ mask) for i in range(size)])]
  transfers between devices with their start and end apart: 68 -> 62, of which waited for: 27 -> 25; matrix products, arithmetic and copies ran while one was open for 5% -> 6% of each run, Pallas kernels for 17% -> 19%
where the time goes in v3:
time: 370 us; the launch traced here: 368 us
  waiting for transfers between devices  145 us (39%)
  Pallas kernels  105 us (28%)
  starting transfers between devices  71.7 us (19%)
  other arithmetic  20.1 us (5%)
  between operations  16.6 us (4%)
  local copies, waits for them, and re-layouts  10.5 us (3%)
    ppermute x48, waiting for transfers between devices, send(): return lax.ppermute(value, axis, [(i, i ^ mask) for i in range(size)])  130 us
    pallas_call x22, Pallas kernels, run(): pl.pallas_call(kernel, out_shape=out, grid_spec=pltpu.PrefetchScalarGridS...  105 us
    ppermute x48, starting transfers between devices, send(): return lax.ppermute(value, axis, [(i, i ^ mask) for i in range(size)])  40.8 us
    all_to_all x4, starting transfers between devices, exchange(): return lax.all_to_all(rows, ALL, split_axis=0, concat_axis=0, tiled=True)  17 us
    ppermute x3, starting transfers between devices, gather_out(): wo = jnp.where(rel == j, lax.ppermute(w_out, axes, pairs), wo)  10.1 us
    ppermute x6, waiting for transfers between devices, state_in(): lax.ppermute(state, 'shard', [(i, i ^ j) for i in range(4)])  9.98 us
    unnamed x136, local copies, waits for them, and re-layouts  8.54 us
  transfers between devices with their start and end apart: 62, of which 25 were waited for; matrix products, arithmetic and copies ran while one was open for 6% of the time, Pallas kernels for 19%

profile of v3, /device:TPU:0, one launch (start us, length us, event | category | flops | bytes accessed | tf_op | source)
XLA Modules:
  0.0 368.4 jit_solution(483345774830973610)
XLA Ops:
  8.1 3.5 shard_map.187
  11.6 7.3 %all-to-all-start = ((bf16[32,8,1024]{2,1,0:T(8,128)(2,1)}), bf16[32,8,1024]{2,1,0:T(8,128)(2,1)S(1)}, u32[]{:S(2)}, u32[]{:S(2)}) async-start(bf16[32,8,1024]{2,1,0:T(8,128)(2,1)} %bitcast.6), calls=%async_computation | async-start | bytes 1048576 | tf_op jit(solution)/shard_map/all_to_all | solution.py:1161
  18.9 1.7 shard_map.188.w0
  20.6 1.8 collective-permute-start.3
  22.5 1.5 collective-permute-start.4
  25.6 4.8 %shard_map.192 = bf16[2112,256]{1,0:T(8,128)(2,1)} custom-call(s32[8]{0:T(128)S(1)} %stack.23.info, bf16[256,5632]{1,0:T(8,128)(2,1)} %fin.1, bf16[704,1024]{1,0:T(8,128)(2,1)} %down.1), custom_call_target="tpu_custom_call" | custom-call | tf_op jit(solution)/shard_map/pallas_call | solution.py:356
  30.6 4.5 %all-to-all-done = bf16[32,8,1024]{2,1,0:T(8,128)(2,1)S(1)} async-done(((bf16[32,8,1024]{2,1,0:T(8,128)(2,1)}), bf16[32,8,1024]{2,1,0:T(8,128)(2,1)S(1)}, u32[]{:S(2)}, u32[]{:S(2)}) %all-to-all-start) | async-done | bytes 524320 | tf_op jit(solution)/shard_map/all_to_all | solution.py:1161
  37.1 3.4 all-to-all-start.1
  40.6 14.5 %collective-permute-done.r1 = bf16[256,1024]{1,0:T(8,128)(2,1)} collective-permute-done((bf16[256,1024]{1,0:T(8,128)(2,1)S(1)}, bf16[256,1024]{1,0:T(8,128)(2,1)}, u32[]{:S(2)}, u32[]{:S(2)}) %collective-permute-start) | collective-permute-done | bytes 524320 | tf_op jit(solution)/shard_map/ppermute | solution.py:21
  55.3 3.9 %collective-permute-start.11 = (bf16[256,1024]{1,0:T(8,128)(2,1)}, bf16[256,1024]{1,0:T(8,128)(2,1)}, u32[]{:S(2)}, u32[]{:S(2)}) collective-permute-start(bf16[256,1024]{1,0:T(8,128)(2,1)} %param.21), channel_id=1, source_target_pairs={{0,3},{5,6},{10,9},{15,12},{16,19},{21,22},{26,25},{31,28}} | collective-permute-start | bytes 1572872 | tf_op jit(solution)/shard_map/ppermute | solution.py:554
  59.2 2.1 collective-permute-start.12
  62.0 4.1 %collective-permute-start.13 = (bf16[256,1024]{1,0:T(8,128)(2,1)}, bf16[256,1024]{1,0:T(8,128)(2,1)}, u32[]{:S(2)}, u32[]{:S(2)}) collective-permute-start(bf16[256,1024]{1,0:T(8,128)(2,1)} %param.21), channel_id=1, source_target_pairs={{0,1},{5,4},{10,11},{15,14},{16,17},{21,20},{26,27},{31,30}} | collective-permute-start | bytes 1572872 | tf_op jit(solution)/shard_map/ppermute | solution.py:554
  67.1 10.1 %shard_map.189 = (bf16[4,256,1024]{2,1,0:T(8,128)(2,1)}, bf16[4,256,1024]{2,1,0:T(8,128)(2,1)}, f32[4,256,256]{2,1,0:T(8,128)}, f32[4,256,256]{2,1,0:T(8,128)}, ...) custom-call(s32[8]{0:T(128)S(1)} %stack.23.info, ...), custom_call_target="tpu_custom_call" | custom-call | tf_op jit(solution)/shard_map/pallas_call | solution.py:356
  78.2 4.1 %collective-permute-done.7 = bf16[2,128,128]{2,1,0:T(8,128)(2,1)S(1)} collective-permute-done((bf16[2,128,128]{2,1,0:T(8,128)(2,1)S(1)}, bf16[2,128,128]{2,1,0:T(8,128)(2,1)S(1)}, u32[]{:S(2)}, u32[]{:S(2)}) %collective-permute-start.7) | collective-permute-done | bytes 65568 | tf_op jit(solution)/shard_map/ppermute | solution.py:1189
  83.8 5.1 %collective-permute-done.9 = bf16[2,128,128]{2,1,0:T(8,128)(2,1)S(1)} collective-permute-done((bf16[2,128,128]{2,1,0:T(8,128)(2,1)S(1)}, bf16[2,128,128]{2,1,0:T(8,128)(2,1)S(1)}, u32[]{:S(2)}, u32[]{:S(2)}) %collective-permute-start.9) | collective-permute-done | bytes 65568 | tf_op jit(solution)/shard_map/ppermute | solution.py:1189
  89.0 2.6 collective-permute-start.10
  92.8 2.8 shard_map.190.local
  97.5 3.7 %shard_map.191 = (f32[4,256,256]{2,1,0:T(8,128)S(1)}, bf16[4,256,256]{2,1,0:T(8,128)(2,1)S(1)}, bf16[2,256,1024]{2,1,0:T(8,128)(2,1)S(1)}, bf16[2,256,1024]{2,1,0:T(8,128)(2,1)S(1)}) custom-call(s32[8]{0:T(128)S(1)} %stack.23.info, s32[8]{0:T(128)S(1)} %select_reduce_fusion.ends, f32[8]{0:T(128)S(1)} %copy-done.35, f32[4,256,256]{2,1,0:T(8,128)S(1)} %shard_map.190.local, ...), custom_call_target="tpu_custom_call" | custom-call | tf_op jit(solution)/shard_map/pallas_call | solution.py:356
  102.3 2.7 collective-permute-done.14
  105.3 2.0 collective-permute-start.15
  107.9 2.3 collective-permute-done.16.g2
  111.7 19.1 %collective-permute-done.15 = bf16[2,256,1024]{2,1,0:T(8,128)(2,1)S(1)} collective-permute-done((bf16[2,256,1024]{2,1,0:T(8,128)(2,1)S(1)}, bf16[2,256,1024]{2,1,0:T(8,128)(2,1)S(1)}, u32[]{:S(2)}, u32[]{:S(2)}) %collective-permute-start.15) | collective-permute-done | bytes 1048608 | tf_op jit(solution)/shard_map/ppermute | solution.py:21
  131.3 2.8 collective-permute-done.18.tb
  134.1 19.3 %shard_map.193 = (bf16[4,256,1024]{2,1,0:T(8,128)(2,1)S(1)}, bf16[4,256,1024]{2,1,0:T(8,128)(2,1)S(1)}, bf16[4,256,704]{2,1,0:T(8,128)(2,1)S(1)}, bf16[4,256,704...) custom-call(s32[8]{0:T(128)S(1)} %stack.23.info, ...), custom_call_target="tpu_custom_call" | custom-call | tf_op jit(solution)/shard_map/pallas_call | solution.py:356
  153.5 3.5 shard_map.196
  158.8 1.8 collective-permute-start.22
  161.3 3.5 shard_map.194
  165.9 3.8 %shard_map.195 = (bf16[2,704,256]{2,1,0:T(8,128)(2,1)S(1)}, bf16[2,704,256]{2,1,0:T(8,128)(2,1)}) custom-call(s32[8]{0:T(128)S(1)} %stack.23.info, bf16[1024,1024]{1,0:T(8,128)(2,1)S(1)} %bitcast.116, bf16[1024,704]{1,0:T(8,128)(2,1)S(1)} %bitcast.123), custom_call_target="tpu_custom_call" | custom-call | tf_op jit(solution)/shard_map/pallas_call | solution.py:356
  169.7 5.9 %collective-permute-done.23 = bf16[2,704,256]{2,1,0:T(8,128)(2,1)S(1)} collective-permute-done((bf16[2,704,256]{2,1,0:T(8,128)(2,1)S(1)}, bf16[2,704,256]{2,1,0:T(8,128)(2,1)S(1)}, u32[]{:S(2)}, u32[]{:S(2)}) %collective-permute-start.23) | collective-permute-done | bytes 720928 | tf_op jit(solution)/shard_map/ppermute | solution.py:21
  175.8 8.2 %collective-permute-done.22 = bf16[2,256,1024]{2,1,0:T(8,128)(2,1)S(1)} collective-permute-done((bf16[2,256,1024]{2,1,0:T(8,128)(2,1)S(1)}, bf16[2,256,1024]{2,1,0:T(8,128)(2,1)S(1)}, u32[]{:S(2)}, u32[]{:S(2)}) %collective-permute-start.22) | collective-permute-done | bytes 1048608 | tf_op jit(solution)/shard_map/ppermute | solution.py:21
  184.6 1.3 fusion.1
  185.9 1.7 collective-permute-start.24
  189.8 8.0 %shard_map.197 = (bf16[4,256,1024]{2,1,0:T(8,128)(2,1)S(1)}, bf16[4,256,256]{2,1,0:T(8,128)(2,1)S(1)}, bf16[4,256,256]{2,1,0:T(8,128)(2,1)S(1)}, f32[4,2,128,128...) custom-call(s32[8]{0:T(128)S(1)} %stack.23.info, s32[8]{0:T(128)S(1)} %select_reduce_fusion.ends, ...), custom_call_target="tpu_custom_call" | custom-call | tf_op jit(solution)/shard_map/pallas_call | solution.py:356
  201.4 4.2 %shard_map.199 = (f32[4,256,256]{2,1,0:T(8,128)S(1)}, f32[4,256,256]{2,1,0:T(8,128)S(1)}, f32[4,256,256]{2,1,0:T(8,128)S(1)}) custom-call(s32[8]{0:T(128)S(1)} %stack.23.info, s32[8]{0:T(128)S(1)} %select_reduce_fusion.ends, f32[8]{0:T(128)S(1)} %copy-done.35, bf16[4,256,256]{2,1,0:T(8,128)(2,1)S(1)} %copy-done.3, bf16[4,256,256]{2,1,0:T(8,128)(2,1)S(1)} %copy-done.8, ...), custom_call_target="tpu_custom_call" | custom-call | tf_op jit(solution)/shard_map/pallas_call | solution.py:356
  205.7 1.5 collective-permute-start.27
  207.9 4.0 %shard_map.198 = (bf16[2,512,256]{2,1,0:T(8,128)(2,1)S(1)}, bf16[2,512,256]{2,1,0:T(8,128)(2,1)}) custom-call(s32[8]{0:T(128)S(1)} %stack.23.info, bf16[1024,256]{1,0:T(8,128)(2,1)S(1)} %bitcast.126, bf16[1024,1024]{1,0:T(8,128)(2,1)S(1)} %bitcast.117, bf16[1024,1024]{1,0:T(8,128)(2,1)S(1)} %bitcast.112, bf16[1024,256]{1,0:T(8,128)(2,1)S(1)} %bitcast.119), custom_call_target="tpu_custom_call" | custom-call | tf_op jit(solution)/shard_map/pallas_call | solution.py:356
  212.9 2.3 collective-permute-done.27
  216.3 7.2 %shard_map.200 = (bf16[4,256,768]{2,1,0:T(8,128)(2,1)S(1)}, bf16[2,256,1024]{2,1,0:T(8,128)(2,1)S(1)}, bf16[2,256,1024]{2,1,0:T(8,128)(2,1)S(1)}) custom-call(s32[8]{0:T(128)S(1)} %stack.23.info, s32[8]{0:T(128)S(1)} %select_reduce_fusion.ends, f32[8]{0:T(128)S(1)} %copy-done.35, f32[4,256,256]{2,1,0:T(8,128)S(1)} %get-tuple-element.147.gq, ...), custom_call_target="tpu_custom_call" | custom-call | tf_op jit(solution)/shard_map/pallas_call | solution.py:356
  228.5 1.5 collective-permute-start.41
  230.0 4.4 %shard_map.201 = (bf16[2,768,256]{2,1,0:T(8,128)(2,1)S(1)}, bf16[2,768,256]{2,1,0:T(8,128)(2,1)}) custom-call(s32[8]{0:T(128)S(1)} %stack.23.info, bf16[1024,1024]{1,0:T(8,128)(2,1)S(1)} %bitcast.113, bf16[1024,768]{1,0:T(8,128)(2,1)S(1)} %bitcast.122), custom_call_target="tpu_custom_call" | custom-call | tf_op jit(solution)/shard_map/pallas_call | solution.py:356
  235.0 15.6 %collective-permute-done.35.got = bf16[256,1024]{1,0:T(8,128)(2,1)S(1)} collective-permute-done((bf16[256,1024]{1,0:T(8,128)(2,1)S(1)}, bf16[256,1024]{1,0:T(8,128)(2,1)S(1)}, u32[]{:S(2)}, u32[]{:S(2)}) %collective-permute-start.35) | collective-permute-done | bytes 524320 | tf_op jit(solution)/shard_map/ppermute | solution.py:21
  252.1 3.6 all-to-all-start.3
  255.7 1.6 add_convert_fusion.6
  257.3 1.4 collective-permute-start.40
  259.9 1.5 collective-permute-start.43
  261.5 8.4 %collective-permute-done.41 = bf16[1408,256]{1,0:T(8,128)(2,1)} collective-permute-done((bf16[1408,256]{1,0:T(8,128)(2,1)}, bf16[1408,256]{1,0:T(8,128)(2,1)}, u32[]{:S(2)}, u32[]{:S(2)}) %collective-permute-start.41) | collective-permute-done | bytes 720928 | tf_op jit(solution)/shard_map/ppermute | solution.py:21
  269.9 2.2 add_convert_fusion.5.p0
  273.1 2.3 collective-permute-start.44
  275.5 1.5 add_convert_fusion.4
  277.8 1.5 collective-permute-start.37
  280.6 2.8 all-to-all-start.2
  283.4 2.2 shard_map.205
  285.6 16.0 %collective-permute-done.45.p2 = bf16[1408,256]{1,0:T(8,128)(2,1)} collective-permute-done((bf16[1408,256]{1,0:T(8,128)(2,1)}, bf16[1408,256]{1,0:T(8,128)(2,1)}, u32[]{:S(2)}, u32[]{:S(2)}) %collective-permute-start.45) | collective-permute-done | bytes 720928 | tf_op jit(solution)/shard_map/ppermute | solution.py:21
  301.6 8.7 %collective-permute-done.44 = bf16[1216,256]{1,0:T(8,128)(2,1)} collective-permute-done((bf16[1216,256]{1,0:T(8,128)(2,1)}, bf16[1216,256]{1,0:T(8,128)(2,1)}, u32[]{:S(2)}, u32[]{:S(2)}) %collective-permute-start.44) | collective-permute-done | bytes 622624 | tf_op jit(solution)/shard_map/ppermute | solution.py:21
  312.3 1.8 fusion.2
  314.1 2.7 collective-permute-start.38
  316.8 16.3 %collective-permute-done.46.p2.d2 = bf16[1216,256]{1,0:T(8,128)(2,1)S(1)} collective-permute-done((bf16[1216,256]{1,0:T(8,128)(2,1)S(1)}, bf16[1216,256]{1,0:T(8,128)(2,1)S(1)}, u32[]{:S(2)}, u32[]{:S(2)}) %collective-permute-start.46) | collective-permute-done | bytes 622624 | tf_op jit(solution)/shard_map/ppermute | solution.py:21
  334.2 6.0 %shard_map.206 = f32[256,5632]{1,0:T(8,128)} custom-call(s32[8]{0:T(128)S(1)} %stack.23.info, bf16[1408,256]{1,0:T(8,128)(2,1)} %add_convert_fusion.5.p0, bf16[1408,256]{1,0:T(8,128)(2,1)} %collective-permute-done.47.p1, bf16[1408,256]{1,0:T(8,128)(2,1)} %collective-permute-done.45.p2, bf16[1408,256]{1,0:T(8,128)(2,1)} %collective-permute-done.48.p3), custom_call_target="tpu_custom_call" | custom-call | tf_op jit(solution)/shard_map/pallas_call | solution.py:356
  341.6 2.7 collective-permute-start.53
  345.0 1.9 collective-permute-start.54
  346.9 3.9 %shard_map.207 = f32[704,1024]{1,0:T(8,128)} custom-call(s32[8]{0:T(128)S(1)} %stack.23.info, bf16[1216,256]{1,0:T(8,128)(2,1)} %copy-done.36, bf16[1216,256]{1,0:T(8,128)(2,1)} %copy-done.37, bf16[1216,256]{1,0:T(8,128)(2,1)} %copy-done.39, bf16[1216,256]{1,0:T(8,128)(2,1)} %copy-done.38), custom_call_target="tpu_custom_call" | custom-call | tf_op jit(solution)/shard_map/pallas_call | solution.py:356
  350.8 2.2 collective-permute-done.50.q2
  353.7 1.7 collective-permute-done.56.q3
  356.1 5.4 %shard_map.208 = (f32[256,1024]{1,0:T(8,128)}, f32[256,1024]{1,0:T(8,128)}, f32[256,1024]{1,0:T(8,128)}, f32[256,1024]{1,0:T(8,128)}, f32[256,1024]{1,0:T(8,128)}) custom-call(s32[8]{0:T(128)S(1)} %stack.23.info, bf16[768,256]{1,0:T(8,128)(2,1)} %copy-done.54, bf16[768,256]{1,0:T(8,128)(2,1)} %copy-done.62, bf16[768,256]{1,0:T(8,128)(2,1)} %copy-done.61, ...), custom_call_target="tpu_custom_call" | custom-call | tf_op jit(solution)/shard_map/pallas_call | solution.py:356
  (276 shorter events, 45.4 us)
Async XLA Ops:
  11.6 54.6 %copy-start.4 = (bf16[4,256,256]{2,1,0:T(8,128)(2,1)}, bf16[4,256,256]{2,1,0:T(8,128)(2,1)S(1)}, u32[]{:S(2)}) copy-start(bf16[4,256,256]{2,1,0:T(8,128)(2,1)S(1)} %get-tuple-element.158.enter) | copy-start | bytes 1572868
  11.6 23.6 %all-to-all-start = ((bf16[32,8,1024]{2,1,0:T(8,128)(2,1)}), bf16[32,8,1024]{2,1,0:T(8,128)(2,1)S(1)}, u32[]{:S(2)}, u32[]{:S(2)}) async-start(bf16[32,8,1024]{2,1,0:T(8,128)(2,1)} %bitcast.6), calls=%async_computation | async-start | bytes 1048576 | tf_op jit(solution)/shard_map/all_to_all | solution.py:1161
  18.9 115.2 %all-gather.3.cloned.1.call-start = ((), (), s32[]{:S(2)}) async-start(), calls=%async_computation.4 | async-start | bytes 5406720 | tf_op jit(solution)/shard_map/all_gather | solution.py:1215
  20.6 34.7 %collective-permute-start.3 = (bf16[1024,256]{1,0:T(8,128)(2,1)S(1)}, bf16[1024,256]{1,0:T(8,128)(2,1)S(1)}, u32[]{:S(2)}, u32[]{:S(2)}) collective-permute-start(bf16[1024,256]{1,0:T(8,128)(2,1)S(1)} %shard_map.188.w0), channel_id=1, source_target_pairs={{0,1},{1,0},{2,3},{3,2},{4,5},{5,4},{6,7},{7,6},{8,9},{9,8},{10,11... | collective-permute-start | bytes 1572872 | tf_op jit(solution)/shard_map/ppermute | solution.py:21
  22.5 36.8 %collective-permute-start.4 = (bf16[1024,256]{1,0:T(8,128)(2,1)S(1)}, bf16[1024,256]{1,0:T(8,128)(2,1)S(1)}, u32[]{:S(2)}, u32[]{:S(2)}) collective-permute-start(bf16[1024,256]{1,0:T(8,128)(2,1)S(1)} %shard_map.188.w0), channel_id=1, source_target_pairs={{0,2},{1,3},{2,0},{3,1},{4,6},{5,7},{6,4},{7,5},{8,10},{9,11},{10,... | collective-permute-start | bytes 1572872 | tf_op jit(solution)/shard_map/ppermute | solution.py:21
  23.9 38.1 %collective-permute-start.5 = (bf16[1024,256]{1,0:T(8,128)(2,1)S(1)}, bf16[1024,256]{1,0:T(8,128)(2,1)S(1)}, u32[]{:S(2)}, u32[]{:S(2)}) collective-permute-start(bf16[1024,256]{1,0:T(8,128)(2,1)S(1)} %shard_map.188.w0), channel_id=1, source_target_pairs={{0,3},{1,2},{2,1},{3,0},{4,7},{5,6},{6,5},{7,4},{8,11},{9,10},{10,... | collective-permute-start | bytes 1572872 | tf_op jit(solution)/shard_map/ppermute | solution.py:21
  35.2 19.9 %collective-permute-start = (bf16[256,1024]{1,0:T(8,128)(2,1)S(1)}, bf16[256,1024]{1,0:T(8,128)(2,1)}, u32[]{:S(2)}, u32[]{:S(2)}) collective-permute-start(bf16[256,1024]{1,0:T(8,128)(2,1)S(1)} %bitcast.128), channel_id=1, source_target_pairs={{0,8},{8,0},{1,9},{9,1},{2,10},{10,2},{3,11},{11,3},{4,12},{12,4},... | collective-permute-start | bytes 1572872 | tf_op jit(solution)/shard_map/ppermute | solution.py:21
  37.1 45.3 %all-to-all-start.1 = ((bf16[32,8,1024]{2,1,0:T(8,128)(2,1)}), bf16[32,8,1024]{2,1,0:T(8,128)(2,1)}, u32[]{:S(2)}, u32[]{:S(2)}) async-start(bf16[32,8,1024]{2,1,0:T(8,128)(2,1)} %bitcast.8), calls=%async_computation.1 | async-start | bytes 1048576 | tf_op jit(solution)/shard_map/all_to_all | solution.py:1161
  40.5 25.6 %collective-permute-start.1 = (bf16[256,1024]{1,0:T(8,128)(2,1)S(1)}, bf16[256,1024]{1,0:T(8,128)(2,1)S(1)}, u32[]{:S(2)}, u32[]{:S(2)}) collective-permute-start(bf16[256,1024]{1,0:T(8,128)(2,1)S(1)} %bitcast.129), channel_id=1, source_target_pairs={{0,4},{4,0},{1,5},{5,1},{2,6},{6,2},{3,7},{7,3},{8,12},{12,8},{9,1... | collective-permute-start | bytes 1572872 | tf_op jit(solution)/shard_map/ppermute | solution.py:21
  55.1 11.0 %collective-permute-start.2 = (bf16[256,1024]{1,0:T(8,128)(2,1)}, bf16[256,1024]{1,0:T(8,128)(2,1)S(1)}, u32[]{:S(2)}, u32[]{:S(2)}) collective-permute-start(bf16[256,1024]{1,0:T(8,128)(2,1)} %collective-permute-done.r1), channel_id=1, source_target_pairs={{0,4},{4,0},{1,5},{5,1},{2,6},{6,2},{3,7},{7,3},{8,12},{12,8},{9,1... | collective-permute-start | bytes 1572872 | tf_op jit(solution)/shard_map/ppermute | solution.py:21
  55.3 36.3 %collective-permute-start.11 = (bf16[256,1024]{1,0:T(8,128)(2,1)}, bf16[256,1024]{1,0:T(8,128)(2,1)}, u32[]{:S(2)}, u32[]{:S(2)}) collective-permute-start(bf16[256,1024]{1,0:T(8,128)(2,1)} %param.21), channel_id=1, source_target_pairs={{0,3},{5,6},{10,9},{15,12},{16,19},{21,22},{26,25},{31,28}} | collective-permute-start | bytes 1572872 | tf_op jit(solution)/shard_map/ppermute | solution.py:554
  59.2 32.3 %collective-permute-start.12 = (bf16[256,1024]{1,0:T(8,128)(2,1)}, bf16[256,1024]{1,0:T(8,128)(2,1)}, u32[]{:S(2)}, u32[]{:S(2)}) collective-permute-start(bf16[256,1024]{1,0:T(8,128)(2,1)} %param.21), channel_id=1, source_target_pairs={{0,2},{5,7},{10,8},{15,13},{16,18},{21,23},{26,24},{31,29}} | collective-permute-start | bytes 1572872 | tf_op jit(solution)/shard_map/ppermute | solution.py:554
  62.0 29.6 %collective-permute-start.13 = (bf16[256,1024]{1,0:T(8,128)(2,1)}, bf16[256,1024]{1,0:T(8,128)(2,1)}, u32[]{:S(2)}, u32[]{:S(2)}) collective-permute-start(bf16[256,1024]{1,0:T(8,128)(2,1)} %param.21), channel_id=1, source_target_pairs={{0,1},{5,4},{10,11},{15,14},{16,17},{21,20},{26,27},{31,30}} | collective-permute-start | bytes 1572872 | tf_op jit(solution)/shard_map/ppermute | solution.py:554
  78.0 4.3 %collective-permute-start.7 = (bf16[2,128,128]{2,1,0:T(8,128)(2,1)S(1)}, bf16[2,128,128]{2,1,0:T(8,128)(2,1)S(1)}, u32[]{:S(2)}, u32[]{:S(2)}) collective-permute-start(bf16[2,128,128]{2,1,0:T(8,128)(2,1)S(1)} %get-tuple-element.106), channel_id=1, source_target_pairs={{0,1},{1,0},{2,3},{3,2},{4,5},{5,4},{6,7},{7,6},{8,9},{9,8},{10,11... | collective-permute-start | bytes 196616 | tf_op jit(solution)/shard_map/ppermute | solution.py:1189
  78.1 5.0 %collective-permute-start.8 = (bf16[2,128,128]{2,1,0:T(8,128)(2,1)S(1)}, bf16[2,128,128]{2,1,0:T(8,128)(2,1)S(1)}, u32[]{:S(2)}, u32[]{:S(2)}) collective-permute-start(bf16[2,128,128]{2,1,0:T(8,128)(2,1)S(1)} %get-tuple-element.106), channel_id=1, source_target_pairs={{0,2},{1,3},{2,0},{3,1},{4,6},{5,7},{6,4},{7,5},{8,10},{9,11},{10,... | collective-permute-start | bytes 196616 | tf_op jit(solution)/shard_map/ppermute | solution.py:1189
  82.3 6.5 %collective-permute-start.9 = (bf16[2,128,128]{2,1,0:T(8,128)(2,1)S(1)}, bf16[2,128,128]{2,1,0:T(8,128)(2,1)S(1)}, u32[]{:S(2)}, u32[]{:S(2)}) collective-permute-start(bf16[2,128,128]{2,1,0:T(8,128)(2,1)S(1)} %get-tuple-element.106), channel_id=1, source_target_pairs={{0,3},{1,2},{2,1},{3,0},{4,7},{5,6},{6,5},{7,4},{8,11},{9,10},{10,... | collective-permute-start | bytes 196616 | tf_op jit(solution)/shard_map/ppermute | solution.py:1189
  83.2 14.3 %collective-permute-start.6 = (bf16[256,1024]{1,0:T(8,128)(2,1)}, bf16[256,1024]{1,0:T(8,128)(2,1)S(1)}, u32[]{:S(2)}, u32[]{:S(2)}) collective-permute-start(bf16[256,1024]{1,0:T(8,128)(2,1)} %bitcast.9.g0), channel_id=1, source_target_pairs={{0,8},{8,0},{1,9},{9,1},{2,10},{10,2},{3,11},{11,3},{4,12},{12,4},... | collective-permute-start | bytes 1572872 | tf_op jit(solution)/shard_map/ppermute | solution.py:21
  89.0 7.8 %collective-permute-start.10 = (f32[2,128,128]{2,1,0:T(8,128)S(1)}, f32[2,128,128]{2,1,0:T(8,128)S(1)}, u32[]{:S(2)}, u32[]{:S(2)}) collective-permute-start(f32[2,128,128]{2,1,0:T(8,128)S(1)} %fusion.12), channel_id=1, source_target_pairs={{0,16},{16,0},{1,17},{17,1},{2,18},{18,2},{3,19},{19,3},{4,20},{20... | collective-permute-start | bytes 393224 | tf_op jit(solution)/shard_map/ppermute | solution.py:21
  102.3 2.7 collective-permute-start.14
  105.3 25.5 %collective-permute-start.15 = (bf16[2,256,1024]{2,1,0:T(8,128)(2,1)S(1)}, bf16[2,256,1024]{2,1,0:T(8,128)(2,1)S(1)}, u32[]{:S(2)}, u32[]{:S(2)}) collective-permute-start(bf16[2,256,1024]{2,1,0:T(8,128)(2,1)S(1)} %add_convert_fusion.3), channel_id=1, source_target_pairs={{0,8},{8,0},{1,9},{9,1},{2,10},{10,2},{3,11},{11,3},{4,12},{12,4},... | collective-permute-start | bytes 3145736 | tf_op jit(solution)/shard_map/ppermute | solution.py:21
  107.3 2.8 collective-permute-start.16
  107.3 2.8 collective-permute-start.17
  131.2 2.9 collective-permute-start.18
  153.3 5.1 %collective-permute-start.21 = (bf16[2,256,1024]{2,1,0:T(8,128)(2,1)S(1)}, bf16[2,256,1024]{2,1,0:T(8,128)(2,1)S(1)}, u32[]{:S(2)}, u32[]{:S(2)}) collective-permute-start(bf16[2,256,1024]{2,1,0:T(8,128)(2,1)S(1)} %get-tuple-element.115), channel_id=1, source_target_pairs={{0,4},{4,0},{1,5},{5,1},{2,6},{6,2},{3,7},{7,3},{8,12},{12,8},{9,1... | collective-permute-start | bytes 3145736 | tf_op jit(solution)/shard_map/ppermute | solution.py:21
  157.1 18.5 %collective-permute-start.23 = (bf16[2,704,256]{2,1,0:T(8,128)(2,1)S(1)}, bf16[2,704,256]{2,1,0:T(8,128)(2,1)S(1)}, u32[]{:S(2)}, u32[]{:S(2)}) collective-permute-start(bf16[2,704,256]{2,1,0:T(8,128)(2,1)S(1)} %get-tuple-element.126), channel_id=1, source_target_pairs={{0,1},{1,0},{2,3},{3,2},{4,5},{5,4},{6,7},{7,6},{8,9},{9,8},{10,11... | collective-permute-start | bytes 2162696 | tf_op jit(solution)/shard_map/ppermute | solution.py:21
  158.8 25.2 %collective-permute-start.22 = (bf16[2,256,1024]{2,1,0:T(8,128)(2,1)S(1)}, bf16[2,256,1024]{2,1,0:T(8,128)(2,1)S(1)}, u32[]{:S(2)}, u32[]{:S(2)}) collective-permute-start(bf16[2,256,1024]{2,1,0:T(8,128)(2,1)S(1)} %add_convert_fusion.1), channel_id=1, source_target_pairs={{0,8},{8,0},{1,9},{9,1},{2,10},{10,2},{3,11},{11,3},{4,12},{12,4},... | collective-permute-start | bytes 3145736 | tf_op jit(solution)/shard_map/ppermute | solution.py:21
  160.7 23.8 %collective-permute-start.20 = (bf16[256,1024]{1,0:T(8,128)(2,1)S(1)}, bf16[256,1024]{1,0:T(8,128)(2,1)S(1)}, u32[]{:S(2)}, u32[]{:S(2)}) collective-permute-start(bf16[256,1024]{1,0:T(8,128)(2,1)S(1)} %get-tuple-element.199), channel_id=1, source_target_pairs={{0,4},{4,0},{1,5},{5,1},{2,6},{6,2},{3,7},{7,3},{8,12},{12,8},{9,1... | collective-permute-start | bytes 1572872 | tf_op jit(solution)/shard_map/ppermute | solution.py:21
  160.8 23.8 %collective-permute-start.19 = (bf16[256,1024]{1,0:T(8,128)(2,1)S(1)}, bf16[256,1024]{1,0:T(8,128)(2,1)S(1)}, u32[]{:S(2)}, u32[]{:S(2)}) collective-permute-start(bf16[256,1024]{1,0:T(8,128)(2,1)S(1)} %get-tuple-element.200), channel_id=1, source_target_pairs={{0,4},{4,0},{1,5},{5,1},{2,6},{6,2},{3,7},{7,3},{8,12},{12,8},{9,1... | collective-permute-start | bytes 1572872 | tf_op jit(solution)/shard_map/ppermute | solution.py:21
  164.8 22.8 %collective-permute-start.25 = (bf16[2,704,256]{2,1,0:T(8,128)(2,1)S(1)}, bf16[2,704,256]{2,1,0:T(8,128)(2,1)S(1)}, u32[]{:S(2)}, u32[]{:S(2)}) collective-permute-start(bf16[2,704,256]{2,1,0:T(8,128)(2,1)S(1)} %get-tuple-element.119), channel_id=1, source_target_pairs={{0,2},{1,3},{2,0},{3,1},{4,6},{5,7},{6,4},{7,5},{8,10},{9,11},{10,... | collective-permute-start | bytes 2162696 | tf_op jit(solution)/shard_map/ppermute | solution.py:21
  184.4 4.3 %collective-permute-start.26 = (bf16[2,256,1024]{2,1,0:T(8,128)(2,1)S(1)}, bf16[2,256,1024]{2,1,0:T(8,128)(2,1)S(1)}, u32[]{:S(2)}, u32[]{:S(2)}) collective-permute-start(bf16[2,256,1024]{2,1,0:T(8,128)(2,1)S(1)} %add_convert_fusion.ua), channel_id=1, source_target_pairs={{0,4},{4,0},{1,5},{5,1},{2,6},{6,2},{3,7},{7,3},{8,12},{12,8},{9,1... | collective-permute-start | bytes 3145736 | tf_op jit(solution)/shard_map/ppermute | solution.py:21
  185.9 21.4 %collective-permute-start.24 = (bf16[256,1024]{1,0:T(8,128)(2,1)S(1)}, bf16[256,1024]{1,0:T(8,128)(2,1)S(1)}, u32[]{:S(2)}, u32[]{:S(2)}) collective-permute-start(bf16[256,1024]{1,0:T(8,128)(2,1)S(1)} %get-tuple-element.129), channel_id=1, source_target_pairs={{0,8},{8,0},{1,9},{9,1},{2,10},{10,2},{3,11},{11,3},{4,12},{12,4},... | collective-permute-start | bytes 1572872 | tf_op jit(solution)/shard_map/ppermute | solution.py:21
  187.9 24.9 %collective-permute-start.31 = (bf16[704,256]{1,0:T(8,128)(2,1)S(1)}, bf16[704,256]{1,0:T(8,128)(2,1)S(1)}, u32[]{:S(2)}, u32[]{:S(2)}) collective-permute-start(bf16[704,256]{1,0:T(8,128)(2,1)S(1)} %slice_bitcast_fusion.10), channel_id=1, source_target_pairs={{0,1},{1,0},{2,3},{3,2},{4,5},{5,4},{6,7},{7,6},{8,9},{9,8},{10,11... | collective-permute-start | bytes 1081352 | tf_op jit(solution)/shard_map/ppermute | solution.py:21
  197.8 7.8 %collective-permute-start.28 = (bf16[2,128,128]{2,1,0:T(8,128)(2,1)S(1)}, bf16[2,128,128]{2,1,0:T(8,128)(2,1)S(1)}, u32[]{:S(2)}, u32[]{:S(2)}) collective-permute-start(bf16[2,128,128]{2,1,0:T(8,128)(2,1)S(1)} %get-tuple-element.135), channel_id=1, source_target_pairs={{0,1},{1,0},{2,3},{3,2},{4,5},{5,4},{6,7},{7,6},{8,9},{9,8},{10,11... | collective-permute-start | bytes 196616 | tf_op jit(solution)/shard_map/ppermute | solution.py:1189
  199.1 8.0 %collective-permute-start.29 = (bf16[2,128,128]{2,1,0:T(8,128)(2,1)S(1)}, bf16[2,128,128]{2,1,0:T(8,128)(2,1)S(1)}, u32[]{:S(2)}, u32[]{:S(2)}) collective-permute-start(bf16[2,128,128]{2,1,0:T(8,128)(2,1)S(1)} %get-tuple-element.135), channel_id=1, source_target_pairs={{0,2},{1,3},{2,0},{3,1},{4,6},{5,7},{6,4},{7,5},{8,10},{9,11},{10,... | collective-permute-start | bytes 196616 | tf_op jit(solution)/shard_map/ppermute | solution.py:1189
  200.1 7.1 %collective-permute-start.30 = (bf16[2,128,128]{2,1,0:T(8,128)(2,1)S(1)}, bf16[2,128,128]{2,1,0:T(8,128)(2,1)S(1)}, u32[]{:S(2)}, u32[]{:S(2)}) collective-permute-start(bf16[2,128,128]{2,1,0:T(8,128)(2,1)S(1)} %get-tuple-element.135), channel_id=1, source_target_pairs={{0,3},{1,2},{2,1},{3,0},{4,7},{5,6},{6,5},{7,4},{8,11},{9,10},{10,... | collective-permute-start | bytes 196616 | tf_op jit(solution)/shard_map/ppermute | solution.py:1189
  205.7 9.5 %collective-permute-start.27 = (bf16[704,256]{1,0:T(8,128)(2,1)S(1)}, bf16[704,256]{1,0:T(8,128)(2,1)S(1)}, u32[]{:S(2)}, u32[]{:S(2)}) collective-permute-start(bf16[704,256]{1,0:T(8,128)(2,1)S(1)} %slice_bitcast_fusion.11), channel_id=1, source_target_pairs={{0,2},{1,3},{2,0},{3,1},{4,6},{5,7},{6,4},{7,5},{8,10},{9,11},{10,... | collective-permute-start | bytes 1081352 | tf_op jit(solution)/shard_map/ppermute | solution.py:21
  207.3 8.9 %collective-permute-start.32 = (f32[2,128,128]{2,1,0:T(8,128)S(1)}, f32[2,128,128]{2,1,0:T(8,128)S(1)}, u32[]{:S(2)}, u32[]{:S(2)}) collective-permute-start(f32[2,128,128]{2,1,0:T(8,128)S(1)} %fusion.15), channel_id=1, source_target_pairs={{0,16},{16,0},{1,17},{17,1},{2,18},{18,2},{3,19},{19,3},{4,20},{20... | collective-permute-start | bytes 393224 | tf_op jit(solution)/shard_map/ppermute | solution.py:21
  223.6 2.0 collective-permute-start.34
  223.7 2.6 collective-permute-start.33
  224.2 31.5 %collective-permute-start.39 = (bf16[2,704,256]{2,1,0:T(8,128)(2,1)}, bf16[2,704,256]{2,1,0:T(8,128)(2,1)}, u32[]{:S(2)}, u32[]{:S(2)}) collective-permute-start(bf16[2,704,256]{2,1,0:T(8,128)(2,1)} %get-tuple-element.162), channel_id=1, source_target_pairs={{0,1},{1,0},{2,3},{3,2},{4,5},{5,4},{6,7},{7,6},{8,9},{9,8},{10,11... | collective-permute-start | bytes 2162696 | tf_op jit(solution)/shard_map/ppermute | solution.py:21
  226.7 23.9 %collective-permute-start.35 = (bf16[256,1024]{1,0:T(8,128)(2,1)S(1)}, bf16[256,1024]{1,0:T(8,128)(2,1)S(1)}, u32[]{:S(2)}, u32[]{:S(2)}) collective-permute-start(bf16[256,1024]{1,0:T(8,128)(2,1)S(1)} %get-tuple-element.193), channel_id=1, source_target_pairs={{0,8},{8,0},{1,9},{9,1},{2,10},{10,2},{3,11},{11,3},{4,12},{12,4},... | collective-permute-start | bytes 1572872 | tf_op jit(solution)/shard_map/ppermute | solution.py:21
  227.2 31.5 %collective-permute-start.42 = (bf16[2,512,256]{2,1,0:T(8,128)(2,1)}, bf16[2,512,256]{2,1,0:T(8,128)(2,1)}, u32[]{:S(2)}, u32[]{:S(2)}) collective-permute-start(bf16[2,512,256]{2,1,0:T(8,128)(2,1)} %get-tuple-element.142), channel_id=1, source_target_pairs={{0,2},{1,3},{2,0},{3,1},{4,6},{5,7},{6,4},{7,5},{8,10},{9,11},{10,... | collective-permute-start | bytes 1572872 | tf_op jit(solution)/shard_map/ppermute | solution.py:21
  228.5 41.4 %collective-permute-start.41 = (bf16[1408,256]{1,0:T(8,128)(2,1)}, bf16[1408,256]{1,0:T(8,128)(2,1)}, u32[]{:S(2)}, u32[]{:S(2)}) collective-permute-start(bf16[1408,256]{1,0:T(8,128)(2,1)} %pad_maximum_fusion), channel_id=1, source_target_pairs={{0,16},{16,0},{1,17},{17,1},{2,18},{18,2},{3,19},{19,3},{4,20},{20... | collective-permute-start | bytes 2162696 | tf_op jit(solution)/shard_map/ppermute | solution.py:21
  234.3 41.1 %collective-permute-start.36 = (bf16[2,768,256]{2,1,0:T(8,128)(2,1)}, bf16[2,768,256]{2,1,0:T(8,128)(2,1)}, u32[]{:S(2)}, u32[]{:S(2)}) collective-permute-start(bf16[2,768,256]{2,1,0:T(8,128)(2,1)} %get-tuple-element.156), channel_id=1, source_target_pairs={{0,1},{1,0},{2,3},{3,2},{4,5},{5,4},{6,7},{7,6},{8,9},{9,8},{10,11... | collective-permute-start | bytes 2359304 | tf_op jit(solution)/shard_map/ppermute | solution.py:21
  252.1 28.5 %all-to-all-start.3 = ((bf16[32,8,1024]{2,1,0:T(8,128)(2,1)}), bf16[32,8,1024]{2,1,0:T(8,128)(2,1)}, u32[]{:S(2)}, u32[]{:S(2)}) async-start(bf16[32,8,1024]{2,1,0:T(8,128)(2,1)} %bitcast.120), calls=%async_computation.3 | async-start | bytes 1048576 | tf_op jit(solution)/shard_map/all_to_all | solution.py:1161
  257.3 14.8 %collective-permute-start.40 = (bf16[704,256]{1,0:T(8,128)(2,1)S(1)}, bf16[704,256]{1,0:T(8,128)(2,1)S(1)}, u32[]{:S(2)}, u32[]{:S(2)}) collective-permute-start(bf16[704,256]{1,0:T(8,128)(2,1)S(1)} %slice_bitcast_fusion.6), channel_id=1, source_target_pairs={{0,2},{1,3},{2,0},{3,1},{4,6},{5,7},{6,4},{7,5},{8,10},{9,11},{10,... | collective-permute-start | bytes 1081352 | tf_op jit(solution)/shard_map/ppermute | solution.py:21
  259.9 12.1 %collective-permute-start.43 = (bf16[512,256]{1,0:T(8,128)(2,1)S(1)}, bf16[512,256]{1,0:T(8,128)(2,1)S(1)}, u32[]{:S(2)}, u32[]{:S(2)}) collective-permute-start(bf16[512,256]{1,0:T(8,128)(2,1)S(1)} %slice_bitcast_fusion.13), channel_id=1, source_target_pairs={{0,1},{1,0},{2,3},{3,2},{4,5},{5,4},{6,7},{7,6},{8,9},{9,8},{10,11... | collective-permute-start | bytes 786440 | tf_op jit(solution)/shard_map/ppermute | solution.py:21
  272.1 29.6 %collective-permute-start.45 = (bf16[1408,256]{1,0:T(8,128)(2,1)}, bf16[1408,256]{1,0:T(8,128)(2,1)}, u32[]{:S(2)}, u32[]{:S(2)}) collective-permute-start(bf16[1408,256]{1,0:T(8,128)(2,1)} %add_convert_fusion.5.p0), channel_id=1, source_target_pairs={{0,8},{8,0},{1,9},{9,1},{2,10},{10,2},{3,11},{11,3},{4,12},{12,4},... | collective-permute-start | bytes 2162696 | tf_op jit(solution)/shard_map/ppermute | solution.py:21
  273.1 37.2 %collective-permute-start.44 = (bf16[1216,256]{1,0:T(8,128)(2,1)}, bf16[1216,256]{1,0:T(8,128)(2,1)}, u32[]{:S(2)}, u32[]{:S(2)}) collective-permute-start(bf16[1216,256]{1,0:T(8,128)(2,1)} %pad_maximum_fusion.1), channel_id=1, source_target_pairs={{0,16},{16,0},{1,17},{17,1},{2,18},{18,2},{3,19},{19,3},{4,20},{20... | collective-permute-start | bytes 1867784 | tf_op jit(solution)/shard_map/ppermute | solution.py:21
  277.8 34.5 %collective-permute-start.37 = (bf16[768,256]{1,0:T(8,128)(2,1)}, bf16[768,256]{1,0:T(8,128)(2,1)}, u32[]{:S(2)}, u32[]{:S(2)}) collective-permute-start(bf16[768,256]{1,0:T(8,128)(2,1)} %slice_bitcast_fusion.4), channel_id=1, source_target_pairs={{0,2},{1,3},{2,0},{3,1},{4,6},{5,7},{6,4},{7,5},{8,10},{9,11},{10,... | collective-permute-start | bytes 1179656 | tf_op jit(solution)/shard_map/ppermute | solution.py:21
  280.6 52.5 %all-to-all-start.2 = ((bf16[32,8,1024]{2,1,0:T(8,128)(2,1)}), bf16[32,8,1024]{2,1,0:T(8,128)(2,1)S(1)}, u32[]{:S(2)}, u32[]{:S(2)}) async-start(bf16[32,8,1024]{2,1,0:T(8,128)(2,1)} %bitcast.121), calls=%async_computation.2 | async-start | bytes 1048576 | tf_op jit(solution)/shard_map/all_to_all | solution.py:1161
  311.6 32.7 %copy-start.36 = (bf16[1216,256]{1,0:T(8,128)(2,1)}, bf16[1216,256]{1,0:T(8,128)(2,1)S(1)}, u32[]{:S(2)}) copy-start(bf16[1216,256]{1,0:T(8,128)(2,1)S(1)} %add_convert_fusion.9.p0.d0) | copy-start | bytes 1867780
  311.6 21.5 %collective-permute-start.46 = (bf16[1216,256]{1,0:T(8,128)(2,1)S(1)}, bf16[1216,256]{1,0:T(8,128)(2,1)S(1)}, u32[]{:S(2)}, u32[]{:S(2)}) collective-permute-start(bf16[1216,256]{1,0:T(8,128)(2,1)S(1)} %add_convert_fusion.9.p0.d0), channel_id=1, source_target_pairs={{0,8},{8,0},{1,9},{9,1},{2,10},{10,2},{3,11},{11,3},{4,12},{12,4},... | collective-permute-start | bytes 1867784 | tf_op jit(solution)/shard_map/ppermute | solution.py:21
  311.7 22.6 %collective-permute-start.47 = (bf16[1408,256]{1,0:T(8,128)(2,1)}, bf16[1408,256]{1,0:T(8,128)(2,1)}, u32[]{:S(2)}, u32[]{:S(2)}) collective-permute-start(bf16[1408,256]{1,0:T(8,128)(2,1)} %add_convert_fusion.5.p0), channel_id=1, source_target_pairs={{0,4},{4,0},{1,5},{5,1},{2,6},{6,2},{3,7},{7,3},{8,12},{12,8},{9,1... | collective-permute-start | bytes 2162696 | tf_op jit(solution)/shard_map/ppermute | solution.py:21
  311.8 22.5 %collective-permute-start.48 = (bf16[1408,256]{1,0:T(8,128)(2,1)}, bf16[1408,256]{1,0:T(8,128)(2,1)}, u32[]{:S(2)}, u32[]{:S(2)}) collective-permute-start(bf16[1408,256]{1,0:T(8,128)(2,1)} %collective-permute-done.45.p2), channel_id=1, source_target_pairs={{0,4},{4,0},{1,5},{5,1},{2,6},{6,2},{3,7},{7,3},{8,12},{12,8},{9,1... | collective-permute-start | bytes 2162696 | tf_op jit(solution)/shard_map/ppermute | solution.py:21
  314.1 26.1 %collective-permute-start.38 = (bf16[768,256]{1,0:T(8,128)(2,1)}, bf16[768,256]{1,0:T(8,128)(2,1)}, u32[]{:S(2)}, u32[]{:S(2)}) collective-permute-start(bf16[768,256]{1,0:T(8,128)(2,1)} %fusion.2), channel_id=1, source_target_pairs={{0,16},{16,0},{1,17},{17,1},{2,18},{18,2},{3,19},{19,3},{4,20},{20... | collective-permute-start | bytes 1179656 | tf_op jit(solution)/shard_map/ppermute | solution.py:21
  316.8 24.7 %collective-permute-start.51 = (bf16[1216,256]{1,0:T(8,128)(2,1)S(1)}, bf16[1216,256]{1,0:T(8,128)(2,1)S(1)}, u32[]{:S(2)}, u32[]{:S(2)}) collective-permute-start(bf16[1216,256]{1,0:T(8,128)(2,1)S(1)} %add_convert_fusion.9.p0.d0), channel_id=1, source_target_pairs={{0,4},{4,0},{1,5},{5,1},{2,6},{6,2},{3,7},{7,3},{8,12},{12,8},{9,1... | collective-permute-start | bytes 1867784 | tf_op jit(solution)/shard_map/ppermute | solution.py:21
  333.1 8.4 %collective-permute-start.52 = (bf16[1216,256]{1,0:T(8,128)(2,1)S(1)}, bf16[1216,256]{1,0:T(8,128)(2,1)S(1)}, u32[]{:S(2)}, u32[]{:S(2)}) collective-permute-start(bf16[1216,256]{1,0:T(8,128)(2,1)S(1)} %collective-permute-done.46.p2.d2), channel_id=1, source_target_pairs={{0,4},{4,0},{1,5},{5,1},{2,6},{6,2},{3,7},{7,3},{8,12},{12,8},{9,1... | collective-permute-start | bytes 1867784 | tf_op jit(solution)/shard_map/ppermute | solution.py:21
  341.4 11.6 %collective-permute-start.50 = (bf16[768,256]{1,0:T(8,128)(2,1)S(1)}, bf16[768,256]{1,0:T(8,128)(2,1)S(1)}, u32[]{:S(2)}, u32[]{:S(2)}) collective-permute-start(bf16[768,256]{1,0:T(8,128)(2,1)S(1)} %add_convert_fusion.11.q0), channel_id=1, source_target_pairs={{0,8},{8,0},{1,9},{9,1},{2,10},{10,2},{3,11},{11,3},{4,12},{12,4},... | collective-permute-start | bytes 1179656 | tf_op jit(solution)/shard_map/ppermute | solution.py:21
  341.6 11.4 %collective-permute-start.53 = (bf16[256,256]{1,0:T(8,128)(2,1)S(1)}, bf16[256,256]{1,0:T(8,128)(2,1)S(1)}, u32[]{:S(2)}, u32[]{:S(2)}) collective-permute-start(bf16[256,256]{1,0:T(8,128)(2,1)S(1)} %get-tuple-element.192), channel_id=1, source_target_pairs={{0,1},{1,0},{2,3},{3,2},{4,5},{5,4},{6,7},{7,6},{8,9},{9,8},{10,11... | collective-permute-start | bytes 393224 | tf_op jit(solution)/shard_map/ppermute | solution.py:21
  345.0 8.6 %collective-permute-start.54 = (bf16[256,256]{1,0:T(8,128)(2,1)S(1)}, bf16[256,256]{1,0:T(8,128)(2,1)S(1)}, u32[]{:S(2)}, u32[]{:S(2)}) collective-permute-start(bf16[256,256]{1,0:T(8,128)(2,1)S(1)} %get-tuple-element.190), channel_id=1, source_target_pairs={{0,2},{1,3},{2,0},{3,1},{4,6},{5,7},{6,4},{7,5},{8,10},{9,11},{10,... | collective-permute-start | bytes 393224 | tf_op jit(solution)/shard_map/ppermute | solution.py:21
  346.9 6.7 %collective-permute-start.55 = (bf16[256,256]{1,0:T(8,128)(2,1)S(1)}, bf16[256,256]{1,0:T(8,128)(2,1)S(1)}, u32[]{:S(2)}, u32[]{:S(2)}) collective-permute-start(bf16[256,256]{1,0:T(8,128)(2,1)S(1)} %get-tuple-element.191), channel_id=1, source_target_pairs={{0,3},{1,2},{2,1},{3,0},{4,7},{5,6},{6,5},{7,4},{8,11},{9,10},{10,... | collective-permute-start | bytes 393224 | tf_op jit(solution)/shard_map/ppermute | solution.py:21
  346.9 6.8 %collective-permute-start.49 = (bf16[768,256]{1,0:T(8,128)(2,1)S(1)}, bf16[768,256]{1,0:T(8,128)(2,1)S(1)}, u32[]{:S(2)}, u32[]{:S(2)}) collective-permute-start(bf16[768,256]{1,0:T(8,128)(2,1)S(1)} %add_convert_fusion.11.q0), channel_id=1, source_target_pairs={{0,4},{4,0},{1,5},{5,1},{2,6},{6,2},{3,7},{7,3},{8,12},{12,8},{9,1... | collective-permute-start | bytes 1179656 | tf_op jit(solution)/shard_map/ppermute | solution.py:21
  353.6 1.8 collective-permute-start.56
  (66 other events, 526.9 us)
Sparse Core Ops, SparseCore 0:
  35.3 72.5 all-gather.2

commit v4 on v3

--- a/solution.py
+++ b/solution.py
@@ -718,8 +718,29 @@
     )
 
 
-def sglu_kernel(info, enter, x, ta, tb, g0, g1, g2, g3, w,
-                g, n2, product, gg, gu, r_keep, r_give, n_keep, n_give, wd, scr, back):
+def order_kernel(enter, g0, g1, g2, g3, g):
+    i = pl.program_id(0)
+    for t, raw in enumerate((g0, g1, g2, g3)):
+
+        @pl.when(i == t)
+        def _():
+            g[0] = dot(enter[0], raw[...]).astype(BF)
+
+
+def order(enter, raws):
+    return run(
+        order_kernel,
+        sds((TEAM, ROWS, WIDTH)),
+        (),
+        (enter, *raws),
+        grid=(TEAM,),
+        in_specs=[BY_I, *[full(ROWS, WIDTH)] * 4],
+        out_specs=BY_I_WIDE,
+    )
+
+
+def sglu_kernel(info, x, ta, tb, g, w,
+                n2, product, gg, gu, r_keep, r_give, n_keep, n_give, wd, scr, back):
     i = pl.program_id(0)
     pieces = [w.at[p] for p in range(N_SHARD)]
 
@@ -729,12 +750,6 @@
             for c in range(4):
                 at = 2 * FF_OWN + c * FF_PART
                 wd[p * FF_PART : (p + 1) * FF_PART, c * 256 : (c + 1) * 256] = w[p, at : at + FF_PART]
-
-    for t, raw in enumerate((g0, g1, g2, g3)):
-
-        @pl.when(i == t)
-        def _():
-            g[0] = dot(enter[0], raw[...]).astype(BF)
 
     att = jnp.where(i < 2, ta[0].astype(F32), tb[0].astype(F32))
     scr[...] = rms(x[0].astype(F32) + att).astype(BF)
@@ -755,26 +770,19 @@
     halves(i, dot(prod, wd[...]).astype(BF), r_keep, r_give)
 
 
-def sglu(info, enter, x, ta, tb, raws, w_ff):
+def sglu(info, x, ta, tb, g, w_ff):
     hid = pl.BlockSpec((1, ROWS, FF_OWN), lambda i, *_: (i, 0, 0))
     hid_out = sds((TEAM, ROWS, FF_OWN))
-    wide = sds((TEAM, ROWS, WIDTH))
     return run(
         sglu_kernel,
-        (wide, wide, hid_out, hid_out, hid_out, PAIR, PAIR, PAIR, PAIR),
+        (sds((TEAM, ROWS, WIDTH)), hid_out, hid_out, hid_out, PAIR, PAIR, PAIR, PAIR),
         (info,),
-        (enter, x, ta, tb, *raws, w_ff),
+        (x, ta, tb, g, w_ff),
         grid=(TEAM,),
-        in_specs=[BY_I, BY_I_WIDE, KEEP, GIVE, *[full(ROWS, WIDTH)] * 4, full(*w_ff.shape)],
-        out_specs=[BY_I_WIDE, BY_I_WIDE, hid, hid, hid, KEEP, GIVE, KEEP, GIVE],
-        scratch=[
-            pltpu.VMEM((FF_OWN, WIDTH), BF),
-            pltpu.VMEM((ROWS, WIDTH), BF),
-            pltpu.VMEM((ROWS, WIDTH), BF),
-        ],
-        mib=34,
-        flops=12 << 30,
-        nbytes=28 << 20,
+        in_specs=[BY_I_WIDE, KEEP, GIVE, BY_I_WIDE, full(*w_ff.shape)],
+        out_specs=[BY_I_WIDE, hid, hid, hid, KEEP, GIVE, KEEP, GIVE],
+        scratch=[pltpu.VMEM((FF_OWN, WIDTH), BF), pltpu.VMEM((ROWS, WIDTH), BF), pltpu.VMEM((ROWS, WIDTH), BF)],
+        mib=30,
     )
 
 
@@ -1241,8 +1249,9 @@
     s_in, _ = state_in(state, f_near, f_whole, f_cross)
     local = attend_local(scal, q, k, v)
     mixed, gated, a_keep, a_give = carry_in((after(info, g_raws[1]), *scal[1:]), local, q, pu, kv, s_in, wo)
-    ta, tb, _ = team_sum(a_keep, a_give, hold=(g_raws[2], g_raws[3]))
-    g, n2, product, gg, gu, r_keep, r_give, n_keep, n_give = sglu(info, *far(enter), x, ta, *far(tb), far(*g_raws), *far(w_ff))
+    g = order(*far(enter), far(*g_raws))
+    ta, tb, _ = team_sum(a_keep, a_give, hold=(g,))
+    n2, product, gg, gu, r_keep, r_give, n_keep, n_give = sglu(info, x, ta, *far(tb, g), *far(w_ff))
     n_got = send(n_give, "core", 1)
     d_gate = hidden_grads(info, n2, gg, 1)
     n_half = (n_keep.astype(F32) + n_got.astype(F32)).astype(BF)
@@ -1278,12 +1287,12 @@
     ou_own, ou_other = hop(d_ou, 2, hold=(down_other,))
     fin_sum = over_zh(fin, hold=(ou_other,))
     fin_pair = send(fin_sum, "zl", 1)
+    fin_all = [fin_sum, send(fin_sum, "core", 1), fin_pair, send(fin_pair, "core", 1)]
     down_ou = joined((hop_two(down_own, down_other, 1), hop_two(ou_own, ou_other, 2)), hold=(fin_sum,))
     qkv_own, qkv_other = hop(d_qkv, 1, hold=(last_sent,))
     qkv = joined((hop_two(qkv_own, qkv_other, 1),))
     down_sum = over_zh(down_ou, hold=(fin_pair, input_grad))
     down_pair = send(down_sum, "zl", 1)
-    fin_all = [fin_sum, send(fin_sum, "core", 1), fin_pair, send(fin_pair, "core", 1)]
     down_all = [down_sum, send(down_sum, "core", 1), down_pair, send(down_pair, "core", 1)]
     grad_fin = fin_out(info, far(*fin_all))
     grad_down = down_out(info, far(*down_all))
@@ -1293,9 +1302,9 @@
         top = [p[FF_OWN : FF_OWN + 256] for p in down_all]
         piece = jnp.where(pick < 2, jnp.where(pick == 0, top[0], top[1]), jnp.where(pick == 2, top[2], top[3]))
         outs.append(piece if j == 0 else send(piece, "shard", j))
-    qkv_sum = over_zh(qkv, hold=(down_pair, output, grad_fin))
+    qkv_sum = over_zh(qkv, hold=(down_pair, output, fin_all[3]))
     qkv_pair = send(qkv_sum, "zl", 1)
-    qkv_late = after(qkv_pair, grad_down, *outs[1:])
+    qkv_late = after(qkv_pair, grad_fin, grad_down, *outs[1:])
     qkv_all = [qkv_sum, send(qkv_sum, "core", 1), qkv_late, send(qkv_late, "core", 1)]
     grad_q, grad_k, grad_v, grad_u, grad_out = last_out(info, far(*qkv_all, *down_all, *outs))
     return (output, input_grad, grad_q, grad_k, grad_v, grad_u, grad_out, grad_fin, grad_down)

time: 370 us -> 368 us (level)
  waiting for transfers between devices: 145 us -> 136 us
    ppermute x48, waiting for transfers between devices: 130 us -> 122 us  [send(): return lax.ppermute(value, axis, [(i, i ^ mask) for i in range(size)])]
    pallas_call x22 -> x23, Pallas kernels: 105 us -> 106 us  [run(): pl.pallas_call(kernel, out_shape=out, grid_spec=pltpu.PrefetchScalarGridS...]
    unnamed x136 -> x156, local copies, waits for them, and re-layouts: 8.54 us -> 9.87 us
  transfers between devices with their start and end apart: 62 -> 62, of which waited for: 25 -> 22; matrix products, arithmetic and copies ran while one was open for 6% -> 7% of each run, Pallas kernels for 19% -> 20%
where the time goes in v4:
time: 368 us; the launch traced here: 366 us
  waiting for transfers between devices  136 us (37%)
  Pallas kernels  106 us (29%)
  starting transfers between devices  70.7 us (19%)
  other arithmetic  23.3 us (6%)
  between operations  16.6 us (5%)
  local copies, waits for them, and re-layouts  13.1 us (4%)
    ppermute x48, waiting for transfers between devices, send(): return lax.ppermute(value, axis, [(i, i ^ mask) for i in range(size)])  122 us
    pallas_call x23, Pallas kernels, run(): pl.pallas_call(kernel, out_shape=out, grid_spec=pltpu.PrefetchScalarGridS...  106 us
    ppermute x48, starting transfers between devices, send(): return lax.ppermute(value, axis, [(i, i ^ mask) for i in range(size)])  41 us
    all_to_all x4, starting transfers between devices, exchange(): return lax.all_to_all(rows, ALL, split_axis=0, concat_axis=0, tiled=True)  17.1 us
    unnamed x156, local copies, waits for them, and re-layouts  9.87 us
    ppermute x6, waiting for transfers between devices, state_in(): lax.ppermute(state, 'shard', [(i, i ^ j) for i in range(4)])  9.07 us
    ppermute x3, starting transfers between devices, gather_out(): wo = jnp.where(rel == j, lax.ppermute(w_out, axes, pairs), wo)  8.9 us
  transfers between devices with their start and end apart: 62, of which 22 were waited for; matrix products, arithmetic and copies ran while one was open for 7% of the time, Pallas kernels for 20%

profile of v4, /device:TPU:0, one launch (start us, length us, event | category | flops | bytes accessed | tf_op | source)
XLA Modules:
  0.0 365.7 jit_solution(7393773041386619981)
XLA Ops:
  8.1 3.5 shard_map.187
  11.6 7.4 %all-to-all-start = ((bf16[32,8,1024]{2,1,0:T(8,128)(2,1)}), bf16[32,8,1024]{2,1,0:T(8,128)(2,1)}, u32[]{:S(2)}, u32[]{:S(2)}) async-start(bf16[32,8,1024]{2,1,0:T(8,128)(2,1)} %bitcast.6), calls=%async_computation | async-start | bytes 1048576 | tf_op jit(solution)/shard_map/all_to_all | solution.py:1169
  19.1 1.7 shard_map.188.w0
  20.8 1.8 collective-permute-start.3
  22.5 1.5 collective-permute-start.4
  25.7 4.8 %shard_map.193 = bf16[2112,256]{1,0:T(8,128)(2,1)} custom-call(s32[8]{0:T(128)S(1)} %stack.23.info, bf16[256,5632]{1,0:T(8,128)(2,1)} %fin.1, bf16[704,1024]{1,0:T(8,128)(2,1)} %down.1), custom_call_target="tpu_custom_call" | custom-call | tf_op jit(solution)/shard_map/pallas_call | solution.py:356
  30.7 4.5 %all-to-all-done = bf16[32,8,1024]{2,1,0:T(8,128)(2,1)} async-done(((bf16[32,8,1024]{2,1,0:T(8,128)(2,1)}), bf16[32,8,1024]{2,1,0:T(8,128)(2,1)}, u32[]{:S(2)}, u32[]{:S(2)}) %all-to-all-start) | async-done | bytes 524320 | tf_op jit(solution)/shard_map/all_to_all | solution.py:1169
  37.2 3.4 all-to-all-start.1
  40.7 14.4 %collective-permute-done.r1 = bf16[256,1024]{1,0:T(8,128)(2,1)S(1)} collective-permute-done((bf16[256,1024]{1,0:T(8,128)(2,1)}, bf16[256,1024]{1,0:T(8,128)(2,1)S(1)}, u32[]{:S(2)}, u32[]{:S(2)}) %collective-permute-start) | collective-permute-done | bytes 524320 | tf_op jit(solution)/shard_map/ppermute | solution.py:21
  57.2 4.1 %collective-permute-start.11 = (bf16[256,1024]{1,0:T(8,128)(2,1)}, bf16[256,1024]{1,0:T(8,128)(2,1)}, u32[]{:S(2)}, u32[]{:S(2)}) collective-permute-start(bf16[256,1024]{1,0:T(8,128)(2,1)} %param.21), channel_id=1, source_target_pairs={{0,3},{5,6},{10,9},{15,12},{16,19},{21,22},{26,25},{31,28}} | collective-permute-start | bytes 1572872 | tf_op jit(solution)/shard_map/ppermute | solution.py:554
  61.3 2.1 collective-permute-start.12
  63.4 2.6 collective-permute-start.13
  67.1 10.1 %shard_map.189 = (bf16[4,256,1024]{2,1,0:T(8,128)(2,1)}, bf16[4,256,1024]{2,1,0:T(8,128)(2,1)}, f32[4,256,256]{2,1,0:T(8,128)}, f32[4,256,256]{2,1,0:T(8,128)}, ...) custom-call(s32[8]{0:T(128)S(1)} %stack.23.info, ...), custom_call_target="tpu_custom_call" | custom-call | tf_op jit(solution)/shard_map/pallas_call | solution.py:356
  78.9 3.9 %collective-permute-done.7 = bf16[2,128,128]{2,1,0:T(8,128)(2,1)S(1)} collective-permute-done((bf16[2,128,128]{2,1,0:T(8,128)(2,1)S(1)}, bf16[2,128,128]{2,1,0:T(8,128)(2,1)S(1)}, u32[]{:S(2)}, u32[]{:S(2)}) %collective-permute-start.7) | collective-permute-done | bytes 65568 | tf_op jit(solution)/shard_map/ppermute | solution.py:1197
  85.0 4.3 %collective-permute-done.9 = bf16[2,128,128]{2,1,0:T(8,128)(2,1)S(1)} collective-permute-done((bf16[2,128,128]{2,1,0:T(8,128)(2,1)S(1)}, bf16[2,128,128]{2,1,0:T(8,128)(2,1)S(1)}, u32[]{:S(2)}, u32[]{:S(2)}) %collective-permute-start.9) | collective-permute-done | bytes 65568 | tf_op jit(solution)/shard_map/ppermute | solution.py:1197
  90.1 2.3 collective-permute-start.10
  93.7 2.8 shard_map.190.local
  98.5 3.7 %shard_map.191 = (f32[4,256,256]{2,1,0:T(8,128)S(1)}, bf16[4,256,256]{2,1,0:T(8,128)(2,1)S(1)}, bf16[2,256,1024]{2,1,0:T(8,128)(2,1)S(1)}, bf16[2,256,1024]{2,1,0:T(8,128)(2,1)S(1)}) custom-call(s32[8]{0:T(128)S(1)} %stack.23.info, s32[8]{0:T(128)S(1)} %select_reduce_fusion.ends, f32[8]{0:T(128)S(1)} %copy-done.38, f32[4,256,256]{2,1,0:T(8,128)S(1)} %shard_map.190.local, ...), custom_call_target="tpu_custom_call" | custom-call | tf_op jit(solution)/shard_map/pallas_call | solution.py:356
  103.1 2.7 collective-permute-done.14
  106.2 2.0 collective-permute-start.15
  108.7 2.3 collective-permute-done.16.g2
  112.6 3.5 shard_map.192.g
  117.5 14.2 %collective-permute-done.15 = bf16[2,256,1024]{2,1,0:T(8,128)(2,1)S(1)} collective-permute-done((bf16[2,256,1024]{2,1,0:T(8,128)(2,1)S(1)}, bf16[2,256,1024]{2,1,0:T(8,128)(2,1)S(1)}, u32[]{:S(2)}, u32[]{:S(2)}) %collective-permute-start.15) | collective-permute-done | bytes 1048608 | tf_op jit(solution)/shard_map/ppermute | solution.py:21
  132.1 2.8 collective-permute-done.18.tb
  134.9 17.4 %shard_map.194 = (bf16[4,256,1024]{2,1,0:T(8,128)(2,1)S(1)}, bf16[4,256,704]{2,1,0:T(8,128)(2,1)S(1)}, bf16[4,256,704]{2,1,0:T(8,128)(2,1)S(1)}, bf16[4,256,704]...) custom-call(s32[8]{0:T(128)S(1)} %stack.23.info, ...), custom_call_target="tpu_custom_call" | custom-call | tf_op jit(solution)/shard_map/pallas_call | solution.py:356
  152.6 3.5 shard_map.197
  156.1 1.5 collective-permute-start.23
  158.0 1.8 collective-permute-start.22
  160.5 3.5 shard_map.195
  165.0 3.8 %shard_map.196 = (bf16[2,704,256]{2,1,0:T(8,128)(2,1)S(1)}, bf16[2,704,256]{2,1,0:T(8,128)(2,1)}) custom-call(s32[8]{0:T(128)S(1)} %stack.23.info, bf16[1024,1024]{1,0:T(8,128)(2,1)S(1)} %bitcast.112, bf16[1024,704]{1,0:T(8,128)(2,1)S(1)} %bitcast.123), custom_call_target="tpu_custom_call" | custom-call | tf_op jit(solution)/shard_map/pallas_call | solution.py:356
  168.9 5.7 %collective-permute-done.23 = bf16[2,704,256]{2,1,0:T(8,128)(2,1)S(1)} collective-permute-done((bf16[2,704,256]{2,1,0:T(8,128)(2,1)S(1)}, bf16[2,704,256]{2,1,0:T(8,128)(2,1)S(1)}, u32[]{:S(2)}, u32[]{:S(2)}) %collective-permute-start.23) | collective-permute-done | bytes 720928 | tf_op jit(solution)/shard_map/ppermute | solution.py:21
  174.8 8.4 %collective-permute-done.22 = bf16[2,256,1024]{2,1,0:T(8,128)(2,1)S(1)} collective-permute-done((bf16[2,256,1024]{2,1,0:T(8,128)(2,1)S(1)}, bf16[2,256,1024]{2,1,0:T(8,128)(2,1)S(1)}, u32[]{:S(2)}, u32[]{:S(2)}) %collective-permute-start.22) | collective-permute-done | bytes 1048608 | tf_op jit(solution)/shard_map/ppermute | solution.py:21
  185.1 1.7 collective-permute-start.24
  188.8 8.1 %shard_map.198 = (bf16[4,256,1024]{2,1,0:T(8,128)(2,1)S(1)}, bf16[4,256,256]{2,1,0:T(8,128)(2,1)S(1)}, bf16[4,256,256]{2,1,0:T(8,128)(2,1)S(1)}, f32[4,2,128,128...) custom-call(s32[8]{0:T(128)S(1)} %stack.23.info, s32[8]{0:T(128)S(1)} %select_reduce_fusion.ends, ...), custom_call_target="tpu_custom_call" | custom-call | tf_op jit(solution)/shard_map/pallas_call | solution.py:356
  196.9 1.5 collective-permute-start.28
  200.5 4.2 %shard_map.200 = (f32[4,256,256]{2,1,0:T(8,128)S(1)}, f32[4,256,256]{2,1,0:T(8,128)S(1)}, f32[4,256,256]{2,1,0:T(8,128)S(1)}) custom-call(s32[8]{0:T(128)S(1)} %stack.23.info, s32[8]{0:T(128)S(1)} %select_reduce_fusion.ends, f32[8]{0:T(128)S(1)} %copy-done.38, bf16[4,256,256]{2,1,0:T(8,128)(2,1)S(1)} %copy-done.5, bf16[4,256,256]{2,1,0:T(8,128)(2,1)S(1)} %copy-done.10, ...), custom_call_target="tpu_custom_call" | custom-call | tf_op jit(solution)/shard_map/pallas_call | solution.py:356
  204.8 1.5 collective-permute-start.27
  206.9 4.0 %shard_map.199 = (bf16[2,512,256]{2,1,0:T(8,128)(2,1)S(1)}, bf16[2,512,256]{2,1,0:T(8,128)(2,1)}) custom-call(s32[8]{0:T(128)S(1)} %stack.23.info, bf16[1024,256]{1,0:T(8,128)(2,1)S(1)} %bitcast.126, bf16[1024,1024]{1,0:T(8,128)(2,1)S(1)} %bitcast.117, bf16[1024,1024]{1,0:T(8,128)(2,1)S(1)} %bitcast.113, bf16[1024,256]{1,0:T(8,128)(2,1)S(1)} %bitcast.119), custom_call_target="tpu_custom_call" | custom-call | tf_op jit(solution)/shard_map/pallas_call | solution.py:356
  211.9 2.4 collective-permute-done.27
  215.5 7.2 %shard_map.201 = (bf16[4,256,768]{2,1,0:T(8,128)(2,1)S(1)}, bf16[2,256,1024]{2,1,0:T(8,128)(2,1)S(1)}, bf16[2,256,1024]{2,1,0:T(8,128)(2,1)S(1)}) custom-call(s32[8]{0:T(128)S(1)} %stack.23.info, s32[8]{0:T(128)S(1)} %select_reduce_fusion.ends, f32[8]{0:T(128)S(1)} %copy-done.38, f32[4,256,256]{2,1,0:T(8,128)S(1)} %get-tuple-element.145.gq, ...), custom_call_target="tpu_custom_call" | custom-call | tf_op jit(solution)/shard_map/pallas_call | solution.py:356
  227.7 1.5 collective-permute-start.41
  229.1 4.4 %shard_map.202 = (bf16[2,768,256]{2,1,0:T(8,128)(2,1)S(1)}, bf16[2,768,256]{2,1,0:T(8,128)(2,1)}) custom-call(s32[8]{0:T(128)S(1)} %stack.23.info, bf16[1024,1024]{1,0:T(8,128)(2,1)S(1)} %bitcast.114, bf16[1024,768]{1,0:T(8,128)(2,1)S(1)} %bitcast.122), custom_call_target="tpu_custom_call" | custom-call | tf_op jit(solution)/shard_map/pallas_call | solution.py:356
  234.3 15.6 %collective-permute-done.35.got = bf16[256,1024]{1,0:T(8,128)(2,1)S(1)} collective-permute-done((bf16[256,1024]{1,0:T(8,128)(2,1)S(1)}, bf16[256,1024]{1,0:T(8,128)(2,1)S(1)}, u32[]{:S(2)}, u32[]{:S(2)}) %collective-permute-start.35) | collective-permute-done | bytes 524320 | tf_op jit(solution)/shard_map/ppermute | solution.py:21
  251.3 3.6 all-to-all-start.3
  255.0 1.6 add_convert_fusion.6
  256.6 1.4 collective-permute-start.40
  259.2 1.5 collective-permute-start.43
  260.7 8.3 %collective-permute-done.41 = bf16[1408,256]{1,0:T(8,128)(2,1)} collective-permute-done((bf16[1408,256]{1,0:T(8,128)(2,1)}, bf16[1408,256]{1,0:T(8,128)(2,1)}, u32[]{:S(2)}, u32[]{:S(2)}) %collective-permute-start.41) | collective-permute-done | bytes 720928 | tf_op jit(solution)/shard_map/ppermute | solution.py:21
  269.1 2.2 add_convert_fusion.5.p0
  272.3 2.1 collective-permute-start.44
  274.5 1.5 add_convert_fusion.4
  276.8 1.8 collective-permute-start.37
  279.8 2.8 all-to-all-start.2
  282.6 2.2 shard_map.206
  284.8 15.9 %collective-permute-done.45.p2 = bf16[1408,256]{1,0:T(8,128)(2,1)} collective-permute-done((bf16[1408,256]{1,0:T(8,128)(2,1)}, bf16[1408,256]{1,0:T(8,128)(2,1)}, u32[]{:S(2)}, u32[]{:S(2)}) %collective-permute-start.45) | collective-permute-done | bytes 720928 | tf_op jit(solution)/shard_map/ppermute | solution.py:21
  300.7 8.8 %collective-permute-done.44 = bf16[1216,256]{1,0:T(8,128)(2,1)} collective-permute-done((bf16[1216,256]{1,0:T(8,128)(2,1)}, bf16[1216,256]{1,0:T(8,128)(2,1)}, u32[]{:S(2)}, u32[]{:S(2)}) %collective-permute-start.44) | collective-permute-done | bytes 622624 | tf_op jit(solution)/shard_map/ppermute | solution.py:21
  310.9 1.9 fusion.2
  312.8 2.7 collective-permute-start.38
  315.8 16.6 %collective-permute-done.46.p2.d2 = bf16[1216,256]{1,0:T(8,128)(2,1)S(1)} collective-permute-done((bf16[1216,256]{1,0:T(8,128)(2,1)S(1)}, bf16[1216,256]{1,0:T(8,128)(2,1)S(1)}, u32[]{:S(2)}, u32[]{:S(2)}) %collective-permute-start.46) | collective-permute-done | bytes 622624 | tf_op jit(solution)/shard_map/ppermute | solution.py:21
  335.6 2.5 collective-permute-start.53
  338.8 1.8 collective-permute-start.54
  340.6 6.0 %shard_map.207 = f32[256,5632]{1,0:T(8,128)} custom-call(s32[8]{0:T(128)S(1)} %stack.23.info, bf16[1408,256]{1,0:T(8,128)(2,1)} %add_convert_fusion.5.p0, bf16[1408,256]{1,0:T(8,128)(2,1)} %collective-permute-done.50.p1, bf16[1408,256]{1,0:T(8,128)(2,1)} %collective-permute-done.45.p2, bf16[1408,256]{1,0:T(8,128)(2,1)} %collective-permute-done.47.p3), custom_call_target="tpu_custom_call" | custom-call | tf_op jit(solution)/shard_map/pallas_call | solution.py:356
  346.7 3.9 %shard_map.208 = f32[704,1024]{1,0:T(8,128)} custom-call(s32[8]{0:T(128)S(1)} %stack.23.info, bf16[1216,256]{1,0:T(8,128)(2,1)} %copy-done.39, bf16[1216,256]{1,0:T(8,128)(2,1)} %copy-done.40, bf16[1216,256]{1,0:T(8,128)(2,1)} %copy-done.42, bf16[1216,256]{1,0:T(8,128)(2,1)} %copy-done.41), custom_call_target="tpu_custom_call" | custom-call | tf_op jit(solution)/shard_map/pallas_call | solution.py:356
  353.4 5.4 %shard_map.209 = (f32[256,1024]{1,0:T(8,128)}, f32[256,1024]{1,0:T(8,128)}, f32[256,1024]{1,0:T(8,128)}, f32[256,1024]{1,0:T(8,128)}, f32[256,1024]{1,0:T(8,128)}) custom-call(s32[8]{0:T(128)S(1)} %stack.23.info, bf16[768,256]{1,0:T(8,128)(2,1)} %copy-done.54, bf16[768,256]{1,0:T(8,128)(2,1)} %copy-done.63, bf16[768,256]{1,0:T(8,128)(2,1)} %copy-done.62, ...), custom_call_target="tpu_custom_call" | custom-call | tf_op jit(solution)/shard_map/pallas_call | solution.py:356
  (297 shorter events, 50.4 us)
Async XLA Ops:
  11.6 54.6 %copy-start.6 = (bf16[4,256,256]{2,1,0:T(8,128)(2,1)}, bf16[4,256,256]{2,1,0:T(8,128)(2,1)S(1)}, u32[]{:S(2)}) copy-start(bf16[4,256,256]{2,1,0:T(8,128)(2,1)S(1)} %get-tuple-element.156.enter) | copy-start | bytes 1572868
  11.6 23.7 %all-to-all-start = ((bf16[32,8,1024]{2,1,0:T(8,128)(2,1)}), bf16[32,8,1024]{2,1,0:T(8,128)(2,1)}, u32[]{:S(2)}, u32[]{:S(2)}) async-start(bf16[32,8,1024]{2,1,0:T(8,128)(2,1)} %bitcast.6), calls=%async_computation | async-start | bytes 1048576 | tf_op jit(solution)/shard_map/all_to_all | solution.py:1169
  19.0 115.9 %all-gather.3.cloned.1.call-start = ((), (), s32[]{:S(2)}) async-start(), calls=%async_computation.4 | async-start | bytes 5406720 | tf_op jit(solution)/shard_map/all_gather | solution.py:1223
  20.8 36.4 %collective-permute-start.3 = (bf16[1024,256]{1,0:T(8,128)(2,1)S(1)}, bf16[1024,256]{1,0:T(8,128)(2,1)S(1)}, u32[]{:S(2)}, u32[]{:S(2)}) collective-permute-start(bf16[1024,256]{1,0:T(8,128)(2,1)S(1)} %shard_map.188.w0), channel_id=1, source_target_pairs={{0,1},{1,0},{2,3},{3,2},{4,5},{5,4},{6,7},{7,6},{8,9},{9,8},{10,11... | collective-permute-start | bytes 1572872 | tf_op jit(solution)/shard_map/ppermute | solution.py:21
  22.5 38.8 %collective-permute-start.4 = (bf16[1024,256]{1,0:T(8,128)(2,1)S(1)}, bf16[1024,256]{1,0:T(8,128)(2,1)}, u32[]{:S(2)}, u32[]{:S(2)}) collective-permute-start(bf16[1024,256]{1,0:T(8,128)(2,1)S(1)} %shard_map.188.w0), channel_id=1, source_target_pairs={{0,2},{1,3},{2,0},{3,1},{4,6},{5,7},{6,4},{7,5},{8,10},{9,11},{10,... | collective-permute-start | bytes 1572872 | tf_op jit(solution)/shard_map/ppermute | solution.py:21
  24.0 39.5 %collective-permute-start.5 = (bf16[1024,256]{1,0:T(8,128)(2,1)S(1)}, bf16[1024,256]{1,0:T(8,128)(2,1)}, u32[]{:S(2)}, u32[]{:S(2)}) collective-permute-start(bf16[1024,256]{1,0:T(8,128)(2,1)S(1)} %shard_map.188.w0), channel_id=1, source_target_pairs={{0,3},{1,2},{2,1},{3,0},{4,7},{5,6},{6,5},{7,4},{8,11},{9,10},{10,... | collective-permute-start | bytes 1572872 | tf_op jit(solution)/shard_map/ppermute | solution.py:21
  35.3 19.8 %collective-permute-start = (bf16[256,1024]{1,0:T(8,128)(2,1)}, bf16[256,1024]{1,0:T(8,128)(2,1)S(1)}, u32[]{:S(2)}, u32[]{:S(2)}) collective-permute-start(bf16[256,1024]{1,0:T(8,128)(2,1)} %bitcast.7.r0), channel_id=1, source_target_pairs={{0,8},{8,0},{1,9},{9,1},{2,10},{10,2},{3,11},{11,3},{4,12},{12,4},... | collective-permute-start | bytes 1572872 | tf_op jit(solution)/shard_map/ppermute | solution.py:21
  37.2 46.8 %all-to-all-start.1 = ((bf16[32,8,1024]{2,1,0:T(8,128)(2,1)}), bf16[32,8,1024]{2,1,0:T(8,128)(2,1)}, u32[]{:S(2)}, u32[]{:S(2)}) async-start(bf16[32,8,1024]{2,1,0:T(8,128)(2,1)} %bitcast.8), calls=%async_computation.1 | async-start | bytes 1048576 | tf_op jit(solution)/shard_map/all_to_all | solution.py:1169
  40.6 25.5 %collective-permute-start.1 = (bf16[256,1024]{1,0:T(8,128)(2,1)}, bf16[256,1024]{1,0:T(8,128)(2,1)S(1)}, u32[]{:S(2)}, u32[]{:S(2)}) collective-permute-start(bf16[256,1024]{1,0:T(8,128)(2,1)} %bitcast.7.r0), channel_id=1, source_target_pairs={{0,4},{4,0},{1,5},{5,1},{2,6},{6,2},{3,7},{7,3},{8,12},{12,8},{9,1... | collective-permute-start | bytes 1572872 | tf_op jit(solution)/shard_map/ppermute | solution.py:21
  55.2 10.9 %collective-permute-start.2 = (bf16[256,1024]{1,0:T(8,128)(2,1)S(1)}, bf16[256,1024]{1,0:T(8,128)(2,1)S(1)}, u32[]{:S(2)}, u32[]{:S(2)}) collective-permute-start(bf16[256,1024]{1,0:T(8,128)(2,1)S(1)} %collective-permute-done.r1), channel_id=1, source_target_pairs={{0,4},{4,0},{1,5},{5,1},{2,6},{6,2},{3,7},{7,3},{8,12},{12,8},{9,1... | collective-permute-start | bytes 1572872 | tf_op jit(solution)/shard_map/ppermute | solution.py:21
  57.2 35.2 %collective-permute-start.11 = (bf16[256,1024]{1,0:T(8,128)(2,1)}, bf16[256,1024]{1,0:T(8,128)(2,1)}, u32[]{:S(2)}, u32[]{:S(2)}) collective-permute-start(bf16[256,1024]{1,0:T(8,128)(2,1)} %param.21), channel_id=1, source_target_pairs={{0,3},{5,6},{10,9},{15,12},{16,19},{21,22},{26,25},{31,28}} | collective-permute-start | bytes 1572872 | tf_op jit(solution)/shard_map/ppermute | solution.py:554
  61.3 31.1 %collective-permute-start.12 = (bf16[256,1024]{1,0:T(8,128)(2,1)}, bf16[256,1024]{1,0:T(8,128)(2,1)}, u32[]{:S(2)}, u32[]{:S(2)}) collective-permute-start(bf16[256,1024]{1,0:T(8,128)(2,1)} %param.21), channel_id=1, source_target_pairs={{0,2},{5,7},{10,8},{15,13},{16,18},{21,23},{26,24},{31,29}} | collective-permute-start | bytes 1572872 | tf_op jit(solution)/shard_map/ppermute | solution.py:554
  63.4 29.0 %collective-permute-start.13 = (bf16[256,1024]{1,0:T(8,128)(2,1)}, bf16[256,1024]{1,0:T(8,128)(2,1)}, u32[]{:S(2)}, u32[]{:S(2)}) collective-permute-start(bf16[256,1024]{1,0:T(8,128)(2,1)} %param.21), channel_id=1, source_target_pairs={{0,1},{5,4},{10,11},{15,14},{16,17},{21,20},{26,27},{31,30}} | collective-permute-start | bytes 1572872 | tf_op jit(solution)/shard_map/ppermute | solution.py:554
  78.0 4.8 %collective-permute-start.7 = (bf16[2,128,128]{2,1,0:T(8,128)(2,1)S(1)}, bf16[2,128,128]{2,1,0:T(8,128)(2,1)S(1)}, u32[]{:S(2)}, u32[]{:S(2)}) collective-permute-start(bf16[2,128,128]{2,1,0:T(8,128)(2,1)S(1)} %get-tuple-element.105), channel_id=1, source_target_pairs={{0,1},{1,0},{2,3},{3,2},{4,5},{5,4},{6,7},{7,6},{8,9},{9,8},{10,11... | collective-permute-start | bytes 196616 | tf_op jit(solution)/shard_map/ppermute | solution.py:1197
  78.8 6.0 %collective-permute-start.8 = (bf16[2,128,128]{2,1,0:T(8,128)(2,1)S(1)}, bf16[2,128,128]{2,1,0:T(8,128)(2,1)S(1)}, u32[]{:S(2)}, u32[]{:S(2)}) collective-permute-start(bf16[2,128,128]{2,1,0:T(8,128)(2,1)S(1)} %get-tuple-element.105), channel_id=1, source_target_pairs={{0,2},{1,3},{2,0},{3,1},{4,6},{5,7},{6,4},{7,5},{8,10},{9,11},{10,... | collective-permute-start | bytes 196616 | tf_op jit(solution)/shard_map/ppermute | solution.py:1197
  82.8 6.5 %collective-permute-start.9 = (bf16[2,128,128]{2,1,0:T(8,128)(2,1)S(1)}, bf16[2,128,128]{2,1,0:T(8,128)(2,1)S(1)}, u32[]{:S(2)}, u32[]{:S(2)}) collective-permute-start(bf16[2,128,128]{2,1,0:T(8,128)(2,1)S(1)} %get-tuple-element.105), channel_id=1, source_target_pairs={{0,3},{1,2},{2,1},{3,0},{4,7},{5,6},{6,5},{7,4},{8,11},{9,10},{10,... | collective-permute-start | bytes 196616 | tf_op jit(solution)/shard_map/ppermute | solution.py:1197
  84.8 13.7 %collective-permute-start.6 = (bf16[256,1024]{1,0:T(8,128)(2,1)}, bf16[256,1024]{1,0:T(8,128)(2,1)S(1)}, u32[]{:S(2)}, u32[]{:S(2)}) collective-permute-start(bf16[256,1024]{1,0:T(8,128)(2,1)} %bitcast.9.g0), channel_id=1, source_target_pairs={{0,8},{8,0},{1,9},{9,1},{2,10},{10,2},{3,11},{11,3},{4,12},{12,4},... | collective-permute-start | bytes 1572872 | tf_op jit(solution)/shard_map/ppermute | solution.py:21
  90.1 7.6 %collective-permute-start.10 = (f32[2,128,128]{2,1,0:T(8,128)S(1)}, f32[2,128,128]{2,1,0:T(8,128)S(1)}, u32[]{:S(2)}, u32[]{:S(2)}) collective-permute-start(f32[2,128,128]{2,1,0:T(8,128)S(1)} %fusion.12), channel_id=1, source_target_pairs={{0,16},{16,0},{1,17},{17,1},{2,18},{18,2},{3,19},{19,3},{4,20},{20... | collective-permute-start | bytes 393224 | tf_op jit(solution)/shard_map/ppermute | solution.py:21
  103.1 2.7 collective-permute-start.14
  106.2 25.5 %collective-permute-start.15 = (bf16[2,256,1024]{2,1,0:T(8,128)(2,1)S(1)}, bf16[2,256,1024]{2,1,0:T(8,128)(2,1)S(1)}, u32[]{:S(2)}, u32[]{:S(2)}) collective-permute-start(bf16[2,256,1024]{2,1,0:T(8,128)(2,1)S(1)} %add_convert_fusion.3), channel_id=1, source_target_pairs={{0,8},{8,0},{1,9},{9,1},{2,10},{10,2},{3,11},{11,3},{4,12},{12,4},... | collective-permute-start | bytes 3145736 | tf_op jit(solution)/shard_map/ppermute | solution.py:21
  108.2 2.8 collective-permute-start.16
  108.2 2.8 collective-permute-start.17
  132.0 2.9 collective-permute-start.18
  152.4 5.2 %collective-permute-start.21 = (bf16[2,256,1024]{2,1,0:T(8,128)(2,1)S(1)}, bf16[2,256,1024]{2,1,0:T(8,128)(2,1)S(1)}, u32[]{:S(2)}, u32[]{:S(2)}) collective-permute-start(bf16[2,256,1024]{2,1,0:T(8,128)(2,1)S(1)} %get-tuple-element.114), channel_id=1, source_target_pairs={{0,4},{4,0},{1,5},{5,1},{2,6},{6,2},{3,7},{7,3},{8,12},{12,8},{9,1... | collective-permute-start | bytes 3145736 | tf_op jit(solution)/shard_map/ppermute | solution.py:21
  156.1 18.5 %collective-permute-start.23 = (bf16[2,704,256]{2,1,0:T(8,128)(2,1)S(1)}, bf16[2,704,256]{2,1,0:T(8,128)(2,1)S(1)}, u32[]{:S(2)}, u32[]{:S(2)}) collective-permute-start(bf16[2,704,256]{2,1,0:T(8,128)(2,1)S(1)} %get-tuple-element.124), channel_id=1, source_target_pairs={{0,1},{1,0},{2,3},{3,2},{4,5},{5,4},{6,7},{7,6},{8,9},{9,8},{10,11... | collective-permute-start | bytes 2162696 | tf_op jit(solution)/shard_map/ppermute | solution.py:21
  158.0 25.2 %collective-permute-start.22 = (bf16[2,256,1024]{2,1,0:T(8,128)(2,1)S(1)}, bf16[2,256,1024]{2,1,0:T(8,128)(2,1)S(1)}, u32[]{:S(2)}, u32[]{:S(2)}) collective-permute-start(bf16[2,256,1024]{2,1,0:T(8,128)(2,1)S(1)} %add_convert_fusion.1), channel_id=1, source_target_pairs={{0,8},{8,0},{1,9},{9,1},{2,10},{10,2},{3,11},{11,3},{4,12},{12,4},... | collective-permute-start | bytes 3145736 | tf_op jit(solution)/shard_map/ppermute | solution.py:21
  159.9 23.8 %collective-permute-start.20 = (bf16[256,1024]{1,0:T(8,128)(2,1)S(1)}, bf16[256,1024]{1,0:T(8,128)(2,1)S(1)}, u32[]{:S(2)}, u32[]{:S(2)}) collective-permute-start(bf16[256,1024]{1,0:T(8,128)(2,1)S(1)} %get-tuple-element.197), channel_id=1, source_target_pairs={{0,4},{4,0},{1,5},{5,1},{2,6},{6,2},{3,7},{7,3},{8,12},{12,8},{9,1... | collective-permute-start | bytes 1572872 | tf_op jit(solution)/shard_map/ppermute | solution.py:21
  160.0 23.8 %collective-permute-start.19 = (bf16[256,1024]{1,0:T(8,128)(2,1)S(1)}, bf16[256,1024]{1,0:T(8,128)(2,1)S(1)}, u32[]{:S(2)}, u32[]{:S(2)}) collective-permute-start(bf16[256,1024]{1,0:T(8,128)(2,1)S(1)} %get-tuple-element.198), channel_id=1, source_target_pairs={{0,4},{4,0},{1,5},{5,1},{2,6},{6,2},{3,7},{7,3},{8,12},{12,8},{9,1... | collective-permute-start | bytes 1572872 | tf_op jit(solution)/shard_map/ppermute | solution.py:21
  164.0 22.8 %collective-permute-start.25 = (bf16[2,704,256]{2,1,0:T(8,128)(2,1)S(1)}, bf16[2,704,256]{2,1,0:T(8,128)(2,1)S(1)}, u32[]{:S(2)}, u32[]{:S(2)}) collective-permute-start(bf16[2,704,256]{2,1,0:T(8,128)(2,1)S(1)} %get-tuple-element.118), channel_id=1, source_target_pairs={{0,2},{1,3},{2,0},{3,1},{4,6},{5,7},{6,4},{7,5},{8,10},{9,11},{10,... | collective-permute-start | bytes 2162696 | tf_op jit(solution)/shard_map/ppermute | solution.py:21
  183.6 4.1 %collective-permute-start.26 = (bf16[2,256,1024]{2,1,0:T(8,128)(2,1)S(1)}, bf16[2,256,1024]{2,1,0:T(8,128)(2,1)S(1)}, u32[]{:S(2)}, u32[]{:S(2)}) collective-permute-start(bf16[2,256,1024]{2,1,0:T(8,128)(2,1)S(1)} %add_convert_fusion.ua), channel_id=1, source_target_pairs={{0,4},{4,0},{1,5},{5,1},{2,6},{6,2},{3,7},{7,3},{8,12},{12,8},{9,1... | collective-permute-start | bytes 3145736 | tf_op jit(solution)/shard_map/ppermute | solution.py:21
  185.1 21.3 %collective-permute-start.24 = (bf16[256,1024]{1,0:T(8,128)(2,1)S(1)}, bf16[256,1024]{1,0:T(8,128)(2,1)S(1)}, u32[]{:S(2)}, u32[]{:S(2)}) collective-permute-start(bf16[256,1024]{1,0:T(8,128)(2,1)S(1)} %get-tuple-element.127), channel_id=1, source_target_pairs={{0,8},{8,0},{1,9},{9,1},{2,10},{10,2},{3,11},{11,3},{4,12},{12,4},... | collective-permute-start | bytes 1572872 | tf_op jit(solution)/shard_map/ppermute | solution.py:21
  187.1 24.7 %collective-permute-start.31 = (bf16[704,256]{1,0:T(8,128)(2,1)S(1)}, bf16[704,256]{1,0:T(8,128)(2,1)S(1)}, u32[]{:S(2)}, u32[]{:S(2)}) collective-permute-start(bf16[704,256]{1,0:T(8,128)(2,1)S(1)} %slice_bitcast_fusion.10), channel_id=1, source_target_pairs={{0,1},{1,0},{2,3},{3,2},{4,5},{5,4},{6,7},{7,6},{8,9},{9,8},{10,11... | collective-permute-start | bytes 1081352 | tf_op jit(solution)/shard_map/ppermute | solution.py:21
  196.9 7.9 %collective-permute-start.28 = (bf16[2,128,128]{2,1,0:T(8,128)(2,1)S(1)}, bf16[2,128,128]{2,1,0:T(8,128)(2,1)S(1)}, u32[]{:S(2)}, u32[]{:S(2)}) collective-permute-start(bf16[2,128,128]{2,1,0:T(8,128)(2,1)S(1)} %get-tuple-element.133), channel_id=1, source_target_pairs={{0,1},{1,0},{2,3},{3,2},{4,5},{5,4},{6,7},{7,6},{8,9},{9,8},{10,11... | collective-permute-start | bytes 196616 | tf_op jit(solution)/shard_map/ppermute | solution.py:1197
  198.4 7.9 %collective-permute-start.29 = (bf16[2,128,128]{2,1,0:T(8,128)(2,1)S(1)}, bf16[2,128,128]{2,1,0:T(8,128)(2,1)S(1)}, u32[]{:S(2)}, u32[]{:S(2)}) collective-permute-start(bf16[2,128,128]{2,1,0:T(8,128)(2,1)S(1)} %get-tuple-element.133), channel_id=1, source_target_pairs={{0,2},{1,3},{2,0},{3,1},{4,6},{5,7},{6,4},{7,5},{8,10},{9,11},{10,... | collective-permute-start | bytes 196616 | tf_op jit(solution)/shard_map/ppermute | solution.py:1197
  199.3 7.0 %collective-permute-start.30 = (bf16[2,128,128]{2,1,0:T(8,128)(2,1)S(1)}, bf16[2,128,128]{2,1,0:T(8,128)(2,1)S(1)}, u32[]{:S(2)}, u32[]{:S(2)}) collective-permute-start(bf16[2,128,128]{2,1,0:T(8,128)(2,1)S(1)} %get-tuple-element.133), channel_id=1, source_target_pairs={{0,3},{1,2},{2,1},{3,0},{4,7},{5,6},{6,5},{7,4},{8,11},{9,10},{10,... | collective-permute-start | bytes 196616 | tf_op jit(solution)/shard_map/ppermute | solution.py:1197
  204.8 9.5 %collective-permute-start.27 = (bf16[704,256]{1,0:T(8,128)(2,1)S(1)}, bf16[704,256]{1,0:T(8,128)(2,1)S(1)}, u32[]{:S(2)}, u32[]{:S(2)}) collective-permute-start(bf16[704,256]{1,0:T(8,128)(2,1)S(1)} %slice_bitcast_fusion.11), channel_id=1, source_target_pairs={{0,2},{1,3},{2,0},{3,1},{4,6},{5,7},{6,4},{7,5},{8,10},{9,11},{10,... | collective-permute-start | bytes 1081352 | tf_op jit(solution)/shard_map/ppermute | solution.py:21
  206.4 8.9 %collective-permute-start.32 = (f32[2,128,128]{2,1,0:T(8,128)S(1)}, f32[2,128,128]{2,1,0:T(8,128)S(1)}, u32[]{:S(2)}, u32[]{:S(2)}) collective-permute-start(f32[2,128,128]{2,1,0:T(8,128)S(1)} %fusion.15), channel_id=1, source_target_pairs={{0,16},{16,0},{1,17},{17,1},{2,18},{18,2},{3,19},{19,3},{4,20},{20... | collective-permute-start | bytes 393224 | tf_op jit(solution)/shard_map/ppermute | solution.py:21
  222.8 2.0 collective-permute-start.34
  222.9 2.6 collective-permute-start.33
  223.4 31.6 %collective-permute-start.39 = (bf16[2,704,256]{2,1,0:T(8,128)(2,1)}, bf16[2,704,256]{2,1,0:T(8,128)(2,1)}, u32[]{:S(2)}, u32[]{:S(2)}) collective-permute-start(bf16[2,704,256]{2,1,0:T(8,128)(2,1)} %get-tuple-element.160), channel_id=1, source_target_pairs={{0,1},{1,0},{2,3},{3,2},{4,5},{5,4},{6,7},{7,6},{8,9},{9,8},{10,11... | collective-permute-start | bytes 2162696 | tf_op jit(solution)/shard_map/ppermute | solution.py:21
  225.9 24.0 %collective-permute-start.35 = (bf16[256,1024]{1,0:T(8,128)(2,1)S(1)}, bf16[256,1024]{1,0:T(8,128)(2,1)S(1)}, u32[]{:S(2)}, u32[]{:S(2)}) collective-permute-start(bf16[256,1024]{1,0:T(8,128)(2,1)S(1)} %get-tuple-element.191), channel_id=1, source_target_pairs={{0,8},{8,0},{1,9},{9,1},{2,10},{10,2},{3,11},{11,3},{4,12},{12,4},... | collective-permute-start | bytes 1572872 | tf_op jit(solution)/shard_map/ppermute | solution.py:21
  226.5 31.5 %collective-permute-start.42 = (bf16[2,512,256]{2,1,0:T(8,128)(2,1)}, bf16[2,512,256]{2,1,0:T(8,128)(2,1)}, u32[]{:S(2)}, u32[]{:S(2)}) collective-permute-start(bf16[2,512,256]{2,1,0:T(8,128)(2,1)} %get-tuple-element.140), channel_id=1, source_target_pairs={{0,2},{1,3},{2,0},{3,1},{4,6},{5,7},{6,4},{7,5},{8,10},{9,11},{10,... | collective-permute-start | bytes 1572872 | tf_op jit(solution)/shard_map/ppermute | solution.py:21
  227.7 41.4 %collective-permute-start.41 = (bf16[1408,256]{1,0:T(8,128)(2,1)}, bf16[1408,256]{1,0:T(8,128)(2,1)}, u32[]{:S(2)}, u32[]{:S(2)}) collective-permute-start(bf16[1408,256]{1,0:T(8,128)(2,1)} %pad_maximum_fusion), channel_id=1, source_target_pairs={{0,16},{16,0},{1,17},{17,1},{2,18},{18,2},{3,19},{19,3},{4,20},{20... | collective-permute-start | bytes 2162696 | tf_op jit(solution)/shard_map/ppermute | solution.py:21
  233.5 40.9 %collective-permute-start.36 = (bf16[2,768,256]{2,1,0:T(8,128)(2,1)}, bf16[2,768,256]{2,1,0:T(8,128)(2,1)}, u32[]{:S(2)}, u32[]{:S(2)}) collective-permute-start(bf16[2,768,256]{2,1,0:T(8,128)(2,1)} %get-tuple-element.154), channel_id=1, source_target_pairs={{0,1},{1,0},{2,3},{3,2},{4,5},{5,4},{6,7},{7,6},{8,9},{9,8},{10,11... | collective-permute-start | bytes 2359304 | tf_op jit(solution)/shard_map/ppermute | solution.py:21
  251.3 28.5 %all-to-all-start.3 = ((bf16[32,8,1024]{2,1,0:T(8,128)(2,1)}), bf16[32,8,1024]{2,1,0:T(8,128)(2,1)}, u32[]{:S(2)}, u32[]{:S(2)}) async-start(bf16[32,8,1024]{2,1,0:T(8,128)(2,1)} %bitcast.120), calls=%async_computation.3 | async-start | bytes 1048576 | tf_op jit(solution)/shard_map/all_to_all | solution.py:1169
  256.6 14.7 %collective-permute-start.40 = (bf16[704,256]{1,0:T(8,128)(2,1)S(1)}, bf16[704,256]{1,0:T(8,128)(2,1)S(1)}, u32[]{:S(2)}, u32[]{:S(2)}) collective-permute-start(bf16[704,256]{1,0:T(8,128)(2,1)S(1)} %slice_bitcast_fusion.6), channel_id=1, source_target_pairs={{0,2},{1,3},{2,0},{3,1},{4,6},{5,7},{6,4},{7,5},{8,10},{9,11},{10,... | collective-permute-start | bytes 1081352 | tf_op jit(solution)/shard_map/ppermute | solution.py:21
  259.2 12.0 %collective-permute-start.43 = (bf16[512,256]{1,0:T(8,128)(2,1)S(1)}, bf16[512,256]{1,0:T(8,128)(2,1)S(1)}, u32[]{:S(2)}, u32[]{:S(2)}) collective-permute-start(bf16[512,256]{1,0:T(8,128)(2,1)S(1)} %slice_bitcast_fusion.13), channel_id=1, source_target_pairs={{0,1},{1,0},{2,3},{3,2},{4,5},{5,4},{6,7},{7,6},{8,9},{9,8},{10,11... | collective-permute-start | bytes 786440 | tf_op jit(solution)/shard_map/ppermute | solution.py:21
  271.2 29.5 %collective-permute-start.45 = (bf16[1408,256]{1,0:T(8,128)(2,1)}, bf16[1408,256]{1,0:T(8,128)(2,1)}, u32[]{:S(2)}, u32[]{:S(2)}) collective-permute-start(bf16[1408,256]{1,0:T(8,128)(2,1)} %add_convert_fusion.5.p0), channel_id=1, source_target_pairs={{0,8},{8,0},{1,9},{9,1},{2,10},{10,2},{3,11},{11,3},{4,12},{12,4},... | collective-permute-start | bytes 2162696 | tf_op jit(solution)/shard_map/ppermute | solution.py:21
  272.3 37.2 %collective-permute-start.44 = (bf16[1216,256]{1,0:T(8,128)(2,1)}, bf16[1216,256]{1,0:T(8,128)(2,1)}, u32[]{:S(2)}, u32[]{:S(2)}) collective-permute-start(bf16[1216,256]{1,0:T(8,128)(2,1)} %pad_maximum_fusion.1), channel_id=1, source_target_pairs={{0,16},{16,0},{1,17},{17,1},{2,18},{18,2},{3,19},{19,3},{4,20},{20... | collective-permute-start | bytes 1867784 | tf_op jit(solution)/shard_map/ppermute | solution.py:21
  276.8 34.1 %collective-permute-start.37 = (bf16[768,256]{1,0:T(8,128)(2,1)}, bf16[768,256]{1,0:T(8,128)(2,1)}, u32[]{:S(2)}, u32[]{:S(2)}) collective-permute-start(bf16[768,256]{1,0:T(8,128)(2,1)} %slice_bitcast_fusion.4), channel_id=1, source_target_pairs={{0,2},{1,3},{2,0},{3,1},{4,6},{5,7},{6,4},{7,5},{8,10},{9,11},{10,... | collective-permute-start | bytes 1179656 | tf_op jit(solution)/shard_map/ppermute | solution.py:21
  279.8 29.7 %copy-start.52 = (bf16[512,256]{1,0:T(8,128)(2,1)S(1)}, bf16[512,256]{1,0:T(8,128)(2,1)}, u32[]{:S(2)}) copy-start(bf16[512,256]{1,0:T(8,128)(2,1)} %copy-done.51) | copy-start | bytes 786436
  279.8 53.0 %all-to-all-start.2 = ((bf16[32,8,1024]{2,1,0:T(8,128)(2,1)}), bf16[32,8,1024]{2,1,0:T(8,128)(2,1)S(1)}, u32[]{:S(2)}, u32[]{:S(2)}) async-start(bf16[32,8,1024]{2,1,0:T(8,128)(2,1)} %bitcast.121), calls=%async_computation.2 | async-start | bytes 1048576 | tf_op jit(solution)/shard_map/all_to_all | solution.py:1169
  310.8 21.6 %collective-permute-start.46 = (bf16[1216,256]{1,0:T(8,128)(2,1)S(1)}, bf16[1216,256]{1,0:T(8,128)(2,1)S(1)}, u32[]{:S(2)}, u32[]{:S(2)}) collective-permute-start(bf16[1216,256]{1,0:T(8,128)(2,1)S(1)} %add_convert_fusion.9.p0.d0), channel_id=1, source_target_pairs={{0,8},{8,0},{1,9},{9,1},{2,10},{10,2},{3,11},{11,3},{4,12},{12,4},... | collective-permute-start | bytes 1867784 | tf_op jit(solution)/shard_map/ppermute | solution.py:21
  310.8 23.3 %collective-permute-start.47 = (bf16[1408,256]{1,0:T(8,128)(2,1)}, bf16[1408,256]{1,0:T(8,128)(2,1)}, u32[]{:S(2)}, u32[]{:S(2)}) collective-permute-start(bf16[1408,256]{1,0:T(8,128)(2,1)} %collective-permute-done.45.p2), channel_id=1, source_target_pairs={{0,4},{4,0},{1,5},{5,1},{2,6},{6,2},{3,7},{7,3},{8,12},{12,8},{9,1... | collective-permute-start | bytes 2162696 | tf_op jit(solution)/shard_map/ppermute | solution.py:21
  312.8 21.3 %collective-permute-start.38 = (bf16[768,256]{1,0:T(8,128)(2,1)}, bf16[768,256]{1,0:T(8,128)(2,1)}, u32[]{:S(2)}, u32[]{:S(2)}) collective-permute-start(bf16[768,256]{1,0:T(8,128)(2,1)} %fusion.2), channel_id=1, source_target_pairs={{0,16},{16,0},{1,17},{17,1},{2,18},{18,2},{3,19},{19,3},{4,20},{20... | collective-permute-start | bytes 1179656 | tf_op jit(solution)/shard_map/ppermute | solution.py:21
  315.5 20.0 %collective-permute-start.51 = (bf16[1216,256]{1,0:T(8,128)(2,1)S(1)}, bf16[1216,256]{1,0:T(8,128)(2,1)S(1)}, u32[]{:S(2)}, u32[]{:S(2)}) collective-permute-start(bf16[1216,256]{1,0:T(8,128)(2,1)S(1)} %add_convert_fusion.9.p0.d0), channel_id=1, source_target_pairs={{0,4},{4,0},{1,5},{5,1},{2,6},{6,2},{3,7},{7,3},{8,12},{12,8},{9,1... | collective-permute-start | bytes 1867784 | tf_op jit(solution)/shard_map/ppermute | solution.py:21
  332.4 3.2 collective-permute-start.52
  332.4 8.3 %collective-permute-start.50 = (bf16[1408,256]{1,0:T(8,128)(2,1)}, bf16[1408,256]{1,0:T(8,128)(2,1)}, u32[]{:S(2)}, u32[]{:S(2)}) collective-permute-start(bf16[1408,256]{1,0:T(8,128)(2,1)} %add_convert_fusion.5.p0), channel_id=1, source_target_pairs={{0,4},{4,0},{1,5},{5,1},{2,6},{6,2},{3,7},{7,3},{8,12},{12,8},{9,1... | collective-permute-start | bytes 2162696 | tf_op jit(solution)/shard_map/ppermute | solution.py:21
  335.3 15.3 %collective-permute-start.49 = (bf16[768,256]{1,0:T(8,128)(2,1)S(1)}, bf16[768,256]{1,0:T(8,128)(2,1)S(1)}, u32[]{:S(2)}, u32[]{:S(2)}) collective-permute-start(bf16[768,256]{1,0:T(8,128)(2,1)S(1)} %add_convert_fusion.11.q0), channel_id=1, source_target_pairs={{0,8},{8,0},{1,9},{9,1},{2,10},{10,2},{3,11},{11,3},{4,12},{12,4},... | collective-permute-start | bytes 1179656 | tf_op jit(solution)/shard_map/ppermute | solution.py:21
  335.6 15.0 %collective-permute-start.53 = (bf16[256,256]{1,0:T(8,128)(2,1)S(1)}, bf16[256,256]{1,0:T(8,128)(2,1)S(1)}, u32[]{:S(2)}, u32[]{:S(2)}) collective-permute-start(bf16[256,256]{1,0:T(8,128)(2,1)S(1)} %get-tuple-element.190), channel_id=1, source_target_pairs={{0,1},{1,0},{2,3},{3,2},{4,5},{5,4},{6,7},{7,6},{8,9},{9,8},{10,11... | collective-permute-start | bytes 393224 | tf_op jit(solution)/shard_map/ppermute | solution.py:21
  338.8 11.9 %collective-permute-start.54 = (bf16[256,256]{1,0:T(8,128)(2,1)S(1)}, bf16[256,256]{1,0:T(8,128)(2,1)S(1)}, u32[]{:S(2)}, u32[]{:S(2)}) collective-permute-start(bf16[256,256]{1,0:T(8,128)(2,1)S(1)} %get-tuple-element.188), channel_id=1, source_target_pairs={{0,2},{1,3},{2,0},{3,1},{4,6},{5,7},{6,4},{7,5},{8,10},{9,11},{10,... | collective-permute-start | bytes 393224 | tf_op jit(solution)/shard_map/ppermute | solution.py:21
  340.6 10.1 %collective-permute-start.55 = (bf16[256,256]{1,0:T(8,128)(2,1)S(1)}, bf16[256,256]{1,0:T(8,128)(2,1)S(1)}, u32[]{:S(2)}, u32[]{:S(2)}) collective-permute-start(bf16[256,256]{1,0:T(8,128)(2,1)S(1)} %get-tuple-element.189), channel_id=1, source_target_pairs={{0,3},{1,2},{2,1},{3,0},{4,7},{5,6},{6,5},{7,4},{8,11},{9,10},{10,... | collective-permute-start | bytes 393224 | tf_op jit(solution)/shard_map/ppermute | solution.py:21
  346.6 4.7 %collective-permute-start.48 = (bf16[768,256]{1,0:T(8,128)(2,1)S(1)}, bf16[768,256]{1,0:T(8,128)(2,1)S(1)}, u32[]{:S(2)}, u32[]{:S(2)}) collective-permute-start(bf16[768,256]{1,0:T(8,128)(2,1)S(1)} %add_convert_fusion.11.q0), channel_id=1, source_target_pairs={{0,4},{4,0},{1,5},{5,1},{2,6},{6,2},{3,7},{7,3},{8,12},{12,8},{9,1... | collective-permute-start | bytes 1179656 | tf_op jit(solution)/shard_map/ppermute | solution.py:21
  350.7 1.9 collective-permute-start.56
  (76 other events, 553.1 us)
Sparse Core Ops, SparseCore 0:
  35.4 72.6 all-gather.2

commit v5 on v4

--- a/solution.py
+++ b/solution.py
@@ -442,7 +442,7 @@
     return pl.ds(pl.multiple_of(place(info, j) * 256, 256), 256)
 
 
-def rows_kernel(info, deal, tok, cot, leave, enter, sent_x, sent_g):
+def rows_kernel(info, deal, tok, leave, sent_x):
     dev = info[3]
     d = deal[...]
     owner = lax.shift_right_logical(d, 8)
@@ -467,7 +467,12 @@
     lv = jnp.where(column == c_i.astype(F32), 1.0, 0.0).astype(BF)
     leave[...] = lv
     sent_x[...] = dot(lv, tok[...]).astype(BF)
-    sent_g[...] = dot(lv, cot[...]).astype(BF)
+
+
+def orders_kernel(info, deal, leave, cot, enter, sent_g):
+    sent_g[...] = dot(leave[...], cot[...]).astype(BF)
+    r_i = lax.broadcasted_iota(jnp.int32, (ROWS, ROWS), 0)
+    c_i = lax.broadcasted_iota(jnp.int32, (ROWS, ROWS), 1)
     for i in range(TEAM):
         a = info[0] ^ rel_of(i)
         at = (info[4] * TEAM + a) * N_SHARD + info[1]
@@ -480,16 +485,26 @@
         enter[i] = jnp.where(slot == c_i.astype(F32), 1.0, 0.0).astype(BF)
 
 
-def exchange_rows(info, by_device, tokens_in, cotangent):
-    return run(
+def exchange_rows(info, by_device, tokens_in):
+    leave, sent_x = run(
         rows_kernel,
-        (sds((ROWS, ROWS)), sds((TEAM, ROWS, ROWS)), sds((ROWS, WIDTH)), sds((ROWS, WIDTH))),
+        (sds((ROWS, ROWS)), sds((ROWS, WIDTH))),
         (info,),
-        (by_device, tokens_in, cotangent),
-        in_specs=[full(DEVICES, ROWS), full(ROWS, WIDTH), full(ROWS, WIDTH)],
-        out_specs=[full(ROWS, ROWS), full(TEAM, ROWS, ROWS), full(ROWS, WIDTH), full(ROWS, WIDTH)],
-        flops=4 << 28,
-        nbytes=3 << 20,
+        (by_device, tokens_in),
+        in_specs=[full(DEVICES, ROWS), full(ROWS, WIDTH)],
+        out_specs=[full(ROWS, ROWS), full(ROWS, WIDTH)],
+    )
+    return leave, sent_x
+
+
+def exchange_orders(info, by_device, leave, cotangent):
+    return run(
+        orders_kernel,
+        (sds((TEAM, ROWS, ROWS)), sds((ROWS, WIDTH))),
+        (info,),
+        (by_device, leave, cotangent),
+        in_specs=[full(DEVICES, ROWS), full(ROWS, ROWS), full(ROWS, WIDTH)],
+        out_specs=[full(TEAM, ROWS, ROWS), full(ROWS, WIDTH)],
     )
 
 
@@ -1215,10 +1230,11 @@
     scal = (info, ends, decay_rates)
     by_device = deal_order.reshape(2, N_SHARD, TEAM, ROWS).transpose(0, 2, 1, 3).reshape(DEVICES, ROWS)
 
-    leave, enter, sent_x, sent_g = exchange_rows(info, by_device, *far(tokens_in, cotangent))
+    leave, sent_x = exchange_rows(info, by_device, *far(tokens_in))
     raw_x = exchange(sent_x)
     quarter = take_quarter(after(info, sent_x), *far(w_query, w_key, w_value, w_ugate))
     w_proj = gather_pieces(quarter)
+    enter, sent_g = exchange_orders(after(info, quarter), by_device, leave, *far(cotangent))
     bundle = ff_bundle(after(info, quarter), *far(w_ffin, w_ffdown))
     w_ff = lax.all_gather(after(bundle, raw_x), "shard", axis=0)
     wo = gather_out(w_out, me, shard)

time: 368 us -> 374 us (1.016)
  waiting for transfers between devices: 136 us -> 141 us
    all_to_all x4, waiting for transfers between devices: 4.51 us -> 22 us  [exchange(): return lax.all_to_all(rows, ALL, split_axis=0, concat_axis=0, tiled=True)]
    ppermute x48, waiting for transfers between devices: 122 us -> 112 us  [send(): return lax.ppermute(value, axis, [(i, i ^ mask) for i in range(size)])]
    pallas_call x23 -> x24, Pallas kernels: 106 us -> 107 us  [run(): pl.pallas_call(kernel, out_shape=out, grid_spec=pltpu.PrefetchScalarGridS...]
    unnamed x156 -> x140, local copies, waits for them, and re-layouts: 9.87 us -> 9.85 us
  transfers between devices with their start and end apart: 62 -> 62, of which waited for: 22 -> 23; matrix products, arithmetic and copies ran while one was open for 7% -> 6% of each run, Pallas kernels for 20% -> 20%
where the time goes in v5:
time: 374 us; the launch traced here: 372 us
  waiting for transfers between devices  141 us (38%)
  Pallas kernels  107 us (29%)
  starting transfers between devices  72.7 us (19%)
  other arithmetic  20.4 us (5%)
  between operations  16.6 us (4%)
  local copies, waits for them, and re-layouts  13.9 us (4%)
    ppermute x48, waiting for transfers between devices, send(): return lax.ppermute(value, axis, [(i, i ^ mask) for i in range(size)])  112 us
    pallas_call x24, Pallas kernels, run(): pl.pallas_call(kernel, out_shape=out, grid_spec=pltpu.PrefetchScalarGridS...  107 us
    ppermute x48, starting transfers between devices, send(): return lax.ppermute(value, axis, [(i, i ^ mask) for i in range(size)])  40.4 us
    all_to_all x4, waiting for transfers between devices, exchange(): return lax.all_to_all(rows, ALL, split_axis=0, concat_axis=0, tiled=True)  22 us
    all_to_all x4, starting transfers between devices, exchange(): return lax.all_to_all(rows, ALL, split_axis=0, concat_axis=0, tiled=True)  19.1 us
    unnamed x140, local copies, waits for them, and re-layouts  9.85 us
    ppermute x3, starting transfers between devices, gather_out(): wo = jnp.where(rel == j, lax.ppermute(w_out, axes, pairs), wo)  9.46 us
    ppermute x6, waiting for transfers between devices, state_in(): lax.ppermute(state, 'shard', [(i, i ^ j) for i in range(4)])  7.61 us
  transfers between devices with their start and end apart: 62, of which 23 were waited for; matrix products, arithmetic and copies ran while one was open for 6% of the time, Pallas kernels for 20%

profile of v5, /device:TPU:0, one launch (start us, length us, event | category | flops | bytes accessed | tf_op | source)
XLA Modules:
  0.0 372.4 jit_solution(11857489383120086067)
XLA Ops:
  8.1 3.1 shard_map.187
  11.2 7.4 %all-to-all-start = ((bf16[32,8,1024]{2,1,0:T(8,128)(2,1)}), bf16[32,8,1024]{2,1,0:T(8,128)(2,1)}, u32[]{:S(2)}, u32[]{:S(2)}) async-start(bf16[32,8,1024]{2,1,0:T(8,128)(2,1)} %bitcast.6), calls=%async_computation | async-start | bytes 1048576 | tf_op jit(solution)/shard_map/all_to_all | solution.py:1184
  18.7 1.7 shard_map.188.w0
  20.4 1.8 collective-permute-start.3
  22.2 1.5 collective-permute-start.4
  25.4 4.8 %shard_map.194 = bf16[2112,256]{1,0:T(8,128)(2,1)} custom-call(s32[8]{0:T(128)S(1)} %stack.23.info, bf16[256,5632]{1,0:T(8,128)(2,1)} %fin.1, bf16[704,1024]{1,0:T(8,128)(2,1)} %down.1), custom_call_target="tpu_custom_call" | custom-call | tf_op jit(solution)/shard_map/pallas_call | solution.py:356
  30.4 4.5 %all-to-all-done = bf16[32,8,1024]{2,1,0:T(8,128)(2,1)} async-done(((bf16[32,8,1024]{2,1,0:T(8,128)(2,1)}), bf16[32,8,1024]{2,1,0:T(8,128)(2,1)}, u32[]{:S(2)}, u32[]{:S(2)}) %all-to-all-start) | async-done | bytes 524320 | tf_op jit(solution)/shard_map/all_to_all | solution.py:1184
  36.2 2.9 shard_map.189
  39.7 3.4 all-to-all-start.1
  43.3 9.5 %collective-permute-done.r1 = bf16[256,1024]{1,0:T(8,128)(2,1)} collective-permute-done((bf16[256,1024]{1,0:T(8,128)(2,1)}, bf16[256,1024]{1,0:T(8,128)(2,1)}, u32[]{:S(2)}, u32[]{:S(2)}) %collective-permute-start) | collective-permute-done | bytes 524320 | tf_op jit(solution)/shard_map/ppermute | solution.py:21
  54.6 3.3 collective-permute-start.11
  57.9 2.1 collective-permute-start.12
  60.0 1.7 collective-permute-done.5.w3
  61.7 4.1 %collective-permute-start.13 = (bf16[256,1024]{1,0:T(8,128)(2,1)}, bf16[256,1024]{1,0:T(8,128)(2,1)}, u32[]{:S(2)}, u32[]{:S(2)}) collective-permute-start(bf16[256,1024]{1,0:T(8,128)(2,1)} %param.21), channel_id=1, source_target_pairs={{0,1},{5,4},{10,11},{15,14},{16,17},{21,20},{26,27},{31,30}} | collective-permute-start | bytes 1572872 | tf_op jit(solution)/shard_map/ppermute | solution.py:569
  66.8 10.1 %shard_map.190 = (bf16[4,256,1024]{2,1,0:T(8,128)(2,1)}, bf16[4,256,1024]{2,1,0:T(8,128)(2,1)}, f32[4,256,256]{2,1,0:T(8,128)}, f32[4,256,256]{2,1,0:T(8,128)}, ...) custom-call(s32[8]{0:T(128)S(1)} %stack.23.info, ...), custom_call_target="tpu_custom_call" | custom-call | tf_op jit(solution)/shard_map/pallas_call | solution.py:356
  78.6 3.5 collective-permute-done.7
  84.7 4.1 %collective-permute-done.9 = bf16[2,128,128]{2,1,0:T(8,128)(2,1)S(1)} collective-permute-done((bf16[2,128,128]{2,1,0:T(8,128)(2,1)S(1)}, bf16[2,128,128]{2,1,0:T(8,128)(2,1)S(1)}, u32[]{:S(2)}, u32[]{:S(2)}) %collective-permute-start.9) | collective-permute-done | bytes 65568 | tf_op jit(solution)/shard_map/ppermute | solution.py:1212
  89.5 2.4 collective-permute-start.10
  93.2 2.8 shard_map.191.local
  96.0 1.5 collective-permute-done.10
  98.3 3.7 %shard_map.192 = (f32[4,256,256]{2,1,0:T(8,128)S(1)}, bf16[4,256,256]{2,1,0:T(8,128)(2,1)S(1)}, bf16[2,256,1024]{2,1,0:T(8,128)(2,1)S(1)}, bf16[2,256,1024]{2,1,0:T(8,128)(2,1)S(1)}) custom-call(s32[8]{0:T(128)S(1)} %stack.23.info, s32[8]{0:T(128)S(1)} %select_reduce_fusion.ends, f32[8]{0:T(128)S(1)} %copy-done.34, f32[4,256,256]{2,1,0:T(8,128)S(1)} %shard_map.191.local, ...), custom_call_target="tpu_custom_call" | custom-call | tf_op jit(solution)/shard_map/pallas_call | solution.py:356
  103.0 2.7 collective-permute-done.14
  106.1 1.9 collective-permute-start.15
  108.5 2.3 collective-permute-done.16.g2
  112.4 3.5 shard_map.193.g
  115.9 1.4 copy-done
  117.3 14.2 %collective-permute-done.15 = bf16[2,256,1024]{2,1,0:T(8,128)(2,1)S(1)} collective-permute-done((bf16[2,256,1024]{2,1,0:T(8,128)(2,1)S(1)}, bf16[2,256,1024]{2,1,0:T(8,128)(2,1)S(1)}, u32[]{:S(2)}, u32[]{:S(2)}) %collective-permute-start.15) | collective-permute-done | bytes 1048608 | tf_op jit(solution)/shard_map/ppermute | solution.py:21
  131.9 2.8 collective-permute-done.18.tb
  134.7 17.5 %shard_map.195 = (bf16[4,256,1024]{2,1,0:T(8,128)(2,1)S(1)}, bf16[4,256,704]{2,1,0:T(8,128)(2,1)S(1)}, bf16[4,256,704]{2,1,0:T(8,128)(2,1)S(1)}, bf16[4,256,704]...) custom-call(s32[8]{0:T(128)S(1)} %stack.23.info, ...), custom_call_target="tpu_custom_call" | custom-call | tf_op jit(solution)/shard_map/pallas_call | solution.py:356
  152.4 3.6 shard_map.198
  156.0 1.5 collective-permute-start.23
  157.9 1.8 collective-permute-start.22
  160.4 3.6 shard_map.196
  164.9 3.0 shard_map.197
  167.9 6.6 %collective-permute-done.23 = bf16[2,704,256]{2,1,0:T(8,128)(2,1)S(1)} collective-permute-done((bf16[2,704,256]{2,1,0:T(8,128)(2,1)S(1)}, bf16[2,704,256]{2,1,0:T(8,128)(2,1)S(1)}, u32[]{:S(2)}, u32[]{:S(2)}) %collective-permute-start.23) | collective-permute-done | bytes 720928 | tf_op jit(solution)/shard_map/ppermute | solution.py:21
  174.7 8.4 %collective-permute-done.22 = bf16[2,256,1024]{2,1,0:T(8,128)(2,1)S(1)} collective-permute-done((bf16[2,256,1024]{2,1,0:T(8,128)(2,1)S(1)}, bf16[2,256,1024]{2,1,0:T(8,128)(2,1)S(1)}, u32[]{:S(2)}, u32[]{:S(2)}) %collective-permute-start.22) | collective-permute-done | bytes 1048608 | tf_op jit(solution)/shard_map/ppermute | solution.py:21
  185.8 1.7 collective-permute-start.24
  189.5 8.1 %shard_map.199 = (bf16[4,256,1024]{2,1,0:T(8,128)(2,1)S(1)}, bf16[4,256,256]{2,1,0:T(8,128)(2,1)S(1)}, bf16[4,256,256]{2,1,0:T(8,128)(2,1)S(1)}, f32[4,2,128,128...) custom-call(s32[8]{0:T(128)S(1)} %stack.23.info, s32[8]{0:T(128)S(1)} %select_reduce_fusion.ends, ...), custom_call_target="tpu_custom_call" | custom-call | tf_op jit(solution)/shard_map/pallas_call | solution.py:356
  199.5 1.7 collective-permute-start.30
  201.3 4.3 %shard_map.201 = (f32[4,256,256]{2,1,0:T(8,128)S(1)}, f32[4,256,256]{2,1,0:T(8,128)S(1)}, f32[4,256,256]{2,1,0:T(8,128)S(1)}) custom-call(s32[8]{0:T(128)S(1)} %stack.23.info, s32[8]{0:T(128)S(1)} %select_reduce_fusion.ends, f32[8]{0:T(128)S(1)} %copy-done.34, bf16[4,256,256]{2,1,0:T(8,128)(2,1)S(1)} %copy-done.5, bf16[4,256,256]{2,1,0:T(8,128)(2,1)S(1)} %copy-done.10, ...), custom_call_target="tpu_custom_call" | custom-call | tf_op jit(solution)/shard_map/pallas_call | solution.py:356
  207.3 3.2 shard_map.200
  210.7 4.3 %collective-permute-done.31 = bf16[704,256]{1,0:T(8,128)(2,1)S(1)} collective-permute-done((bf16[704,256]{1,0:T(8,128)(2,1)S(1)}, bf16[704,256]{1,0:T(8,128)(2,1)S(1)}, u32[]{:S(2)}, u32[]{:S(2)}) %collective-permute-start.31) | collective-permute-done | bytes 360480 | tf_op jit(solution)/shard_map/ppermute | solution.py:21
  215.3 7.3 %shard_map.202 = (bf16[4,256,768]{2,1,0:T(8,128)(2,1)S(1)}, bf16[2,256,1024]{2,1,0:T(8,128)(2,1)S(1)}, bf16[2,256,1024]{2,1,0:T(8,128)(2,1)S(1)}) custom-call(s32[8]{0:T(128)S(1)} %stack.23.info, s32[8]{0:T(128)S(1)} %select_reduce_fusion.ends, f32[8]{0:T(128)S(1)} %copy-done.34, f32[4,256,256]{2,1,0:T(8,128)S(1)} %get-tuple-element.145.gq, ...), custom_call_target="tpu_custom_call" | custom-call | tf_op jit(solution)/shard_map/pallas_call | solution.py:356
  227.3 2.0 collective-permute-start.41
  229.3 4.4 %shard_map.203 = (bf16[2,768,256]{2,1,0:T(8,128)(2,1)S(1)}, bf16[2,768,256]{2,1,0:T(8,128)(2,1)}) custom-call(s32[8]{0:T(128)S(1)} %stack.23.info, bf16[1024,1024]{1,0:T(8,128)(2,1)S(1)} %bitcast.114, bf16[1024,768]{1,0:T(8,128)(2,1)S(1)} %bitcast.122), custom_call_target="tpu_custom_call" | custom-call | tf_op jit(solution)/shard_map/pallas_call | solution.py:356
  233.7 1.4 collective-permute-start.36
  235.1 14.5 %collective-permute-done.35.got = bf16[256,1024]{1,0:T(8,128)(2,1)S(1)} collective-permute-done((bf16[256,1024]{1,0:T(8,128)(2,1)S(1)}, bf16[256,1024]{1,0:T(8,128)(2,1)S(1)}, u32[]{:S(2)}, u32[]{:S(2)}) %collective-permute-start.35) | collective-permute-done | bytes 524320 | tf_op jit(solution)/shard_map/ppermute | solution.py:21
  251.4 2.2 collective-permute-start.40
  254.8 6.6 %collective-permute-done.41 = bf16[1408,256]{1,0:T(8,128)(2,1)S(1)} collective-permute-done((bf16[1408,256]{1,0:T(8,128)(2,1)S(1)}, bf16[1408,256]{1,0:T(8,128)(2,1)S(1)}, u32[]{:S(2)}, u32[]{:S(2)}) %collective-permute-start.41) | collective-permute-done | bytes 720928 | tf_op jit(solution)/shard_map/ppermute | solution.py:21
  262.5 4.0 %all-to-all-start.3 = ((bf16[32,8,1024]{2,1,0:T(8,128)(2,1)}), bf16[32,8,1024]{2,1,0:T(8,128)(2,1)}, u32[]{:S(2)}, u32[]{:S(2)}) async-start(bf16[32,8,1024]{2,1,0:T(8,128)(2,1)} %bitcast.120), calls=%async_computation.3 | async-start | bytes 1048576 | tf_op jit(solution)/shard_map/all_to_all | solution.py:1184
  269.9 2.5 collective-permute-start.44
  272.5 1.5 add_convert_fusion.4
  277.4 17.5 %all-to-all-done.3 = bf16[32,8,1024]{2,1,0:T(8,128)(2,1)} async-done(((bf16[32,8,1024]{2,1,0:T(8,128)(2,1)}), bf16[32,8,1024]{2,1,0:T(8,128)(2,1)}, u32[]{:S(2)}, u32[]{:S(2)}) %all-to-all-start.3) | async-done | bytes 524320 | tf_op jit(solution)/shard_map/all_to_all | solution.py:1184
  294.9 4.2 %all-to-all-start.2 = ((bf16[32,8,1024]{2,1,0:T(8,128)(2,1)}), bf16[32,8,1024]{2,1,0:T(8,128)(2,1)S(1)}, u32[]{:S(2)}, u32[]{:S(2)}) async-start(bf16[32,8,1024]{2,1,0:T(8,128)(2,1)} %bitcast.121), calls=%async_computation.2 | async-start | bytes 1048576 | tf_op jit(solution)/shard_map/all_to_all | solution.py:1184
  299.1 2.2 shard_map.207
  301.4 12.7 %collective-permute-done.44 = bf16[1216,256]{1,0:T(8,128)(2,1)} collective-permute-done((bf16[1216,256]{1,0:T(8,128)(2,1)}, bf16[1216,256]{1,0:T(8,128)(2,1)}, u32[]{:S(2)}, u32[]{:S(2)}) %collective-permute-start.44) | collective-permute-done | bytes 622624 | tf_op jit(solution)/shard_map/ppermute | solution.py:21
  316.7 2.4 collective-permute-start.38
  319.3 20.8 %collective-permute-done.46.p2.d2 = bf16[1216,256]{1,0:T(8,128)(2,1)S(1)} collective-permute-done((bf16[1216,256]{1,0:T(8,128)(2,1)S(1)}, bf16[1216,256]{1,0:T(8,128)(2,1)S(1)}, u32[]{:S(2)}, u32[]{:S(2)}) %collective-permute-start.46) | collective-permute-done | bytes 622624 | tf_op jit(solution)/shard_map/ppermute | solution.py:21
  343.8 1.4 collective-permute-start.54
  345.2 1.4 collective-permute-start.53
  347.4 6.0 %shard_map.208 = f32[256,5632]{1,0:T(8,128)} custom-call(s32[8]{0:T(128)S(1)} %stack.23.info, bf16[1408,256]{1,0:T(8,128)(2,1)} %add_convert_fusion.5.p0, bf16[1408,256]{1,0:T(8,128)(2,1)} %collective-permute-done.50.p1, bf16[1408,256]{1,0:T(8,128)(2,1)} %collective-permute-done.45.p2, bf16[1408,256]{1,0:T(8,128)(2,1)} %collective-permute-done.47.p3), custom_call_target="tpu_custom_call" | custom-call | tf_op jit(solution)/shard_map/pallas_call | solution.py:356
  353.4 3.9 %shard_map.209 = f32[704,1024]{1,0:T(8,128)} custom-call(s32[8]{0:T(128)S(1)} %stack.23.info, bf16[1216,256]{1,0:T(8,128)(2,1)} %copy-done.35, bf16[1216,256]{1,0:T(8,128)(2,1)} %copy-done.36, bf16[1216,256]{1,0:T(8,128)(2,1)} %copy-done.38, bf16[1216,256]{1,0:T(8,128)(2,1)} %copy-done.37), custom_call_target="tpu_custom_call" | custom-call | tf_op jit(solution)/shard_map/pallas_call | solution.py:356
  358.0 1.3 collective-permute-done.56.q3
  360.1 5.4 %shard_map.210 = (f32[256,1024]{1,0:T(8,128)}, f32[256,1024]{1,0:T(8,128)}, f32[256,1024]{1,0:T(8,128)}, f32[256,1024]{1,0:T(8,128)}, f32[256,1024]{1,0:T(8,128)}) custom-call(s32[8]{0:T(128)S(1)} %stack.23.info, bf16[768,256]{1,0:T(8,128)(2,1)} %copy-done.47, bf16[768,256]{1,0:T(8,128)(2,1)} %copy-done.55, bf16[768,256]{1,0:T(8,128)(2,1)} %copy-done.54, ...), custom_call_target="tpu_custom_call" | custom-call | tf_op jit(solution)/shard_map/pallas_call | solution.py:356
  (282 shorter events, 52.3 us)
Async XLA Ops:
  11.2 23.7 %all-to-all-start = ((bf16[32,8,1024]{2,1,0:T(8,128)(2,1)}), bf16[32,8,1024]{2,1,0:T(8,128)(2,1)}, u32[]{:S(2)}, u32[]{:S(2)}) async-start(bf16[32,8,1024]{2,1,0:T(8,128)(2,1)} %bitcast.6), calls=%async_computation | async-start | bytes 1048576 | tf_op jit(solution)/shard_map/all_to_all | solution.py:1184
  18.7 116.1 %all-gather.3.cloned.1.call-start = ((), (), s32[]{:S(2)}) async-start(), calls=%async_computation.4 | async-start | bytes 5406720 | tf_op jit(solution)/shard_map/all_gather | solution.py:1239
  20.4 34.2 %collective-permute-start.3 = (bf16[1024,256]{1,0:T(8,128)(2,1)S(1)}, bf16[1024,256]{1,0:T(8,128)(2,1)S(1)}, u32[]{:S(2)}, u32[]{:S(2)}) collective-permute-start(bf16[1024,256]{1,0:T(8,128)(2,1)S(1)} %shard_map.188.w0), channel_id=1, source_target_pairs={{0,1},{1,0},{2,3},{3,2},{4,5},{5,4},{6,7},{7,6},{8,9},{9,8},{10,11... | collective-permute-start | bytes 1572872 | tf_op jit(solution)/shard_map/ppermute | solution.py:21
  22.2 35.7 %collective-permute-start.4 = (bf16[1024,256]{1,0:T(8,128)(2,1)S(1)}, bf16[1024,256]{1,0:T(8,128)(2,1)S(1)}, u32[]{:S(2)}, u32[]{:S(2)}) collective-permute-start(bf16[1024,256]{1,0:T(8,128)(2,1)S(1)} %shard_map.188.w0), channel_id=1, source_target_pairs={{0,2},{1,3},{2,0},{3,1},{4,6},{5,7},{6,4},{7,5},{8,10},{9,11},{10,... | collective-permute-start | bytes 1572872 | tf_op jit(solution)/shard_map/ppermute | solution.py:21
  23.6 38.0 %collective-permute-start.5 = (bf16[1024,256]{1,0:T(8,128)(2,1)S(1)}, bf16[1024,256]{1,0:T(8,128)(2,1)}, u32[]{:S(2)}, u32[]{:S(2)}) collective-permute-start(bf16[1024,256]{1,0:T(8,128)(2,1)S(1)} %shard_map.188.w0), channel_id=1, source_target_pairs={{0,3},{1,2},{2,1},{3,0},{4,7},{5,6},{6,5},{7,4},{8,11},{9,10},{10,... | collective-permute-start | bytes 1572872 | tf_op jit(solution)/shard_map/ppermute | solution.py:21
  35.0 17.8 %collective-permute-start = (bf16[256,1024]{1,0:T(8,128)(2,1)}, bf16[256,1024]{1,0:T(8,128)(2,1)}, u32[]{:S(2)}, u32[]{:S(2)}) collective-permute-start(bf16[256,1024]{1,0:T(8,128)(2,1)} %bitcast.7.r0), channel_id=1, source_target_pairs={{0,8},{8,0},{1,9},{9,1},{2,10},{10,2},{3,11},{11,3},{4,12},{12,4},... | collective-permute-start | bytes 1572872 | tf_op jit(solution)/shard_map/ppermute | solution.py:21
  39.0 37.8 %copy-start.6 = (bf16[4,256,256]{2,1,0:T(8,128)(2,1)}, bf16[4,256,256]{2,1,0:T(8,128)(2,1)S(1)}, u32[]{:S(2)}) copy-start(bf16[4,256,256]{2,1,0:T(8,128)(2,1)S(1)} %get-tuple-element.156.enter) | copy-start | bytes 1572868
  39.7 43.6 %all-to-all-start.1 = ((bf16[32,8,1024]{2,1,0:T(8,128)(2,1)}), bf16[32,8,1024]{2,1,0:T(8,128)(2,1)}, u32[]{:S(2)}, u32[]{:S(2)}) async-start(bf16[32,8,1024]{2,1,0:T(8,128)(2,1)} %bitcast.8), calls=%async_computation.1 | async-start | bytes 1048576 | tf_op jit(solution)/shard_map/all_to_all | solution.py:1184
  43.2 22.6 %collective-permute-start.1 = (bf16[256,1024]{1,0:T(8,128)(2,1)}, bf16[256,1024]{1,0:T(8,128)(2,1)S(1)}, u32[]{:S(2)}, u32[]{:S(2)}) collective-permute-start(bf16[256,1024]{1,0:T(8,128)(2,1)} %bitcast.7.r0), channel_id=1, source_target_pairs={{0,4},{4,0},{1,5},{5,1},{2,6},{6,2},{3,7},{7,3},{8,12},{12,8},{9,1... | collective-permute-start | bytes 1572872 | tf_op jit(solution)/shard_map/ppermute | solution.py:21
  52.8 13.0 %collective-permute-start.2 = (bf16[256,1024]{1,0:T(8,128)(2,1)}, bf16[256,1024]{1,0:T(8,128)(2,1)S(1)}, u32[]{:S(2)}, u32[]{:S(2)}) collective-permute-start(bf16[256,1024]{1,0:T(8,128)(2,1)} %collective-permute-done.r1), channel_id=1, source_target_pairs={{0,4},{4,0},{1,5},{5,1},{2,6},{6,2},{3,7},{7,3},{8,12},{12,8},{9,1... | collective-permute-start | bytes 1572872 | tf_op jit(solution)/shard_map/ppermute | solution.py:21
  54.6 37.2 %collective-permute-start.11 = (bf16[256,1024]{1,0:T(8,128)(2,1)}, bf16[256,1024]{1,0:T(8,128)(2,1)}, u32[]{:S(2)}, u32[]{:S(2)}) collective-permute-start(bf16[256,1024]{1,0:T(8,128)(2,1)} %param.21), channel_id=1, source_target_pairs={{0,3},{5,6},{10,9},{15,12},{16,19},{21,22},{26,25},{31,28}} | collective-permute-start | bytes 1572872 | tf_op jit(solution)/shard_map/ppermute | solution.py:569
  57.9 34.0 %collective-permute-start.12 = (bf16[256,1024]{1,0:T(8,128)(2,1)}, bf16[256,1024]{1,0:T(8,128)(2,1)}, u32[]{:S(2)}, u32[]{:S(2)}) collective-permute-start(bf16[256,1024]{1,0:T(8,128)(2,1)} %param.21), channel_id=1, source_target_pairs={{0,2},{5,7},{10,8},{15,13},{16,18},{21,23},{26,24},{31,29}} | collective-permute-start | bytes 1572872 | tf_op jit(solution)/shard_map/ppermute | solution.py:569
  61.7 30.2 %collective-permute-start.13 = (bf16[256,1024]{1,0:T(8,128)(2,1)}, bf16[256,1024]{1,0:T(8,128)(2,1)}, u32[]{:S(2)}, u32[]{:S(2)}) collective-permute-start(bf16[256,1024]{1,0:T(8,128)(2,1)} %param.21), channel_id=1, source_target_pairs={{0,1},{5,4},{10,11},{15,14},{16,17},{21,20},{26,27},{31,30}} | collective-permute-start | bytes 1572872 | tf_op jit(solution)/shard_map/ppermute | solution.py:569
  77.7 4.5 %collective-permute-start.7 = (bf16[2,128,128]{2,1,0:T(8,128)(2,1)S(1)}, bf16[2,128,128]{2,1,0:T(8,128)(2,1)S(1)}, u32[]{:S(2)}, u32[]{:S(2)}) collective-permute-start(bf16[2,128,128]{2,1,0:T(8,128)(2,1)S(1)} %get-tuple-element.106), channel_id=1, source_target_pairs={{0,1},{1,0},{2,3},{3,2},{4,5},{5,4},{6,7},{7,6},{8,9},{9,8},{10,11... | collective-permute-start | bytes 196616 | tf_op jit(solution)/shard_map/ppermute | solution.py:1212
  78.6 4.8 %collective-permute-start.8 = (bf16[2,128,128]{2,1,0:T(8,128)(2,1)S(1)}, bf16[2,128,128]{2,1,0:T(8,128)(2,1)S(1)}, u32[]{:S(2)}, u32[]{:S(2)}) collective-permute-start(bf16[2,128,128]{2,1,0:T(8,128)(2,1)S(1)} %get-tuple-element.106), channel_id=1, source_target_pairs={{0,2},{1,3},{2,0},{3,1},{4,6},{5,7},{6,4},{7,5},{8,10},{9,11},{10,... | collective-permute-start | bytes 196616 | tf_op jit(solution)/shard_map/ppermute | solution.py:1212
  82.2 6.5 %collective-permute-start.9 = (bf16[2,128,128]{2,1,0:T(8,128)(2,1)S(1)}, bf16[2,128,128]{2,1,0:T(8,128)(2,1)S(1)}, u32[]{:S(2)}, u32[]{:S(2)}) collective-permute-start(bf16[2,128,128]{2,1,0:T(8,128)(2,1)S(1)} %get-tuple-element.106), channel_id=1, source_target_pairs={{0,3},{1,2},{2,1},{3,0},{4,7},{5,6},{6,5},{7,4},{8,11},{9,10},{10,... | collective-permute-start | bytes 196616 | tf_op jit(solution)/shard_map/ppermute | solution.py:1212
  83.4 14.9 %collective-permute-start.6 = (bf16[256,1024]{1,0:T(8,128)(2,1)}, bf16[256,1024]{1,0:T(8,128)(2,1)S(1)}, u32[]{:S(2)}, u32[]{:S(2)}) collective-permute-start(bf16[256,1024]{1,0:T(8,128)(2,1)} %bitcast.9.g0), channel_id=1, source_target_pairs={{0,8},{8,0},{1,9},{9,1},{2,10},{10,2},{3,11},{11,3},{4,12},{12,4},... | collective-permute-start | bytes 1572872 | tf_op jit(solution)/shard_map/ppermute | solution.py:21
  89.5 8.0 %collective-permute-start.10 = (f32[2,128,128]{2,1,0:T(8,128)S(1)}, f32[2,128,128]{2,1,0:T(8,128)S(1)}, u32[]{:S(2)}, u32[]{:S(2)}) collective-permute-start(f32[2,128,128]{2,1,0:T(8,128)S(1)} %fusion.12), channel_id=1, source_target_pairs={{0,16},{16,0},{1,17},{17,1},{2,18},{18,2},{3,19},{19,3},{4,20},{20... | collective-permute-start | bytes 393224 | tf_op jit(solution)/shard_map/ppermute | solution.py:21
  103.0 2.7 collective-permute-start.14
  106.1 25.4 %collective-permute-start.15 = (bf16[2,256,1024]{2,1,0:T(8,128)(2,1)S(1)}, bf16[2,256,1024]{2,1,0:T(8,128)(2,1)S(1)}, u32[]{:S(2)}, u32[]{:S(2)}) collective-permute-start(bf16[2,256,1024]{2,1,0:T(8,128)(2,1)S(1)} %add_convert_fusion.3), channel_id=1, source_target_pairs={{0,8},{8,0},{1,9},{9,1},{2,10},{10,2},{3,11},{11,3},{4,12},{12,4},... | collective-permute-start | bytes 3145736 | tf_op jit(solution)/shard_map/ppermute | solution.py:21
  108.0 2.8 collective-permute-start.16
  108.0 2.8 collective-permute-start.17
  131.9 2.9 collective-permute-start.18
  152.2 5.3 %collective-permute-start.21 = (bf16[2,256,1024]{2,1,0:T(8,128)(2,1)S(1)}, bf16[2,256,1024]{2,1,0:T(8,128)(2,1)S(1)}, u32[]{:S(2)}, u32[]{:S(2)}) collective-permute-start(bf16[2,256,1024]{2,1,0:T(8,128)(2,1)S(1)} %get-tuple-element.114), channel_id=1, source_target_pairs={{0,4},{4,0},{1,5},{5,1},{2,6},{6,2},{3,7},{7,3},{8,12},{12,8},{9,1... | collective-permute-start | bytes 3145736 | tf_op jit(solution)/shard_map/ppermute | solution.py:21
  156.0 18.5 %collective-permute-start.23 = (bf16[2,704,256]{2,1,0:T(8,128)(2,1)S(1)}, bf16[2,704,256]{2,1,0:T(8,128)(2,1)S(1)}, u32[]{:S(2)}, u32[]{:S(2)}) collective-permute-start(bf16[2,704,256]{2,1,0:T(8,128)(2,1)S(1)} %get-tuple-element.124), channel_id=1, source_target_pairs={{0,1},{1,0},{2,3},{3,2},{4,5},{5,4},{6,7},{7,6},{8,9},{9,8},{10,11... | collective-permute-start | bytes 2162696 | tf_op jit(solution)/shard_map/ppermute | solution.py:21
  157.9 25.2 %collective-permute-start.22 = (bf16[2,256,1024]{2,1,0:T(8,128)(2,1)S(1)}, bf16[2,256,1024]{2,1,0:T(8,128)(2,1)S(1)}, u32[]{:S(2)}, u32[]{:S(2)}) collective-permute-start(bf16[2,256,1024]{2,1,0:T(8,128)(2,1)S(1)} %add_convert_fusion.1), channel_id=1, source_target_pairs={{0,8},{8,0},{1,9},{9,1},{2,10},{10,2},{3,11},{11,3},{4,12},{12,4},... | collective-permute-start | bytes 3145736 | tf_op jit(solution)/shard_map/ppermute | solution.py:21
  159.8 23.9 %collective-permute-start.19 = (bf16[256,1024]{1,0:T(8,128)(2,1)S(1)}, bf16[256,1024]{1,0:T(8,128)(2,1)S(1)}, u32[]{:S(2)}, u32[]{:S(2)}) collective-permute-start(bf16[256,1024]{1,0:T(8,128)(2,1)S(1)} %get-tuple-element.198), channel_id=1, source_target_pairs={{0,4},{4,0},{1,5},{5,1},{2,6},{6,2},{3,7},{7,3},{8,12},{12,8},{9,1... | collective-permute-start | bytes 1572872 | tf_op jit(solution)/shard_map/ppermute | solution.py:21
  159.9 23.8 %collective-permute-start.20 = (bf16[256,1024]{1,0:T(8,128)(2,1)S(1)}, bf16[256,1024]{1,0:T(8,128)(2,1)S(1)}, u32[]{:S(2)}, u32[]{:S(2)}) collective-permute-start(bf16[256,1024]{1,0:T(8,128)(2,1)S(1)} %get-tuple-element.197), channel_id=1, source_target_pairs={{0,4},{4,0},{1,5},{5,1},{2,6},{6,2},{3,7},{7,3},{8,12},{12,8},{9,1... | collective-permute-start | bytes 1572872 | tf_op jit(solution)/shard_map/ppermute | solution.py:21
  164.0 21.9 %collective-permute-start.25 = (bf16[2,704,256]{2,1,0:T(8,128)(2,1)S(1)}, bf16[2,704,256]{2,1,0:T(8,128)(2,1)S(1)}, u32[]{:S(2)}, u32[]{:S(2)}) collective-permute-start(bf16[2,704,256]{2,1,0:T(8,128)(2,1)S(1)} %get-tuple-element.118), channel_id=1, source_target_pairs={{0,2},{1,3},{2,0},{3,1},{4,6},{5,7},{6,4},{7,5},{8,10},{9,11},{10,... | collective-permute-start | bytes 2162696 | tf_op jit(solution)/shard_map/ppermute | solution.py:21
  183.6 4.3 %collective-permute-start.26 = (bf16[2,256,1024]{2,1,0:T(8,128)(2,1)S(1)}, bf16[2,256,1024]{2,1,0:T(8,128)(2,1)S(1)}, u32[]{:S(2)}, u32[]{:S(2)}) collective-permute-start(bf16[2,256,1024]{2,1,0:T(8,128)(2,1)S(1)} %add_convert_fusion.ua), channel_id=1, source_target_pairs={{0,4},{4,0},{1,5},{5,1},{2,6},{6,2},{3,7},{7,3},{8,12},{12,8},{9,1... | collective-permute-start | bytes 3145736 | tf_op jit(solution)/shard_map/ppermute | solution.py:21
  185.0 25.6 %collective-permute-start.27 = (bf16[704,256]{1,0:T(8,128)(2,1)S(1)}, bf16[704,256]{1,0:T(8,128)(2,1)S(1)}, u32[]{:S(2)}, u32[]{:S(2)}) collective-permute-start(bf16[704,256]{1,0:T(8,128)(2,1)S(1)} %slice_bitcast_fusion.11), channel_id=1, source_target_pairs={{0,2},{1,3},{2,0},{3,1},{4,6},{5,7},{6,4},{7,5},{8,10},{9,11},{10,... | collective-permute-start | bytes 1081352 | tf_op jit(solution)/shard_map/ppermute | solution.py:21
  185.8 20.9 %collective-permute-start.24 = (bf16[256,1024]{1,0:T(8,128)(2,1)S(1)}, bf16[256,1024]{1,0:T(8,128)(2,1)S(1)}, u32[]{:S(2)}, u32[]{:S(2)}) collective-permute-start(bf16[256,1024]{1,0:T(8,128)(2,1)S(1)} %get-tuple-element.127), channel_id=1, source_target_pairs={{0,8},{8,0},{1,9},{9,1},{2,10},{10,2},{3,11},{11,3},{4,12},{12,4},... | collective-permute-start | bytes 1572872 | tf_op jit(solution)/shard_map/ppermute | solution.py:21
  197.7 7.9 %collective-permute-start.28 = (bf16[2,128,128]{2,1,0:T(8,128)(2,1)S(1)}, bf16[2,128,128]{2,1,0:T(8,128)(2,1)S(1)}, u32[]{:S(2)}, u32[]{:S(2)}) collective-permute-start(bf16[2,128,128]{2,1,0:T(8,128)(2,1)S(1)} %get-tuple-element.133), channel_id=1, source_target_pairs={{0,1},{1,0},{2,3},{3,2},{4,5},{5,4},{6,7},{7,6},{8,9},{9,8},{10,11... | collective-permute-start | bytes 196616 | tf_op jit(solution)/shard_map/ppermute | solution.py:1212
  198.7 7.9 %collective-permute-start.29 = (bf16[2,128,128]{2,1,0:T(8,128)(2,1)S(1)}, bf16[2,128,128]{2,1,0:T(8,128)(2,1)S(1)}, u32[]{:S(2)}, u32[]{:S(2)}) collective-permute-start(bf16[2,128,128]{2,1,0:T(8,128)(2,1)S(1)} %get-tuple-element.133), channel_id=1, source_target_pairs={{0,2},{1,3},{2,0},{3,1},{4,6},{5,7},{6,4},{7,5},{8,10},{9,11},{10,... | collective-permute-start | bytes 196616 | tf_op jit(solution)/shard_map/ppermute | solution.py:1212
  199.5 7.1 %collective-permute-start.30 = (bf16[2,128,128]{2,1,0:T(8,128)(2,1)S(1)}, bf16[2,128,128]{2,1,0:T(8,128)(2,1)S(1)}, u32[]{:S(2)}, u32[]{:S(2)}) collective-permute-start(bf16[2,128,128]{2,1,0:T(8,128)(2,1)S(1)} %get-tuple-element.133), channel_id=1, source_target_pairs={{0,3},{1,2},{2,1},{3,0},{4,7},{5,6},{6,5},{7,4},{8,11},{9,10},{10,... | collective-permute-start | bytes 196616 | tf_op jit(solution)/shard_map/ppermute | solution.py:1212
  205.5 9.5 %collective-permute-start.31 = (bf16[704,256]{1,0:T(8,128)(2,1)S(1)}, bf16[704,256]{1,0:T(8,128)(2,1)S(1)}, u32[]{:S(2)}, u32[]{:S(2)}) collective-permute-start(bf16[704,256]{1,0:T(8,128)(2,1)S(1)} %slice_bitcast_fusion.10), channel_id=1, source_target_pairs={{0,1},{1,0},{2,3},{3,2},{4,5},{5,4},{6,7},{7,6},{8,9},{9,8},{10,11... | collective-permute-start | bytes 1081352 | tf_op jit(solution)/shard_map/ppermute | solution.py:21
  206.8 8.4 %collective-permute-start.32 = (f32[2,128,128]{2,1,0:T(8,128)S(1)}, f32[2,128,128]{2,1,0:T(8,128)S(1)}, u32[]{:S(2)}, u32[]{:S(2)}) collective-permute-start(f32[2,128,128]{2,1,0:T(8,128)S(1)} %fusion.15), channel_id=1, source_target_pairs={{0,16},{16,0},{1,17},{17,1},{2,18},{18,2},{3,19},{19,3},{4,20},{20... | collective-permute-start | bytes 393224 | tf_op jit(solution)/shard_map/ppermute | solution.py:21
  222.7 2.0 collective-permute-start.33
  222.7 2.6 collective-permute-start.34
  223.2 27.1 %collective-permute-start.39 = (bf16[2,704,256]{2,1,0:T(8,128)(2,1)S(1)}, bf16[2,704,256]{2,1,0:T(8,128)(2,1)S(1)}, u32[]{:S(2)}, u32[]{:S(2)}) collective-permute-start(bf16[2,704,256]{2,1,0:T(8,128)(2,1)S(1)} %get-tuple-element.160), channel_id=1, source_target_pairs={{0,1},{1,0},{2,3},{3,2},{4,5},{5,4},{6,7},{7,6},{8,9},{9,8},{10,11... | collective-permute-start | bytes 2162696 | tf_op jit(solution)/shard_map/ppermute | solution.py:21
  225.8 23.9 %collective-permute-start.35 = (bf16[256,1024]{1,0:T(8,128)(2,1)S(1)}, bf16[256,1024]{1,0:T(8,128)(2,1)S(1)}, u32[]{:S(2)}, u32[]{:S(2)}) collective-permute-start(bf16[256,1024]{1,0:T(8,128)(2,1)S(1)} %get-tuple-element.191), channel_id=1, source_target_pairs={{0,8},{8,0},{1,9},{9,1},{2,10},{10,2},{3,11},{11,3},{4,12},{12,4},... | collective-permute-start | bytes 1572872 | tf_op jit(solution)/shard_map/ppermute | solution.py:21
  226.1 27.5 %collective-permute-start.42 = (bf16[2,512,256]{2,1,0:T(8,128)(2,1)S(1)}, bf16[2,512,256]{2,1,0:T(8,128)(2,1)S(1)}, u32[]{:S(2)}, u32[]{:S(2)}) collective-permute-start(bf16[2,512,256]{2,1,0:T(8,128)(2,1)S(1)} %get-tuple-element.140), channel_id=1, source_target_pairs={{0,2},{1,3},{2,0},{3,1},{4,6},{5,7},{6,4},{7,5},{8,10},{9,11},{10,... | collective-permute-start | bytes 1572872 | tf_op jit(solution)/shard_map/ppermute | solution.py:21
  227.3 34.1 %collective-permute-start.41 = (bf16[1408,256]{1,0:T(8,128)(2,1)S(1)}, bf16[1408,256]{1,0:T(8,128)(2,1)S(1)}, u32[]{:S(2)}, u32[]{:S(2)}) collective-permute-start(bf16[1408,256]{1,0:T(8,128)(2,1)S(1)} %pad_maximum_fusion), channel_id=1, source_target_pairs={{0,16},{16,0},{1,17},{17,1},{2,18},{18,2},{3,19},{19,3},{4,20},{20... | collective-permute-start | bytes 2162696 | tf_op jit(solution)/shard_map/ppermute | solution.py:21
  233.7 38.7 %collective-permute-start.36 = (bf16[2,768,256]{2,1,0:T(8,128)(2,1)}, bf16[2,768,256]{2,1,0:T(8,128)(2,1)}, u32[]{:S(2)}, u32[]{:S(2)}) collective-permute-start(bf16[2,768,256]{2,1,0:T(8,128)(2,1)} %get-tuple-element.154), channel_id=1, source_target_pairs={{0,1},{1,0},{2,3},{3,2},{4,5},{5,4},{6,7},{7,6},{8,9},{9,8},{10,11... | collective-permute-start | bytes 2359304 | tf_op jit(solution)/shard_map/ppermute | solution.py:21
  251.4 16.3 %collective-permute-start.40 = (bf16[704,256]{1,0:T(8,128)(2,1)}, bf16[704,256]{1,0:T(8,128)(2,1)}, u32[]{:S(2)}, u32[]{:S(2)}) collective-permute-start(bf16[704,256]{1,0:T(8,128)(2,1)} %slice_bitcast_fusion.6), channel_id=1, source_target_pairs={{0,2},{1,3},{2,0},{3,1},{4,6},{5,7},{6,4},{7,5},{8,10},{9,11},{10,... | collective-permute-start | bytes 1081352 | tf_op jit(solution)/shard_map/ppermute | solution.py:21
  254.6 12.0 %collective-permute-start.43 = (bf16[512,256]{1,0:T(8,128)(2,1)S(1)}, bf16[512,256]{1,0:T(8,128)(2,1)}, u32[]{:S(2)}, u32[]{:S(2)}) collective-permute-start(bf16[512,256]{1,0:T(8,128)(2,1)S(1)} %slice_bitcast_fusion.13), channel_id=1, source_target_pairs={{0,1},{1,0},{2,3},{3,2},{4,5},{5,4},{6,7},{7,6},{8,9},{9,8},{10,11... | collective-permute-start | bytes 786440 | tf_op jit(solution)/shard_map/ppermute | solution.py:21
  262.5 38.9 %collective-permute-start.45 = (bf16[1408,256]{1,0:T(8,128)(2,1)}, bf16[1408,256]{1,0:T(8,128)(2,1)}, u32[]{:S(2)}, u32[]{:S(2)}) collective-permute-start(bf16[1408,256]{1,0:T(8,128)(2,1)} %add_convert_fusion.5.p0), channel_id=1, source_target_pairs={{0,8},{8,0},{1,9},{9,1},{2,10},{10,2},{3,11},{11,3},{4,12},{12,4},... | collective-permute-start | bytes 2162696 | tf_op jit(solution)/shard_map/ppermute | solution.py:21
  262.5 32.4 %all-to-all-start.3 = ((bf16[32,8,1024]{2,1,0:T(8,128)(2,1)}), bf16[32,8,1024]{2,1,0:T(8,128)(2,1)}, u32[]{:S(2)}, u32[]{:S(2)}) async-start(bf16[32,8,1024]{2,1,0:T(8,128)(2,1)} %bitcast.120), calls=%async_computation.3 | async-start | bytes 1048576 | tf_op jit(solution)/shard_map/all_to_all | solution.py:1184
  269.9 44.2 %collective-permute-start.44 = (bf16[1216,256]{1,0:T(8,128)(2,1)}, bf16[1216,256]{1,0:T(8,128)(2,1)}, u32[]{:S(2)}, u32[]{:S(2)}) collective-permute-start(bf16[1216,256]{1,0:T(8,128)(2,1)} %pad_maximum_fusion.1), channel_id=1, source_target_pairs={{0,16},{16,0},{1,17},{17,1},{2,18},{18,2},{3,19},{19,3},{4,20},{20... | collective-permute-start | bytes 1867784 | tf_op jit(solution)/shard_map/ppermute | solution.py:21
  274.8 40.7 %collective-permute-start.37 = (bf16[768,256]{1,0:T(8,128)(2,1)}, bf16[768,256]{1,0:T(8,128)(2,1)}, u32[]{:S(2)}, u32[]{:S(2)}) collective-permute-start(bf16[768,256]{1,0:T(8,128)(2,1)} %slice_bitcast_fusion.4), channel_id=1, source_target_pairs={{0,2},{1,3},{2,0},{3,1},{4,6},{5,7},{6,4},{7,5},{8,10},{9,11},{10,... | collective-permute-start | bytes 1179656 | tf_op jit(solution)/shard_map/ppermute | solution.py:21
  277.4 36.8 %copy-start.40 = (bf16[704,256]{1,0:T(8,128)(2,1)S(1)}, bf16[704,256]{1,0:T(8,128)(2,1)}, u32[]{:S(2)}) copy-start(bf16[704,256]{1,0:T(8,128)(2,1)} %copy-done.39) | copy-start | bytes 1081348
  294.9 45.7 %all-to-all-start.2 = ((bf16[32,8,1024]{2,1,0:T(8,128)(2,1)}), bf16[32,8,1024]{2,1,0:T(8,128)(2,1)S(1)}, u32[]{:S(2)}, u32[]{:S(2)}) async-start(bf16[32,8,1024]{2,1,0:T(8,128)(2,1)} %bitcast.121), calls=%async_computation.2 | async-start | bytes 1048576 | tf_op jit(solution)/shard_map/all_to_all | solution.py:1184
  315.4 24.7 %collective-permute-start.46 = (bf16[1216,256]{1,0:T(8,128)(2,1)S(1)}, bf16[1216,256]{1,0:T(8,128)(2,1)S(1)}, u32[]{:S(2)}, u32[]{:S(2)}) collective-permute-start(bf16[1216,256]{1,0:T(8,128)(2,1)S(1)} %add_convert_fusion.9.p0.d0), channel_id=1, source_target_pairs={{0,8},{8,0},{1,9},{9,1},{2,10},{10,2},{3,11},{11,3},{4,12},{12,4},... | collective-permute-start | bytes 1867784 | tf_op jit(solution)/shard_map/ppermute | solution.py:21
  315.4 26.2 %collective-permute-start.47 = (bf16[1408,256]{1,0:T(8,128)(2,1)}, bf16[1408,256]{1,0:T(8,128)(2,1)}, u32[]{:S(2)}, u32[]{:S(2)}) collective-permute-start(bf16[1408,256]{1,0:T(8,128)(2,1)} %collective-permute-done.45.p2), channel_id=1, source_target_pairs={{0,4},{4,0},{1,5},{5,1},{2,6},{6,2},{3,7},{7,3},{8,12},{12,8},{9,1... | collective-permute-start | bytes 2162696 | tf_op jit(solution)/shard_map/ppermute | solution.py:21
  316.7 25.0 %collective-permute-start.38 = (bf16[768,256]{1,0:T(8,128)(2,1)S(1)}, bf16[768,256]{1,0:T(8,128)(2,1)}, u32[]{:S(2)}, u32[]{:S(2)}) collective-permute-start(bf16[768,256]{1,0:T(8,128)(2,1)S(1)} %fusion.2), channel_id=1, source_target_pairs={{0,16},{16,0},{1,17},{17,1},{2,18},{18,2},{3,19},{19,3},{4,20},{20... | collective-permute-start | bytes 1179656 | tf_op jit(solution)/shard_map/ppermute | solution.py:21
  319.1 23.8 %collective-permute-start.51 = (bf16[1216,256]{1,0:T(8,128)(2,1)S(1)}, bf16[1216,256]{1,0:T(8,128)(2,1)S(1)}, u32[]{:S(2)}, u32[]{:S(2)}) collective-permute-start(bf16[1216,256]{1,0:T(8,128)(2,1)S(1)} %add_convert_fusion.9.p0.d0), channel_id=1, source_target_pairs={{0,4},{4,0},{1,5},{5,1},{2,6},{6,2},{3,7},{7,3},{8,12},{12,8},{9,1... | collective-permute-start | bytes 1867784 | tf_op jit(solution)/shard_map/ppermute | solution.py:21
  340.1 2.9 collective-permute-start.52
  340.1 7.3 %collective-permute-start.50 = (bf16[1408,256]{1,0:T(8,128)(2,1)}, bf16[1408,256]{1,0:T(8,128)(2,1)}, u32[]{:S(2)}, u32[]{:S(2)}) collective-permute-start(bf16[1408,256]{1,0:T(8,128)(2,1)} %add_convert_fusion.5.p0), channel_id=1, source_target_pairs={{0,4},{4,0},{1,5},{5,1},{2,6},{6,2},{3,7},{7,3},{8,12},{12,8},{9,1... | collective-permute-start | bytes 2162696 | tf_op jit(solution)/shard_map/ppermute | solution.py:21
  342.8 14.6 %collective-permute-start.49 = (bf16[768,256]{1,0:T(8,128)(2,1)S(1)}, bf16[768,256]{1,0:T(8,128)(2,1)S(1)}, u32[]{:S(2)}, u32[]{:S(2)}) collective-permute-start(bf16[768,256]{1,0:T(8,128)(2,1)S(1)} %add_convert_fusion.11.q0), channel_id=1, source_target_pairs={{0,8},{8,0},{1,9},{9,1},{2,10},{10,2},{3,11},{11,3},{4,12},{12,4},... | collective-permute-start | bytes 1179656 | tf_op jit(solution)/shard_map/ppermute | solution.py:21
  343.8 13.6 %collective-permute-start.54 = (bf16[256,256]{1,0:T(8,128)(2,1)S(1)}, bf16[256,256]{1,0:T(8,128)(2,1)S(1)}, u32[]{:S(2)}, u32[]{:S(2)}) collective-permute-start(bf16[256,256]{1,0:T(8,128)(2,1)S(1)} %get-tuple-element.188), channel_id=1, source_target_pairs={{0,2},{1,3},{2,0},{3,1},{4,6},{5,7},{6,4},{7,5},{8,10},{9,11},{10,... | collective-permute-start | bytes 393224 | tf_op jit(solution)/shard_map/ppermute | solution.py:21
  345.2 12.2 %collective-permute-start.53 = (bf16[256,256]{1,0:T(8,128)(2,1)S(1)}, bf16[256,256]{1,0:T(8,128)(2,1)S(1)}, u32[]{:S(2)}, u32[]{:S(2)}) collective-permute-start(bf16[256,256]{1,0:T(8,128)(2,1)S(1)} %get-tuple-element.190), channel_id=1, source_target_pairs={{0,1},{1,0},{2,3},{3,2},{4,5},{5,4},{6,7},{7,6},{8,9},{9,8},{10,11... | collective-permute-start | bytes 393224 | tf_op jit(solution)/shard_map/ppermute | solution.py:21
  346.6 10.8 %collective-permute-start.55 = (bf16[256,256]{1,0:T(8,128)(2,1)S(1)}, bf16[256,256]{1,0:T(8,128)(2,1)S(1)}, u32[]{:S(2)}, u32[]{:S(2)}) collective-permute-start(bf16[256,256]{1,0:T(8,128)(2,1)S(1)} %get-tuple-element.189), channel_id=1, source_target_pairs={{0,3},{1,2},{2,1},{3,0},{4,7},{5,6},{6,5},{7,4},{8,11},{9,10},{10,... | collective-permute-start | bytes 393224 | tf_op jit(solution)/shard_map/ppermute | solution.py:21
  353.4 4.7 %collective-permute-start.48 = (bf16[768,256]{1,0:T(8,128)(2,1)S(1)}, bf16[768,256]{1,0:T(8,128)(2,1)S(1)}, u32[]{:S(2)}, u32[]{:S(2)}) collective-permute-start(bf16[768,256]{1,0:T(8,128)(2,1)S(1)} %add_convert_fusion.11.q0), channel_id=1, source_target_pairs={{0,4},{4,0},{1,5},{5,1},{2,6},{6,2},{3,7},{7,3},{8,12},{12,8},{9,1... | collective-permute-start | bytes 1179656 | tf_op jit(solution)/shard_map/ppermute | solution.py:21
  357.5 1.9 collective-permute-start.56
  (68 other events, 468.2 us)
Sparse Core Ops, SparseCore 0:
  35.0 72.7 all-gather.2
